TPU v7x, 32 devices: a whole 2x2x4 slice. The times are simulated.
32 devices in a mesh: seq: 8 (over y, x, core), tp: 4 (over z).
Axes of the slice: x: 2, y: 2, z: 4, core: 2. Of those that a mesh axis runs over, the one named last changes fastest.
Arguments:
- block_input: bfloat16 [4, 4096, 1792], P(None, 'seq'), may hold values from -6 to 6
- gain_first: bfloat16 [1792], replicated, may hold values from 0.5 to 1.5
- frozen_mixer_weight: bfloat16 [1792, 16, 704], P(None, 'tp'), may hold values from -0.125 to 0.125
- conv_filter: bfloat16 [3, 1792], P(None, 'tp'), may hold values from -2.5 to 2.5
- frozen_output_weight: bfloat16 [1792, 1792], P('tp'), may hold values from -0.125 to 0.125
- gain_second: bfloat16 [1792], replicated, may hold values from 0.5 to 1.5
- frozen_gate_up_weight: bfloat16 [1792, 2, 4864], P(None, None, 'tp'), may hold values from -0.125 to 0.125
- frozen_down_weight: bfloat16 [4864, 1792], P('tp'), may hold values from -0.15625 to 0.15625
- mixer_left: bfloat16 [8, 1792, 16], replicated, may hold values from -0.125 to 0.125
- mixer_right: bfloat16 [8, 16, 16, 704], P(None, None, 'tp'), may hold values from -0.75 to 0.75
- output_left: bfloat16 [8, 1792, 16], P(None, 'tp'), may hold values from -0.125 to 0.125
- output_right: bfloat16 [8, 16, 1792], replicated, may hold values from -0.75 to 0.75
- gateup_left: bfloat16 [8, 1792, 16], replicated, may hold values from -0.125 to 0.125
- gateup_right: bfloat16 [8, 16, 2, 4864], P(None, None, None, 'tp'), may hold values from -0.75 to 0.75
- down_left: bfloat16 [8, 4864, 16], P(None, 'tp'), may hold values from -0.15625 to 0.15625
- down_right: bfloat16 [8, 16, 1792], replicated, may hold values from -0.75 to 0.75
- adapter_index: int32 [4], replicated, may hold values from 0 to 7, as said below
- seq_lengths: int32 [4], replicated, may hold values from 2048 to 4096, as said below
- out_cotangent: bfloat16 [4, 4096, 1792], P(None, 'seq'), may hold values from -6 to 6
Outputs:
- block_output: bfloat16 [4, 4096, 1792], P(None, 'seq')
- input_grad: bfloat16 [4, 4096, 1792], P(None, 'seq')
- grad_mixer_left: float32 [8, 1792, 16], replicated
- grad_mixer_right: float32 [8, 16, 16, 704], P(None, None, 'tp')
- grad_output_left: float32 [8, 1792, 16], P(None, 'tp')
- grad_output_right: float32 [8, 16, 1792], replicated
- grad_gateup_left: float32 [8, 1792, 16], replicated
- grad_gateup_right: float32 [8, 16, 2, 4864], P(None, None, None, 'tp')
- grad_down_left: float32 [8, 4864, 16], P(None, 'tp')
- grad_down_right: float32 [8, 16, 1792], replicated
Inputs may be any that keep to these rules, and one draw needn't show every extreme that they name: `adapter_index`: different sequences use different adapters; one sequence uses adapter 8 - 1. `seq_lengths`: one sequence of every draw is full (4096); if there are two or more, another has 2048.
All inputs are finite; a program needn't handle non-finite values.
Results may differ from a plain program's by a relative error of at most 0.025.
Values may be sent and summed in bfloat16 or wider, within the bound.
A program may use at most 576 MiB of HBM per device.

v0:
```python
import jax
import jax.numpy as jnp
import numpy as np
from jax import lax
from jax.sharding import PartitionSpec as P

HD = 112
FD = 16
R = 16
NA = 8
KW = 3
WIN = 64
HCOLS = 704


epsilon = 1e-05
masked = -1e30
highest_precision = lax.Precision.HIGHEST


def from_behind(array, axis, by):
    count = lax.axis_size(axis)
    pairs = [(i, i + by) for i in range(count) if 0 <= i + by < count]
    return lax.ppermute(array, axis, pairs)


def carried_in(array, axis, join, neutral, backward):
    count = lax.axis_size(axis)
    place = lax.axis_index(axis)
    ahead = count - 1 - place if backward else place
    gathered = lax.all_gather(array.astype(jnp.bfloat16), axis)
    state = jnp.zeros_like(array) + jnp.asarray(neutral, array.dtype)

    def one(hop, state):
        source = count - 1 - hop if backward else hop
        return join(state, lax.dynamic_index_in_dim(gathered, source, 0, False).astype(array.dtype))

    return lax.fori_loop(0, ahead, one, state)


def taylor(vector):
    leading, trailing = np.triu_indices(vector.shape[-1])
    weights = np.where(leading == trailing, np.sqrt(0.5), 1.0).astype(np.float32)
    square_terms = vector[..., leading] * vector[..., trailing] * weights
    constant = jnp.ones(vector.shape[:-1] + (1,), jnp.float32)
    return jnp.concatenate([constant, vector, square_terms], -1)


def norm_rows(vector, gain_vector):
    row_scale = lax.rsqrt(jnp.mean(vector * vector, -1, keepdims=True) + epsilon)
    return (vector * row_scale * gain_vector, row_scale)


def norm_back(vector, row_scale, gain_vector, upstream):
    inner_mean = jnp.mean(vector * gain_vector * upstream, -1, keepdims=True)
    return (
        row_scale * gain_vector * upstream - vector * row_scale * row_scale * row_scale * inner_mean
    )


def silu_slope(vector):
    sigmoid = jax.nn.sigmoid(vector)
    return sigmoid * (1.0 + vector * (1.0 - sigmoid))


def add_states(earlier_part, later_part):
    return earlier_part + later_part


def slices(projected_rows):
    query_lin = projected_rows[..., :FD] * FD ** (-0.25)
    key_lin = projected_rows[..., FD : 2 * FD] * FD ** (-0.25)
    column = 2 * FD
    return [query_lin, key_lin] + [
        projected_rows[..., column + HD * number : column + HD * (number + 1)]
        for number in range(6)
    ]


def flat_dot(left_rows, matrix):
    lead_shape = left_rows.shape[:-1]
    result = jnp.dot(
        left_rows.reshape(-1, left_rows.shape[-1]), matrix, preferred_element_type=jnp.float32
    )
    return result.reshape(lead_shape + (matrix.shape[1],))


def flat_dot_back(left_rows, matrix):
    lead_shape = left_rows.shape[:-1]
    result = jnp.einsum(
        "lc,dc->ld",
        left_rows.reshape(-1, left_rows.shape[-1]),
        matrix,
        preferred_element_type=jnp.float32,
    )
    return result.reshape(lead_shape + (matrix.shape[0],))


def mixer_input(xfull, gain_vector, left_adapter_table, right_table, weight):
    sequences, length, hidden_model_width = xfull.shape
    normed, row_scale = norm_rows(xfull, gain_vector)
    rounded_values = normed.astype(jnp.bfloat16)
    rank_part = jnp.einsum(
        "foc,fcn->fon", rounded_values, left_adapter_table, preferred_element_type=jnp.float32
    ).astype(jnp.bfloat16)
    projected_rows = flat_dot(rounded_values, weight.reshape(hidden_model_width, -1))
    projected_rows = projected_rows + jnp.einsum(
        "slr,src->slc",
        rank_part,
        right_table.reshape(sequences, R, -1),
        preferred_element_type=jnp.float32,
    )
    return (
        row_scale,
        rounded_values,
        rank_part,
        projected_rows.reshape(sequences, length, weight.shape[1], weight.shape[2]),
    )


def mixer_parts(pieces, lin_feats, received, prior_state, conv_filter, first_row):
    feat_query, feat_key, value_round = lin_feats
    query_win, key_win, value_win, conv_input, conv_gate = pieces[3:]
    length = value_round.shape[1]
    causal = jnp.tril(jnp.ones((length, length), jnp.bool_))
    lin_scores = jnp.einsum(
        "slhf,smhf->shlm", feat_query, feat_key, preferred_element_type=jnp.float32
    )
    lin_scores = jnp.where(causal, lin_scores, 0.0)
    numerator = jnp.einsum(
        "shlm,smhd->slhd", lin_scores, value_round.astype(jnp.float32), precision=highest_precision
    )
    numerator = numerator + jnp.einsum(
        "slhf,shfd->slhd", feat_query.astype(jnp.float32), prior_state, precision=highest_precision
    )
    lin_scale = lax.rsqrt(jnp.mean(numerator * numerator, -1, keepdims=True) + epsilon)
    conv_prev, key_prev, value_prev = received
    query_round = query_win.astype(jnp.bfloat16)
    all_keys = jnp.concatenate([key_prev, key_win.astype(jnp.bfloat16)], 1)
    all_values = jnp.concatenate([value_prev, value_win.astype(jnp.bfloat16)], 1)
    query_pos = first_row + jnp.arange(length, dtype=jnp.int32)
    key_pos = first_row - WIN + jnp.arange(length + WIN, dtype=jnp.int32)
    allowed = (
        (key_pos[None, :] >= 0)
        & (key_pos[None, :] <= query_pos[:, None])
        & (key_pos[None, :] > query_pos[:, None] - WIN)
    )
    scores = jnp.einsum(
        "slhd,smhd->shlm", query_round, all_keys, preferred_element_type=jnp.float32
    ) * HD ** (-0.5)
    scores = jnp.where(allowed, scores, masked)
    largest = jnp.max(scores, -1, keepdims=True)
    expo = jnp.exp(scores - largest)
    win_prob = expo / jnp.sum(expo, -1, keepdims=True)
    prob_round = win_prob.astype(jnp.bfloat16)
    win_out = jnp.einsum(
        "shlm,smhd->slhd", prob_round, all_values, preferred_element_type=jnp.float32
    )
    conv_all = jnp.concatenate([conv_prev, conv_input.astype(jnp.bfloat16)], 1).astype(jnp.float32)
    conv_taps = conv_filter.astype(jnp.float32).reshape(KW, -1, HD)
    conv_out = conv_taps[0] * conv_all[:, KW - 1 :]
    for offset in range(1, KW):
        conv_out = (
            conv_out + conv_taps[offset] * conv_all[:, KW - 1 - offset : KW - 1 - offset + length]
        )
    gate_act = jax.nn.silu(conv_gate)
    mixed = numerator * lin_scale + win_out + conv_out * gate_act
    kept_values = (
        lin_scores,
        numerator,
        lin_scale,
        query_round,
        all_keys,
        all_values,
        win_prob,
        prob_round,
        conv_out,
        gate_act,
    )
    return (mixed, kept_values)


def tail_add(local_rows, extra_rows):
    width_rows = local_rows.shape[1] - extra_rows.shape[1]
    return local_rows + jnp.pad(extra_rows, ((0, 0), (width_rows, 0), (0, 0), (0, 0)))


def body(
    block_input,
    gain_first,
    frozen_mixer_weight,
    conv_filter,
    frozen_output_weight,
    gain_second,
    frozen_gate_up_weight,
    frozen_down_weight,
    mixer_left,
    mixer_right,
    output_left,
    output_right,
    gateup_left,
    gateup_right,
    down_left,
    down_right,
    adapter_index,
    seq_lengths,
    out_cotangent,
):
    sequences, length, hidden_model_width = block_input.shape
    first_row = lax.axis_index("seq") * length
    onehot = (adapter_index[:, None] == jnp.arange(NA, dtype=jnp.int32)[None, :]).astype(
        jnp.bfloat16
    )

    def select(table):
        return jnp.einsum(
            "se,e...->s...", onehot, table, preferred_element_type=jnp.float32
        ).astype(jnp.bfloat16)

    select_mixer_left = select(mixer_left)
    pick_mixer_right = select(mixer_right)
    select_output_left = select(output_left)
    select_output_right = select(output_right)
    select_gate_up_left = select(gateup_left)
    pick_gateup_right = select(gateup_right)
    pick_down_left = select(down_left)
    select_down_right = select(down_right)
    gain_one = gain_first.astype(jnp.float32)
    gain_two = gain_second.astype(jnp.float32)
    xfull = block_input.astype(jnp.float32)
    scale_one, pre_mixer_rounded, mixer_adapter_rank, projected_rows = mixer_input(
        xfull, gain_one, select_mixer_left, pick_mixer_right, frozen_mixer_weight
    )
    pieces = slices(projected_rows)
    lin_feats = (
        taylor(pieces[0]).astype(jnp.bfloat16),
        taylor(pieces[1]).astype(jnp.bfloat16),
        pieces[2].astype(jnp.bfloat16),
    )
    tail_rows = (
        pieces[6][:, length - (KW - 1) :].astype(jnp.bfloat16),
        pieces[4][:, length - WIN :].astype(jnp.bfloat16),
        pieces[5][:, length - WIN :].astype(jnp.bfloat16),
    )
    received = from_behind((tail_rows[0], tail_rows[1], tail_rows[2]), "seq", 1)
    local_state = jnp.einsum(
        "smhf,smhd->shfd", lin_feats[1], lin_feats[2], preferred_element_type=jnp.float32
    )
    prior_state = carried_in(local_state, "seq", add_states, jnp.zeros_like(local_state), False)
    mixed, kept_values = mixer_parts(
        pieces, lin_feats, received, prior_state, conv_filter, first_row
    )
    mixer_rounded_input = mixed.reshape(sequences, length, -1).astype(jnp.bfloat16)
    output_adapter_rank = jnp.einsum(
        "foc,fcn->fon", mixer_rounded_input, select_output_left, preferred_element_type=jnp.float32
    )
    out_extra = jnp.einsum(
        "fjt,ftg->fjg",
        output_adapter_rank,
        select_output_right.astype(jnp.float32),
        precision=highest_precision,
    )
    first_branch_path = flat_dot(mixer_rounded_input, frozen_output_weight) + out_extra
    middle = xfull + lax.psum(first_branch_path.astype(jnp.bfloat16), "tp").astype(jnp.float32)
    normed_two, scale_two = norm_rows(middle, gain_two)
    pre_feed_rounded = normed_two.astype(jnp.bfloat16)
    gate_adapter_rank = jnp.einsum(
        "foc,fcn->fon", pre_feed_rounded, select_gate_up_left, preferred_element_type=jnp.float32
    ).astype(jnp.bfloat16)
    gate_up_hidden = flat_dot(
        pre_feed_rounded, frozen_gate_up_weight.reshape(hidden_model_width, -1)
    )
    gate_up_hidden = gate_up_hidden + jnp.einsum(
        "slr,src->slc",
        gate_adapter_rank,
        pick_gateup_right.reshape(sequences, R, -1),
        preferred_element_type=jnp.float32,
    )
    gate_up_hidden = gate_up_hidden.reshape(sequences, length, 2, -1)
    gate_act = jax.nn.silu(gate_up_hidden[:, :, 0])
    hidden_activation = (gate_act * gate_up_hidden[:, :, 1]).astype(jnp.bfloat16)
    down_adapter_rank = jnp.einsum(
        "slf,sfr->slr", hidden_activation, pick_down_left, preferred_element_type=jnp.float32
    )
    down_extra = jnp.einsum(
        "fjt,ftg->fjg",
        down_adapter_rank,
        select_down_right.astype(jnp.float32),
        precision=highest_precision,
    )
    second_branch_path = flat_dot(hidden_activation, frozen_down_weight) + down_extra
    block_output = (
        middle + lax.psum(second_branch_path.astype(jnp.bfloat16), "tp").astype(jnp.float32)
    ).astype(jnp.bfloat16)
    positions = first_row + jnp.arange(length, dtype=jnp.int32)
    valid_mask = (positions[None, :] < seq_lengths[:, None]).astype(jnp.float32)
    upstream = out_cotangent.astype(jnp.float32) * valid_mask[:, :, None]
    down_projection_gradient = upstream.astype(jnp.bfloat16)
    down_rgrad = jnp.einsum(
        "qeh,qph->qep",
        down_projection_gradient,
        select_down_right,
        preferred_element_type=jnp.float32,
    )
    hidden_grad = flat_dot_back(down_projection_gradient, frozen_down_weight)
    hidden_grad = hidden_grad + jnp.einsum(
        "slr,sfr->slf", down_rgrad, pick_down_left.astype(jnp.float32), precision=highest_precision
    )
    down_left_part = jnp.einsum(
        "slf,slr->sfr",
        hidden_activation.astype(jnp.float32),
        down_rgrad,
        precision=highest_precision,
    )
    down_right_part = jnp.einsum(
        "jzv,jzw->jvw",
        down_adapter_rank,
        down_projection_gradient.astype(jnp.float32),
        precision=highest_precision,
    )
    gate_grad = hidden_grad * gate_up_hidden[:, :, 1] * silu_slope(gate_up_hidden[:, :, 0])
    up_grad = hidden_grad * gate_act
    gateup_grad = (
        jnp.stack([gate_grad, up_grad], 2).astype(jnp.bfloat16).reshape(sequences, length, -1)
    )
    gate_up_right_gradient = jnp.einsum(
        "slc,src->slr",
        gateup_grad,
        pick_gateup_right.reshape(sequences, R, -1),
        preferred_element_type=jnp.float32,
    )
    second_extra = jnp.einsum(
        "beh,bxh->bex",
        gate_up_right_gradient,
        select_gate_up_left.astype(jnp.float32),
        precision=highest_precision,
    )
    gateup_right_part = jnp.einsum(
        "slr,slc->src", gate_adapter_rank, gateup_grad, preferred_element_type=jnp.float32
    )
    gateup_left_part = jnp.einsum(
        "cup,cuq->cpq",
        pre_feed_rounded.astype(jnp.float32),
        gate_up_right_gradient,
        precision=highest_precision,
    )
    second_grad = (
        flat_dot_back(gateup_grad, frozen_gate_up_weight.reshape(hidden_model_width, -1))
        + second_extra
    )
    second_sum = lax.psum(second_grad.astype(jnp.bfloat16), "tp").astype(jnp.float32)
    middle_grad = upstream + norm_back(middle, scale_two, gain_two, second_sum)
    mixer_projected_heads = middle_grad.astype(jnp.bfloat16)
    output_right_gradient = jnp.einsum(
        "qeh,qph->qep",
        mixer_projected_heads,
        select_output_right,
        preferred_element_type=jnp.float32,
    )
    mixed_grad = flat_dot_back(mixer_projected_heads, frozen_output_weight)
    mixed_grad = mixed_grad + jnp.einsum(
        "beh,bxh->bex",
        output_right_gradient,
        select_output_left.astype(jnp.float32),
        precision=highest_precision,
    )
    output_left_part = jnp.einsum(
        "cup,cuq->cpq",
        mixer_rounded_input.astype(jnp.float32),
        output_right_gradient,
        precision=highest_precision,
    )
    output_right_part = jnp.einsum(
        "jzv,jzw->jvw",
        output_adapter_rank,
        mixer_projected_heads.astype(jnp.float32),
        precision=highest_precision,
    )
    mixed_grad = mixed_grad.reshape(sequences, length, -1, HD)
    feat_query, feat_key, value_round = lin_feats
    (
        lin_scores,
        numerator,
        lin_scale,
        query_round,
        all_keys,
        all_values,
        win_prob,
        prob_round,
        conv_out,
        conv_act,
    ) = kept_values
    lin_mean = jnp.mean(numerator * mixed_grad, -1, keepdims=True)
    numer_grad = (
        lin_scale * mixed_grad - numerator * lin_scale * lin_scale * lin_scale * lin_mean
    ).astype(jnp.bfloat16)
    local_back = jnp.einsum(
        "slhf,slhd->shfd", feat_query, numer_grad, preferred_element_type=jnp.float32
    )
    later_state = carried_in(local_back, "seq", add_states, jnp.zeros_like(local_back), True)
    numer_wide = numer_grad.astype(jnp.float32)
    causal = jnp.tril(jnp.ones((length, length), jnp.bool_))
    score_lin_grad = jnp.where(
        causal,
        jnp.einsum("slhd,smhd->shlm", numer_grad, value_round, preferred_element_type=jnp.float32),
        0.0,
    )
    query_feat_grad = jnp.einsum(
        "shlm,smhf->slhf", score_lin_grad, feat_key.astype(jnp.float32), precision=highest_precision
    )
    query_feat_grad = query_feat_grad + jnp.einsum(
        "slhd,shfd->slhf", numer_wide, prior_state, precision=highest_precision
    )
    key_feat_grad = jnp.einsum(
        "shlm,slhf->smhf",
        score_lin_grad,
        feat_query.astype(jnp.float32),
        precision=highest_precision,
    )
    key_feat_grad = key_feat_grad + jnp.einsum(
        "smhd,shfd->smhf", value_round.astype(jnp.float32), later_state, precision=highest_precision
    )
    value_lin_grad = jnp.einsum(
        "shlm,slhd->smhd", lin_scores, numer_wide, precision=highest_precision
    )
    value_lin_grad = value_lin_grad + jnp.einsum(
        "smhf,shfd->smhd", feat_key.astype(jnp.float32), later_state, precision=highest_precision
    )
    query_lin_grad = jax.vjp(taylor, pieces[0])[1](query_feat_grad)[0] * FD ** (-0.25)
    key_lin_grad = jax.vjp(taylor, pieces[1])[1](key_feat_grad)[0] * FD ** (-0.25)
    win_up = mixed_grad.astype(jnp.bfloat16)
    prob_grad = jnp.einsum(
        "slhd,smhd->shlm", win_up, all_values, preferred_element_type=jnp.float32
    )
    prob_total = jnp.sum(win_prob * prob_grad, -1, keepdims=True)
    score_round = (win_prob * (prob_grad - prob_total)).astype(jnp.bfloat16)
    query_win_grad = jnp.einsum(
        "shlm,smhd->slhd", score_round, all_keys, preferred_element_type=jnp.float32
    ) * HD ** (-0.5)
    keys_grad = jnp.einsum(
        "shlm,slhd->smhd", score_round, query_round, preferred_element_type=jnp.float32
    ) * HD ** (-0.5)
    values_grad = jnp.einsum(
        "shlm,slhd->smhd", prob_round, win_up, preferred_element_type=jnp.float32
    )
    conv_taps = conv_filter.astype(jnp.float32).reshape(KW, -1, HD)
    conv_grad = mixed_grad * conv_act
    gate_conv_grad = mixed_grad * conv_out * silu_slope(pieces[7])
    conv_in_grad = jnp.pad(conv_taps[0] * conv_grad, ((0, 0), (KW - 1, 0), (0, 0), (0, 0)))
    for offset in range(1, KW):
        conv_in_grad = conv_in_grad + jnp.pad(
            conv_taps[offset] * conv_grad, ((0, 0), (KW - 1 - offset, offset), (0, 0), (0, 0))
        )
    returned = (
        from_behind(conv_in_grad[:, : KW - 1].astype(jnp.bfloat16), "seq", -1).astype(jnp.float32),
        from_behind(keys_grad[:, :WIN].astype(jnp.bfloat16), "seq", -1).astype(jnp.float32),
        from_behind(values_grad[:, :WIN].astype(jnp.bfloat16), "seq", -1).astype(jnp.float32),
    )
    conv_input_grad = tail_add(conv_in_grad[:, KW - 1 :], returned[0])
    key_win_grad = tail_add(keys_grad[:, WIN:], returned[1])
    value_win_grad = tail_add(values_grad[:, WIN:], returned[2])
    projected_grad = jnp.concatenate(
        [
            query_lin_grad,
            key_lin_grad,
            value_lin_grad,
            query_win_grad,
            key_win_grad,
            value_win_grad,
            conv_input_grad,
            gate_conv_grad,
        ],
        -1,
    )
    projected_grad = projected_grad.astype(jnp.bfloat16).reshape(sequences, length, -1)
    mixer_right_gradient = jnp.einsum(
        "slc,src->slr",
        projected_grad,
        pick_mixer_right.reshape(sequences, R, -1),
        preferred_element_type=jnp.float32,
    )
    first_extra = jnp.einsum(
        "beh,bxh->bex",
        mixer_right_gradient,
        select_mixer_left.astype(jnp.float32),
        precision=highest_precision,
    )
    mixer_right_part = jnp.einsum(
        "slr,slc->src", mixer_adapter_rank, projected_grad, preferred_element_type=jnp.float32
    )
    mixer_left_part = jnp.einsum(
        "cup,cuq->cpq",
        pre_mixer_rounded.astype(jnp.float32),
        mixer_right_gradient,
        precision=highest_precision,
    )
    first_grad = (
        flat_dot_back(projected_grad, frozen_mixer_weight.reshape(hidden_model_width, -1))
        + first_extra
    )
    first_sum = lax.psum(first_grad.astype(jnp.bfloat16), "tp").astype(jnp.float32)
    input_grad = (middle_grad + norm_back(xfull, scale_one, gain_one, first_sum)).astype(
        jnp.bfloat16
    )
    onehot_wide = onehot.astype(jnp.float32)

    def spread(per_sequence):
        return jnp.einsum("se,s...->e...", onehot_wide, per_sequence, precision=highest_precision)

    shared_left_mixer = spread(mixer_left_part)
    shared_right_output = spread(output_right_part)
    shared_left_gateup = spread(gateup_left_part)
    shared_right_down = spread(down_right_part)
    owned_right_mixer = spread(mixer_right_part).reshape(NA, R, -1, HCOLS)
    owned_left_output = spread(output_left_part)
    owned_right_gateup = spread(gateup_right_part).reshape(NA, R, 2, -1)
    owned_left_down = spread(down_left_part)
    shared = lax.psum(
        (shared_left_mixer, shared_right_output, shared_left_gateup, shared_right_down),
        ("seq", "tp"),
    )
    owned = (
        lax.psum(owned_right_mixer.astype(jnp.bfloat16), "seq").astype(jnp.float32),
        lax.psum(owned_left_output.astype(jnp.bfloat16), "seq").astype(jnp.float32),
        lax.psum(owned_right_gateup.astype(jnp.bfloat16), "seq").astype(jnp.float32),
        lax.psum(owned_left_down.astype(jnp.bfloat16), "seq").astype(jnp.float32),
    )
    return (
        block_output,
        input_grad,
        shared[0],
        owned[0],
        owned[1],
        shared[1],
        shared[2],
        owned[2],
        owned[3],
        shared[3],
    )


def solution(mesh):
    return jax.shard_map(
        body,
        mesh=mesh,
        in_specs=(
            P(None, "seq", None),
            P(),
            P(None, "tp", None),
            P(None, "tp"),
            P("tp", None),
            P(),
            P(None, None, "tp"),
            P("tp", None),
            P(),
            P(None, None, "tp", None),
            P(None, "tp", None),
            P(),
            P(),
            P(None, None, None, "tp"),
            P(None, "tp", None),
            P(),
            P(),
            P(),
            P(None, "seq", None),
        ),
        out_specs=(
            P(None, "seq", None),
            P(None, "seq", None),
            P(),
            P(None, None, "tp", None),
            P(None, "tp", None),
            P(),
            P(),
            P(None, None, None, "tp"),
            P(None, "tp", None),
            P(),
        ),
        check_vma=False,
    )
```

profile of v0, /device:TPU:0, one launch (start us, length us, event | category | flops | bytes accessed | tf_op | source)
XLA Modules:
  0.0 2034.7 jit_solution(10121072256170554866)
XLA Ops:
  29.3 31.0 %convolution_add_fusion.1 = f32[4,512,2816]{2,1,0:T(8,128)} fusion(f32[4,512,2816]{2,1,0:T(8,128)} %fusion.194, bf16[1792,2816,1]{0,1,2:T(8,128)(2,1)} %bitcast.260, bf16[4,512,1792]{2,1,0:T(8,128)(2,1)} %param.43, f32[1792]{0:T(1024)S(1)} %convert_element_type.243, f32[4,512]{1,0:T(4,128)S(1)} %add_rsqrt_fusion.2), kind=kOutput, calls=%fused_computation.71 | convolution fusion | flops 20689977344 | bytes 63585280 | tf_op jit(solution)/shard_map/dot_general | solution.py:82
  60.3 23.4 %copy.160 = f32[4,512,2816]{1,2,0:T(8,128)} copy(f32[4,512,2816]{2,1,0:T(8,128)} %convolution_add_fusion.1) | data formatting | bytes 46137344 | tf_op jit(solution)/shard_map/add | solution.py:107
  142.7 14.5 fusion.58
  230.9 15.1 fusion.74
  268.3 15.3 fusion.46
  283.6 240.7 %all-reduce.15.cloned.1.call-done = bf16[4,512,1792]{2,1,0:T(8,128)(2,1)} async-done(((bf16[4,512,1792]{2,1,0:T(8,128)(2,1)}), bf16[4,512,1792]{2,1,0:T(8,128)(2,1)}) %all-reduce.15.cloned.1.call-update) | async-done | bytes 7340048 | tf_op jit(solution)/shard_map/psum | solution.py:264
  556.2 28.0 %convolution_add_fusion = f32[4,512,2432]{2,1,0:T(8,128)} fusion(f32[4,512,2432]{2,1,0:T(8,128)} %fusion.195, bf16[4,512,1792]{2,1,0:T(8,128)(2,1)} %multiply_convert_fusion.1, bf16[1792,2432,1]{0,1,2:T(8,128)(2,1)} %bitcast.261), kind=kOutput, calls=%fused_computation.61 | convolution fusion | flops 17855938560 | bytes 55902208 | tf_op jit(solution)/shard_map/dot_general | solution.py:82
  584.2 19.8 copy.180
  603.9 16.1 multiply_bitcast_fusion.1
  646.6 26.4 %fusion.32 = f32[4,512,1792,1]{2,1,0,3:T(8,128)} fusion(bf16[1792,2,1216]{0,2,1:T(8,128)(2,1)} %param.49, bf16[4,512,1,1216]{1,3,0,2:T(8,128)(2,1)S(1)} %copy-done.30, bf16[4,512,1,1216]{1,3,0,2:T(8,128)(2,1)S(1)} %bitcast.257), kind=kOutput, calls=%fused_computation.76 | convolution fusion | flops 17855938560 | bytes 33357824 | tf_op jit(solution)/shard_map/lc,dc->ld/dot_general | solution.py:90
  739.3 204.0 %all-reduce.17.cloned.1.call-done = bf16[4,512,1792]{2,1,0:T(8,128)(2,1)} async-done(((bf16[4,512,1792]{2,1,0:T(8,128)(2,1)}), bf16[4,512,1792]{2,1,0:T(8,128)(2,1)}) %all-reduce.17.cloned.1.call-update) | async-done | bytes 7340048 | tf_op jit(solution)/shard_map/psum | solution.py:351
  1006.4 14.3 multiply_reduce_fusion
  1052.9 15.8 fusion.5
  1095.3 14.1 fusion.3
  1126.8 22.4 %fusion.55 = (f32[136,4,512,4]{2,0,3,1:T(8,128)}, f32[136,4,512,4]{2,0,3,1:T(8,128)}, f32[136,4,512,4]{2,0,3,1:T(8,128)}, f32[136,4,512,4]{2,0,3,1:T(8,128)}) fusion(f32[136,4,512,4]{2,3,1,0:T(4,128)} %gather_fusion.2, f32[4,512,4,153]{1,3,2,0:T(8,128)S(1)} %add_bitcast_fusion, f32[136]{0:T(256)S(1)} %copy-done.102, f32[136,4,512,4]{2,3,1,0:T(4,128)} %gather_fusion.3, ...), kind=kLoop, calls=%fused_computation.106 | loop fusion | flops 6684672 | bytes 44565024 | tf_op jit(solution)/shard_map/transpose(jvp())/mul | solution.py:44
  1172.1 19.1 scatter_fusion.2
  1192.1 27.7 %scatter_fusion.3 = f32[4,512,4,16]{1,2,3,0:T(4,128)} fusion(f32[4,512,4,16]{1,2,3,0:T(4,128)} %broadcast.176.clone.1, s32[136]{0:T(256)S(1)} %copy-done.100, f32[136,4,512,4]{2,3,1,0:T(4,128)} %copy.203), kind=kCustom, calls=%fused_computation.7 | custom fusion | flops 1114112 | bytes 13369888 | tf_op jit(solution)/shard_map/transpose(jvp())/scatter-add | solution.py:44
  1219.9 18.4 scatter_fusion.1
  1238.3 19.1 scatter_fusion
  1303.1 27.0 %fusion.26 = f32[4,512,1792,1]{2,1,3,0:T(8,128)S(1)} fusion(bf16[4,512,4,704]{1,3,2,0:T(8,128)(2,1)} %copy-done.12, bf16[1792,4,704]{0,2,1:T(8,128)(2,1)} %param.45), kind=kOutput, calls=%fused_computation.62 | convolution fusion | flops 20669530112 | bytes 36306944 | tf_op jit(solution)/shard_map/lc,dc->ld/dot_general | solution.py:90
  1338.7 15.0 all-reduce.21.cloned.1.call-done
  1362.3 138.2 %all-reduce.19.cloned.1.call-done = (f32[8,1792,16]{1,0,2:T(8,128)}, f32[8,16,1792]{2,0,1:T(8,128)}, f32[8,1792,16]{1,0,2:T(8,128)}, f32[8,16,1792]{2,0,1:T(8,128)}) async-done(((f32[8,1792,16]{1,0,2:T(8,128)}, f32[8,16,1792]{2,0,1:T(8,128)}, f32[8,1792,16]{1,0,2:T(8,128)}, f32[8,16,1792]{2,0,1:T(8,128)}), (f32[8,1792,16]{1,0,2:T(8,128)}, f32[8,16,1792]{2,0,1:T(8,128)}, f32[8,1792,16]{1,0,2:T(8,128)}, ...) | async-done | bytes 3670032 | tf_op jit(solution)/shard_map/psum | solution.py:518
  1509.0 488.5 %all-reduce.23.cloned.1.call-done = (bf16[4,512,1792]{2,1,0:T(8,128)(2,1)}, bf16[4,512,1792]{2,1,0:T(8,128)(2,1)}) async-done(((bf16[4,512,1792]{2,1,0:T(8,128)(2,1)}, bf16[4,512,1792]{2,1,0:T(8,128)(2,1)}), (bf16[4,512,1792]{2,1,0:T(8,128)(2,1)}, bf16[4,512,1792]{2,1,0:T(8,128)(2,1)})) %all-reduce.23.cloned.1.call-update) | async-done | bytes 14680080 | tf_op jit(solution)/shard_map/psum | solution.py:293
  2005.4 22.2 %fusion.16 = (bf16[4,512,1792]{2,1,0:T(8,128)(2,1)}, bf16[4,512,1792]{2,1,0:T(8,128)(2,1)}) fusion(bf16[4,512,1792]{2,1,0:T(8,128)(2,1)} %param.43, bf16[4,512,1792]{2,1,0:T(8,128)(2,1)S(1)} %copy-done.20, f32[4,512]{1,0:T(4,128)S(1)} %broadcast_multiply_fusion.4, f32[1792]{0:T(1024)S(1)} %copy-done.79, f32[4,512]{1,0:T(4,128)S(1)} %copy-done.83, ...), kind=kLoop, calls=%fused_computation.43 | loop fusion | flops 99090432 | bytes 58775552 | tf_op jit(solution)/shard_map/convert_element_type | solution.py:502
  (447 shorter events, 553.5 us)
Async XLA Ops:
  7.2 239.2 %copy-start = (bf16[448,1792]{1,0:T(8,128)(2,1)S(1)}, bf16[448,1792]{1,0:T(8,128)(2,1)}, u32[]{:S(2)}) copy-start(bf16[448,1792]{1,0:T(8,128)(2,1)} %param.47) | copy-start | bytes 4816900
  7.2 215.3 %all-gather.5.cloned.1.call-start = ((), (), s32[]{:S(2)}) async-start(), calls=%async_computation.2 | async-start | bytes 5640192 | tf_op jit(solution)/shard_map/all_gather | solution.py:31
  85.8 71.4 %copy-start.31 = (bf16[4,512,4,16]{1,3,2,0:T(8,128)(2,1)}, bf16[4,512,4,16]{1,3,2,0:T(8,128)(2,1)S(1)}, u32[]{:S(2)}) copy-start(bf16[4,512,4,16]{1,3,2,0:T(8,128)(2,1)S(1)} %get-tuple-element.164) | copy-start | bytes 786436
  142.7 80.5 %copy-start.68 = (bf16[153]{0:T(256)(128)(2,1)}, bf16[153]{0:T(256)(128)(2,1)S(1)}, u32[]{:S(2)}) copy-start(bf16[153]{0:T(256)(128)(2,1)S(1)} %pad.52.clone) | copy-start | bytes 922
  159.7 364.6 %all-reduce.15.cloned.1.call-start = ((), (), s32[]{:S(2)}) async-start(), calls=%async_computation | async-start | bytes 14680064 | tf_op jit(solution)/shard_map/psum | solution.py:264
  161.8 42.7 %collective-permute-start.2 = (bf16[4,2,4,112]{1,3,2,0:T(8,128)(2,1)}, bf16[4,2,4,112]{1,3,2,0:T(8,128)(2,1)}, u32[]{:S(2)}, u32[]{:S(2)}) collective-permute-start(bf16[4,2,4,112]{1,3,2,0:T(8,128)(2,1)} %slice.139), channel_id=1, source_target_pairs={{0,4},{4,8},{8,12},{12,16},{16,20},{20,24},{24,28},{1,5},{5,9},{9,... | collective-permute-start | bytes 21512 | tf_op jit(solution)/shard_map/ppermute | solution.py:24
  167.4 41.9 %collective-permute-start.1 = (bf16[4,64,4,112]{1,3,2,0:T(8,128)(2,1)}, bf16[4,64,4,112]{1,3,2,0:T(8,128)(2,1)}, u32[]{:S(2)}, u32[]{:S(2)}) collective-permute-start(bf16[4,64,4,112]{1,3,2,0:T(8,128)(2,1)} %get-tuple-element.169), channel_id=1, source_target_pairs={{0,4},{4,8},{8,12},{12,16},{16,20},{20,24},{24,28},{1,5},{5,9},{9,... | collective-permute-start | bytes 688136 | tf_op jit(solution)/shard_map/ppermute | solution.py:24
  171.9 59.0 %collective-permute-start = (bf16[4,64,4,112]{1,3,2,0:T(8,128)(2,1)}, bf16[4,64,4,112]{1,3,2,0:T(8,128)(2,1)}, u32[]{:S(2)}, u32[]{:S(2)}) collective-permute-start(bf16[4,64,4,112]{1,3,2,0:T(8,128)(2,1)} %get-tuple-element.170), channel_id=1, source_target_pairs={{0,4},{4,8},{8,12},{12,16},{16,20},{20,24},{24,28},{1,5},{5,9},{9,... | collective-permute-start | bytes 688136 | tf_op jit(solution)/shard_map/ppermute | solution.py:24
  174.6 71.5 %copy-start.53 = (bf16[4,448,16]{1,0,2:T(4,128)(2,1)}, bf16[4,448,16]{1,0,2:T(4,128)(2,1)S(1)}, u32[]{:S(2)}) copy-start(bf16[4,448,16]{1,0,2:T(4,128)(2,1)S(1)} %convolution_convert_fusion.14) | copy-start | bytes 172036
  181.8 27.5 %copy-start.28 = (bf16[4,512,4,112]{1,3,2,0:T(8,128)(2,1)}, bf16[4,512,4,112]{1,3,2,0:T(8,128)(2,1)S(1)}, u32[]{:S(2)}) copy-start(bf16[4,512,4,112]{1,3,2,0:T(8,128)(2,1)S(1)} %get-tuple-element.171) | copy-start | bytes 5505028
  258.9 684.4 %all-reduce.17.cloned.1.call-start = ((), (), s32[]{:S(2)}) async-start(), calls=%async_computation.1 | async-start | bytes 14680064 | tf_op jit(solution)/shard_map/psum | solution.py:351
  259.9 272.0 %copy-start.63 = (f32[1792]{0:T(1024)}, f32[1792]{0:T(1024)S(1)}, u32[]{:S(2)}) copy-start(f32[1792]{0:T(1024)S(1)} %convert_element_type.258) | copy-start | bytes 21508
  261.1 692.9 %copy-start.58 = (f32[4,512]{1,0:T(4,128)}, f32[4,512]{1,0:T(4,128)S(1)}, u32[]{:S(2)}) copy-start(f32[4,512]{1,0:T(4,128)S(1)} %compare_convert_fusion) | copy-start | bytes 24580
  268.3 335.6 %copy-start.72 = (f32[4,512,16]{1,2,0:T(8,128)}, f32[4,512,16]{1,2,0:T(8,128)S(1)}, u32[]{:S(2)}) copy-start(f32[4,512,16]{1,2,0:T(8,128)S(1)} %fusion.44) | copy-start | bytes 393220
  687.5 421.9 %all-gather.7.cloned.1.call-start = ((), (), s32[]{:S(2)}) async-start(), calls=%async_computation.3 | async-start | bytes 5640192 | tf_op jit(solution)/shard_map/all_gather | solution.py:31
  727.9 215.4 %copy-start.64 = (f32[1792]{0:T(1024)S(1)}, f32[1792]{0:T(1024)}, u32[]{:S(2)}) copy-start(f32[1792]{0:T(1024)} %copy-done.63) | copy-start | bytes 21508
  739.3 214.7 %copy-start.76 = (f32[4,512]{1,0:T(4,128)S(1)}, f32[4,512]{1,0:T(4,128)}, u32[]{:S(2)}) copy-start(f32[4,512]{1,0:T(4,128)} %copy-done.75) | copy-start | bytes 24580
  996.3 277.8 %collective-permute-start.4 = (bf16[4,64,4,112]{1,3,2,0:T(8,128)(2,1)}, bf16[4,64,4,112]{1,3,2,0:T(8,128)(2,1)}, u32[]{:S(2)}, u32[]{:S(2)}) collective-permute-start(bf16[4,64,4,112]{1,3,2,0:T(8,128)(2,1)} %slice.232), channel_id=1, source_target_pairs={{4,0},{8,4},{12,8},{16,12},{20,16},{24,20},{28,24},{5,1},{9,5},{13... | collective-permute-start | bytes 688136 | tf_op jit(solution)/shard_map/ppermute | solution.py:24
  999.3 69.4 %copy-start.18 = (bf16[4,512,4,112]{1,3,2,0:T(8,128)(2,1)}, bf16[4,512,4,112]{1,3,2,0:T(8,128)(2,1)S(1)}, u32[]{:S(2)}) copy-start(bf16[4,512,4,112]{1,3,2,0:T(8,128)(2,1)S(1)} %subtract_convert_fusion) | copy-start | bytes 5505028
  1002.7 274.7 %collective-permute-start.5 = (bf16[4,2,4,112]{1,3,2,0:T(8,128)(2,1)}, bf16[4,2,4,112]{1,3,2,0:T(8,128)(2,1)}, u32[]{:S(2)}, u32[]{:S(2)}) collective-permute-start(bf16[4,2,4,112]{1,3,2,0:T(8,128)(2,1)} %slice.231), channel_id=1, source_target_pairs={{4,0},{8,4},{12,8},{16,12},{20,16},{24,20},{28,24},{5,1},{9,5},{13... | collective-permute-start | bytes 21512 | tf_op jit(solution)/shard_map/ppermute | solution.py:24
  1006.3 347.4 %all-reduce.21.cloned.1.call-start = ((), (), s32[]{:S(2)}) async-start(), calls=%async_computation.5 | async-start | bytes 3801088 | tf_op jit(solution)/shard_map/psum | solution.py:524
  1041.7 229.0 %collective-permute-start.3 = (bf16[4,64,4,112]{1,3,2,0:T(8,128)(2,1)}, bf16[4,64,4,112]{1,3,2,0:T(8,128)(2,1)}, u32[]{:S(2)}, u32[]{:S(2)}) collective-permute-start(bf16[4,64,4,112]{1,3,2,0:T(8,128)(2,1)} %slice.233), channel_id=1, source_target_pairs={{4,0},{8,4},{12,8},{16,12},{20,16},{24,20},{28,24},{5,1},{9,5},{13... | collective-permute-start | bytes 688136 | tf_op jit(solution)/shard_map/ppermute | solution.py:24
  1295.1 205.4 %all-reduce.19.cloned.1.call-start = ((), (), s32[]{:S(2)}) async-start(), calls=%async_computation.4 | async-start | bytes 7340032 | tf_op jit(solution)/shard_map/psum | solution.py:518
  1303.0 694.5 %all-reduce.23.cloned.1.call-start = ((), (), s32[]{:S(2)}) async-start(), calls=%async_computation.6 | async-start | bytes 29360128 | tf_op jit(solution)/shard_map/psum | solution.py:293
  (115 other events, 976.9 us)
Sparse Core Ops, SparseCore 0:
  159.9 45.9 all-gather.4
  259.0 265.2 all-reduce.14
  687.6 255.6 all-reduce.16
  1006.4 41.3 all-gather.6
  1295.2 58.4 all-reduce.20
  1360.8 139.6 all-reduce.18
  1503.8 493.6 all-reduce.22
where the time goes:
time: 2040 us; the launch traced here: 2030 us
  waiting for transfers between devices  1090 us (53%)
  matrix products  463 us (23%)
  other arithmetic  280 us (14%)
  local copies, waits for them, and re-layouts  173 us (8%)
    psum x1, waiting for transfers between devices, body(): lax.psum(second_branch_path.astype(jnp.bfloat16), 'tp').astype(jnp.float32)  489 us
    psum x1, waiting for transfers between devices, body(): lax.psum(first_branch_path.astype(jnp.bfloat16), 'tp').astype(jnp.float32)  241 us
    psum x1, waiting for transfers between devices, body(): lax.psum(second_grad.astype(jnp.bfloat16), 'tp').astype(jnp.float32)  204 us
    psum x1, waiting for transfers between devices, body(): lax.psum((shared_left_mixer, shared_right_output, shared_left_gateup, sha...  138 us
    scatter-add x4, other arithmetic, taylor(): square_terms = vector[..., leading] * vector[..., trailing] * weights  84.3 us
    dot_general x4, matrix products, flat_dot(): jnp.dot(left_rows.reshape(-1, left_rows.shape[-1]), matrix, preferred_ele...  76.2 us
    dot_general x4, matrix products, flat_dot_back(): jnp.einsum('lc,dc->ld', left_rows.reshape(-1, left_rows.shape[-1]), matri...  72.2 us
    gather x4, local copies, waits for them, and re-layouts, taylor(): square_terms = vector[..., leading] * vector[..., trailing] * weights  44 us
  transfers between devices with their start and end apart: 13, of which 5 were waited for; matrix products, arithmetic and copies ran while one was open for 23% of the time, Pallas kernels for 0%

commit v1 on v0

v1 whole, which is shorter than its diff:
```python
import functools

import jax
import jax.numpy as jnp
import numpy as np
from jax import lax
from jax.experimental import pallas as pl
from jax.experimental.pallas import tpu as pltpu
from jax.sharding import Mesh
from jax.sharding import PartitionSpec as P

HD = 112
PD = 128
FD = 16
R = 16
NA = 8
KW = 3
WIN = 64
HCOLS = 704
SLOTS = 4
HEAD_PAD = 7 * PD
FEATS = 1 + FD + FD * (FD + 1) // 2
STATE = 160
CHUNK = 256
QB = 128

epsilon = 1e-05
masked = -1e30
f32 = jnp.float32
bf16 = jnp.bfloat16
ANY = pl.BlockSpec(memory_space=pl.ANY)


def nn(a, b):
    return lax.dot_general(a, b, (((1,), (0,)), ((), ())), preferred_element_type=f32)


def nt(a, b):
    return lax.dot_general(a, b, (((1,), (1,)), ((), ())), preferred_element_type=f32)


def tn(a, b):
    return lax.dot_general(a, b, (((0,), (0,)), ((), ())), preferred_element_type=f32)


def feature_tables():
    leading, trailing = np.triu_indices(FD)
    pick = np.zeros((PD, 1280), np.float32)
    bias = np.zeros((1, 512), np.float32)
    coef = np.zeros((1, 256), np.float32)
    bias[0, 0] = 1.0
    bias[0, 256 : 256 + 1 + FD] = 1.0
    coef[0, : 1 + FD] = 1.0
    coef[0, 1 + FD : FEATS] = np.where(leading == trailing, np.sqrt(0.5), 1.0)
    for base, row in ((0, 0), (512, FD)):
        for i in range(FD):
            pick[row + i, base + 1 + i] = 0.5
        for n, (i, j) in enumerate(zip(leading, trailing)):
            pick[row + i, base + 1 + FD + n] = 0.5
            pick[row + j, base + 256 + 1 + FD + n] = 0.5
    for i in range(FD):
        pick[FD + i, 1024 + i] = 0.25
        pick[i, 1152 + FD + i] = 0.25
    return pick, bias, coef


HEAD_SEGMENTS = [(0, 2 * FD, 0)] + [(2 * FD + HD * i, HD, PD * (i + 1)) for i in range(6)]
M_ROWS = HCOLS + HD
M_CUT = 2 * FD + 3 * HD


def place():
    j = lax.rem(lax.axis_index("chip"), 4)
    return j // 2, lax.rem(j, 2)


def run_copies(copies, sems, start):
    for number, (src, dst) in enumerate(copies):
        copy = pltpu.make_async_copy(src, dst, sems.at[start + number])
        copy.start()


def wait_copies(copies, sems, start):
    for number, (src, dst) in enumerate(copies):
        pltpu.make_async_copy(src, dst, sems.at[start + number]).wait()


def spread_pieces(refs, cut, rows, dest, base, width, offset_of):
    y, x = place()
    z_ref, x_ref, y_ref, da_ref, db_ref = refs
    copies = []
    for kind, yy, xx in (("z", y, x), ("x", y, 1 - x), ("y", 1 - y, x), ("d", 1 - y, 1 - x)):
        cols = pl.ds(pl.multiple_of(xx * width, PD), width)
        for first, count in rows:
            spans = [(first, count)]
            if kind == "d" and first < cut < first + count:
                spans = [(first, cut - first), (cut, first + count - cut)]
            for row, size in spans:
                if kind == "d":
                    src = da_ref if row < cut else db_ref
                    src = src.at[pl.ds(row if row < cut else row - cut, size)]
                else:
                    src = {"z": z_ref, "x": x_ref, "y": y_ref}[kind].at[pl.ds(row, size)]
                start = pl.multiple_of(base + offset_of(row, yy), 16)
                copies.append((src, dest.at[pl.ds(start, size), cols]))
    return copies


def mixer_offset(row, yy):
    for first, count, at in HEAD_SEGMENTS:
        if first <= row < first + count:
            return yy * HEAD_PAD + at + row - first
    return None


MIXER_ROWS = [(first, count) for first, count, _ in HEAD_SEGMENTS]


def mixer_copies(refs, own, dest, base):
    if own:
        core = lax.axis_index("core")
        copies = []
        for head in range(2):
            for first, count, at in HEAD_SEGMENTS:
                src = pl.multiple_of(2 * HCOLS * core + HCOLS * head + first, 16)
                copies.append(
                    (refs[0].at[pl.ds(src, count)], dest.at[pl.ds(base + HEAD_PAD * head + at, count)])
                )
        return copies
    return spread_pieces(refs, M_CUT, MIXER_ROWS, dest, base, dest.shape[1] // 2, mixer_offset)


def mixer_pads(dest, base):
    for head in range(2):
        for first, count, at in HEAD_SEGMENTS:
            start = base + HEAD_PAD * head + at + count
            dest[start : start + PD - count] = jnp.zeros((PD - count, dest.shape[1]), bf16)


def output_copies(refs, own, dest, base):
    if own:
        core = lax.axis_index("core")
        return [
            (
                refs[0].at[pl.ds(pl.multiple_of(2 * HD * core + HD * head, 16), HD)],
                dest.at[pl.ds(base + PD * head, HD)],
            )
            for head in range(2)
        ]
    return spread_pieces(
        refs, M_CUT, [(HCOLS, HD)], dest, base, dest.shape[1] // 2, lambda row, yy: yy * PD + row - HCOLS
    )


def output_pads(dest, base):
    for head in range(2):
        start = base + PD * head + HD
        dest[start : start + PD - HD] = jnp.zeros((PD - HD, dest.shape[1]), bf16)


def feed_cut(quarter):
    return quarter + (quarter // 2 + 15) // 16 * 16


def feed_copies(refs, own, dest, half, pad):
    if own:
        core = lax.axis_index("core")
        wg, wd = refs
        spots = [(wg, 0, 0), (wg, 2 * half, pad), (wd, 0, 2 * pad)]
        return [
            (
                ref.at[pl.ds(pl.multiple_of(half * core + first, 16), half)],
                dest.at[pl.ds(at, half)],
            )
            for ref, first, at in spots
        ]
    quarter = half // 2

    def offset_of(row, yy):
        return row // quarter * pad + yy * quarter + row % quarter

    rows = [(quarter * i, quarter) for i in range(3)]
    return spread_pieces(
        refs, feed_cut(quarter), rows, dest, 0, dest.shape[1] // 2, offset_of
    )


def feed_pads(dest, half, pad):
    for i in range(3):
        dest[pad * i + half : pad * (i + 1)] = jnp.zeros((pad - half, dest.shape[1]), bf16)


def features(picked, bias, coef, at):
    one = picked[:, at : at + 256] + bias[:, :256]
    two = picked[:, at + 256 : at + 512] + bias[:, 256:]
    return one, two, one * two * coef


class Table:
    def __init__(self, pad):
        sizes = (2 * HEAD_PAD, 2 * PD, 2 * pad, pad, 2 * PD)
        starts = np.cumsum((0,) + sizes)
        self.right, self.left, self.gate, self.down, self.taps = (
            slice(int(a), int(a) + n) for a, n in zip(starts, sizes)
        )
        self.edges = [int(a) for a in starts]


def params(mib, **more):
    return pltpu.CompilerParams(vmem_limit_bytes=mib * 2**20, **more)


def project_kernel(own, first, rank, table, pick, bias, coef, *rest):
    count = 1 if own else 5
    refs = rest[:count]
    proj, tails, state, weight, sems = rest[count:]
    copies = mixer_copies(refs, own, weight, 0)
    run_copies(copies, sems, 0)
    mixer_pads(weight, 0)
    wait_copies(copies, sems, 0)
    blocks = first.shape[0] // CHUNK
    for head in range(2):
        cols = pl.ds(HEAD_PAD * head, HEAD_PAD)

        def one(block, carry):
            rows = pl.ds(pl.multiple_of(block * CHUNK, CHUNK), CHUNK)
            result = nt(first[rows, :], weight[cols, :]) + nn(rank[rows, :], table[:, cols])
            rounded = result.astype(bf16)
            proj[rows, cols] = rounded
            picked = nn(rounded[:, :PD], pick[...][:, 512:1024])
            _, _, feat = features(picked, bias[...], coef[...], 0)
            return carry + tn(feat.astype(bf16), rounded[:, PD : 2 * PD])

        total = lax.fori_loop(0, blocks, one, jnp.zeros((256, PD), f32))
        state[head] = total[:STATE].astype(bf16)
        last = first.shape[0]
        at = HEAD_PAD * head
        tails[head, 0:WIN, 0:PD] = proj[last - WIN :, at + 3 * PD : at + 4 * PD]
        tails[head, 0:WIN, PD : 2 * PD] = proj[last - WIN :, at + 4 * PD : at + 5 * PD]
        tails[head, WIN : WIN + 16, 0:PD] = proj[last - 16 :, at + 5 * PD : at + 6 * PD]
        tails[head, WIN : WIN + 16, PD : 2 * PD] = jnp.zeros((16, PD), bf16)


def project(own, first, rank, table, tables, refs):
    rows, width = first.shape
    vm = pl.BlockSpec(memory_space=pltpu.VMEM)
    return pl.pallas_call(
        functools.partial(project_kernel, own),
        out_shape=(
            jax.ShapeDtypeStruct((rows, 2 * HEAD_PAD), bf16),
            jax.ShapeDtypeStruct((2, WIN + 16, 2 * PD), bf16),
            jax.ShapeDtypeStruct((2, STATE, PD), bf16),
        ),
        in_specs=[vm] * 6 + [ANY] * len(refs),
        out_specs=(vm, vm, vm),
        scratch_shapes=[pltpu.VMEM((2 * HEAD_PAD, width), bf16), pltpu.SemaphoreType.DMA((40,))],
        compiler_params=params(48),
        cost_estimate=pl.CostEstimate(
            flops=100_000_000, bytes_accessed=300_000, transcendentals=0
        ),
        name="project",
    )(first, rank, table, *tables, *refs)


def window_mask(number):
    query = lax.broadcasted_iota(jnp.int32, (QB, QB + WIN), 0)
    key = lax.broadcasted_iota(jnp.int32, (QB, QB + WIN), 1)
    allowed = (key > query) & (key <= query + WIN)
    if number == 0:
        lead = jnp.where(lax.axis_index("chip") > 0, 0, WIN)
        allowed = allowed & (key >= lead)
    return allowed


def window_prob(query, keys, number):
    scores = nt(query, keys) * HD ** (-0.5)
    scores = jnp.where(window_mask(number), scores, masked)
    largest = jnp.max(scores, -1, keepdims=True)
    expo = jnp.exp(scores - largest)
    return expo / jnp.sum(expo, -1, keepdims=True)


def causal_mask():
    row = lax.broadcasted_iota(jnp.int32, (CHUNK, CHUNK), 0)
    col = lax.broadcasted_iota(jnp.int32, (CHUNK, CHUNK), 1)
    return col <= row


def conv_of(conv, taps, start, count):
    result = taps[0:1] * conv[pl.ds(16 + start, count), :]
    for offset in range(1, KW):
        result = result + taps[offset : offset + 1] * conv[pl.ds(16 + start - offset, count), :]
    return result


def attend_kernel(spots, proj, tails, prior, table, pick, bias, coef, mixed, numer, keys, vals, conv):
    rows = proj.shape[0]
    keys[0:WIN, :] = tails[0, 0:WIN, 0:PD]
    vals[0:WIN, :] = tails[0, 0:WIN, PD : 2 * PD]
    conv[0:16, :] = tails[0, WIN : WIN + 16, 0:PD].astype(f32)
    keys[WIN:, :] = proj[:, 3 * PD : 4 * PD]
    vals[WIN:, :] = proj[:, 4 * PD : 5 * PD]
    conv[16:, :] = proj[:, 5 * PD : 6 * PD].astype(f32)
    tap = head_taps(spots, table)
    state = prior[0]
    causal = causal_mask()
    for chunk in range(rows // CHUNK):
        at = chunk * CHUNK
        span = slice(at, at + CHUNK)
        base = proj[span, 0:PD]
        value = proj[span, PD : 2 * PD]
        picked = nn(base, pick[:, :1152])
        _, _, feat_q = features(picked, bias[...], coef[...], 0)
        _, _, feat_k = features(picked, bias[...], coef[...], 512)
        score = nt(base, picked[:, 1024:1152].astype(bf16))
        weight = jnp.where(causal, 1.0 + score + 0.5 * score * score, 0.0).astype(bf16)
        total = nn(weight, value) + nn(feat_q.astype(bf16), state.astype(bf16))
        state = state + tn(feat_k.astype(bf16), value)
        parts = []
        for number in range(chunk * CHUNK // QB, (chunk + 1) * CHUNK // QB):
            query = proj[number * QB : (number + 1) * QB, 2 * PD : 3 * PD]
            prob = window_prob(query, keys[number * QB : number * QB + QB + WIN, :], number)
            parts.append(nn(prob.astype(bf16), vals[number * QB : number * QB + QB + WIN, :]))
        window = jnp.concatenate(parts, 0)
        scale = lax.rsqrt(jnp.sum(total * total, -1, keepdims=True) * (1.0 / HD) + epsilon)
        gate = proj[span, 6 * PD : 7 * PD].astype(f32)
        branch = conv_of(conv, tap, at, CHUNK) * (gate * jax.nn.sigmoid(gate))
        mixed[span, :] = (total * scale + window + branch).astype(bf16)
        numer[span, :] = total.astype(bf16)


def head_taps(spots, table):
    start = pl.multiple_of(spots.taps.start + PD * pl.program_id(0), PD)
    return table[:, pl.ds(start, PD)].astype(f32)


def attend(spots, proj, tails, prior, table, tables):
    rows = proj.shape[0]
    whole = lambda a: pl.BlockSpec(a.shape, lambda h: (0,) * a.ndim)
    return pl.pallas_call(
        functools.partial(attend_kernel, spots),
        grid=(2,),
        out_shape=(
            jax.ShapeDtypeStruct((rows, 2 * PD), bf16),
            jax.ShapeDtypeStruct((rows, 2 * PD), bf16),
        ),
        in_specs=[
            pl.BlockSpec((rows, HEAD_PAD), lambda h: (0, h)),
            pl.BlockSpec((1, WIN + 16, 2 * PD), lambda h: (h, 0, 0)),
            pl.BlockSpec((1, 256, PD), lambda h: (h, 0, 0)),
            whole(table),
        ]
        + [whole(t) for t in tables],
        out_specs=(
            pl.BlockSpec((rows, PD), lambda h: (0, h)),
            pl.BlockSpec((rows, PD), lambda h: (0, h)),
        ),
        scratch_shapes=[
            pltpu.VMEM((rows + WIN, PD), bf16),
            pltpu.VMEM((rows + WIN, PD), bf16),
            pltpu.VMEM((rows + 16, PD), f32),
        ],
        compiler_params=params(48),
        cost_estimate=pl.CostEstimate(
            flops=100_000_000, bytes_accessed=300_000, transcendentals=0
        ),
        name="attend",
    )(proj, tails, prior, table, *tables)


def mix_out_kernel(spots, *refs):
    mixed = refs[0:4]
    lefts = refs[4:8]
    right = refs[8]
    sources = refs[9 : 9 + 1 + 15]
    part, rank, weight, sems = refs[25:]
    groups = []
    for slot in range(SLOTS):
        pieces = sources[0:1] if slot == 0 else sources[1 + 5 * (slot - 1) : 1 + 5 * slot]
        groups.append(output_copies(pieces, slot == 0, weight, 2 * PD * slot))

    @pl.when(pl.program_id(0) == 0)
    def _():
        for slot in range(SLOTS):
            run_copies(groups[slot], sems, 8 * slot)
            output_pads(weight, 2 * PD * slot)
        for slot in range(SLOTS):
            wait_copies(groups[slot], sems, 8 * slot)

    total = jnp.zeros(part.shape, f32)
    rank_sum = jnp.zeros((part.shape[0], R), f32)
    for slot in range(SLOTS):
        total = total + nn(mixed[slot][...], weight[2 * PD * slot : 2 * PD * (slot + 1), :])
        rank_sum = rank_sum + nt(mixed[slot][...], lefts[slot][:, spots.left])
    total = total + nn(rank_sum.astype(bf16), right[...])
    part[...] = total.astype(bf16)
    rank[...] = rank_sum


def mix_out(spots, mixed, lefts, right, sources):
    rows = mixed[0].shape[0]
    width = right.shape[1]
    block = CHUNK
    steps = rows // block
    whole = lambda a: pl.BlockSpec(a.shape, lambda i: (0,) * a.ndim)
    return pl.pallas_call(
        functools.partial(mix_out_kernel, spots),
        grid=(steps,),
        out_shape=(
            jax.ShapeDtypeStruct((rows, width), bf16),
            jax.ShapeDtypeStruct((rows, R), f32),
        ),
        in_specs=[pl.BlockSpec((block, 2 * PD), lambda i: (i, 0))] * 4
        + [whole(a) for a in lefts]
        + [whole(right)]
        + [ANY] * len(sources),
        out_specs=(
            pl.BlockSpec((block, width), lambda i: (i, 0)),
            pl.BlockSpec((block, R), lambda i: (i, 0)),
        ),
        scratch_shapes=[pltpu.VMEM((SLOTS * 2 * PD, width), bf16), pltpu.SemaphoreType.DMA((32,))],
        compiler_params=params(48),
        cost_estimate=pl.CostEstimate(
            flops=100_000_000, bytes_accessed=300_000, transcendentals=0
        ),
        name="mix_out",
    )(*mixed, *lefts, right, *sources)


def feed_kernel(own, last, half, pad, spots, *refs):
    second, grad, grank, rgrad, table, dright, gleft = refs[:7]
    right, left = table.at[:, spots.gate], table.at[:, spots.down]
    count = 2 if own else 5
    refs = refs[7:]
    sources, refs = refs[:count], refs[count:]
    if not own:
        (down_in, back_in, ranks_in), refs = refs[:3], refs[3:]
    down_out, back_out, ranks_out, right_grad, left_grad, weight, sems = refs
    copies = feed_copies(sources, own, weight, half, pad)

    @pl.when(pl.program_id(0) == 0)
    def _():
        run_copies(copies, sems, 0)
        feed_pads(weight, half, pad)
        right_grad[...] = jnp.zeros(right_grad.shape, f32)
        left_grad[...] = jnp.zeros(left_grad.shape, f32)
        wait_copies(copies, sems, 0)

    gate_up = nt(second[...], weight[0 : 2 * pad, :]) + nn(grank[...], right[...])
    gate, up = gate_up[:, :pad], gate_up[:, pad:]
    sig = jax.nn.sigmoid(gate)
    act = gate * sig
    hidden = (act * up).astype(bf16)
    hidden_grad = nt(grad[...], weight[2 * pad :, :]) + nn(rgrad[...], left[...])
    gate_grad = hidden_grad * up * (sig * (1.0 + gate * (1.0 - sig)))
    both = jnp.concatenate([gate_grad.astype(bf16), (hidden_grad * act).astype(bf16)], 1)
    down = nn(hidden, weight[2 * pad :, :])
    back = nn(both, weight[0 : 2 * pad, :])
    down_rank = nt(hidden, left[...])
    back_rank = nt(both, right[...])
    if not own:
        down = down + down_in[...]
        back = back + back_in[...]
        down_rank = down_rank + ranks_in[:, :R]
        back_rank = back_rank + ranks_in[:, R:]
    ranks_out[:, :R] = down_rank
    ranks_out[:, R:] = back_rank
    if last:
        down = down + nn(down_rank.astype(bf16), dright[...])
        back = back + nn(back_rank.astype(bf16), gleft[...])
    down_out[...] = down.astype(down_out.dtype)
    back_out[...] = back.astype(back_out.dtype)
    right_grad[...] += tn(grank[...], both)
    left_grad[...] += tn(rgrad[...], hidden)


def feed(own, last, half, spots, second, grad, grank, rgrad, table, dright, gleft, sources, carry):
    rows, width = second.shape
    pad = spots.down.stop - spots.down.start
    block = CHUNK
    kind = bf16 if last else f32
    whole = lambda a: pl.BlockSpec(a.shape, lambda i: (0,) * a.ndim)
    wide = pl.BlockSpec((block, width), lambda i: (i, 0))
    thin = pl.BlockSpec((block, R), lambda i: (i, 0))
    pair = pl.BlockSpec((block, 2 * R), lambda i: (i, 0))
    return pl.pallas_call(
        functools.partial(feed_kernel, own, last, half, pad, spots),
        grid=(rows // block,),
        out_shape=(
            jax.ShapeDtypeStruct((rows, width), kind),
            jax.ShapeDtypeStruct((rows, width), kind),
            jax.ShapeDtypeStruct((rows, 2 * R), f32),
            jax.ShapeDtypeStruct((R, 2 * pad), f32),
            jax.ShapeDtypeStruct((R, pad), f32),
        ),
        in_specs=[wide, wide, thin, thin, whole(table), whole(dright), whole(gleft)]
        + [ANY] * len(sources)
        + ([] if own else [wide, wide, pair]),
        out_specs=(
            wide,
            wide,
            pair,
            pl.BlockSpec((R, 2 * pad), lambda i: (0, 0)),
            pl.BlockSpec((R, pad), lambda i: (0, 0)),
        ),
        scratch_shapes=[pltpu.VMEM((3 * pad, width), bf16), pltpu.SemaphoreType.DMA((16,))],
        compiler_params=params(56),
        cost_estimate=pl.CostEstimate(
            flops=100_000_000, bytes_accessed=300_000, transcendentals=0
        ),
        name="feed",
    )(second, grad, grank, rgrad, table, dright, gleft, *sources, *carry)


def turn_kernel(own, spots, *refs):
    mixer_up, orgrad, table, numer, mixed, base0, base1, head_rows, tails = refs[:9]
    left, taps = table.at[:, spots.left], table.at[:, spots.taps]
    pick, bias, coef = refs[9:12]
    count = 1 if own else 5
    sources = refs[12 : 12 + count]
    up_out, grad_out, state, lent, left_grad, weight, sems = refs[12 + count :]
    copies = output_copies(sources, own, weight, 0)
    run_copies(copies, sems, 0)
    output_pads(weight, 0)
    wait_copies(copies, sems, 0)
    rows = mixer_up.shape[0]

    def one(block, carry):
        span = pl.ds(pl.multiple_of(block * CHUNK, CHUNK), CHUNK)
        both = nt(mixer_up[span, :], weight[...]) + nn(orgrad[span, :], left[...])
        result = []
        for head in range(2):
            cols = slice(PD * head, PD * (head + 1))
            up = both[:, cols]
            total = numer[span, cols].astype(f32)
            scale = lax.rsqrt(jnp.sum(total * total, -1, keepdims=True) * (1.0 / HD) + epsilon)
            inner = jnp.sum(total * up, -1, keepdims=True) * (1.0 / HD)
            grad = (scale * up - total * (scale * scale * scale * inner)).astype(bf16)
            up_out[span, cols] = up.astype(bf16)
            grad_out[span, cols] = grad
            base = (base0 if head == 0 else base1)[span, :]
            _, _, feat = features(nn(base, pick[:, 0:512]), bias[...], coef[...], 0)
            result.append(carry[head] + tn(feat.astype(bf16), grad))
        result.append(carry[2] + tn(orgrad[span, :], mixed[span, :]))
        return tuple(result)

    zero = jnp.zeros((256, PD), f32)
    done = lax.fori_loop(
        0, rows // CHUNK, one, (zero, zero, jnp.zeros((R, 2 * PD), f32))
    )
    left_grad[...] = done[2]
    for head in range(2):
        state[head] = done[head][:STATE].astype(bf16)
        at = HEAD_PAD * head
        query = head_rows[:, at + 2 * PD : at + 3 * PD]
        keys = jnp.concatenate([tails[head, 0:WIN, 0:PD], head_rows[:, at + 3 * PD : at + 4 * PD]], 0)
        vals = jnp.concatenate(
            [tails[head, 0:WIN, PD : 2 * PD], head_rows[:, at + 4 * PD : at + 5 * PD]], 0
        )
        prob = window_prob(query, keys, 0)
        up = up_out[0:QB, PD * head : PD * (head + 1)]
        prob_grad = nt(up, vals)
        inner = jnp.sum(prob * prob_grad, -1, keepdims=True)
        score = (prob * (prob_grad - inner)).astype(bf16)
        lent[head, 0:WIN, 0:PD] = (tn(score, query)[:WIN] * HD ** (-0.5)).astype(bf16)
        lent[head, 0:WIN, PD : 2 * PD] = tn(prob.astype(bf16), up)[:WIN].astype(bf16)
        tap = taps[:, PD * head : PD * (head + 1)].astype(f32)
        gate = head_rows[0:16, at + 6 * PD : at + 7 * PD].astype(f32)
        flow = up_out[0:16, PD * head : PD * (head + 1)].astype(f32) * (gate * jax.nn.sigmoid(gate))
        row0 = tap[2:3] * flow[0:1]
        row1 = tap[1:2] * flow[0:1] + tap[2:3] * flow[1:2]
        index = lax.broadcasted_iota(jnp.int32, (16, PD), 0)
        lent[head, WIN : WIN + 16, 0:PD] = jnp.where(
            index == 14, row0, jnp.where(index == 15, row1, 0.0)
        ).astype(bf16)
        lent[head, WIN : WIN + 16, PD : 2 * PD] = jnp.zeros((16, PD), bf16)


def turn(own, spots, mixer_up, orgrad, table, numer, mixed, proj, tails, tables, sources):
    rows, width = mixer_up.shape
    whole = lambda a: pl.BlockSpec(a.shape, lambda i: (0,) * a.ndim)
    flat = lambda *shape: pl.BlockSpec(shape, lambda i: (0,) * len(shape))
    return pl.pallas_call(
        functools.partial(turn_kernel, own, spots),
        grid=(1,),
        out_shape=(
            jax.ShapeDtypeStruct((rows, 2 * PD), bf16),
            jax.ShapeDtypeStruct((rows, 2 * PD), bf16),
            jax.ShapeDtypeStruct((2, STATE, PD), bf16),
            jax.ShapeDtypeStruct((2, WIN + 16, 2 * PD), bf16),
            jax.ShapeDtypeStruct((R, 2 * PD), f32),
        ),
        in_specs=[
            whole(mixer_up),
            whole(orgrad),
            whole(table),
            whole(numer),
            whole(mixed),
            pl.BlockSpec((rows, PD), lambda i: (0, 0)),
            pl.BlockSpec((rows, PD), lambda i: (0, 7)),
            pl.BlockSpec((QB, 2 * HEAD_PAD), lambda i: (0, 0)),
            whole(tails),
        ]
        + [whole(t) for t in tables]
        + [ANY] * len(sources),
        out_specs=(
            flat(rows, 2 * PD),
            flat(rows, 2 * PD),
            flat(2, STATE, PD),
            flat(2, WIN + 16, 2 * PD),
            flat(R, 2 * PD),
        ),
        scratch_shapes=[pltpu.VMEM((2 * PD, width), bf16), pltpu.SemaphoreType.DMA((8,))],
        compiler_params=params(48),
        cost_estimate=pl.CostEstimate(
            flops=100_000_000, bytes_accessed=300_000, transcendentals=0
        ),
        name="turn",
    )(mixer_up, orgrad, table, numer, mixed, proj, proj, proj, tails, *tables, *sources)


def attend_back_kernel(
    spots, proj, tails, prior, later, lent, ups, grads, table, rank, pick, bias, coef,
    out, rank_grad, right_grad, keys, vals, conv, flow, dkeys, dvals, states
):
    rows = proj.shape[0]
    chunks = rows // CHUNK
    keys[0:WIN, :] = tails[0, 0:WIN, 0:PD]
    vals[0:WIN, :] = tails[0, 0:WIN, PD : 2 * PD]
    conv[0:16, :] = tails[0, WIN : WIN + 16, 0:PD].astype(f32)
    keys[WIN:, :] = proj[:, 3 * PD : 4 * PD]
    vals[WIN:, :] = proj[:, 4 * PD : 5 * PD]
    conv[16:, :] = proj[:, 5 * PD : 6 * PD].astype(f32)
    tap = head_taps(spots, table)
    right = table.at[:, pl.ds(pl.multiple_of(HEAD_PAD * pl.program_id(0), PD), HEAD_PAD)]
    dkeys[...] = jnp.zeros(dkeys.shape, f32)
    dvals[...] = jnp.zeros(dvals.shape, f32)
    dkeys[rows:, :] = lent[0, 0:WIN, 0:PD].astype(f32)
    dvals[rows:, :] = lent[0, 0:WIN, PD : 2 * PD].astype(f32)
    flow[rows:, :] = jnp.zeros((16, PD), f32)
    state = prior[0]
    for chunk in range(chunks):
        span = slice(chunk * CHUNK, (chunk + 1) * CHUNK)
        states[chunk] = state.astype(bf16)
        if chunk + 1 < chunks:
            _, _, feat = features(nn(proj[span, 0:PD], pick[:, 512:1024]), bias[...], coef[...], 0)
            state = state + tn(feat.astype(bf16), proj[span, PD : 2 * PD])
    follow = later[0]
    causal = causal_mask()
    coefs = coef[...]
    for chunk in range(chunks - 1, -1, -1):
        at = chunk * CHUNK
        span = slice(at, at + CHUNK)
        base = proj[span, 0:PD]
        value = proj[span, PD : 2 * PD]
        grad = grads[span, :]
        picked = nn(base, pick[...])
        q_one, q_two, feat_q = features(picked, bias[...], coefs, 0)
        k_one, k_two, feat_k = features(picked, bias[...], coefs, 512)
        key_low = picked[:, 1024:1152].astype(bf16)
        query_high = picked[:, 1152:1280].astype(bf16)
        score = nt(base, key_low)
        weight = jnp.where(causal, 1.0 + score + 0.5 * score * score, 0.0).astype(bf16)
        slope = jnp.where(causal, nt(grad, value) * (1.0 + score), 0.0).astype(bf16)
        follow_round = follow.astype(bf16)
        q_up = nt(grad, states[chunk]) * coefs
        k_up = nt(value, follow_round) * coefs
        low = nn(slope, key_low) + tn(slope, query_high)
        low = low + nt((q_up * q_two).astype(bf16), pick[:, 0:256])
        low = low + nt((q_up * q_one).astype(bf16), pick[:, 256:512])
        low = low + nt((k_up * k_two).astype(bf16), pick[:, 512:768])
        low = low + nt((k_up * k_one).astype(bf16), pick[:, 768:1024])
        out[span, 0:PD] = low.astype(bf16)
        out[span, PD : 2 * PD] = (
            tn(weight, grad) + nn(feat_k.astype(bf16), follow_round)
        ).astype(bf16)
        follow = follow + tn(feat_q.astype(bf16), grad)
        gate = proj[span, 6 * PD : 7 * PD].astype(f32)
        up = ups[span, :].astype(f32)
        sig = jax.nn.sigmoid(gate)
        flow[span, :] = up * gate * sig
        slope_gate = sig * (1.0 + gate * (1.0 - sig))
        out[span, 6 * PD : 7 * PD] = (up * conv_of(conv, tap, at, CHUNK) * slope_gate).astype(bf16)
    for number in range(rows // QB):
        span = slice(number * QB, (number + 1) * QB)
        band = slice(number * QB, number * QB + QB + WIN)
        query = proj[span, 2 * PD : 3 * PD]
        key = keys[band, :]
        prob = window_prob(query, key, number)
        up = ups[span, :]
        prob_grad = nt(up, vals[band, :])
        inner = jnp.sum(prob * prob_grad, -1, keepdims=True)
        score = (prob * (prob_grad - inner)).astype(bf16)
        out[span, 2 * PD : 3 * PD] = (nn(score, key) * HD ** (-0.5)).astype(bf16)
        dkeys[band, :] += tn(score, query) * HD ** (-0.5)
        dvals[band, :] += tn(prob.astype(bf16), up)
    out[:, 3 * PD : 4 * PD] = dkeys[WIN:, :].astype(bf16)
    out[:, 4 * PD : 5 * PD] = dvals[WIN:, :].astype(bf16)
    grad_in = tap[0:1] * flow[0:rows, :]
    for offset in range(1, KW):
        grad_in = grad_in + tap[offset : offset + 1] * flow[offset : offset + rows, :]
    out[:, 5 * PD : 6 * PD] = grad_in.astype(bf16)
    last = slice(rows - 16, rows)
    edge = grad_in[rows - 16 :, :] + lent[0, WIN : WIN + 16, 0:PD].astype(f32)
    out[last, 5 * PD : 6 * PD] = edge.astype(bf16)
    right_grad[...] = tn(rank[...], out[...])

    @pl.when(pl.program_id(0) == 0)
    def _():
        rank_grad[...] = nt(out[...], right[...])

    @pl.when(pl.program_id(0) > 0)
    def _():
        rank_grad[...] += nt(out[...], right[...])


def attend_back(spots, proj, tails, prior, later, lent, ups, grads, table, rank, tables):
    rows = proj.shape[0]
    whole = lambda a: pl.BlockSpec(a.shape, lambda h: (0,) * a.ndim)
    head = pl.BlockSpec((rows, HEAD_PAD), lambda h: (0, h))
    edge = pl.BlockSpec((1, WIN + 16, 2 * PD), lambda h: (h, 0, 0))
    state = pl.BlockSpec((1, 256, PD), lambda h: (h, 0, 0))
    column = pl.BlockSpec((rows, PD), lambda h: (0, h))
    return pl.pallas_call(
        functools.partial(attend_back_kernel, spots),
        grid=(2,),
        out_shape=(
            jax.ShapeDtypeStruct((rows, 2 * HEAD_PAD), bf16),
            jax.ShapeDtypeStruct((rows, R), f32),
            jax.ShapeDtypeStruct((R, 2 * HEAD_PAD), f32),
        ),
        in_specs=[head, edge, state, state, edge, column, column, whole(table), whole(rank)]
        + [whole(t) for t in tables],
        out_specs=(
            head,
            pl.BlockSpec((rows, R), lambda h: (0, 0)),
            pl.BlockSpec((R, HEAD_PAD), lambda h: (0, h)),
        ),
        scratch_shapes=[
            pltpu.VMEM((rows + WIN, PD), bf16),
            pltpu.VMEM((rows + WIN, PD), bf16),
            pltpu.VMEM((rows + 16, PD), f32),
            pltpu.VMEM((rows + 16, PD), f32),
            pltpu.VMEM((rows + WIN, PD), f32),
            pltpu.VMEM((rows + WIN, PD), f32),
            pltpu.VMEM((rows // CHUNK, 256, PD), bf16),
        ],
        compiler_params=params(48),
        cost_estimate=pl.CostEstimate(
            flops=100_000_000, bytes_accessed=300_000, transcendentals=0
        ),
        name="attend_back",
    )(proj, tails, prior, later, lent, ups, grads, table, rank, *tables)


def first_back_kernel(*refs):
    grads = refs[0:4]
    rank_grad, left = refs[4:6]
    sources = refs[6 : 6 + 16]
    part, weight, sems = refs[22:]
    groups = []
    size = 2 * HEAD_PAD
    for slot in range(SLOTS):
        pieces = sources[0:1] if slot == 0 else sources[1 + 5 * (slot - 1) : 1 + 5 * slot]
        groups.append(mixer_copies(pieces, slot == 0, weight, size * slot))
    begin = pl.program_id(0) == 0

    @pl.when(begin)
    def _():
        for slot in range(SLOTS):
            run_copies(groups[slot], sems, 40 * slot)
        for slot in range(SLOTS):
            mixer_pads(weight, size * slot)

    total = nn(rank_grad[...].astype(bf16), left[...])
    for slot in range(SLOTS):

        @pl.when(begin)
        def _():
            wait_copies(groups[slot], sems, 40 * slot)

        total = total + nn(grads[slot][...], weight[size * slot : size * (slot + 1), :])
    part[...] = total.astype(bf16)


def first_back(number, grads, rank_grad, left, sources):
    rows = rank_grad.shape[0]
    width = left.shape[1]
    block = rows // 4
    whole = lambda a: pl.BlockSpec(a.shape, lambda i: (0,) * a.ndim)
    size = 2 * HEAD_PAD
    return pl.pallas_call(
        first_back_kernel,
        grid=(2,),
        out_shape=jax.ShapeDtypeStruct((rows // 2, width), bf16),
        in_specs=[pl.BlockSpec((block, size), lambda i: (2 * i + number, 0))] * 4
        + [pl.BlockSpec((block, R), lambda i: (2 * i + number, 0)), whole(left)]
        + [ANY] * len(sources),
        out_specs=pl.BlockSpec((block, width), lambda i: (i, 0)),
        scratch_shapes=[pltpu.VMEM((SLOTS * size, width), bf16), pltpu.SemaphoreType.DMA((160,))],
        compiler_params=params(56),
        cost_estimate=pl.CostEstimate(
            flops=100_000_000, bytes_accessed=300_000, transcendentals=0
        ),
        name="first_back",
    )(*grads, rank_grad, left, *sources)


def norm_two_kernel(own, other, wide, gain, left, middle, second, rank):
    total = wide[...].astype(f32) + (own[...].astype(f32) + other[...].astype(f32))
    scale = lax.rsqrt(jnp.mean(total * total, -1, keepdims=True) + epsilon)
    rounded = (total * scale * gain[...]).astype(bf16)
    middle[...] = total
    second[...] = rounded
    rank[...] = nn(rounded, left[...]).astype(bf16)


def norm_two(own, other, wide, gain, left):
    rows, width = own.shape
    block = pl.BlockSpec((CHUNK, width), lambda i: (i, 0))
    whole = lambda a: pl.BlockSpec(a.shape, lambda i: (0,) * a.ndim)
    return pl.pallas_call(
        norm_two_kernel,
        grid=(rows // CHUNK,),
        out_shape=(
            jax.ShapeDtypeStruct((rows, width), f32),
            jax.ShapeDtypeStruct((rows, width), bf16),
            jax.ShapeDtypeStruct((rows, R), bf16),
        ),
        in_specs=[block, block, block, whole(gain), whole(left)],
        out_specs=(block, block, pl.BlockSpec((CHUNK, R), lambda i: (i, 0))),
        compiler_params=params(40),
        cost_estimate=pl.CostEstimate(
            flops=100_000_000, bytes_accessed=300_000, transcendentals=0
        ),
        name="norm_two",
    )(own, other, wide, gain, left)


def back_two_kernel(own, other, middle, upstream, gain, right, mixer_up, rgrad):
    vector = middle[...]
    scale = lax.rsqrt(jnp.mean(vector * vector, -1, keepdims=True) + epsilon)
    flow = gain[...] * (own[...].astype(f32) + other[...].astype(f32))
    inner = jnp.mean(vector * flow, -1, keepdims=True)
    total = upstream[...].astype(f32) + scale * flow - vector * (scale * scale * scale * inner)
    rounded = total.astype(bf16)
    mixer_up[...] = rounded
    rgrad[...] = nt(rounded, right[...]).astype(bf16)


def back_two(own, other, middle, upstream, gain, right):
    rows, width = own.shape
    block = pl.BlockSpec((CHUNK, width), lambda i: (i, 0))
    whole = lambda a: pl.BlockSpec(a.shape, lambda i: (0,) * a.ndim)
    return pl.pallas_call(
        back_two_kernel,
        grid=(rows // CHUNK,),
        out_shape=(
            jax.ShapeDtypeStruct((rows, width), bf16),
            jax.ShapeDtypeStruct((rows, R), bf16),
        ),
        in_specs=[block, block, block, block, whole(gain), whole(right)],
        out_specs=(block, pl.BlockSpec((CHUNK, R), lambda i: (i, 0))),
        compiler_params=params(40),
        cost_estimate=pl.CostEstimate(
            flops=100_000_000, bytes_accessed=300_000, transcendentals=0
        ),
        name="back_two",
    )(own, other, middle, upstream, gain, right)


def swap_core(array):
    return lax.ppermute(array, "core", [(0, 1), (1, 0)])


def swap_chip(array, bit):
    count = lax.axis_size("chip")
    return lax.ppermute(array, "chip", [(i, i ^ bit) for i in range(count)])


def swap_tp(array, bit):
    return lax.ppermute(array, "tp", [(i, i ^ bit) for i in range(4)])


def both_cores(own):
    other = swap_core(own)
    lead = lax.axis_index("core") == 0
    return jnp.concatenate([jnp.where(lead, own, other), jnp.where(lead, other, own)], 0)


def own_rows(array, core):
    half = array.shape[0] // 2
    return lax.dynamic_slice_in_dim(array, core * half, half, 0)


def hold_kernel(*refs):
    pass


def hold(*arrays, after=()):
    return pl.pallas_call(
        hold_kernel,
        out_shape=tuple(jax.ShapeDtypeStruct(a.shape, a.dtype) for a in arrays),
        in_specs=[ANY] * (len(arrays) + len(after)),
        out_specs=(ANY,) * len(arrays),
        input_output_aliases={i: i for i in range(len(arrays))},
        compiler_params=pltpu.CompilerParams(has_side_effects=True),
        name="hold",
    )(*arrays, *after)


def hop_xy(piece):
    return swap_chip(piece, 1), swap_chip(piece, 2)


def hop_diag(from_x, from_y, cut):
    return swap_chip(from_y[:cut], 1), swap_chip(from_x[cut:], 2)


def cross(array):
    return lax.ppermute(array, "tp", [(1, 2), (2, 1)])


def edge(array):
    return lax.ppermute(array, "tp", [(1, 0), (2, 3)])


def pick_inner(inner_array, edge_array):
    z = lax.axis_index("tp")
    return jnp.where((z == 1) | (z == 2), inner_array, edge_array)


def add_swapped(array, bit):
    other = swap_chip(array, bit)
    return (array.astype(f32) + other.astype(f32)).astype(array.dtype)


def add_rest(array):
    bit = 2
    while bit < lax.axis_size("chip"):
        array = add_swapped(array, bit)
        bit *= 2
    return array


def neighbour_chip(array, by):
    count = lax.axis_size("chip")
    pairs = [(i, i + by) for i in range(count) if 0 <= i + by < count]
    return lax.ppermute(array, "chip", pairs)


def carried(states, backward):
    if backward and lax.axis_size("chip") == 4:
        return tuple(swap_chip(states, bit) for bit in (1, 2, 3))
    return (lax.all_gather(states, "chip"),)


def carried_sum(parts, backward):
    chip = lax.axis_index("chip")
    if len(parts) > 1:
        total = 0.0
        for bit, part in zip((1, 2, 3), parts):
            other = chip ^ bit
            ahead = (other > chip) if backward else (other < chip)
            total = total + jnp.where(ahead, part.astype(f32), 0.0)
    else:
        index = jnp.arange(lax.axis_size("chip"), dtype=jnp.int32)
        ahead = (index > chip) if backward else (index < chip)
        total = jnp.sum(jnp.where(ahead[:, None, None, None], parts[0].astype(f32), 0.0), 0)
    return jnp.pad(total, ((0, 0), (0, 256 - STATE), (0, 0)))


def stack_tp(parts):
    z = lax.axis_index("tp")
    result = jnp.zeros((SLOTS,) + parts[0].shape, parts[0].dtype)
    for slot, part in enumerate(parts):
        result = lax.dynamic_update_index_in_dim(result, part, z ^ slot, 0)
    return result


def pad_heads(table):
    lead = table.shape[:-2]
    heads = table.shape[-2]
    zero = [(0, 0)] * (len(lead) + 1)
    low = jnp.pad(table[..., : 2 * FD], zero + [(0, PD - 2 * FD)])
    high = table[..., 2 * FD :].reshape(lead + (heads, 6, HD))
    high = jnp.pad(high, zero + [(0, 0), (0, PD - HD)]).reshape(lead + (heads, 6 * PD))
    return jnp.concatenate([low, high], -1).reshape(lead + (heads * HEAD_PAD,))


def trim_heads(table):
    lead = table.shape[:-1]
    table = table.reshape(lead + (2, 7, PD))
    low = table[..., 0, : 2 * FD]
    high = table[..., 1:, :HD].reshape(lead + (2, 6 * HD))
    return jnp.concatenate([low, high], -1)


def pad_last(table, size):
    return jnp.pad(table, [(0, 0)] * (table.ndim - 1) + [(0, size - table.shape[-1])])


def norm_rows(vector, gain_vector):
    row_scale = lax.rsqrt(jnp.mean(vector * vector, -1, keepdims=True) + epsilon)
    return (vector * row_scale * gain_vector, row_scale)


def norm_back(vector, row_scale, gain_vector, upstream):
    inner_mean = jnp.mean(vector * gain_vector * upstream, -1, keepdims=True)
    return (
        row_scale * gain_vector * upstream - vector * row_scale * row_scale * row_scale * inner_mean
    )


def body(
    block_input,
    gain_first,
    frozen_mixer_weight,
    conv_filter,
    frozen_output_weight,
    gain_second,
    frozen_gate_up_weight,
    frozen_down_weight,
    mixer_left,
    mixer_right,
    output_left,
    output_right,
    gateup_left,
    gateup_right,
    down_left,
    down_right,
    adapter_index,
    seq_lengths,
    out_cotangent,
):
    chip = lax.axis_index("chip")
    core = lax.axis_index("core")
    z = lax.axis_index("tp")
    y, x = place()
    sequences, length, width = block_input.shape
    rows = 2 * length
    heads_here = frozen_mixer_weight.shape[1]
    ff_here = frozen_down_weight.shape[0]
    half = ff_here // 2
    pad = (half + PD - 1) // PD * PD
    quarter = half // 2

    pick, bias, coef = feature_tables()
    tables = (jnp.asarray(pick, bf16), jnp.asarray(bias), jnp.asarray(coef))

    w_mix = jnp.transpose(frozen_mixer_weight, (1, 2, 0)).reshape(heads_here * HCOLS, width)
    w_gate = jnp.transpose(frozen_gate_up_weight, (1, 2, 0)).reshape(2 * ff_here, width)
    w_out = frozen_output_weight
    w_down = frozen_down_weight
    side = width // 2

    def cut(matrix, start, count):
        return lax.dynamic_slice(matrix, (start, x * side), (count, side))

    mixer_piece = jnp.concatenate(
        [
            cut(w_mix, 2 * HCOLS * core + HCOLS * y, HCOLS),
            cut(w_out, 2 * HD * core + HD * y, HD),
        ],
        0,
    )
    feed_piece = jnp.concatenate(
        [
            cut(w_gate, half * core + quarter * y, quarter),
            cut(w_gate, ff_here + half * core + quarter * y, quarter),
            cut(w_down, half * core + quarter * y, quarter),
        ],
        0,
    )
    slot_seq = z ^ jnp.arange(SLOTS, dtype=jnp.int32)
    slot_adapter = jnp.sum(
        jnp.where(slot_seq[:, None] == jnp.arange(SLOTS)[None, :], adapter_index[None, :], 0), 1
    )
    onehot = slot_adapter[:, None] == jnp.arange(NA, dtype=jnp.int32)[None, :]

    def select(table):
        return jnp.einsum(
            "se,e...->s...", onehot.astype(bf16), table, preferred_element_type=f32
        ).astype(bf16)

    mine = slot_adapter[0]
    my_mixer_left = lax.dynamic_index_in_dim(mixer_left, mine, 0, False)
    my_output_right = lax.dynamic_index_in_dim(output_right, mine, 0, False)
    my_gateup_left = lax.dynamic_index_in_dim(gateup_left, mine, 0, False)
    my_down_right = lax.dynamic_index_in_dim(down_right, mine, 0, False)
    right_table = pad_heads(
        select(lax.dynamic_slice_in_dim(mixer_right, 2 * core, 2, 2))
    )
    out_table = lax.dynamic_slice_in_dim(jnp.swapaxes(output_left, 1, 2), 2 * HD * core, 2 * HD, 2)
    out_table = pad_last(select(out_table).reshape(SLOTS, R, 2, HD), PD).reshape(SLOTS, R, 2 * PD)
    gate_table = lax.dynamic_slice_in_dim(gateup_right, half * core, half, 3)
    gate_table = pad_last(select(gate_table), pad).reshape(SLOTS, R, 2 * pad)
    down_table = lax.dynamic_slice_in_dim(jnp.swapaxes(down_left, 1, 2), half * core, half, 2)
    down_table = pad_last(select(down_table), pad)
    taps = lax.dynamic_slice_in_dim(conv_filter, 2 * HD * core, 2 * HD, 1)
    taps = pad_last(taps.reshape(KW, 2, HD), PD).reshape(KW, 2 * PD)
    taps = jnp.broadcast_to(jnp.pad(taps, ((0, R - KW), (0, 0))), (SLOTS, R, 2 * PD))
    packed = jnp.concatenate([right_table, out_table, gate_table, down_table, taps], 2)
    spots = Table(pad)

    gain_one = gain_first.astype(f32)
    gain_two = gain_second.astype(f32)[None, :]
    own_input = lax.dynamic_index_in_dim(block_input, z, 0, False)
    own_cotangent = lax.dynamic_index_in_dim(out_cotangent, z, 0, False)
    my_length = lax.dynamic_index_in_dim(seq_lengths, z, 0, False)
    upstream_own = jnp.where(
        (((chip * 2 + core) * length + jnp.arange(length, dtype=jnp.int32)) < my_length)[:, None],
        own_cotangent,
        0.0,
    ).astype(bf16)

    e_m, c_m = swap_tp(mixer_piece, 1), cross(mixer_piece)
    both_input = both_cores(own_input)
    first = norm_rows(both_input.astype(f32), gain_one)[0].astype(bf16)
    mixer_rank = nn(first, my_mixer_left).astype(bf16)
    e_m, c_m, mixer_rank, packed = hold(e_m, c_m, mixer_rank, packed)

    projs, tails, states = [], [], []
    borrowed, prior, mixed, numer = [None] * SLOTS, [None] * SLOTS, [], []
    slots = [packed[0], None, None, None]

    def attend_slot(slot):
        out = attend(spots, projs[slot], borrowed[slot], prior[slot], slots[slot], tables)
        for kept, value in zip((mixed, numer), out):
            kept.append(value)

    def project_slot(slot, refs):
        out = project(slot == 0, first, mixer_rank, slots[slot], tables, refs)
        for kept, value in zip((projs, tails, states), out):
            kept.append(value)

    def exchange(slot):
        edges_here = jnp.concatenate(tails[slot : slot + 2], 0).reshape(4, 2 * (WIN + 16), PD)
        states_here = jnp.concatenate(states[slot : slot + 2], 0)
        return lax.all_gather(jnp.concatenate([states_here, edges_here], 1), "chip")

    def use_exchange(slot, gathered):
        total = carried_sum((gathered[:, :, :STATE],), False)
        before = lax.dynamic_index_in_dim(gathered, jnp.maximum(chip - 1, 0), 0, False)
        before = jnp.where(chip > 0, before[:, STATE:], 0.0).astype(bf16)
        before = before.reshape(4, WIN + 16, 2 * PD)
        borrowed[slot], borrowed[slot + 1] = before[:2], before[2:]
        prior[slot], prior[slot + 1] = total[:2], total[2:]

    x1, y1 = hop_xy(e_m)
    c2_m, f_m = cross(e_m), edge(c_m)
    table1 = swap_tp(packed[1], 1)
    project_slot(0, (w_mix,))
    slot2 = pick_inner(c2_m, f_m)
    x1, y1, slot2, c2_m, c_m, tails[0], states[0], table1, feed_piece, packed = hold(
        x1, y1, slot2, c2_m, c_m, tails[0], states[0], table1, feed_piece, packed
    )
    slots[1] = table1
    d1 = hop_diag(x1, y1, M_CUT)
    x2, y2 = hop_xy(slot2)
    f2_m = edge(c2_m)
    table2, table3 = swap_tp(packed[2], 2), swap_tp(packed[3], 3)
    slot3 = pick_inner(c_m, f2_m)
    x2, y2, slot3, feed_piece, table2, table3, *d1 = hold(
        x2, y2, slot3, feed_piece, table2, table3, *d1
    )
    slots[2], slots[3] = table2, table3
    d2 = hop_diag(x2, y2, M_CUT)
    x3, y3 = hop_xy(slot3)
    e_f = swap_tp(feed_piece, 1)
    set1 = (e_m, x1, y1, *d1)
    project_slot(1, set1)
    x3, y3, e_f, tails[0], tails[1], states[0], states[1], upstream_own, *d2 = hold(
        x3, y3, e_f, tails[0], tails[1], states[0], states[1], upstream_own, *d2
    )
    d3 = hop_diag(x3, y3, M_CUT)
    c_f = cross(feed_piece)
    exchanged = exchange(0)
    set2 = (slot2, x2, y2, *d2)
    project_slot(2, set2)
    upstream = both_cores(upstream_own)
    down_rgrad = nt(upstream, my_down_right).astype(bf16)
    c_f, states[2], down_rgrad, *d3 = hold(c_f, states[2], down_rgrad, *d3)
    fx1, fy1 = hop_xy(e_f)
    c2_f, f_f = cross(e_f), edge(c_f)
    set3 = (slot3, x3, y3, *d3)
    project_slot(3, set3)
    fslot2 = pick_inner(c2_f, f_f)
    fx1, fy1, fslot2, c2_f, c_f, tails[3], states[2], states[3], exchanged = hold(
        fx1, fy1, fslot2, c2_f, c_f, tails[3], states[2], states[3], exchanged
    )
    use_exchange(0, exchanged)
    fd1 = hop_diag(fx1, fy1, feed_cut(quarter))
    fx2, fy2 = hop_xy(fslot2)
    f2_f = edge(c2_f)
    exchanged = exchange(2)
    attend_slot(0)
    attend_slot(1)
    fslot3 = pick_inner(c_f, f2_f)
    fx2, fy2, fslot3, mixed[0], mixed[1], exchanged, *fd1 = hold(
        fx2, fy2, fslot3, mixed[0], mixed[1], exchanged, *fd1
    )
    use_exchange(2, exchanged)
    fd2 = hop_diag(fx2, fy2, feed_cut(quarter))
    fx3, fy3 = hop_xy(fslot3)
    attend_slot(2)
    attend_slot(3)
    sets = list(set1) + list(set2) + list(set3)
    out_part, out_rank = mix_out(spots, mixed, slots, my_output_right, [w_out] + sets)
    other_part = swap_core(out_part)
    middle, second, gate_rank = norm_two(out_part, other_part, both_input, gain_two, my_gateup_left)
    weights_feed = [
        (w_gate, w_down),
        (e_f, fx1, fy1, *fd1),
        None,
        None,
    ]

    gateup_left_t = my_gateup_left.T
    carry = ()
    gate_grads, down_grads = [], []
    for slot in range(SLOTS):
        out = feed(
            slot == 0,
            slot == SLOTS - 1,
            half,
            spots,
            second,
            upstream,
            gate_rank,
            down_rgrad,
            slots[slot],
            my_down_right,
            gateup_left_t,
            weights_feed[slot],
            carry,
        )
        carry = list(out[:3])
        if slot == 0:
            fx3, fy3, carry[2], *fd2 = hold(fx3, fy3, carry[2], *fd2)
            weights_feed[2] = (fslot2, fx2, fy2, *fd2)
            fd3 = hop_diag(fx3, fy3, feed_cut(quarter))
        if slot == 1:
            carry[2], *fd3 = hold(carry[2], *fd3)
            weights_feed[3] = (fslot3, fx3, fy3, *fd3)
        gate_grads.append(out[3])
        down_grads.append(out[4])
    down_part, back_part, ranks = carry
    down_rank, gateup_rgrad = ranks[:, :R].astype(bf16), ranks[:, R:].astype(bf16)
    other_back = swap_core(back_part)
    other_down = swap_core(own_rows(down_part, 1 - core))
    own_down = own_rows(down_part, core).astype(f32)
    own_output = own_rows(middle, core) + (own_down + other_down.astype(f32))
    own_output = own_output.astype(bf16)
    mixer_up, output_rgrad = back_two(
        back_part, other_back, middle, upstream, gain_two, my_output_right
    )

    ups, grads, back_states, lent, left_grads = [], [], [], [], []

    def back_exchange(slot):
        edges_here = jnp.concatenate(lent[slot : slot + 2], 0)
        states_here = jnp.concatenate(back_states[slot : slot + 2], 0)
        return (neighbour_chip(edges_here, -1),) + carried(states_here, True)

    weights_out = [(w_out,), set1, set2, set3]
    for slot in range(SLOTS):
        out = turn(
            slot == 0,
            spots,
            mixer_up,
            output_rgrad,
            slots[slot],
            numer[slot],
            mixed[slot],
            projs[slot],
            borrowed[slot],
            tables,
            weights_out[slot],
        )
        for kept, value in zip((ups, grads, back_states, lent, left_grads), out):
            kept.append(value)
        if slot == 1:
            *both, own_output = hold(*lent, *back_states, own_output)
            lent, back_states = both[:2], both[2:]
            block_output = lax.all_gather(own_output, "tp")
            crossing = back_exchange(0)
    lent[2], lent[3], back_states[2], back_states[3], *crossing = hold(
        *lent[2:], *back_states[2:], *crossing
    )

    def back_slot(slot, returned, later):
        pair = slice(slot % 2 * 2, slot % 2 * 2 + 2)
        return attend_back(
            spots,
            projs[slot],
            borrowed[slot],
            prior[slot],
            later[pair],
            returned[pair],
            ups[slot],
            grads[slot],
            slots[slot],
            mixer_rank,
            tables,
        )

    returned, later = crossing[0], carried_sum(crossing[1:], True)
    crossing = back_exchange(2)
    backs = [back_slot(0, returned, later), back_slot(1, returned, later)]
    early_rank = backs[0][1] + backs[1][1]
    shared = jnp.stack(
        [
            tn(out_rank.astype(bf16), mixer_up),
            tn(gateup_rgrad, second),
            tn(down_rank, upstream),
        ]
    )
    owned = jnp.stack(
        [jnp.concatenate([left_grads[i], gate_grads[i], down_grads[i]], 1) for i in range(SLOTS)]
    ).astype(bf16)
    shared, owned, early_rank, *crossing = hold(shared, owned, early_rank, *crossing)
    returned, later = crossing[0], carried_sum(crossing[1:], True)
    shared_x, owned_x = swap_chip(shared, 1), swap_chip(owned, 1)
    backs = backs + [back_slot(2, returned, later), back_slot(3, returned, later)]
    rank_grad = early_rank + backs[2][1] + backs[3][1]
    rank_grad, shared_x, owned_x = hold(rank_grad, shared_x, owned_x)

    def join(array, other):
        return (array.astype(f32) + other.astype(f32)).astype(array.dtype)

    def by_core(own, other):
        lead = core == 0
        return jnp.stack([jnp.where(lead, own, other), jnp.where(lead, other, own)])

    def slots_of(owned, shared):
        flat = shared.reshape(-1)
        size = owned.size // SLOTS
        sent = [jnp.concatenate([owned[k].reshape(-1), flat.astype(bf16)]) for k in range(SLOTS)]
        got = [sent[0]] + [swap_tp(sent[bit], bit) for bit in (1, 2, 3)]
        return got, lambda got: (
            jnp.stack([g[:size].reshape(owned.shape[1:]) for g in got]).astype(f32),
            [g[size:].reshape(shared.shape).astype(f32) for g in got],
        )

    shared, owned = join(shared, shared_x), join(owned, owned_x)
    shared, owned = add_rest(shared), add_rest(owned)
    mixer_all = jnp.concatenate(
        [
            jnp.stack([back[2] for back in backs]),
            tn(rank_grad.astype(bf16), first)[None],
        ],
        0,
    ).astype(bf16)
    proj_grads = [back[0] for back in backs]
    left_t = my_mixer_left.T
    flat_mix = [w_mix] + sets
    part_a = first_back(0, proj_grads, rank_grad, left_t, flat_mix)
    part_a, rank_grad, mixer_all, shared, owned = hold(
        part_a, rank_grad, mixer_all, shared, owned, after=(block_output,)
    )
    block = length // 2

    def finish(part, number):
        here = lax.dynamic_slice_in_dim(part, core * block, block, 0)
        there = lax.dynamic_slice_in_dim(part, (1 - core) * block, block, 0)
        total = here.astype(f32) + swap_core(there).astype(f32)
        wide = own_input[number * block : (number + 1) * block].astype(f32)
        scale_one = lax.rsqrt(jnp.mean(wide * wide, -1, keepdims=True) + epsilon)
        straight = lax.dynamic_slice_in_dim(
            mixer_up, core * length + number * block, block, 0
        ).astype(f32)
        return (straight + norm_back(wide, scale_one, gain_one, total)).astype(bf16)

    done_a = finish(part_a, 0)
    e_a, c_a = swap_tp(done_a, 1), cross(done_a)
    mixer_x = swap_chip(mixer_all, 1)
    shared_core, owned_core = swap_core(shared), swap_core(owned)
    part_b = first_back(1, proj_grads, rank_grad, left_t, flat_mix)
    e_a, c_a, part_b, mixer_x, shared_core, owned_core = hold(
        e_a, c_a, part_b, mixer_x, shared_core, owned_core
    )
    done_b = finish(part_b, 1)
    c2_a, f_a = cross(e_a), edge(c_a)
    e_b, c_b = swap_tp(done_b, 1), cross(done_b)
    mixer_all = add_rest(join(mixer_all, mixer_x))
    shared = shared + shared_core
    owned = jnp.swapaxes(by_core(owned, owned_core), 0, 1)
    c2_a, f_a, e_b, c_b, mixer_all, shared, owned = hold(
        c2_a, f_a, e_b, c_b, mixer_all, shared, owned
    )
    f2_a, c2_b, f_b = edge(c2_a), cross(e_b), edge(c_b)
    mixer_core = swap_core(mixer_all)
    f2_a, c2_b, f_b, mixer_core, shared, owned = hold(f2_a, c2_b, f_b, mixer_core, shared, owned)
    f2_b = edge(c2_b)
    mixer_owned = jnp.swapaxes(by_core(mixer_all[:SLOTS], mixer_core[:SLOTS]), 0, 1)
    mixer_shared = mixer_all[SLOTS].astype(f32) + mixer_core[SLOTS].astype(f32)
    early, split_early = slots_of(owned, shared)
    late, split_late = slots_of(mixer_owned, mixer_shared)
    owned, shared = split_early(early)
    right_sum, mixer_shared = split_late(late)
    z_a = [done_a, e_a, pick_inner(c2_a, f_a), pick_inner(c_a, f2_a)]
    z_b = [done_b, e_b, pick_inner(c2_b, f_b), pick_inner(c_b, f2_b)]
    input_grad = jnp.zeros(block_input.shape, bf16)
    for number, parts in enumerate((z_a, z_b)):
        for slot, part in enumerate(parts):
            input_grad = lax.dynamic_update_slice(
                input_grad, part[None], (z ^ slot, number * block, 0)
            )

    slot_hot = onehot.astype(f32)

    def spread(hot, parts):
        shape = (NA,) + (1,) * parts[0].ndim
        return sum(hot[i].reshape(shape) * parts[i][None] for i in range(SLOTS))

    grad_mixer_left = jnp.swapaxes(spread(slot_hot, mixer_shared), 1, 2)
    grad_output_right = spread(slot_hot, [s[0] for s in shared])
    grad_gateup_left = jnp.swapaxes(spread(slot_hot, [s[1] for s in shared]), 1, 2)
    grad_down_right = spread(slot_hot, [s[2] for s in shared])
    first_edge = 2 * HEAD_PAD
    edges = [edge_at - first_edge for edge_at in spots.edges]
    b, c, d = [owned[..., edges[i] : edges[i + 1]] for i in (1, 2, 3)]
    a = jnp.moveaxis(trim_heads(right_sum), 1, 2).reshape(SLOTS, R, heads_here, HCOLS)
    grad_mixer_right = spread(slot_hot, a)
    b = b.reshape(SLOTS, 2, R, 2, PD)[..., :HD]
    b = jnp.moveaxis(b, 1, 2).reshape(SLOTS, R, heads_here * HD)
    grad_output_left = jnp.swapaxes(spread(slot_hot, b), 1, 2)
    c = c.reshape(SLOTS, 2, R, 2, pad)[..., :half]
    c = jnp.moveaxis(c, 1, 3).reshape(SLOTS, R, 2, ff_here)
    grad_gateup_right = spread(slot_hot, c)
    d = jnp.moveaxis(d[..., :half], 1, 2).reshape(SLOTS, R, ff_here)
    grad_down_left = jnp.swapaxes(spread(slot_hot, d), 1, 2)
    return (
        block_output,
        input_grad,
        grad_mixer_left,
        grad_mixer_right,
        grad_output_left,
        grad_output_right,
        grad_gateup_left,
        grad_gateup_right,
        grad_down_left,
        grad_down_right,
    )


def solution(mesh):
    seq, tp = mesh.devices.shape
    fine = Mesh(mesh.devices.reshape(seq // 2, 2, tp), ("chip", "core", "tp"))
    where = ("chip", "core")
    return jax.shard_map(
        body,
        mesh=fine,
        in_specs=(
            P(None, where, None),
            P(),
            P(None, "tp", None),
            P(None, "tp"),
            P("tp", None),
            P(),
            P(None, None, "tp"),
            P("tp", None),
            P(),
            P(None, None, "tp", None),
            P(None, "tp", None),
            P(),
            P(),
            P(None, None, None, "tp"),
            P(None, "tp", None),
            P(),
            P(),
            P(),
            P(None, where, None),
        ),
        out_specs=(
            P(None, where, None),
            P(None, where, None),
            P(),
            P(None, None, "tp", None),
            P(None, "tp", None),
            P(),
            P(),
            P(None, None, None, "tp"),
            P(None, "tp", None),
            P(),
        ),
        check_vma=False,
    )
```

time: 2040 us -> 997 us (0.49)
  waiting for transfers between devices: 1090 us -> 216 us
  matrix products: 463 us -> 9.39 us
  Pallas kernels: 0 us -> 409 us
  other arithmetic: 280 us -> 99.1 us
  starting transfers between devices: 14.8 us -> 102 us
  local copies, waits for them, and re-layouts: 173 us -> 130 us
    psum x5 -> x0, waiting for transfers between devices: 1090 us -> none  [the longest x1 489 us: body(): lax.psum(second_branch_path.astype(jnp.bfloat16), 'tp').astype(jnp.float32)]
    dot_general x65 -> x10, matrix products: 450 us -> 9.39 us  [the longest x4 5.37 us: tn(): lax.dot_general(a, b, (((0,), (0,)), ((), ())), preferred_element_type=f32)]
    pallas_call x0 -> x42, Pallas kernels: none -> 409 us  [the longest x4 109 us: feed(): pl.pallas_call(functools.partial(feed_kernel, own, last, half, pad, spots...]
    ppermute x6 -> x77, waiting for transfers between devices: 0.02 us -> 216 us  [the longest x8 94.9 us: edge(): return lax.ppermute(array, 'tp', [(1, 0), (2, 3)])]
    ppermute x6 -> x77, starting transfers between devices: 14.3 us -> 102 us  [the longest x36 43.2 us: swap_chip(): return lax.ppermute(array, 'chip', [(i, i ^ bit) for i in range(count)])]
    scatter-add x4 -> x0, other arithmetic: 84.3 us -> none  [taylor(): square_terms = vector[..., leading] * vector[..., trailing] * weights]
    convert_element_type x14 -> x15, other arithmetic: 90.2 us -> 19.2 us  [the longest x1 5.13 us: body(): own_output = own_output.astype(bf16)]
    gather x4 -> x0, local copies, waits for them, and re-layouts: 44 us -> none  [taylor(): square_terms = vector[..., leading] * vector[..., trailing] * weights]
  transfers between devices with their start and end apart: 13 -> 80, of which waited for: 5 -> 25; matrix products, arithmetic and copies ran while one was open for 23% -> 16% of each run, Pallas kernels for 0% -> 30%
where the time goes in v1:
time: 997 us; the launch traced here: 984 us
  Pallas kernels  409 us (41%)
  waiting for transfers between devices  216 us (22%)
  local copies, waits for them, and re-layouts  130 us (13%)
  starting transfers between devices  102 us (10%)
  other arithmetic  99.1 us (10%)
  between operations  17.9 us (2%)
    pallas_call x4, Pallas kernels, feed(): pl.pallas_call(functools.partial(feed_kernel, own, last, half, pad, spots...  109 us
    ppermute x8, waiting for transfers between devices, edge(): return lax.ppermute(array, 'tp', [(1, 0), (2, 3)])  94.9 us
    pallas_call x4, Pallas kernels, attend_back(): pl.pallas_call(functools.partial(attend_back_kernel, spots), grid=(2,), o...  81.2 us
    pallas_call x4, Pallas kernels, project(): pl.pallas_call(functools.partial(project_kernel, own), out_shape=(jax.Sha...  72 us
    ppermute x36, waiting for transfers between devices, swap_chip(): return lax.ppermute(array, 'chip', [(i, i ^ bit) for i in range(count)])  63.2 us
    unnamed x443, local copies, waits for them, and re-layouts  55.6 us
    pallas_call x2, Pallas kernels, first_back(): pl.pallas_call(first_back_kernel, grid=(2,), out_shape=jax.ShapeDtypeStru...  50.8 us
    ppermute x13, waiting for transfers between devices, swap_tp(): return lax.ppermute(array, 'tp', [(i, i ^ bit) for i in range(4)])  48.4 us
  transfers between devices with their start and end apart: 80, of which 25 were waited for; matrix products, arithmetic and copies ran while one was open for 16% of the time, Pallas kernels for 30%

profile of v1, /device:TPU:0, one launch (start us, length us, event | category | flops | bytes accessed | tf_op | source)
XLA Modules:
  0.0 983.9 jit_solution(14575480237048773322)
XLA Ops:
  62.8 17.2 %project.4 = (bf16[1024,1792]{1,0:T(8,128)(2,1)S(1)}, bf16[2,80,256]{2,1,0:T(8,128)(2,1)S(1)}, bf16[2,160,128]{2,1,0:T(8,128)(2,1)S(1)}) custom-call(bf16[1024,1792]{1,0:T(8,128)(2,1)} %copy-done.136, bf16[1024,16]{1,0:T(8,128)(2,1)S(1)} %copy-done.27, bf16[16,4224]{1,0:T(8,128)(2,1)S(1)} %get-tuple-element.421.table.refs_4_.refs_2_, ...), custom_call_target="tpu_custom_call" | custom-call | flops 100000000 | bytes 300000 | tf_op jit(solution)/shard_map/project/pallas_call | solution.py:247
  105.3 24.3 %collective-permute-done.10 = bf16[816,896]{1,0:T(8,128)(2,1)S(1)} collective-permute-done((bf16[816,896]{1,0:T(8,128)(2,1)}, bf16[816,896]{1,0:T(8,128)(2,1)S(1)}, u32[]{:S(2)}, u32[]{:S(2)}) %collective-permute-start.10) | collective-permute-done | bytes 1462304 | tf_op jit(solution)/shard_map/ppermute | solution.py:925
  158.2 18.2 %project.5 = (bf16[1024,1792]{1,0:T(8,128)(2,1)}, bf16[2,80,256]{2,1,0:T(8,128)(2,1)S(1)}, bf16[2,160,128]{2,1,0:T(8,128)(2,1)S(1)}) custom-call(bf16[1024,1792]{1,0:T(8,128)(2,1)} %copy-done.136, bf16[1024,16]{1,0:T(8,128)(2,1)S(1)} %copy-done.27, bf16[16,4224]{1,0:T(8,128)(2,1)S(1)} %copy-done.45, bf16[128,1280]{1,0:T(8,128)(2,1)S(1)} %copy-done.11, ...), custom_call_target="tpu_custom_call" | custom-call | flops 100000000 | bytes 300000 | tf_op jit(solution)/shard_map/project/pallas_call | solution.py:247
  177.7 12.1 %collective-permute-done.18.refs_8_ = bf16[368,896]{1,0:T(8,128)(2,1)S(1)} collective-permute-done((bf16[368,896]{1,0:T(8,128)(2,1)}, bf16[368,896]{1,0:T(8,128)(2,1)S(1)}, u32[]{:S(2)}, u32[]{:S(2)}) %collective-permute-start.18) | collective-permute-done | bytes 659488 | tf_op jit(solution)/shard_map/ppermute | solution.py:878
  211.1 18.1 %project.6 = (bf16[1024,1792]{1,0:T(8,128)(2,1)}, bf16[2,80,256]{2,1,0:T(8,128)(2,1)S(1)}, bf16[2,160,128]{2,1,0:T(8,128)(2,1)S(1)}) custom-call(bf16[1024,1792]{1,0:T(8,128)(2,1)} %copy-done.136, bf16[1024,16]{1,0:T(8,128)(2,1)S(1)} %copy-done.27, bf16[16,4224]{1,0:T(8,128)(2,1)} %get-tuple-element.223.table.refs_6_.refs_4_.refs_2_, ...), custom_call_target="tpu_custom_call" | custom-call | flops 100000000 | bytes 300000 | tf_op jit(solution)/shard_map/project/pallas_call | solution.py:247
  239.2 18.5 %project.7 = (bf16[1024,1792]{1,0:T(8,128)(2,1)}, bf16[2,80,256]{2,1,0:T(8,128)(2,1)S(1)}, bf16[2,160,128]{2,1,0:T(8,128)(2,1)S(1)}) custom-call(bf16[1024,1792]{1,0:T(8,128)(2,1)} %copy-done.136, bf16[1024,16]{1,0:T(8,128)(2,1)S(1)} %copy-done.27, bf16[16,4224]{1,0:T(8,128)(2,1)S(1)} %copy-done.41, bf16[128,1280]{1,0:T(8,128)(2,1)S(1)} %copy-done.11, ...), custom_call_target="tpu_custom_call" | custom-call | flops 100000000 | bytes 300000 | tf_op jit(solution)/shard_map/project/pallas_call | solution.py:247
  257.8 16.9 %collective-permute-done.27 = bf16[912,896]{1,0:T(8,128)(2,1)} collective-permute-done((bf16[912,896]{1,0:T(8,128)(2,1)}, bf16[912,896]{1,0:T(8,128)(2,1)}, u32[]{:S(2)}, u32[]{:S(2)}) %collective-permute-start.27) | collective-permute-done | bytes 1634336 | tf_op jit(solution)/shard_map/ppermute | solution.py:925
  331.0 26.9 %collective-permute-done.32.refs_7_ = bf16[448,896]{1,0:T(8,128)(2,1)} collective-permute-done((bf16[448,896]{1,0:T(8,128)(2,1)}, bf16[448,896]{1,0:T(8,128)(2,1)}, u32[]{:S(2)}, u32[]{:S(2)}) %collective-permute-start.32) | collective-permute-done | bytes 802848 | tf_op jit(solution)/shard_map/ppermute | solution.py:878
  382.5 10.7 %mix_out.1 = (bf16[1024,1792]{1,0:T(8,128)(2,1)}, f32[1024,16]{1,0:T(8,128)S(1)}) custom-call(bf16[1024,256]{1,0:T(8,128)(2,1)S(1)} %copy-done.52, bf16[1024,256]{1,0:T(8,128)(2,1)S(1)} %copy-done.50, bf16[1024,256]{1,0:T(8,128)(2,1)S(1)} %get-tuple-element.259.refs_2_.refs_4_, bf16[1024,256]{1,0:T(8,128)(2,1)S(1)} %get-tuple-element.261.refs_3_.refs_4_, ...), custom_call_target="tpu_custom_call" | custom-call | flops 100000000 | bytes 300000 | tf_op jit(solution)/shard_map/mix_out/pallas_call | solution.py:406
  422.7 25.4 %feed.4 = (f32[1024,1792]{1,0:T(8,128)}, f32[1024,1792]{1,0:T(8,128)}, f32[1024,32]{1,0:T(8,128)}, f32[16,1280]{1,0:T(8,128)}, f32[16,640]{1,0:T(8,128)}) custom-call(bf16[1024,1792]{1,0:T(8,128)(2,1)} %copy-done.4, bf16[1024,1792]{1,0:T(8,128)(2,1)} %pad_maximum_fusion.1.refs_1_.upstream, bf16[1024,16]{1,0:T(8,128)(2,1)} %copy-done.55, ...), custom_call_target="tpu_custom_call" | custom-call | flops 100000000 | bytes 300000 | tf_op jit(solution)/shard_map/feed/pallas_call | solution.py:486
  454.5 27.2 %feed.5 = (f32[1024,1792]{1,0:T(8,128)}, f32[1024,1792]{1,0:T(8,128)}, f32[1024,32]{1,0:T(8,128)}, f32[16,1280]{1,0:T(8,128)}, f32[16,640]{1,0:T(8,128)}) custom-call(bf16[1024,1792]{1,0:T(8,128)(2,1)} %copy-done.4, bf16[1024,1792]{1,0:T(8,128)(2,1)} %pad_maximum_fusion.1.refs_1_.upstream, bf16[1024,16]{1,0:T(8,128)(2,1)} %copy-done.55, ...), custom_call_target="tpu_custom_call" | custom-call | flops 100000000 | bytes 300000 | tf_op jit(solution)/shard_map/feed/pallas_call | solution.py:486
  481.8 27.0 %feed.6 = (f32[1024,1792]{1,0:T(8,128)}, f32[1024,1792]{1,0:T(8,128)}, f32[1024,32]{1,0:T(8,128)}, f32[16,1280]{1,0:T(8,128)}, f32[16,640]{1,0:T(8,128)}) custom-call(bf16[1024,1792]{1,0:T(8,128)(2,1)} %copy-done.4, bf16[1024,1792]{1,0:T(8,128)(2,1)} %pad_maximum_fusion.1.refs_1_.upstream, bf16[1024,16]{1,0:T(8,128)(2,1)} %copy-done.55, ...), custom_call_target="tpu_custom_call" | custom-call | flops 100000000 | bytes 300000 | tf_op jit(solution)/shard_map/feed/pallas_call | solution.py:486
  508.8 29.0 %feed.7 = (bf16[1024,1792]{1,0:T(8,128)(2,1)}, bf16[1024,1792]{1,0:T(8,128)(2,1)}, f32[1024,32]{1,0:T(8,128)}, f32[16,1280]{1,0:T(8,128)}, f32[16,640]{1,0:T(8,128)}) custom-call(bf16[1024,1792]{1,0:T(8,128)(2,1)} %copy-done.4, bf16[1024,1792]{1,0:T(8,128)(2,1)} %pad_maximum_fusion.1.refs_1_.upstream, bf16[1024,16]{1,0:T(8,128)(2,1)} %copy-done.55, ...), custom_call_target="tpu_custom_call" | custom-call | flops 100000000 | bytes 300000 | tf_op jit(solution)/shard_map/feed/pallas_call | solution.py:486
  595.8 10.8 %turn.7 = (bf16[1024,256]{1,0:T(8,128)(2,1)S(1)}, bf16[1024,256]{1,0:T(8,128)(2,1)S(1)}, bf16[2,160,128]{2,1,0:T(8,128)(2,1)S(1)}, bf16[2,80,256]{2,1,0:T(8,128)(2,1)S(1)}, f32[16,256]{1,0:T(8,128)S(1)}) custom-call(bf16[1024,1792]{1,0:T(8,128)(2,1)} %copy-done.2, bf16[1024,16]{1,0:T(8,128)(2,1)S(1)} %copy-done.54, bf16[16,4224]{1,0:T(8,128)(2,1)S(1)} %copy-done.42, ...), custom_call_target="tpu_custom_call" | custom-call | flops 100000000 | bytes 300000 | tf_op jit(solution)/shard_map/turn/pallas_call | solution.py:583
  608.9 10.1 %turn.6 = (bf16[1024,256]{1,0:T(8,128)(2,1)S(1)}, bf16[1024,256]{1,0:T(8,128)(2,1)S(1)}, bf16[2,160,128]{2,1,0:T(8,128)(2,1)S(1)}, bf16[2,80,256]{2,1,0:T(8,128)(2,1)S(1)}, f32[16,256]{1,0:T(8,128)S(1)}) custom-call(bf16[1024,1792]{1,0:T(8,128)(2,1)} %copy-done.2, bf16[1024,16]{1,0:T(8,128)(2,1)S(1)} %copy-done.54, ...), custom_call_target="tpu_custom_call" | custom-call | flops 100000000 | bytes 300000 | tf_op jit(solution)/shard_map/turn/pallas_call | solution.py:583
  633.7 20.3 %attend_back.5 = (bf16[1024,1792]{1,0:T(8,128)(2,1)}, f32[1024,16]{1,0:T(8,128)S(1)}, f32[16,1792]{1,0:T(8,128)S(1)}) custom-call(bf16[1024,1792]{1,0:T(8,128)(2,1)} %get-tuple-element.247.proj.refs_5_.refs_6_.refs_7_, bf16[2,80,256]{2,1,0:T(8,128)(2,1)S(1)} %copy-done.82, f32[2,256,128]{2,1,0:T(8,128)S(1)} %copy-done.65, ...), custom_call_target="tpu_custom_call" | custom-call | flops 100000000 | bytes 300000 | tf_op jit(solution)/shard_map/attend_back/pallas_call | solution.py:724
  654.0 20.2 %attend_back.4 = (bf16[1024,1792]{1,0:T(8,128)(2,1)}, f32[1024,16]{1,0:T(8,128)S(1)}, f32[16,1792]{1,0:T(8,128)S(1)}) custom-call(bf16[1024,1792]{1,0:T(8,128)(2,1)} %copy-done.6, bf16[2,80,256]{2,1,0:T(8,128)(2,1)S(1)} %copy-done.76, f32[2,256,128]{2,1,0:T(8,128)S(1)} %copy-done.63, f32[2,256,128]{2,1,0:T(8,128)S(1)} %get-tuple-element.447.later, ...), custom_call_target="tpu_custom_call" | custom-call | flops 100000000 | bytes 300000 | tf_op jit(solution)/shard_map/attend_back/pallas_call | solution.py:724
  682.4 20.3 %attend_back.7 = (bf16[1024,1792]{1,0:T(8,128)(2,1)}, f32[1024,16]{1,0:T(8,128)S(1)}, f32[16,1792]{1,0:T(8,128)S(1)}) custom-call(bf16[1024,1792]{1,0:T(8,128)(2,1)} %get-tuple-element.260.proj.refs_5_.refs_6_.refs_7_, bf16[2,80,256]{2,1,0:T(8,128)(2,1)S(1)} %copy-done.79, f32[2,256,128]{2,1,0:T(8,128)S(1)} %copy-done.61, ...), custom_call_target="tpu_custom_call" | custom-call | flops 100000000 | bytes 300000 | tf_op jit(solution)/shard_map/attend_back/pallas_call | solution.py:724
  702.8 20.4 %attend_back.6 = (bf16[1024,1792]{1,0:T(8,128)(2,1)}, f32[1024,16]{1,0:T(8,128)S(1)}, f32[16,1792]{1,0:T(8,128)S(1)}) custom-call(bf16[1024,1792]{1,0:T(8,128)(2,1)} %get-tuple-element.257.proj.refs_5_.refs_6_.refs_7_, bf16[2,80,256]{2,1,0:T(8,128)(2,1)S(1)} %copy-done.73, f32[2,256,128]{2,1,0:T(8,128)S(1)} %copy-done.59, ...), custom_call_target="tpu_custom_call" | custom-call | flops 100000000 | bytes 300000 | tf_op jit(solution)/shard_map/attend_back/pallas_call | solution.py:724
  730.4 25.6 %first_back.2.refs_0_ = bf16[512,1792]{1,0:T(8,128)(2,1)} custom-call(bf16[1024,1792]{1,0:T(8,128)(2,1)} %get-tuple-element.316.refs_0_, bf16[1024,1792]{1,0:T(8,128)(2,1)} %get-tuple-element.319.refs_1_, bf16[1024,1792]{1,0:T(8,128)(2,1)} %get-tuple-element.346.refs_2_, bf16[1024,1792]{1,0:T(8,128)(2,1)} %get-tuple-element.349.refs_3_, ...), custom_call_target="tpu_custom_call" | custom-call | flops 100000000 | bytes 300000 | tf_op jit(solution)/shard_map/first_back/pallas_call | solution.py:792
  778.8 25.2 %first_back.3.refs_2_ = bf16[512,1792]{1,0:T(8,128)(2,1)} custom-call(bf16[1024,1792]{1,0:T(8,128)(2,1)} %get-tuple-element.316.refs_0_, bf16[1024,1792]{1,0:T(8,128)(2,1)} %get-tuple-element.319.refs_1_, bf16[1024,1792]{1,0:T(8,128)(2,1)} %get-tuple-element.346.refs_2_, bf16[1024,1792]{1,0:T(8,128)(2,1)} %get-tuple-element.349.refs_3_, ...), custom_call_target="tpu_custom_call" | custom-call | flops 100000000 | bytes 300000 | tf_op jit(solution)/shard_map/first_back/pallas_call | solution.py:792
  835.7 18.9 %collective-permute-done.63.refs_2_ = bf16[256,1792]{1,0:T(8,128)(2,1)S(1)} collective-permute-done((bf16[256,1792]{1,0:T(8,128)(2,1)S(1)}, bf16[256,1792]{1,0:T(8,128)(2,1)S(1)}, u32[]{:S(2)}, u32[]{:S(2)}) %collective-permute-start.63) | collective-permute-done | bytes 917536 | tf_op jit(solution)/shard_map/ppermute | solution.py:882
  862.9 18.1 %collective-permute-done.66.refs_0_ = bf16[256,1792]{1,0:T(8,128)(2,1)S(1)} collective-permute-done((bf16[256,1792]{1,0:T(8,128)(2,1)}, bf16[256,1792]{1,0:T(8,128)(2,1)S(1)}, u32[]{:S(2)}, u32[]{:S(2)}) %collective-permute-start.66) | collective-permute-done | bytes 917536 | tf_op jit(solution)/shard_map/ppermute | solution.py:925
  881.0 18.0 %collective-permute-done.68.refs_2_ = bf16[256,1792]{1,0:T(8,128)(2,1)S(1)} collective-permute-done((bf16[256,1792]{1,0:T(8,128)(2,1)}, bf16[256,1792]{1,0:T(8,128)(2,1)S(1)}, u32[]{:S(2)}, u32[]{:S(2)}) %collective-permute-start.68) | collective-permute-done | bytes 917536 | tf_op jit(solution)/shard_map/ppermute | solution.py:925
  (889 shorter events, 486.7 us)
Async XLA Ops:
  7.2 279.5 %all-gather.7.cloned.1.call-start = ((), (), s32[]{:S(2)}) async-start(), calls=%async_computation | async-start | bytes 1638400 | tf_op jit(solution)/shard_map/all_gather | solution.py:1140
  91.2 49.1 %collective-permute-start.8 = (bf16[816,896]{1,0:T(8,128)(2,1)}, bf16[816,896]{1,0:T(8,128)(2,1)S(1)}, u32[]{:S(2)}, u32[]{:S(2)}) collective-permute-start(bf16[816,896]{1,0:T(8,128)(2,1)} %get-tuple-element.204.rest_0_.refs_15_.refs_12_), channel_id=1, source_target_pairs={{0,8},{8,0},{16,24},{24,16},{1,9},{9,1},{17,25},{25,17},{2,10},{10... | collective-permute-start | bytes 4386824 | tf_op jit(solution)/shard_map/ppermute | solution.py:878
  92.7 48.5 %collective-permute-start.9 = (bf16[816,896]{1,0:T(8,128)(2,1)}, bf16[816,896]{1,0:T(8,128)(2,1)S(1)}, u32[]{:S(2)}, u32[]{:S(2)}) collective-permute-start(bf16[816,896]{1,0:T(8,128)(2,1)} %get-tuple-element.204.rest_0_.refs_15_.refs_12_), channel_id=1, source_target_pairs={{0,16},{8,24},{16,0},{24,8},{1,17},{9,25},{17,1},{25,9},{2,18},{10... | collective-permute-start | bytes 4386824 | tf_op jit(solution)/shard_map/ppermute | solution.py:878
  142.8 51.3 %collective-permute-start.17 = (bf16[912,896]{1,0:T(8,128)(2,1)}, bf16[912,896]{1,0:T(8,128)(2,1)}, u32[]{:S(2)}, u32[]{:S(2)}) collective-permute-start(bf16[912,896]{1,0:T(8,128)(2,1)} %get-tuple-element.212), channel_id=1, source_target_pairs={{0,1},{1,0},{2,3},{3,2},{4,5},{5,4},{6,7},{7,6},{8,9},{9,8},{10,11... | collective-permute-start | bytes 4902920 | tf_op jit(solution)/shard_map/ppermute | solution.py:882
  145.8 48.3 %collective-permute-start.15 = (bf16[816,896]{1,0:T(8,128)(2,1)}, bf16[816,896]{1,0:T(8,128)(2,1)}, u32[]{:S(2)}, u32[]{:S(2)}) collective-permute-start(bf16[816,896]{1,0:T(8,128)(2,1)} %get-tuple-element.211.rest_0_.refs_20_.refs_12_.refs_17_), channel_id=1, source_target_pairs={{0,8},{8,0},{16,24},{24,16},{1,9},{9,1},{17,25},{25,17},{2,10},{10... | collective-permute-start | bytes 4386824 | tf_op jit(solution)/shard_map/ppermute | solution.py:878
  207.8 49.9 %collective-permute-start.22 = (bf16[912,896]{1,0:T(8,128)(2,1)}, bf16[912,896]{1,0:T(8,128)(2,1)}, u32[]{:S(2)}, u32[]{:S(2)}) collective-permute-start(bf16[912,896]{1,0:T(8,128)(2,1)} %get-tuple-element.222.refs_7_), channel_id=1, source_target_pairs={{1,2},{2,1},{5,6},{6,5},{9,10},{10,9},{13,14},{14,13},{17,18},{18,... | collective-permute-start | bytes 4902920 | tf_op jit(solution)/shard_map/ppermute | solution.py:921
  237.2 120.8 %all-gather.9.cloned.1.call-start = ((), (), s32[]{:S(2)}) async-start(), calls=%async_computation.1 | async-start | bytes 1638400 | tf_op jit(solution)/shard_map/all_gather | solution.py:1140
  237.2 48.2 %collective-permute-start.20 = (bf16[912,896]{1,0:T(8,128)(2,1)}, bf16[912,896]{1,0:T(8,128)(2,1)S(1)}, u32[]{:S(2)}, u32[]{:S(2)}) collective-permute-start(bf16[912,896]{1,0:T(8,128)(2,1)} %get-tuple-element.222.refs_7_), channel_id=1, source_target_pairs={{0,8},{8,0},{16,24},{24,16},{1,9},{9,1},{17,25},{25,17},{2,10},{10... | collective-permute-start | bytes 4902920 | tf_op jit(solution)/shard_map/ppermute | solution.py:878
  238.7 48.0 %collective-permute-start.21 = (bf16[912,896]{1,0:T(8,128)(2,1)}, bf16[912,896]{1,0:T(8,128)(2,1)}, u32[]{:S(2)}, u32[]{:S(2)}) collective-permute-start(bf16[912,896]{1,0:T(8,128)(2,1)} %get-tuple-element.222.refs_7_), channel_id=1, source_target_pairs={{0,16},{8,24},{16,0},{24,8},{1,17},{9,25},{17,1},{25,9},{2,18},{10... | collective-permute-start | bytes 4902920 | tf_op jit(solution)/shard_map/ppermute | solution.py:878
  291.6 467.2 %all-gather.11.cloned.1.call-start = ((), (), s32[]{:S(2)}) async-start(), calls=%async_computation.2 | async-start | bytes 9175040 | tf_op jit(solution)/shard_map/all_gather | solution.py:1286
  292.1 65.9 %collective-permute-start.28 = (bf16[912,896]{1,0:T(8,128)(2,1)}, bf16[912,896]{1,0:T(8,128)(2,1)}, u32[]{:S(2)}, u32[]{:S(2)}) collective-permute-start(bf16[912,896]{1,0:T(8,128)(2,1)} %get-tuple-element.241.refs_7_), channel_id=1, source_target_pairs={{0,8},{8,0},{16,24},{24,16},{1,9},{9,1},{17,25},{25,17},{2,10},{10... | collective-permute-start | bytes 4902920 | tf_op jit(solution)/shard_map/ppermute | solution.py:878
  293.5 64.4 %collective-permute-start.29 = (bf16[912,896]{1,0:T(8,128)(2,1)}, bf16[912,896]{1,0:T(8,128)(2,1)}, u32[]{:S(2)}, u32[]{:S(2)}) collective-permute-start(bf16[912,896]{1,0:T(8,128)(2,1)} %get-tuple-element.241.refs_7_), channel_id=1, source_target_pairs={{0,16},{8,24},{16,0},{24,8},{1,17},{9,25},{17,1},{25,9},{2,18},{10... | collective-permute-start | bytes 4902920 | tf_op jit(solution)/shard_map/ppermute | solution.py:878
  297.6 60.3 %collective-permute-start.31 = (bf16[464,896]{1,0:T(8,128)(2,1)}, bf16[464,896]{1,0:T(8,128)(2,1)S(1)}, u32[]{:S(2)}, u32[]{:S(2)}) collective-permute-start(bf16[464,896]{1,0:T(8,128)(2,1)} %slice.435), channel_id=1, source_target_pairs={{0,8},{8,0},{16,24},{24,16},{1,9},{9,1},{17,25},{25,17},{2,10},{10... | collective-permute-start | bytes 2494472 | tf_op jit(solution)/shard_map/ppermute | solution.py:878
  300.3 57.6 %collective-permute-start.32 = (bf16[448,896]{1,0:T(8,128)(2,1)}, bf16[448,896]{1,0:T(8,128)(2,1)}, u32[]{:S(2)}, u32[]{:S(2)}) collective-permute-start(bf16[448,896]{1,0:T(8,128)(2,1)} %slice.436), channel_id=1, source_target_pairs={{0,16},{8,24},{16,0},{24,8},{1,17},{9,25},{17,1},{25,9},{2,18},{10... | collective-permute-start | bytes 2408456 | tf_op jit(solution)/shard_map/ppermute | solution.py:878
  394.0 56.3 %collective-permute-start.34 = (bf16[912,896]{1,0:T(8,128)(2,1)}, bf16[912,896]{1,0:T(8,128)(2,1)}, u32[]{:S(2)}, u32[]{:S(2)}) collective-permute-start(bf16[912,896]{1,0:T(8,128)(2,1)} %get-tuple-element.266.refs_7_), channel_id=1, source_target_pairs={{0,8},{8,0},{16,24},{24,16},{1,9},{9,1},{17,25},{25,17},{2,10},{10... | collective-permute-start | bytes 4902920 | tf_op jit(solution)/shard_map/ppermute | solution.py:878
  394.8 55.5 %collective-permute-start.35 = (bf16[912,896]{1,0:T(8,128)(2,1)}, bf16[912,896]{1,0:T(8,128)(2,1)}, u32[]{:S(2)}, u32[]{:S(2)}) collective-permute-start(bf16[912,896]{1,0:T(8,128)(2,1)} %get-tuple-element.266.refs_7_), channel_id=1, source_target_pairs={{0,16},{8,24},{16,0},{24,8},{1,17},{9,25},{17,1},{25,9},{2,18},{10... | collective-permute-start | bytes 4902920 | tf_op jit(solution)/shard_map/ppermute | solution.py:878
  397.5 52.8 %collective-permute-start.36 = (bf16[464,896]{1,0:T(8,128)(2,1)}, bf16[464,896]{1,0:T(8,128)(2,1)}, u32[]{:S(2)}, u32[]{:S(2)}) collective-permute-start(bf16[464,896]{1,0:T(8,128)(2,1)} %slice.445), channel_id=1, source_target_pairs={{0,8},{8,0},{16,24},{24,16},{1,9},{9,1},{17,25},{25,17},{2,10},{10... | collective-permute-start | bytes 2494472 | tf_op jit(solution)/shard_map/ppermute | solution.py:878
  400.8 49.4 %collective-permute-start.37 = (bf16[448,896]{1,0:T(8,128)(2,1)}, bf16[448,896]{1,0:T(8,128)(2,1)}, u32[]{:S(2)}, u32[]{:S(2)}) collective-permute-start(bf16[448,896]{1,0:T(8,128)(2,1)} %slice.446), channel_id=1, source_target_pairs={{0,16},{8,24},{16,0},{24,8},{1,17},{9,25},{17,1},{25,9},{2,18},{10... | collective-permute-start | bytes 2408456 | tf_op jit(solution)/shard_map/ppermute | solution.py:878
  623.5 52.8 %collective-permute-start.47 = (bf16[4,160,128]{2,1,0:T(8,128)(2,1)S(1)}, bf16[4,160,128]{2,1,0:T(8,128)(2,1)}, u32[]{:S(2)}, u32[]{:S(2)}) collective-permute-start(bf16[4,160,128]{2,1,0:T(8,128)(2,1)S(1)} %constant_dynamic-update-slice_fusion.6), channel_id=1, source_target_pairs={{0,8},{8,0},{16,24},{24,16},{1,9},{9,1},{17,25},{25,17},{2,10},{10... | collective-permute-start | bytes 491528 | tf_op jit(solution)/shard_map/ppermute | solution.py:878
  626.1 50.2 %collective-permute-start.48 = (bf16[4,160,128]{2,1,0:T(8,128)(2,1)S(1)}, bf16[4,160,128]{2,1,0:T(8,128)(2,1)}, u32[]{:S(2)}, u32[]{:S(2)}) collective-permute-start(bf16[4,160,128]{2,1,0:T(8,128)(2,1)S(1)} %constant_dynamic-update-slice_fusion.6), channel_id=1, source_target_pairs={{0,16},{8,24},{16,0},{24,8},{1,17},{9,25},{17,1},{25,9},{2,18},{10... | collective-permute-start | bytes 491528 | tf_op jit(solution)/shard_map/ppermute | solution.py:878
  628.2 48.2 %collective-permute-start.49 = (bf16[4,160,128]{2,1,0:T(8,128)(2,1)S(1)}, bf16[4,160,128]{2,1,0:T(8,128)(2,1)}, u32[]{:S(2)}, u32[]{:S(2)}) collective-permute-start(bf16[4,160,128]{2,1,0:T(8,128)(2,1)S(1)} %constant_dynamic-update-slice_fusion.6), channel_id=1, source_target_pairs={{0,24},{8,16},{16,8},{24,0},{1,25},{9,17},{17,9},{25,1},{2,26},{10... | collective-permute-start | bytes 491528 | tf_op jit(solution)/shard_map/ppermute | solution.py:878
  629.1 47.2 %collective-permute-start.46 = (bf16[4,80,256]{2,1,0:T(8,128)(2,1)S(1)}, bf16[4,80,256]{2,1,0:T(8,128)(2,1)}, u32[]{:S(2)}, u32[]{:S(2)}) collective-permute-start(bf16[4,80,256]{2,1,0:T(8,128)(2,1)S(1)} %pad_maximum_fusion.20), channel_id=1, source_target_pairs={{8,0},{16,8},{24,16},{9,1},{17,9},{25,17},{10,2},{18,10},{26,18},{... | collective-permute-start | bytes 491528 | tf_op jit(solution)/shard_map/ppermute | solution.py:949
  676.4 49.0 %collective-permute-start.50 = (f32[3,16,1792]{2,1,0:T(8,128)}, f32[3,16,1792]{2,1,0:T(8,128)}, u32[]{:S(2)}, u32[]{:S(2)}) collective-permute-start(f32[3,16,1792]{2,1,0:T(8,128)} %get-tuple-element.353), channel_id=1, source_target_pairs={{0,8},{8,0},{16,24},{24,16},{1,9},{9,1},{17,25},{25,17},{2,10},{10... | collective-permute-start | bytes 1032200 | tf_op jit(solution)/shard_map/ppermute | solution.py:878
  916.0 52.0 %collective-permute-start.70 = (bf16[256,1792]{1,0:T(8,128)(2,1)S(1)}, bf16[256,1792]{1,0:T(8,128)(2,1)}, u32[]{:S(2)}, u32[]{:S(2)}) collective-permute-start(bf16[256,1792]{1,0:T(8,128)(2,1)S(1)} %copy-done.171), channel_id=1, source_target_pairs={{1,0},{2,3},{5,4},{6,7},{9,8},{10,11},{13,12},{14,15},{17,16},{18,... | collective-permute-start | bytes 2752520 | tf_op jit(solution)/shard_map/ppermute | solution.py:925
  (274 other events, 3040.2 us)
Sparse Core Ops, SparseCore 0:
  237.3 40.6 all-gather.6
  291.7 41.5 all-gather.8
  585.0 134.5 all-gather.10

commit v2 on v1

--- a/solution.py
+++ b/solution.py
@@ -302,7 +302,7 @@
     vals[WIN:, :] = proj[:, 4 * PD : 5 * PD]
     conv[16:, :] = proj[:, 5 * PD : 6 * PD].astype(f32)
     tap = head_taps(spots, table)
-    state = prior[0]
+    state = whole_state(prior[0])
     causal = causal_mask()
     for chunk in range(rows // CHUNK):
         at = chunk * CHUNK
@@ -329,12 +329,16 @@
         numer[span, :] = total.astype(bf16)
 
 
+def whole_state(state):
+    return jnp.concatenate([state, jnp.zeros((256 - STATE, PD), f32)], 0)
+
+
 def head_taps(spots, table):
     start = pl.multiple_of(spots.taps.start + PD * pl.program_id(0), PD)
     return table[:, pl.ds(start, PD)].astype(f32)
 
 
-def attend(spots, proj, tails, prior, table, tables):
+def attend(spots, number, proj, tails, prior, table, tables):
     rows = proj.shape[0]
     whole = lambda a: pl.BlockSpec(a.shape, lambda h: (0,) * a.ndim)
     return pl.pallas_call(
@@ -346,8 +350,8 @@
         ),
         in_specs=[
             pl.BlockSpec((rows, HEAD_PAD), lambda h: (0, h)),
-            pl.BlockSpec((1, WIN + 16, 2 * PD), lambda h: (h, 0, 0)),
-            pl.BlockSpec((1, 256, PD), lambda h: (h, 0, 0)),
+            pl.BlockSpec((1, WIN + 16, 2 * PD), lambda h: (2 * number + h, 0, 0)),
+            pl.BlockSpec((1, STATE, PD), lambda h: (2 * number + h, 0, 0)),
             whole(table),
         ]
         + [whole(t) for t in tables],
@@ -373,7 +377,7 @@
     lefts = refs[4:8]
     right = refs[8]
     sources = refs[9 : 9 + 1 + 15]
-    part, rank, weight, sems = refs[25:]
+    part, rank, kept, weight, sems = refs[25:]
     groups = []
     for slot in range(SLOTS):
         pieces = sources[0:1] if slot == 0 else sources[1 + 5 * (slot - 1) : 1 + 5 * slot]
@@ -395,6 +399,8 @@
     total = total + nn(rank_sum.astype(bf16), right[...])
     part[...] = total.astype(bf16)
     rank[...] = rank_sum
+    rows = kept.shape[0]
+    kept[...] = weight[pl.ds(pl.multiple_of(pl.program_id(0) * rows, rows), rows), :]
 
 
 def mix_out(spots, mixed, lefts, right, sources):
@@ -409,6 +415,7 @@
         out_shape=(
             jax.ShapeDtypeStruct((rows, width), bf16),
             jax.ShapeDtypeStruct((rows, R), f32),
+            jax.ShapeDtypeStruct((SLOTS * 2 * PD, width), bf16),
         ),
         in_specs=[pl.BlockSpec((block, 2 * PD), lambda i: (i, 0))] * 4
         + [whole(a) for a in lefts]
@@ -417,6 +424,7 @@
         out_specs=(
             pl.BlockSpec((block, width), lambda i: (i, 0)),
             pl.BlockSpec((block, R), lambda i: (i, 0)),
+            pl.BlockSpec((SLOTS * 2 * PD // steps, width), lambda i: (i, 0)),
         ),
         scratch_shapes=[pltpu.VMEM((SLOTS * 2 * PD, width), bf16), pltpu.SemaphoreType.DMA((32,))],
         compiler_params=params(48),
@@ -427,42 +435,63 @@
     )(*mixed, *lefts, right, *sources)
 
 
-def feed_kernel(own, last, half, pad, spots, *refs):
-    second, grad, grank, rgrad, table, dright, gleft = refs[:7]
-    right, left = table.at[:, spots.gate], table.at[:, spots.down]
-    count = 2 if own else 5
-    refs = refs[7:]
-    sources, refs = refs[:count], refs[count:]
-    if not own:
+def feed_kernel(slots, last, half, pad, spots, *refs):
+    count = len(slots)
+    fresh = slots[0] == 0
+    second, grad, grank, rgrad, dright, gleft = refs[:6]
+    tables, refs = refs[6 : 6 + count], refs[6 + count :]
+    groups = []
+    sources = []
+    for slot in slots:
+        size = 2 if slot == 0 else 5
+        sources.append(refs[:size])
+        refs = refs[size:]
+    if not fresh:
         (down_in, back_in, ranks_in), refs = refs[:3], refs[3:]
-    down_out, back_out, ranks_out, right_grad, left_grad, weight, sems = refs
-    copies = feed_copies(sources, own, weight, half, pad)
-
-    @pl.when(pl.program_id(0) == 0)
+    down_out, back_out, ranks_out = refs[:3]
+    right_outs, left_outs = refs[3 : 3 + count], refs[3 + count : 3 + 2 * count]
+    weights, sems, *sums = refs[3 + 2 * count :]
+    right_grads, left_grads = sums[:count], sums[count:]
+    for n, slot in enumerate(slots):
+        part = weights.at[3 * pad * n : 3 * pad * (n + 1)]
+        groups.append(feed_copies(sources[n], slot == 0, part, half, pad))
+    begin = pl.program_id(0) == 0
+
+    @pl.when(begin)
     def _():
-        run_copies(copies, sems, 0)
-        feed_pads(weight, half, pad)
-        right_grad[...] = jnp.zeros(right_grad.shape, f32)
-        left_grad[...] = jnp.zeros(left_grad.shape, f32)
-        wait_copies(copies, sems, 0)
-
-    gate_up = nt(second[...], weight[0 : 2 * pad, :]) + nn(grank[...], right[...])
-    gate, up = gate_up[:, :pad], gate_up[:, pad:]
-    sig = jax.nn.sigmoid(gate)
-    act = gate * sig
-    hidden = (act * up).astype(bf16)
-    hidden_grad = nt(grad[...], weight[2 * pad :, :]) + nn(rgrad[...], left[...])
-    gate_grad = hidden_grad * up * (sig * (1.0 + gate * (1.0 - sig)))
-    both = jnp.concatenate([gate_grad.astype(bf16), (hidden_grad * act).astype(bf16)], 1)
-    down = nn(hidden, weight[2 * pad :, :])
-    back = nn(both, weight[0 : 2 * pad, :])
-    down_rank = nt(hidden, left[...])
-    back_rank = nt(both, right[...])
-    if not own:
-        down = down + down_in[...]
-        back = back + back_in[...]
-        down_rank = down_rank + ranks_in[:, :R]
-        back_rank = back_rank + ranks_in[:, R:]
+        for n in range(count):
+            run_copies(groups[n], sems, 16 * n)
+        for n in range(count):
+            feed_pads(weights.at[3 * pad * n : 3 * pad * (n + 1)], half, pad)
+            right_grads[n][...] = jnp.zeros(right_grads[n].shape, f32)
+            left_grads[n][...] = jnp.zeros(left_grads[n].shape, f32)
+
+    down = jnp.zeros(down_out.shape, f32) if fresh else down_in[...]
+    back = jnp.zeros(back_out.shape, f32) if fresh else back_in[...]
+    down_rank = jnp.zeros((down.shape[0], R), f32) if fresh else ranks_in[:, :R]
+    back_rank = jnp.zeros((down.shape[0], R), f32) if fresh else ranks_in[:, R:]
+    for n in range(count):
+
+        @pl.when(begin)
+        def _():
+            wait_copies(groups[n], sems, 16 * n)
+
+        at = 3 * pad * n
+        right, left = tables[n][:, spots.gate], tables[n][:, spots.down]
+        gate_up = nt(second[...], weights[at : at + 2 * pad, :]) + nn(grank[...], right)
+        gate, up = gate_up[:, :pad], gate_up[:, pad:]
+        hidden_grad = nt(grad[...], weights[at + 2 * pad : at + 3 * pad, :]) + nn(rgrad[...], left)
+        sig = jax.nn.sigmoid(gate)
+        act = gate * sig
+        hidden = (act * up).astype(bf16)
+        gate_grad = hidden_grad * up * (sig * (1.0 + gate * (1.0 - sig)))
+        both = jnp.concatenate([gate_grad.astype(bf16), (hidden_grad * act).astype(bf16)], 1)
+        down = down + nn(hidden, weights[at + 2 * pad : at + 3 * pad, :])
+        back = back + nn(both, weights[at : at + 2 * pad, :])
+        down_rank = down_rank + nt(hidden, left)
+        back_rank = back_rank + nt(both, right)
+        right_grads[n][...] += tn(grank[...], both)
+        left_grads[n][...] += tn(rgrad[...], hidden)
     ranks_out[:, :R] = down_rank
     ranks_out[:, R:] = back_rank
     if last:
@@ -470,153 +499,172 @@
         back = back + nn(back_rank.astype(bf16), gleft[...])
     down_out[...] = down.astype(down_out.dtype)
     back_out[...] = back.astype(back_out.dtype)
-    right_grad[...] += tn(grank[...], both)
-    left_grad[...] += tn(rgrad[...], hidden)
-
-
-def feed(own, last, half, spots, second, grad, grank, rgrad, table, dright, gleft, sources, carry):
+
+    @pl.when(pl.program_id(0) == pl.num_programs(0) - 1)
+    def _():
+        for out, total in zip(right_outs + left_outs, right_grads + left_grads):
+            out[...] = total[...].astype(bf16)
+
+
+def feed(slots, last, half, spots, second, grad, grank, rgrad, dright, gleft, tables, sources, carry):
     rows, width = second.shape
     pad = spots.down.stop - spots.down.start
+    count = len(slots)
     block = CHUNK
     kind = bf16 if last else f32
     whole = lambda a: pl.BlockSpec(a.shape, lambda i: (0,) * a.ndim)
     wide = pl.BlockSpec((block, width), lambda i: (i, 0))
     thin = pl.BlockSpec((block, R), lambda i: (i, 0))
     pair = pl.BlockSpec((block, 2 * R), lambda i: (i, 0))
-    return pl.pallas_call(
-        functools.partial(feed_kernel, own, last, half, pad, spots),
+    flat = sum([list(s) for s in sources], [])
+    out = pl.pallas_call(
+        functools.partial(feed_kernel, slots, last, half, pad, spots),
         grid=(rows // block,),
         out_shape=(
             jax.ShapeDtypeStruct((rows, width), kind),
             jax.ShapeDtypeStruct((rows, width), kind),
             jax.ShapeDtypeStruct((rows, 2 * R), f32),
-            jax.ShapeDtypeStruct((R, 2 * pad), f32),
-            jax.ShapeDtypeStruct((R, pad), f32),
-        ),
-        in_specs=[wide, wide, thin, thin, whole(table), whole(dright), whole(gleft)]
-        + [ANY] * len(sources)
-        + ([] if own else [wide, wide, pair]),
-        out_specs=(
-            wide,
-            wide,
-            pair,
-            pl.BlockSpec((R, 2 * pad), lambda i: (0, 0)),
-            pl.BlockSpec((R, pad), lambda i: (0, 0)),
-        ),
-        scratch_shapes=[pltpu.VMEM((3 * pad, width), bf16), pltpu.SemaphoreType.DMA((16,))],
-        compiler_params=params(56),
+        )
+        + (jax.ShapeDtypeStruct((R, 2 * pad), bf16),) * count
+        + (jax.ShapeDtypeStruct((R, pad), bf16),) * count,
+        in_specs=[wide, wide, thin, thin, whole(dright), whole(gleft)]
+        + [whole(t) for t in tables]
+        + [ANY] * len(flat)
+        + ([wide, wide, pair] if carry else []),
+        out_specs=(wide, wide, pair)
+        + (pl.BlockSpec((R, 2 * pad), lambda i: (0, 0)),) * count
+        + (pl.BlockSpec((R, pad), lambda i: (0, 0)),) * count,
+        scratch_shapes=[
+            pltpu.VMEM((3 * pad * count, width), bf16),
+            pltpu.SemaphoreType.DMA((16 * count,)),
+        ]
+        + [pltpu.VMEM((R, 2 * pad), f32)] * count
+        + [pltpu.VMEM((R, pad), f32)] * count,
+        compiler_params=params(58),
         cost_estimate=pl.CostEstimate(
             flops=100_000_000, bytes_accessed=300_000, transcendentals=0
         ),
         name="feed",
-    )(second, grad, grank, rgrad, table, dright, gleft, *sources, *carry)
-
-
-def turn_kernel(own, spots, *refs):
-    mixer_up, orgrad, table, numer, mixed, base0, base1, head_rows, tails = refs[:9]
-    left, taps = table.at[:, spots.left], table.at[:, spots.taps]
-    pick, bias, coef = refs[9:12]
-    count = 1 if own else 5
-    sources = refs[12 : 12 + count]
-    up_out, grad_out, state, lent, left_grad, weight, sems = refs[12 + count :]
-    copies = output_copies(sources, own, weight, 0)
-    run_copies(copies, sems, 0)
-    output_pads(weight, 0)
-    wait_copies(copies, sems, 0)
-    rows = mixer_up.shape[0]
-
-    def one(block, carry):
-        span = pl.ds(pl.multiple_of(block * CHUNK, CHUNK), CHUNK)
-        both = nt(mixer_up[span, :], weight[...]) + nn(orgrad[span, :], left[...])
-        result = []
+    )(second, grad, grank, rgrad, dright, gleft, *tables, *flat, *carry)
+    return list(out[:3]), list(out[3 : 3 + count]), list(out[3 + count :])
+
+
+def turn_kernel(spots, *refs):
+    mixer_up, orgrad, weight = refs[:3]
+    tables, numers, mixeds = refs[3:5], refs[5:7], refs[7:9]
+    bases, heads, tails = refs[9:13], refs[13:15], refs[15]
+    pick, bias, coef = refs[16:19]
+    up_out, grad_out, state, lent, left_out, total_state, left0, left1 = refs[19:]
+    step = pl.program_id(0)
+
+    @pl.when(step == 0)
+    def _():
+        total_state[...] = jnp.zeros(total_state.shape, f32)
+        left0[...] = jnp.zeros(left0.shape, f32)
+        left1[...] = jnp.zeros(left1.shape, f32)
+
+    both = nt(mixer_up[...], weight[...])
+    for n, left_grad in enumerate((left0, left1)):
+        table = tables[n]
+        flow = both[:, 2 * PD * n : 2 * PD * (n + 1)] + nn(orgrad[...], table[:, spots.left])
+        left_grad[...] += tn(orgrad[...], mixeds[n][...])
         for head in range(2):
             cols = slice(PD * head, PD * (head + 1))
-            up = both[:, cols]
-            total = numer[span, cols].astype(f32)
+            wide = slice(PD * (2 * n + head), PD * (2 * n + head + 1))
+            up = flow[:, cols]
+            total = numers[n][:, cols].astype(f32)
             scale = lax.rsqrt(jnp.sum(total * total, -1, keepdims=True) * (1.0 / HD) + epsilon)
             inner = jnp.sum(total * up, -1, keepdims=True) * (1.0 / HD)
             grad = (scale * up - total * (scale * scale * scale * inner)).astype(bf16)
-            up_out[span, cols] = up.astype(bf16)
-            grad_out[span, cols] = grad
-            base = (base0 if head == 0 else base1)[span, :]
-            _, _, feat = features(nn(base, pick[:, 0:512]), bias[...], coef[...], 0)
-            result.append(carry[head] + tn(feat.astype(bf16), grad))
-        result.append(carry[2] + tn(orgrad[span, :], mixed[span, :]))
-        return tuple(result)
-
-    zero = jnp.zeros((256, PD), f32)
-    done = lax.fori_loop(
-        0, rows // CHUNK, one, (zero, zero, jnp.zeros((R, 2 * PD), f32))
-    )
-    left_grad[...] = done[2]
-    for head in range(2):
-        state[head] = done[head][:STATE].astype(bf16)
-        at = HEAD_PAD * head
-        query = head_rows[:, at + 2 * PD : at + 3 * PD]
-        keys = jnp.concatenate([tails[head, 0:WIN, 0:PD], head_rows[:, at + 3 * PD : at + 4 * PD]], 0)
-        vals = jnp.concatenate(
-            [tails[head, 0:WIN, PD : 2 * PD], head_rows[:, at + 4 * PD : at + 5 * PD]], 0
-        )
-        prob = window_prob(query, keys, 0)
-        up = up_out[0:QB, PD * head : PD * (head + 1)]
-        prob_grad = nt(up, vals)
-        inner = jnp.sum(prob * prob_grad, -1, keepdims=True)
-        score = (prob * (prob_grad - inner)).astype(bf16)
-        lent[head, 0:WIN, 0:PD] = (tn(score, query)[:WIN] * HD ** (-0.5)).astype(bf16)
-        lent[head, 0:WIN, PD : 2 * PD] = tn(prob.astype(bf16), up)[:WIN].astype(bf16)
-        tap = taps[:, PD * head : PD * (head + 1)].astype(f32)
-        gate = head_rows[0:16, at + 6 * PD : at + 7 * PD].astype(f32)
-        flow = up_out[0:16, PD * head : PD * (head + 1)].astype(f32) * (gate * jax.nn.sigmoid(gate))
-        row0 = tap[2:3] * flow[0:1]
-        row1 = tap[1:2] * flow[0:1] + tap[2:3] * flow[1:2]
-        index = lax.broadcasted_iota(jnp.int32, (16, PD), 0)
-        lent[head, WIN : WIN + 16, 0:PD] = jnp.where(
-            index == 14, row0, jnp.where(index == 15, row1, 0.0)
-        ).astype(bf16)
-        lent[head, WIN : WIN + 16, PD : 2 * PD] = jnp.zeros((16, PD), bf16)
-
-
-def turn(own, spots, mixer_up, orgrad, table, numer, mixed, proj, tails, tables, sources):
+            up_out[:, wide] = up.astype(bf16)
+            grad_out[:, wide] = grad
+            picked = nn(bases[2 * n + head][...], pick[:, 0:512])
+            _, _, feat = features(picked, bias[...], coef[...], 0)
+            total_state[2 * n + head] += tn(feat.astype(bf16), grad)
+
+    @pl.when(step == pl.num_programs(0) - 1)
+    def _():
+        state[...] = total_state[:, :STATE, :].astype(bf16)
+        left_out[0] = left0[...].astype(bf16)
+        left_out[1] = left1[...].astype(bf16)
+
+    @pl.when(step == 0)
+    def _():
+        for n in range(2):
+            for head in range(2):
+                give_back(
+                    spots, tables[n], heads[n], tails.at[2 * n + head], up_out, lent.at[2 * n + head], n, head
+                )
+
+
+def give_back(spots, table, rows, tails, up_out, lent, n, head):
+    at = HEAD_PAD * head
+    wide = slice(PD * (2 * n + head), PD * (2 * n + head + 1))
+    query = rows[:, at + 2 * PD : at + 3 * PD]
+    keys = jnp.concatenate([tails[0:WIN, 0:PD], rows[:, at + 3 * PD : at + 4 * PD]], 0)
+    vals = jnp.concatenate([tails[0:WIN, PD : 2 * PD], rows[:, at + 4 * PD : at + 5 * PD]], 0)
+    prob = window_prob(query, keys, 0)
+    up = up_out[0:QB, wide]
+    prob_grad = nt(up, vals)
+    inner = jnp.sum(prob * prob_grad, -1, keepdims=True)
+    score = (prob * (prob_grad - inner)).astype(bf16)
+    lent[0:WIN, 0:PD] = (tn(score, query)[:WIN] * HD ** (-0.5)).astype(bf16)
+    lent[0:WIN, PD : 2 * PD] = tn(prob.astype(bf16), up)[:WIN].astype(bf16)
+    start = spots.taps.start + PD * head
+    tap = table[:, start : start + PD].astype(f32)
+    gate = rows[0:16, at + 6 * PD : at + 7 * PD].astype(f32)
+    flow = up_out[0:16, wide].astype(f32) * (gate * jax.nn.sigmoid(gate))
+    row0 = tap[2:3] * flow[0:1]
+    row1 = tap[1:2] * flow[0:1] + tap[2:3] * flow[1:2]
+    index = lax.broadcasted_iota(jnp.int32, (16, PD), 0)
+    edge_rows = jnp.where(index == 14, row0, jnp.where(index == 15, row1, 0.0))
+    lent[WIN : WIN + 16, 0:PD] = edge_rows.astype(bf16)
+    lent[WIN : WIN + 16, PD : 2 * PD] = jnp.zeros((16, PD), bf16)
+
+
+def turn(pair, spots, mixer_up, orgrad, weight, slot_tables, numer, mixed, projs, tails, tables):
     rows, width = mixer_up.shape
     whole = lambda a: pl.BlockSpec(a.shape, lambda i: (0,) * a.ndim)
     flat = lambda *shape: pl.BlockSpec(shape, lambda i: (0,) * len(shape))
+    tall = lambda cols, at: pl.BlockSpec((CHUNK, cols), lambda i: (i, at))
     return pl.pallas_call(
-        functools.partial(turn_kernel, own, spots),
-        grid=(1,),
+        functools.partial(turn_kernel, spots),
+        grid=(rows // CHUNK,),
         out_shape=(
-            jax.ShapeDtypeStruct((rows, 2 * PD), bf16),
-            jax.ShapeDtypeStruct((rows, 2 * PD), bf16),
-            jax.ShapeDtypeStruct((2, STATE, PD), bf16),
-            jax.ShapeDtypeStruct((2, WIN + 16, 2 * PD), bf16),
-            jax.ShapeDtypeStruct((R, 2 * PD), f32),
+            jax.ShapeDtypeStruct((rows, 4 * PD), bf16),
+            jax.ShapeDtypeStruct((rows, 4 * PD), bf16),
+            jax.ShapeDtypeStruct((4, STATE, PD), bf16),
+            jax.ShapeDtypeStruct((4, WIN + 16, 2 * PD), bf16),
+            jax.ShapeDtypeStruct((2, R, 2 * PD), bf16),
         ),
         in_specs=[
-            whole(mixer_up),
-            whole(orgrad),
-            whole(table),
-            whole(numer),
-            whole(mixed),
-            pl.BlockSpec((rows, PD), lambda i: (0, 0)),
-            pl.BlockSpec((rows, PD), lambda i: (0, 7)),
-            pl.BlockSpec((QB, 2 * HEAD_PAD), lambda i: (0, 0)),
-            whole(tails),
+            tall(width, 0),
+            tall(R, 0),
+            pl.BlockSpec((4 * PD, width), lambda i: (pair, 0)),
         ]
-        + [whole(t) for t in tables]
-        + [ANY] * len(sources),
+        + [whole(t) for t in slot_tables]
+        + [tall(2 * PD, 0)] * 4
+        + [tall(PD, 0), tall(PD, 7)] * 2
+        + [pl.BlockSpec((QB, 2 * HEAD_PAD), lambda i: (0, 0))] * 2
+        + [whole(tails)]
+        + [whole(t) for t in tables],
         out_specs=(
-            flat(rows, 2 * PD),
-            flat(rows, 2 * PD),
-            flat(2, STATE, PD),
-            flat(2, WIN + 16, 2 * PD),
-            flat(R, 2 * PD),
-        ),
-        scratch_shapes=[pltpu.VMEM((2 * PD, width), bf16), pltpu.SemaphoreType.DMA((8,))],
+            tall(4 * PD, 0),
+            tall(4 * PD, 0),
+            flat(4, STATE, PD),
+            flat(4, WIN + 16, 2 * PD),
+            flat(2, R, 2 * PD),
+        ),
+        scratch_shapes=[pltpu.VMEM((4, 256, PD), f32)] + [pltpu.VMEM((R, 2 * PD), f32)] * 2,
         compiler_params=params(48),
         cost_estimate=pl.CostEstimate(
             flops=100_000_000, bytes_accessed=300_000, transcendentals=0
         ),
         name="turn",
-    )(mixer_up, orgrad, table, numer, mixed, proj, proj, proj, tails, *tables, *sources)
+    )(
+        mixer_up, orgrad, weight, *slot_tables, *numer, *mixed,
+        projs[0], projs[0], projs[1], projs[1], *projs, tails, *tables,
+    )
 
 
 def attend_back_kernel(
@@ -638,14 +686,14 @@
     dkeys[rows:, :] = lent[0, 0:WIN, 0:PD].astype(f32)
     dvals[rows:, :] = lent[0, 0:WIN, PD : 2 * PD].astype(f32)
     flow[rows:, :] = jnp.zeros((16, PD), f32)
-    state = prior[0]
+    state = whole_state(prior[0])
     for chunk in range(chunks):
         span = slice(chunk * CHUNK, (chunk + 1) * CHUNK)
         states[chunk] = state.astype(bf16)
         if chunk + 1 < chunks:
             _, _, feat = features(nn(proj[span, 0:PD], pick[:, 512:1024]), bias[...], coef[...], 0)
             state = state + tn(feat.astype(bf16), proj[span, PD : 2 * PD])
-    follow = later[0]
+    follow = whole_state(later[0])
     causal = causal_mask()
     coefs = coef[...]
     for chunk in range(chunks - 1, -1, -1):
@@ -703,7 +751,7 @@
     last = slice(rows - 16, rows)
     edge = grad_in[rows - 16 :, :] + lent[0, WIN : WIN + 16, 0:PD].astype(f32)
     out[last, 5 * PD : 6 * PD] = edge.astype(bf16)
-    right_grad[...] = tn(rank[...], out[...])
+    right_grad[...] = tn(rank[...], out[...]).astype(bf16)
 
     @pl.when(pl.program_id(0) == 0)
     def _():
@@ -714,20 +762,20 @@
         rank_grad[...] += nt(out[...], right[...])
 
 
-def attend_back(spots, proj, tails, prior, later, lent, ups, grads, table, rank, tables):
+def attend_back(spots, number, proj, tails, prior, later, lent, ups, grads, table, rank, tables):
     rows = proj.shape[0]
     whole = lambda a: pl.BlockSpec(a.shape, lambda h: (0,) * a.ndim)
     head = pl.BlockSpec((rows, HEAD_PAD), lambda h: (0, h))
-    edge = pl.BlockSpec((1, WIN + 16, 2 * PD), lambda h: (h, 0, 0))
-    state = pl.BlockSpec((1, 256, PD), lambda h: (h, 0, 0))
-    column = pl.BlockSpec((rows, PD), lambda h: (0, h))
+    edge = pl.BlockSpec((1, WIN + 16, 2 * PD), lambda h: (2 * number + h, 0, 0))
+    state = pl.BlockSpec((1, STATE, PD), lambda h: (2 * number + h, 0, 0))
+    column = pl.BlockSpec((rows, PD), lambda h: (0, 2 * number + h))
     return pl.pallas_call(
         functools.partial(attend_back_kernel, spots),
         grid=(2,),
         out_shape=(
             jax.ShapeDtypeStruct((rows, 2 * HEAD_PAD), bf16),
             jax.ShapeDtypeStruct((rows, R), f32),
-            jax.ShapeDtypeStruct((R, 2 * HEAD_PAD), f32),
+            jax.ShapeDtypeStruct((R, 2 * HEAD_PAD), bf16),
         ),
         in_specs=[head, edge, state, state, edge, column, column, whole(table), whole(rank)]
         + [whole(t) for t in tables],
@@ -869,6 +917,70 @@
     )(own, other, middle, upstream, gain, right)
 
 
+def weighted(hot, parts):
+    expert = pl.program_id(0)
+    total = hot[expert, 0] * parts[0].astype(f32)
+    for slot in range(1, SLOTS):
+        total = total + hot[expert, slot] * parts[slot].astype(f32)
+    return total
+
+
+def by_core(flag, mine, other, base):
+    lead = flag[0] > 0
+    one, two = mine[:, :base], other[:, :base]
+    return jnp.where(lead, one, two), jnp.where(lead, two, one)
+
+
+def early_kernel(half, pad, hot, flag, mine, other, *outs):
+    right, gate_left, down_right, out_left, gate_right, down_left = outs
+    width = right.shape[2]
+    base = 2 * PD + 3 * pad
+    own, sibling = weighted(hot, mine), weighted(hot, other)
+    for n, ref in enumerate((right, gate_left, down_right)):
+        cols = slice(base + width * n, base + width * (n + 1))
+        ref[0] = own[:, cols] + sibling[:, cols]
+    cores = by_core(flag, own, sibling, base)
+    out_left[0] = jnp.concatenate(
+        [part[:, PD * h : PD * h + HD] for part in cores for h in range(2)], 1
+    )
+    for g in range(2):
+        at = 2 * PD + pad * g
+        gate_right[0, :, g, :] = jnp.concatenate([part[:, at : at + half] for part in cores], 1)
+    at = 2 * PD + 2 * pad
+    down_left[0] = jnp.concatenate([part[:, at : at + half] for part in cores], 1)
+
+
+def late_kernel(hot, flag, mine, other, right, left):
+    width = left.shape[2]
+    base = 2 * HEAD_PAD
+    own, sibling = weighted(hot, mine), weighted(hot, other)
+    left[0] = own[:, base : base + width] + sibling[:, base : base + width]
+    for core, part in enumerate(by_core(flag, own, sibling, base)):
+        for head in range(2):
+            at = HEAD_PAD * head
+            right[0, :, 2 * core + head, :] = jnp.concatenate(
+                [part[:, at + place_at : at + place_at + size] for _, size, place_at in HEAD_SEGMENTS], 1
+            )
+
+
+def tables_of(kernel, shapes, name, hot, flag, mine, other):
+    whole = lambda a: pl.BlockSpec(a.shape, lambda e: (0,) * a.ndim)
+    smem = pl.BlockSpec(memory_space=pltpu.SMEM)
+    spot = lambda rank: lambda e: (e,) + (0,) * (rank - 1)
+    return pl.pallas_call(
+        kernel,
+        grid=(NA,),
+        out_shape=[jax.ShapeDtypeStruct((NA,) + shape, f32) for shape in shapes],
+        in_specs=[smem, smem, whole(mine), whole(other)],
+        out_specs=[pl.BlockSpec((1,) + shape, spot(len(shape) + 1)) for shape in shapes],
+        compiler_params=params(40),
+        cost_estimate=pl.CostEstimate(
+            flops=100_000_000, bytes_accessed=300_000, transcendentals=0
+        ),
+        name=name,
+    )(hot, flag, mine, other)
+
+
 def swap_core(array):
     return lax.ppermute(array, "core", [(0, 1), (1, 0)])
 
@@ -949,25 +1061,57 @@
     return lax.ppermute(array, "chip", pairs)
 
 
-def carried(states, backward):
-    if backward and lax.axis_size("chip") == 4:
-        return tuple(swap_chip(states, bit) for bit in (1, 2, 3))
-    return (lax.all_gather(states, "chip"),)
-
-
-def carried_sum(parts, backward):
+def swap_states(packed):
+    if lax.axis_size("chip") == 4:
+        return tuple(swap_chip(packed, bit) for bit in (1, 2, 3))
+    return (lax.all_gather(packed, "chip"),)
+
+
+def use_states(parts, backward):
     chip = lax.axis_index("chip")
+    count = lax.axis_size("chip")
     if len(parts) > 1:
         total = 0.0
         for bit, part in zip((1, 2, 3), parts):
             other = chip ^ bit
             ahead = (other > chip) if backward else (other < chip)
-            total = total + jnp.where(ahead, part.astype(f32), 0.0)
+            total = total + jnp.where(ahead, part[:, :STATE].astype(f32), 0.0)
+        near = jnp.where(lax.rem(chip, 2) == (0 if backward else 1), parts[0], parts[2])
     else:
-        index = jnp.arange(lax.axis_size("chip"), dtype=jnp.int32)
+        index = jnp.arange(count, dtype=jnp.int32)
         ahead = (index > chip) if backward else (index < chip)
-        total = jnp.sum(jnp.where(ahead[:, None, None, None], parts[0].astype(f32), 0.0), 0)
-    return jnp.pad(total, ((0, 0), (0, 256 - STATE), (0, 0)))
+        states = parts[0][:, :, :STATE].astype(f32)
+        total = jnp.sum(jnp.where(ahead[:, None, None, None], states, 0.0), 0)
+        at = jnp.minimum(chip + 1, count - 1) if backward else jnp.maximum(chip - 1, 0)
+        near = lax.dynamic_index_in_dim(parts[0], at, 0, False)
+    inside = (chip < count - 1) if backward else (chip > 0)
+    rows = jnp.where(inside, near[:, STATE:], 0.0).astype(bf16)
+    rows = rows.reshape(near.shape[0], WIN + 16, 2 * PD)
+    return total, rows
+
+
+def pack_states(states, rows):
+    return jnp.concatenate([states, rows.reshape(rows.shape[0], 2 * (WIN + 16), PD)], 1)
+
+
+def copy_kernel(source, dest):
+    dest[...] = source[...]
+
+
+def copy_of(array):
+    block = pl.BlockSpec((1,) + array.shape[1:], lambda i: (i, 0, 0))
+    return pl.pallas_call(
+        copy_kernel,
+        grid=(array.shape[0],),
+        out_shape=jax.ShapeDtypeStruct(array.shape, array.dtype),
+        in_specs=[block],
+        out_specs=block,
+        compiler_params=params(32),
+        cost_estimate=pl.CostEstimate(
+            flops=100_000_000, bytes_accessed=300_000, transcendentals=0
+        ),
+        name="copy_of",
+    )(array)
 
 
 def stack_tp(parts):
@@ -986,14 +1130,6 @@
     high = table[..., 2 * FD :].reshape(lead + (heads, 6, HD))
     high = jnp.pad(high, zero + [(0, 0), (0, PD - HD)]).reshape(lead + (heads, 6 * PD))
     return jnp.concatenate([low, high], -1).reshape(lead + (heads * HEAD_PAD,))
-
-
-def trim_heads(table):
-    lead = table.shape[:-1]
-    table = table.reshape(lead + (2, 7, PD))
-    low = table[..., 0, : 2 * FD]
-    high = table[..., 1:, :HD].reshape(lead + (2, 6 * HD))
-    return jnp.concatenate([low, high], -1)
 
 
 def pad_last(table, size):
@@ -1118,14 +1254,15 @@
     both_input = both_cores(own_input)
     first = norm_rows(both_input.astype(f32), gain_one)[0].astype(bf16)
     mixer_rank = nn(first, my_mixer_left).astype(bf16)
-    e_m, c_m, mixer_rank, packed = hold(e_m, c_m, mixer_rank, packed)
+    e_m, c_m, mixer_rank, packed, both_input = hold(e_m, c_m, mixer_rank, packed, both_input)
 
     projs, tails, states = [], [], []
-    borrowed, prior, mixed, numer = [None] * SLOTS, [None] * SLOTS, [], []
+    borrowed, prior, mixed, numer = [None, None], [None, None], [], []
     slots = [packed[0], None, None, None]
 
     def attend_slot(slot):
-        out = attend(spots, projs[slot], borrowed[slot], prior[slot], slots[slot], tables)
+        pair, n = slot // 2, slot % 2
+        out = attend(spots, n, projs[slot], borrowed[pair], prior[pair], slots[slot], tables)
         for kept, value in zip((mixed, numer), out):
             kept.append(value)
 
@@ -1135,17 +1272,12 @@
             kept.append(value)
 
     def exchange(slot):
-        edges_here = jnp.concatenate(tails[slot : slot + 2], 0).reshape(4, 2 * (WIN + 16), PD)
+        rows_here = jnp.concatenate(tails[slot : slot + 2], 0)
         states_here = jnp.concatenate(states[slot : slot + 2], 0)
-        return lax.all_gather(jnp.concatenate([states_here, edges_here], 1), "chip")
+        return lax.all_gather(pack_states(states_here, rows_here), "chip")
 
     def use_exchange(slot, gathered):
-        total = carried_sum((gathered[:, :, :STATE],), False)
-        before = lax.dynamic_index_in_dim(gathered, jnp.maximum(chip - 1, 0), 0, False)
-        before = jnp.where(chip > 0, before[:, STATE:], 0.0).astype(bf16)
-        before = before.reshape(4, WIN + 16, 2 * PD)
-        borrowed[slot], borrowed[slot + 1] = before[:2], before[2:]
-        prior[slot], prior[slot + 1] = total[:2], total[2:]
+        prior[slot // 2], borrowed[slot // 2] = use_states((gathered,), False)
 
     x1, y1 = hop_xy(e_m)
     c2_m, f_m = cross(e_m), edge(c_m)
@@ -1178,136 +1310,135 @@
     exchanged = exchange(0)
     set2 = (slot2, x2, y2, *d2)
     project_slot(2, set2)
-    upstream = both_cores(upstream_own)
-    down_rgrad = nt(upstream, my_down_right).astype(bf16)
-    c_f, states[2], down_rgrad, *d3 = hold(c_f, states[2], down_rgrad, *d3)
+    use_exchange(0, exchanged)
+    d3_a, d3_b, c_f, states[2], upstream_own, prior[0], borrowed[0] = hold(
+        *d3, c_f, states[2], upstream_own, prior[0], borrowed[0]
+    )
     fx1, fy1 = hop_xy(e_f)
     c2_f, f_f = cross(e_f), edge(c_f)
-    set3 = (slot3, x3, y3, *d3)
+    set3 = (slot3, x3, y3, d3_a, d3_b)
     project_slot(3, set3)
     fslot2 = pick_inner(c2_f, f_f)
-    fx1, fy1, fslot2, c2_f, c_f, tails[3], states[2], states[3], exchanged = hold(
-        fx1, fy1, fslot2, c2_f, c_f, tails[3], states[2], states[3], exchanged
-    )
-    use_exchange(0, exchanged)
+    fx1, fy1, fslot2, c2_f, c_f, prior[0], tails[3], states[3] = hold(
+        fx1, fy1, fslot2, c2_f, c_f, prior[0], tails[3], states[3]
+    )
     fd1 = hop_diag(fx1, fy1, feed_cut(quarter))
-    fx2, fy2 = hop_xy(fslot2)
     f2_f = edge(c2_f)
     exchanged = exchange(2)
     attend_slot(0)
     attend_slot(1)
-    fslot3 = pick_inner(c_f, f2_f)
-    fx2, fy2, fslot3, mixed[0], mixed[1], exchanged, *fd1 = hold(
-        fx2, fy2, fslot3, mixed[0], mixed[1], exchanged, *fd1
-    )
+    upstream = both_cores(upstream_own)
+    down_rgrad = nt(upstream, my_down_right).astype(bf16)
+    mixed[0], mixed[1], down_rgrad, upstream, fslot2, exchanged, *fd1 = hold(
+        mixed[0], mixed[1], down_rgrad, upstream, fslot2, exchanged, *fd1
+    )
+    fx2, fy2 = hop_xy(fslot2)
     use_exchange(2, exchanged)
-    fd2 = hop_diag(fx2, fy2, feed_cut(quarter))
-    fx3, fy3 = hop_xy(fslot3)
     attend_slot(2)
     attend_slot(3)
+    fslot3 = pick_inner(c_f, f2_f)
     sets = list(set1) + list(set2) + list(set3)
-    out_part, out_rank = mix_out(spots, mixed, slots, my_output_right, [w_out] + sets)
+    out_part, out_rank, out_weight = mix_out(spots, mixed, slots, my_output_right, [w_out] + sets)
+    fx2, fy2, fslot3, out_part = hold(fx2, fy2, fslot3, out_part)
+
     other_part = swap_core(out_part)
     middle, second, gate_rank = norm_two(out_part, other_part, both_input, gain_two, my_gateup_left)
-    weights_feed = [
-        (w_gate, w_down),
-        (e_f, fx1, fy1, *fd1),
-        None,
-        None,
-    ]
-
     gateup_left_t = my_gateup_left.T
-    carry = ()
-    gate_grads, down_grads = [], []
-    for slot in range(SLOTS):
-        out = feed(
-            slot == 0,
-            slot == SLOTS - 1,
+
+    def feed_slots(which, sources, carry):
+        return feed(
+            which,
+            which[-1] == SLOTS - 1,
             half,
             spots,
             second,
             upstream,
             gate_rank,
             down_rgrad,
-            slots[slot],
             my_down_right,
             gateup_left_t,
-            weights_feed[slot],
+            [slots[k] for k in which],
+            sources,
             carry,
         )
-        carry = list(out[:3])
-        if slot == 0:
-            fx3, fy3, carry[2], *fd2 = hold(fx3, fy3, carry[2], *fd2)
-            weights_feed[2] = (fslot2, fx2, fy2, *fd2)
-            fd3 = hop_diag(fx3, fy3, feed_cut(quarter))
-        if slot == 1:
-            carry[2], *fd3 = hold(carry[2], *fd3)
-            weights_feed[3] = (fslot3, fx3, fy3, *fd3)
-        gate_grads.append(out[3])
-        down_grads.append(out[4])
+
+    fd2 = hop_diag(fx2, fy2, feed_cut(quarter))
+    fx3, fy3 = hop_xy(fslot3)
+    carry, gate_grads, down_grads = feed_slots(
+        (0, 1), [(w_gate, w_down), (e_f, fx1, fy1, *fd1)], []
+    )
+    fx3, fy3, carry[2], *fd2 = hold(fx3, fy3, carry[2], *fd2)
+    fd3 = hop_diag(fx3, fy3, feed_cut(quarter))
+    carry, more_gates, more_downs = feed_slots((2,), [(fslot2, fx2, fy2, *fd2)], carry)
+    gate_grads, down_grads = gate_grads + more_gates, down_grads + more_downs
+    carry[2], *fd3 = hold(carry[2], *fd3)
+    carry, more_gates, more_downs = feed_slots((3,), [(fslot3, fx3, fy3, *fd3)], carry)
+    gate_grads, down_grads = gate_grads + more_gates, down_grads + more_downs
     down_part, back_part, ranks = carry
-    down_rank, gateup_rgrad = ranks[:, :R].astype(bf16), ranks[:, R:].astype(bf16)
     other_back = swap_core(back_part)
+    mixer_up, output_rgrad = back_two(
+        back_part, other_back, middle, upstream, gain_two, my_output_right
+    )
+
+    output_rgrad, down_part, middle, ranks = hold(output_rgrad, down_part, middle, ranks)
     other_down = swap_core(own_rows(down_part, 1 - core))
     own_down = own_rows(down_part, core).astype(f32)
     own_output = own_rows(middle, core) + (own_down + other_down.astype(f32))
     own_output = own_output.astype(bf16)
-    mixer_up, output_rgrad = back_two(
-        back_part, other_back, middle, upstream, gain_two, my_output_right
-    )
-
-    ups, grads, back_states, lent, left_grads = [], [], [], [], []
-
-    def back_exchange(slot):
-        edges_here = jnp.concatenate(lent[slot : slot + 2], 0)
-        states_here = jnp.concatenate(back_states[slot : slot + 2], 0)
-        return (neighbour_chip(edges_here, -1),) + carried(states_here, True)
-
-    weights_out = [(w_out,), set1, set2, set3]
-    for slot in range(SLOTS):
-        out = turn(
-            slot == 0,
+
+    def turn_pair(pair):
+        both = slice(2 * pair, 2 * pair + 2)
+        return turn(
+            pair,
             spots,
             mixer_up,
             output_rgrad,
-            slots[slot],
-            numer[slot],
-            mixed[slot],
-            projs[slot],
-            borrowed[slot],
-            tables,
-            weights_out[slot],
-        )
-        for kept, value in zip((ups, grads, back_states, lent, left_grads), out):
-            kept.append(value)
-        if slot == 1:
-            *both, own_output = hold(*lent, *back_states, own_output)
-            lent, back_states = both[:2], both[2:]
-            block_output = lax.all_gather(own_output, "tp")
-            crossing = back_exchange(0)
-    lent[2], lent[3], back_states[2], back_states[3], *crossing = hold(
-        *lent[2:], *back_states[2:], *crossing
-    )
-
-    def back_slot(slot, returned, later):
-        pair = slice(slot % 2 * 2, slot % 2 * 2 + 2)
-        return attend_back(
-            spots,
-            projs[slot],
-            borrowed[slot],
-            prior[slot],
-            later[pair],
-            returned[pair],
-            ups[slot],
-            grads[slot],
-            slots[slot],
-            mixer_rank,
+            out_weight,
+            slots[both],
+            numer[both],
+            mixed[both],
+            projs[both],
+            borrowed[pair],
             tables,
         )
 
-    returned, later = crossing[0], carried_sum(crossing[1:], True)
-    crossing = back_exchange(2)
-    backs = [back_slot(0, returned, later), back_slot(1, returned, later)]
+    up0, grad0, states0, lent0, left_grads0 = turn_pair(0)
+    states0, lent0, own_output = hold(states0, lent0, own_output)
+    packed0 = pack_states(states0, lent0)
+    block_output = lax.all_gather(own_output, "tp")
+    crossing = swap_states(packed0)
+    up1, grad1, states1, lent1, left_grads1 = turn_pair(1)
+    left_grads = [left_grads0[0], left_grads0[1], left_grads1[0], left_grads1[1]]
+    states1, lent1, ranks, out_rank, *crossing = hold(states1, lent1, ranks, out_rank, *crossing)
+    packed1 = pack_states(states1, lent1)
+    down_rank, gateup_rgrad = ranks[:, :R].astype(bf16), ranks[:, R:].astype(bf16)
+    backs = []
+
+    def back_slots(pair, which, later, returned):
+        for n in which:
+            slot = 2 * pair + n
+            backs.append(
+                attend_back(
+                    spots,
+                    n,
+                    projs[slot],
+                    borrowed[pair],
+                    prior[pair],
+                    later,
+                    returned,
+                    (up0, up1)[pair],
+                    (grad0, grad1)[pair],
+                    slots[slot],
+                    mixer_rank,
+                    tables,
+                )
+            )
+
+    def join(array, other):
+        return (array.astype(f32) + other.astype(f32)).astype(array.dtype)
+
+    next_crossing = swap_states(packed1)
+    back_slots(0, (0, 1), *use_states(crossing, True))
     early_rank = backs[0][1] + backs[1][1]
     shared = jnp.stack(
         [
@@ -1318,47 +1449,41 @@
     )
     owned = jnp.stack(
         [jnp.concatenate([left_grads[i], gate_grads[i], down_grads[i]], 1) for i in range(SLOTS)]
-    ).astype(bf16)
-    shared, owned, early_rank, *crossing = hold(shared, owned, early_rank, *crossing)
-    returned, later = crossing[0], carried_sum(crossing[1:], True)
+    )
+    early_rank, shared, owned, *crossing = hold(early_rank, shared, owned, *next_crossing)
     shared_x, owned_x = swap_chip(shared, 1), swap_chip(owned, 1)
-    backs = backs + [back_slot(2, returned, later), back_slot(3, returned, later)]
-    rank_grad = early_rank + backs[2][1] + backs[3][1]
-    rank_grad, shared_x, owned_x = hold(rank_grad, shared_x, owned_x)
-
-    def join(array, other):
-        return (array.astype(f32) + other.astype(f32)).astype(array.dtype)
-
-    def by_core(own, other):
-        lead = core == 0
-        return jnp.stack([jnp.where(lead, own, other), jnp.where(lead, other, own)])
-
-    def slots_of(owned, shared):
-        flat = shared.reshape(-1)
-        size = owned.size // SLOTS
-        sent = [jnp.concatenate([owned[k].reshape(-1), flat.astype(bf16)]) for k in range(SLOTS)]
-        got = [sent[0]] + [swap_tp(sent[bit], bit) for bit in (1, 2, 3)]
-        return got, lambda got: (
-            jnp.stack([g[:size].reshape(owned.shape[1:]) for g in got]).astype(f32),
-            [g[size:].reshape(shared.shape).astype(f32) for g in got],
-        )
-
-    shared, owned = join(shared, shared_x), join(owned, owned_x)
-    shared, owned = add_rest(shared), add_rest(owned)
+    later, returned = use_states(crossing, True)
+    back_slots(1, (0,), later, returned)
+    early_rank = early_rank + backs[2][1]
+    early_rank, later, shared_x, owned_x = hold(early_rank, later, shared_x, owned_x)
+    shared, owned = add_rest(join(shared, shared_x)), add_rest(join(owned, owned_x))
+    back_slots(1, (1,), later, returned)
+    rank_grad = early_rank + backs[3][1]
+    rank_grad, shared, owned = hold(rank_grad, shared, owned)
+
+    def packs_of(owned, shared):
+        flat = jnp.concatenate(list(shared), 1).astype(bf16)
+        return [jnp.concatenate([owned[k], flat], 1) for k in range(SLOTS)]
+
     mixer_all = jnp.concatenate(
         [
             jnp.stack([back[2] for back in backs]),
-            tn(rank_grad.astype(bf16), first)[None],
+            tn(rank_grad.astype(bf16), first)[None].astype(bf16),
         ],
         0,
-    ).astype(bf16)
+    )
+    mixer_x = swap_chip(mixer_all, 1)
+    early = packs_of(owned, shared)
+    early = [early[0]] + [swap_tp(early[bit], bit) for bit in (1, 2, 3)]
     proj_grads = [back[0] for back in backs]
     left_t = my_mixer_left.T
     flat_mix = [w_mix] + sets
     part_a = first_back(0, proj_grads, rank_grad, left_t, flat_mix)
-    part_a, rank_grad, mixer_all, shared, owned = hold(
-        part_a, rank_grad, mixer_all, shared, owned, after=(block_output,)
-    )
+    part_a, rank_grad, mixer_x, *early = hold(
+        part_a, rank_grad, mixer_x, *early, after=(block_output,)
+    )
+    early = jnp.stack(early)
+    mixer_all = join(mixer_all, mixer_x)
     block = length // 2
 
     def finish(part, number):
@@ -1374,73 +1499,76 @@
 
     done_a = finish(part_a, 0)
     e_a, c_a = swap_tp(done_a, 1), cross(done_a)
-    mixer_x = swap_chip(mixer_all, 1)
-    shared_core, owned_core = swap_core(shared), swap_core(owned)
+    mixer_all = add_rest(mixer_all)
+    early_other = swap_core(early)
     part_b = first_back(1, proj_grads, rank_grad, left_t, flat_mix)
-    e_a, c_a, part_b, mixer_x, shared_core, owned_core = hold(
-        e_a, c_a, part_b, mixer_x, shared_core, owned_core
-    )
+    e_a, c_a, part_b, mixer_all, early_other = hold(e_a, c_a, part_b, mixer_all, early_other)
+    c2_a, f_a = cross(e_a), edge(c_a)
     done_b = finish(part_b, 1)
-    c2_a, f_a = cross(e_a), edge(c_a)
+    done_b, early, early_other, mixer_all = hold(done_b, early, early_other, mixer_all)
     e_b, c_b = swap_tp(done_b, 1), cross(done_b)
-    mixer_all = add_rest(join(mixer_all, mixer_x))
-    shared = shared + shared_core
-    owned = jnp.swapaxes(by_core(owned, owned_core), 0, 1)
-    c2_a, f_a, e_b, c_b, mixer_all, shared, owned = hold(
-        c2_a, f_a, e_b, c_b, mixer_all, shared, owned
+    late = packs_of(mixer_all[:SLOTS], mixer_all[SLOTS:])
+    late1 = swap_tp(late[1], 1)
+    hot = jnp.swapaxes(onehot, 0, 1).astype(f32)
+    flag = jnp.reshape(core == 0, (1,)).astype(jnp.int32)
+    early_tables = tables_of(
+        functools.partial(early_kernel, half, pad),
+        [(R, width)] * 3 + [(R, heads_here * HD), (R, 2, ff_here), (R, ff_here)],
+        "early_tables",
+        hot,
+        flag,
+        early,
+        early_other,
+    )
+    (
+        c2_a, f_a, e_b, c_b, late1, late[2], late[3], done_a, done_b, e_a, block_output
+    ) = hold(
+        c2_a, f_a, e_b, c_b, late1, late[2], late[3], done_a, done_b, e_a, block_output,
+        after=early_tables,
     )
     f2_a, c2_b, f_b = edge(c2_a), cross(e_b), edge(c_b)
-    mixer_core = swap_core(mixer_all)
-    f2_a, c2_b, f_b, mixer_core, shared, owned = hold(f2_a, c2_b, f_b, mixer_core, shared, owned)
+    late2, late3 = swap_tp(late[2], 2), swap_tp(late[3], 3)
+
+    block_output = copy_of(block_output)
+    input_grad = jnp.zeros(block_input.shape, bf16)
+
+    def put(whole, part, slot, number):
+        return lax.dynamic_update_slice(whole, part[None], (z ^ slot, number * block, 0))
+
+    input_grad = put(input_grad, done_a, 0, 0)
+    input_grad = put(input_grad, done_b, 0, 1)
+    input_grad = put(input_grad, e_a, 1, 0)
+    input_grad = put(input_grad, e_b, 1, 1)
+    input_grad = put(input_grad, pick_inner(c2_a, f_a), 2, 0)
+    f2_a, c2_b, f_b, late2, late3, input_grad = hold(
+        f2_a, c2_b, f_b, late2, late3, input_grad, after=(block_output,)
+    )
     f2_b = edge(c2_b)
-    mixer_owned = jnp.swapaxes(by_core(mixer_all[:SLOTS], mixer_core[:SLOTS]), 0, 1)
-    mixer_shared = mixer_all[SLOTS].astype(f32) + mixer_core[SLOTS].astype(f32)
-    early, split_early = slots_of(owned, shared)
-    late, split_late = slots_of(mixer_owned, mixer_shared)
-    owned, shared = split_early(early)
-    right_sum, mixer_shared = split_late(late)
-    z_a = [done_a, e_a, pick_inner(c2_a, f_a), pick_inner(c_a, f2_a)]
-    z_b = [done_b, e_b, pick_inner(c2_b, f_b), pick_inner(c_b, f2_b)]
-    input_grad = jnp.zeros(block_input.shape, bf16)
-    for number, parts in enumerate((z_a, z_b)):
-        for slot, part in enumerate(parts):
-            input_grad = lax.dynamic_update_slice(
-                input_grad, part[None], (z ^ slot, number * block, 0)
-            )
-
-    slot_hot = onehot.astype(f32)
-
-    def spread(hot, parts):
-        shape = (NA,) + (1,) * parts[0].ndim
-        return sum(hot[i].reshape(shape) * parts[i][None] for i in range(SLOTS))
-
-    grad_mixer_left = jnp.swapaxes(spread(slot_hot, mixer_shared), 1, 2)
-    grad_output_right = spread(slot_hot, [s[0] for s in shared])
-    grad_gateup_left = jnp.swapaxes(spread(slot_hot, [s[1] for s in shared]), 1, 2)
-    grad_down_right = spread(slot_hot, [s[2] for s in shared])
-    first_edge = 2 * HEAD_PAD
-    edges = [edge_at - first_edge for edge_at in spots.edges]
-    b, c, d = [owned[..., edges[i] : edges[i + 1]] for i in (1, 2, 3)]
-    a = jnp.moveaxis(trim_heads(right_sum), 1, 2).reshape(SLOTS, R, heads_here, HCOLS)
-    grad_mixer_right = spread(slot_hot, a)
-    b = b.reshape(SLOTS, 2, R, 2, PD)[..., :HD]
-    b = jnp.moveaxis(b, 1, 2).reshape(SLOTS, R, heads_here * HD)
-    grad_output_left = jnp.swapaxes(spread(slot_hot, b), 1, 2)
-    c = c.reshape(SLOTS, 2, R, 2, pad)[..., :half]
-    c = jnp.moveaxis(c, 1, 3).reshape(SLOTS, R, 2, ff_here)
-    grad_gateup_right = spread(slot_hot, c)
-    d = jnp.moveaxis(d[..., :half], 1, 2).reshape(SLOTS, R, ff_here)
-    grad_down_left = jnp.swapaxes(spread(slot_hot, d), 1, 2)
+    late = jnp.stack([late[0], late1, late2, late3])
+    grad_mixer_right, grad_mixer_left = tables_of(
+        late_kernel,
+        [(R, heads_here, HCOLS), (R, width)],
+        "late_tables",
+        hot,
+        flag,
+        late,
+        swap_core(late),
+    )
+    input_grad = put(input_grad, pick_inner(c_a, f2_a), 3, 0)
+    input_grad = put(input_grad, pick_inner(c2_b, f_b), 2, 1)
+    input_grad = put(input_grad, pick_inner(c_b, f2_b), 3, 1)
+    grad_output_right, grad_gateup_left, grad_down_right = early_tables[:3]
+    grad_output_left, grad_gateup_right, grad_down_left = early_tables[3:]
     return (
         block_output,
         input_grad,
-        grad_mixer_left,
+        jnp.swapaxes(grad_mixer_left, 1, 2),
         grad_mixer_right,
-        grad_output_left,
+        jnp.swapaxes(grad_output_left, 1, 2),
         grad_output_right,
-        grad_gateup_left,
+        jnp.swapaxes(grad_gateup_left, 1, 2),
         grad_gateup_right,
-        grad_down_left,
+        jnp.swapaxes(grad_down_left, 1, 2),
         grad_down_right,
     )
 

time: 997 us -> 910 us (0.913)
  waiting for transfers between devices: 216 us -> 167 us
  other arithmetic: 99.1 us -> 80.4 us
    ppermute x36, waiting for transfers between devices: 63.2 us -> 32.9 us  [swap_chip(): return lax.ppermute(array, 'chip', [(i, i ^ bit) for i in range(count)])]
    ppermute x8, waiting for transfers between devices: 94.9 us -> 79.2 us  [edge(): return lax.ppermute(array, 'tp', [(1, 0), (2, 3)])]
    unnamed x443 -> x391, local copies, waits for them, and re-layouts: 55.6 us -> 67.7 us
    add x10 -> x4, other arithmetic: 15.6 us -> 4.07 us  [the longest x2 2.33 us: use_states(): total = total + jnp.where(ahead, part[:, :STATE].astype(f32), 0.0)]
  transfers between devices with their start and end apart: 80 -> 77, of which waited for: 25 -> 21; matrix products, arithmetic and copies ran while one was open for 16% -> 14% of each run, Pallas kernels for 30% -> 41%
where the time goes in v2:
time: 910 us; the launch traced here: 900 us
  Pallas kernels  403 us (44%)
  waiting for transfers between devices  167 us (18%)
  local copies, waits for them, and re-layouts  123 us (14%)
  starting transfers between devices  102 us (11%)
  other arithmetic  80.4 us (9%)
  between operations  16.6 us (2%)
    pallas_call x3, Pallas kernels, feed(): pl.pallas_call(functools.partial(feed_kernel, slots, last, half, pad, spo...  104 us
    pallas_call x4, Pallas kernels, attend_back(): pl.pallas_call(functools.partial(attend_back_kernel, spots), grid=(2,), o...  80.7 us
    ppermute x8, waiting for transfers between devices, edge(): return lax.ppermute(array, 'tp', [(1, 0), (2, 3)])  79.2 us
    pallas_call x4, Pallas kernels, project(): pl.pallas_call(functools.partial(project_kernel, own), out_shape=(jax.Sha...  71.9 us
    unnamed x391, local copies, waits for them, and re-layouts  67.7 us
    pallas_call x2, Pallas kernels, first_back(): pl.pallas_call(first_back_kernel, grid=(2,), out_shape=jax.ShapeDtypeStru...  50.5 us
    ppermute x13, waiting for transfers between devices, swap_tp(): return lax.ppermute(array, 'tp', [(i, i ^ bit) for i in range(4)])  45.5 us
    ppermute x36, starting transfers between devices, swap_chip(): return lax.ppermute(array, 'chip', [(i, i ^ bit) for i in range(count)])  39.5 us
  transfers between devices with their start and end apart: 77, of which 21 were waited for; matrix products, arithmetic and copies ran while one was open for 14% of the time, Pallas kernels for 41%

profile of v2, /device:TPU:0, one launch (start us, length us, event | category | flops | bytes accessed | tf_op | source)
XLA Modules:
  0.0 900.3 jit_solution(9435462756759479000)
XLA Ops:
  63.1 17.2 %project.4 = (bf16[1024,1792]{1,0:T(8,128)(2,1)S(1)}, bf16[2,80,256]{2,1,0:T(8,128)(2,1)S(1)}, bf16[2,160,128]{2,1,0:T(8,128)(2,1)S(1)}) custom-call(bf16[1024,1792]{1,0:T(8,128)(2,1)} %copy-done.107, bf16[1024,16]{1,0:T(8,128)(2,1)S(1)} %copy-done.18, bf16[16,4224]{1,0:T(8,128)(2,1)S(1)} %get-tuple-element.429.table.refs_4_.refs_6_.refs_3_, ...), custom_call_target="tpu_custom_call" | custom-call | flops 100000000 | bytes 300000 | tf_op jit(solution)/shard_map/project/pallas_call | solution.py:247
  105.6 24.3 %collective-permute-done.10 = bf16[816,896]{1,0:T(8,128)(2,1)S(1)} collective-permute-done((bf16[816,896]{1,0:T(8,128)(2,1)}, bf16[816,896]{1,0:T(8,128)(2,1)S(1)}, u32[]{:S(2)}, u32[]{:S(2)}) %collective-permute-start.10) | collective-permute-done | bytes 1462304 | tf_op jit(solution)/shard_map/ppermute | solution.py:1037
  158.4 18.3 %project.5 = (bf16[1024,1792]{1,0:T(8,128)(2,1)}, bf16[2,80,256]{2,1,0:T(8,128)(2,1)S(1)}, bf16[2,160,128]{2,1,0:T(8,128)(2,1)S(1)}) custom-call(bf16[1024,1792]{1,0:T(8,128)(2,1)} %copy-done.107, bf16[1024,16]{1,0:T(8,128)(2,1)S(1)} %copy-done.18, bf16[16,4224]{1,0:T(8,128)(2,1)S(1)} %copy-done.46, bf16[128,1280]{1,0:T(8,128)(2,1)S(1)} %copy-done.7, ...), custom_call_target="tpu_custom_call" | custom-call | flops 100000000 | bytes 300000 | tf_op jit(solution)/shard_map/project/pallas_call | solution.py:247
  178.0 12.1 %collective-permute-done.18.refs_8_ = bf16[368,896]{1,0:T(8,128)(2,1)S(1)} collective-permute-done((bf16[368,896]{1,0:T(8,128)(2,1)}, bf16[368,896]{1,0:T(8,128)(2,1)S(1)}, u32[]{:S(2)}, u32[]{:S(2)}) %collective-permute-start.18) | collective-permute-done | bytes 659488 | tf_op jit(solution)/shard_map/ppermute | solution.py:990
  210.9 17.9 %project.6 = (bf16[1024,1792]{1,0:T(8,128)(2,1)}, bf16[2,80,256]{2,1,0:T(8,128)(2,1)S(1)}, bf16[2,160,128]{2,1,0:T(8,128)(2,1)S(1)}) custom-call(bf16[1024,1792]{1,0:T(8,128)(2,1)} %copy-done.107, bf16[1024,16]{1,0:T(8,128)(2,1)S(1)} %copy-done.18, bf16[16,4224]{1,0:T(8,128)(2,1)} %get-tuple-element.240.table.refs_6_.refs_3_, ...), custom_call_target="tpu_custom_call" | custom-call | flops 100000000 | bytes 300000 | tf_op jit(solution)/shard_map/project/pallas_call | solution.py:247
  237.6 18.6 %project.7 = (bf16[1024,1792]{1,0:T(8,128)(2,1)}, bf16[2,80,256]{2,1,0:T(8,128)(2,1)S(1)}, bf16[2,160,128]{2,1,0:T(8,128)(2,1)S(1)}) custom-call(bf16[1024,1792]{1,0:T(8,128)(2,1)} %copy-done.107, bf16[1024,16]{1,0:T(8,128)(2,1)S(1)} %copy-done.18, bf16[16,4224]{1,0:T(8,128)(2,1)S(1)} %copy-done.42, bf16[128,1280]{1,0:T(8,128)(2,1)S(1)} %copy-done.7, ...), custom_call_target="tpu_custom_call" | custom-call | flops 100000000 | bytes 300000 | tf_op jit(solution)/shard_map/project/pallas_call | solution.py:247
  256.2 17.2 %collective-permute-done.26 = bf16[912,896]{1,0:T(8,128)(2,1)S(1)} collective-permute-done((bf16[912,896]{1,0:T(8,128)(2,1)}, bf16[912,896]{1,0:T(8,128)(2,1)S(1)}, u32[]{:S(2)}, u32[]{:S(2)}) %collective-permute-start.26) | collective-permute-done | bytes 1634336 | tf_op jit(solution)/shard_map/ppermute | solution.py:1037
  327.9 8.2 attend.6
  346.7 11.0 %mix_out.1 = (bf16[1024,1792]{1,0:T(8,128)(2,1)}, f32[1024,16]{1,0:T(8,128)S(1)}, bf16[1024,1792]{1,0:T(8,128)(2,1)}) custom-call(bf16[1024,256]{1,0:T(8,128)(2,1)S(1)} %copy-done.56, bf16[1024,256]{1,0:T(8,128)(2,1)S(1)} %copy-done.59, bf16[1024,256]{1,0:T(8,128)(2,1)S(1)} %get-tuple-element.277.refs_2_.refs_7_, ...), custom_call_target="tpu_custom_call" | custom-call | flops 100000000 | bytes 300000 | tf_op jit(solution)/shard_map/mix_out/pallas_call | solution.py:412
  381.0 45.9 %feed.3 = (f32[1024,1792]{1,0:T(8,128)}, f32[1024,1792]{1,0:T(8,128)}, f32[1024,32]{1,0:T(8,128)}, bf16[16,1280]{1,0:T(8,128)(2,1)}, bf16[16,1280]{1,0:T(8,128)(...) custom-call(bf16[1024,1792]{1,0:T(8,128)(2,1)} %copy-done.8, ...), custom_call_target="tpu_custom_call" | custom-call | flops 100000000 | bytes 300000 | tf_op jit(solution)/shard_map/feed/pallas_call | solution.py:520
  431.9 28.3 %feed.4 = (f32[1024,1792]{1,0:T(8,128)}, f32[1024,1792]{1,0:T(8,128)}, f32[1024,32]{1,0:T(8,128)}, bf16[16,1280]{1,0:T(8,128)(2,1)}, bf16[16,640]{1,0:T(8,128)(2,1)}) custom-call(bf16[1024,1792]{1,0:T(8,128)(2,1)} %copy-done.8, bf16[1024,1792]{1,0:T(8,128)(2,1)} %get-tuple-element.284.refs_1_.upstream, bf16[1024,16]{1,0:T(8,128)(2,1)} %copy-done.69, ...), custom_call_target="tpu_custom_call" | custom-call | flops 100000000 | bytes 300000 | tf_op jit(solution)/shard_map/feed/pallas_call | solution.py:520
  461.4 29.6 %feed.5 = (bf16[1024,1792]{1,0:T(8,128)(2,1)}, bf16[1024,1792]{1,0:T(8,128)(2,1)}, f32[1024,32]{1,0:T(8,128)}, bf16[16,1280]{1,0:T(8,128)(2,1)}, bf16[16,640]{1,0:T(8,128)(2,1)}) custom-call(bf16[1024,1792]{1,0:T(8,128)(2,1)} %copy-done.8, bf16[1024,1792]{1,0:T(8,128)(2,1)} %get-tuple-element.284.refs_1_.upstream, bf16[1024,16]{1,0:T(8,128)(2,1)} %copy-done.69, ...), custom_call_target="tpu_custom_call" | custom-call | flops 100000000 | bytes 300000 | tf_op jit(solution)/shard_map/feed/pallas_call | solution.py:520
  515.2 12.5 %turn.3 = (bf16[1024,512]{1,0:T(8,128)(2,1)S(1)}, bf16[1024,512]{1,0:T(8,128)(2,1)S(1)}, bf16[4,160,128]{2,1,0:T(8,128)(2,1)S(1)}, bf16[4,80,256]{2,1,0:T(8,128)(2,1)S(1)}, bf16[2,16,256]{2,1,0:T(8,128)(2,1)S(1)}) custom-call(bf16[1024,1792]{1,0:T(8,128)(2,1)} %copy-done.14, bf16[1024,16]{1,0:T(8,128)(2,1)S(1)} %copy-done.71, ...), custom_call_target="tpu_custom_call" | custom-call | flops 100000000 | bytes 300000 | tf_op jit(solution)/shard_map/turn/pallas_call | solution.py:630
  537.8 13.0 %turn.2 = (bf16[1024,512]{1,0:T(8,128)(2,1)S(1)}, bf16[1024,512]{1,0:T(8,128)(2,1)S(1)}, bf16[4,160,128]{2,1,0:T(8,128)(2,1)S(1)}, bf16[4,80,256]{2,1,0:T(8,128)(2,1)S(1)}, bf16[2,16,256]{2,1,0:T(8,128)(2,1)S(1)}) custom-call(bf16[1024,1792]{1,0:T(8,128)(2,1)} %copy-done.14, bf16[1024,16]{1,0:T(8,128)(2,1)S(1)} %copy-done.72, ...), custom_call_target="tpu_custom_call" | custom-call | flops 100000000 | bytes 300000 | tf_op jit(solution)/shard_map/turn/pallas_call | solution.py:630
  587.0 19.9 %attend_back.4 = (bf16[1024,1792]{1,0:T(8,128)(2,1)}, f32[1024,16]{1,0:T(8,128)S(1)}, bf16[16,1792]{1,0:T(8,128)(2,1)S(1)}) custom-call(bf16[1024,1792]{1,0:T(8,128)(2,1)} %copy-done.2, bf16[4,80,256]{2,1,0:T(8,128)(2,1)S(1)} %copy-done.37, f32[4,160,128]{2,1,0:T(8,128)S(1)} %copy-done.30, f32[4,160,128]{2,1,0:T(8,128)S(1)} %select_add_fusion.1.later, ...), custom_call_target="tpu_custom_call" | custom-call | flops 100000000 | bytes 300000 | tf_op jit(solution)/shard_map/attend_back/pallas_call | solution.py:772
  607.0 20.5 %attend_back.5 = (bf16[1024,1792]{1,0:T(8,128)(2,1)}, f32[1024,16]{1,0:T(8,128)S(1)}, bf16[16,1792]{1,0:T(8,128)(2,1)S(1)}) custom-call(bf16[1024,1792]{1,0:T(8,128)(2,1)} %get-tuple-element.260.proj.refs_11_.refs_12_.refs_14_, bf16[4,80,256]{2,1,0:T(8,128)(2,1)S(1)} %copy-done.37, f32[4,160,128]{2,1,0:T(8,128)S(1)} %copy-done.30, ...), custom_call_target="tpu_custom_call" | custom-call | flops 100000000 | bytes 300000 | tf_op jit(solution)/shard_map/attend_back/pallas_call | solution.py:772
  639.7 20.1 %attend_back.6 = (bf16[1024,1792]{1,0:T(8,128)(2,1)}, f32[1024,16]{1,0:T(8,128)S(1)}, bf16[16,1792]{1,0:T(8,128)(2,1)S(1)}) custom-call(bf16[1024,1792]{1,0:T(8,128)(2,1)} %get-tuple-element.275.proj.refs_9_.refs_10_.refs_13_, bf16[4,80,256]{2,1,0:T(8,128)(2,1)S(1)} %copy-done.52, f32[4,160,128]{2,1,0:T(8,128)S(1)} %select_reduce_fusion.prior, ...), custom_call_target="tpu_custom_call" | custom-call | flops 100000000 | bytes 300000 | tf_op jit(solution)/shard_map/attend_back/pallas_call | solution.py:772
  666.9 20.1 %attend_back.7 = (bf16[1024,1792]{1,0:T(8,128)(2,1)}, f32[1024,16]{1,0:T(8,128)S(1)}, bf16[16,1792]{1,0:T(8,128)(2,1)S(1)}) custom-call(bf16[1024,1792]{1,0:T(8,128)(2,1)} %get-tuple-element.278.proj.refs_11_.refs_12_.refs_14_, bf16[4,80,256]{2,1,0:T(8,128)(2,1)S(1)} %copy-done.52, f32[4,160,128]{2,1,0:T(8,128)S(1)} %select_reduce_fusion.prior, ...), custom_call_target="tpu_custom_call" | custom-call | flops 100000000 | bytes 300000 | tf_op jit(solution)/shard_map/attend_back/pallas_call | solution.py:772
  700.9 25.3 %first_back.2.refs_0_ = bf16[512,1792]{1,0:T(8,128)(2,1)} custom-call(bf16[1024,1792]{1,0:T(8,128)(2,1)} %get-tuple-element.333.refs_0_, bf16[1024,1792]{1,0:T(8,128)(2,1)} %get-tuple-element.334.refs_1_, bf16[1024,1792]{1,0:T(8,128)(2,1)} %get-tuple-element.356.refs_2_, bf16[1024,1792]{1,0:T(8,128)(2,1)} %get-tuple-element.362.refs_3_, ...), custom_call_target="tpu_custom_call" | custom-call | flops 100000000 | bytes 300000 | tf_op jit(solution)/shard_map/first_back/pallas_call | solution.py:840
  739.4 25.2 %first_back.3.refs_2_ = bf16[512,1792]{1,0:T(8,128)(2,1)} custom-call(bf16[1024,1792]{1,0:T(8,128)(2,1)} %get-tuple-element.333.refs_0_, bf16[1024,1792]{1,0:T(8,128)(2,1)} %get-tuple-element.334.refs_1_, bf16[1024,1792]{1,0:T(8,128)(2,1)} %get-tuple-element.356.refs_2_, bf16[1024,1792]{1,0:T(8,128)(2,1)} %get-tuple-element.362.refs_3_, ...), custom_call_target="tpu_custom_call" | custom-call | flops 100000000 | bytes 300000 | tf_op jit(solution)/shard_map/first_back/pallas_call | solution.py:840
  797.4 21.6 %collective-permute-done.66.refs_4_ = bf16[16,3584]{1,0:T(8,128)(2,1)S(1)} collective-permute-done((bf16[16,3584]{1,0:T(8,128)(2,1)S(1)}, bf16[16,3584]{1,0:T(8,128)(2,1)S(1)}, u32[]{:S(2)}, u32[]{:S(2)}) %collective-permute-start.66) | collective-permute-done | bytes 114720 | tf_op jit(solution)/shard_map/ppermute | solution.py:994
  841.5 14.1 %collective-permute-done.70.refs_3_ = bf16[16,3584]{1,0:T(8,128)(2,1)S(1)} collective-permute-done((bf16[16,3584]{1,0:T(8,128)(2,1)}, bf16[16,3584]{1,0:T(8,128)(2,1)S(1)}, u32[]{:S(2)}, u32[]{:S(2)}) %collective-permute-start.70) | collective-permute-done | bytes 114720 | tf_op jit(solution)/shard_map/ppermute | solution.py:994
  855.6 12.7 %collective-permute-done.69.refs_2_ = bf16[256,1792]{1,0:T(8,128)(2,1)S(1)} collective-permute-done((bf16[256,1792]{1,0:T(8,128)(2,1)}, bf16[256,1792]{1,0:T(8,128)(2,1)S(1)}, u32[]{:S(2)}, u32[]{:S(2)}) %collective-permute-start.69) | collective-permute-done | bytes 917536 | tf_op jit(solution)/shard_map/ppermute | solution.py:1037
  879.7 12.7 %collective-permute-done.72 = bf16[256,1792]{1,0:T(8,128)(2,1)S(1)} collective-permute-done((bf16[256,1792]{1,0:T(8,128)(2,1)}, bf16[256,1792]{1,0:T(8,128)(2,1)S(1)}, u32[]{:S(2)}, u32[]{:S(2)}) %collective-permute-start.72) | collective-permute-done | bytes 917536 | tf_op jit(solution)/shard_map/ppermute | solution.py:1037
  (724 shorter events, 417.3 us)
Async XLA Ops:
  7.2 222.9 %all-gather.7.cloned.1.call-start = ((), (), s32[]{:S(2)}) async-start(), calls=%async_computation | async-start | bytes 1638400 | tf_op jit(solution)/shard_map/all_gather | solution.py:1277
  91.2 49.0 %collective-permute-start.8 = (bf16[816,896]{1,0:T(8,128)(2,1)}, bf16[816,896]{1,0:T(8,128)(2,1)S(1)}, u32[]{:S(2)}, u32[]{:S(2)}) collective-permute-start(bf16[816,896]{1,0:T(8,128)(2,1)} %get-tuple-element.220.rest_0_.refs_15_.refs_12_), channel_id=1, source_target_pairs={{0,8},{8,0},{16,24},{24,16},{1,9},{9,1},{17,25},{25,17},{2,10},{10... | collective-permute-start | bytes 4386824 | tf_op jit(solution)/shard_map/ppermute | solution.py:990
  92.7 48.4 %collective-permute-start.9 = (bf16[816,896]{1,0:T(8,128)(2,1)}, bf16[816,896]{1,0:T(8,128)(2,1)S(1)}, u32[]{:S(2)}, u32[]{:S(2)}) collective-permute-start(bf16[816,896]{1,0:T(8,128)(2,1)} %get-tuple-element.220.rest_0_.refs_15_.refs_12_), channel_id=1, source_target_pairs={{0,16},{8,24},{16,0},{24,8},{1,17},{9,25},{17,1},{25,9},{2,18},{10... | collective-permute-start | bytes 4386824 | tf_op jit(solution)/shard_map/ppermute | solution.py:990
  96.7 43.5 %collective-permute-start.14 = (bf16[448,896]{1,0:T(8,128)(2,1)S(1)}, bf16[448,896]{1,0:T(8,128)(2,1)S(1)}, u32[]{:S(2)}, u32[]{:S(2)}) collective-permute-start(bf16[448,896]{1,0:T(8,128)(2,1)S(1)} %slice.162), channel_id=1, source_target_pairs={{0,16},{8,24},{16,0},{24,8},{1,17},{9,25},{17,1},{25,9},{2,18},{10... | collective-permute-start | bytes 2408456 | tf_op jit(solution)/shard_map/ppermute | solution.py:990
  142.8 51.5 %collective-permute-start.17 = (bf16[912,896]{1,0:T(8,128)(2,1)}, bf16[912,896]{1,0:T(8,128)(2,1)}, u32[]{:S(2)}, u32[]{:S(2)}) collective-permute-start(bf16[912,896]{1,0:T(8,128)(2,1)} %get-tuple-element.228), channel_id=1, source_target_pairs={{0,1},{1,0},{2,3},{3,2},{4,5},{5,4},{6,7},{7,6},{8,9},{9,8},{10,11... | collective-permute-start | bytes 4902920 | tf_op jit(solution)/shard_map/ppermute | solution.py:994
  146.0 48.3 %collective-permute-start.15 = (bf16[816,896]{1,0:T(8,128)(2,1)}, bf16[816,896]{1,0:T(8,128)(2,1)}, u32[]{:S(2)}, u32[]{:S(2)}) collective-permute-start(bf16[816,896]{1,0:T(8,128)(2,1)} %get-tuple-element.227.rest_0_.refs_20_.refs_17_), channel_id=1, source_target_pairs={{0,8},{8,0},{16,24},{24,16},{1,9},{9,1},{17,25},{25,17},{2,10},{10... | collective-permute-start | bytes 4386824 | tf_op jit(solution)/shard_map/ppermute | solution.py:990
  147.4 46.9 %collective-permute-start.16 = (bf16[816,896]{1,0:T(8,128)(2,1)}, bf16[816,896]{1,0:T(8,128)(2,1)}, u32[]{:S(2)}, u32[]{:S(2)}) collective-permute-start(bf16[816,896]{1,0:T(8,128)(2,1)} %get-tuple-element.227.rest_0_.refs_20_.refs_17_), channel_id=1, source_target_pairs={{0,16},{8,24},{16,0},{24,8},{1,17},{9,25},{17,1},{25,9},{2,18},{10... | collective-permute-start | bytes 4386824 | tf_op jit(solution)/shard_map/ppermute | solution.py:990
  151.0 43.2 %collective-permute-start.19 = (bf16[448,896]{1,0:T(8,128)(2,1)}, bf16[448,896]{1,0:T(8,128)(2,1)S(1)}, u32[]{:S(2)}, u32[]{:S(2)}) collective-permute-start(bf16[448,896]{1,0:T(8,128)(2,1)} %slice.164), channel_id=1, source_target_pairs={{0,16},{8,24},{16,0},{24,8},{1,17},{9,25},{17,1},{25,9},{2,18},{10... | collective-permute-start | bytes 2408456 | tf_op jit(solution)/shard_map/ppermute | solution.py:990
  198.8 117.3 %all-gather.9.cloned.1.call-start = ((), (), s32[]{:S(2)}) async-start(), calls=%async_computation.1 | async-start | bytes 1638400 | tf_op jit(solution)/shard_map/all_gather | solution.py:1277
  206.8 49.3 %collective-permute-start.25 = (bf16[912,896]{1,0:T(8,128)(2,1)}, bf16[912,896]{1,0:T(8,128)(2,1)}, u32[]{:S(2)}, u32[]{:S(2)}) collective-permute-start(bf16[912,896]{1,0:T(8,128)(2,1)} %get-tuple-element.250.refs_10_), channel_id=1, source_target_pairs={{1,2},{2,1},{5,6},{6,5},{9,10},{10,9},{13,14},{14,13},{17,18},{18,... | collective-permute-start | bytes 4902920 | tf_op jit(solution)/shard_map/ppermute | solution.py:1033
  234.0 39.4 %collective-permute-start.26 = (bf16[912,896]{1,0:T(8,128)(2,1)}, bf16[912,896]{1,0:T(8,128)(2,1)S(1)}, u32[]{:S(2)}, u32[]{:S(2)}) collective-permute-start(bf16[912,896]{1,0:T(8,128)(2,1)} %get-tuple-element.251.refs_4_), channel_id=1, source_target_pairs={{1,0},{2,3},{5,4},{6,7},{9,8},{10,11},{13,12},{14,15},{17,16},{18,... | collective-permute-start | bytes 4902920 | tf_op jit(solution)/shard_map/ppermute | solution.py:1037
  237.6 68.2 %collective-permute-start.27 = (bf16[512,1792]{1,0:T(8,128)(2,1)}, bf16[512,1792]{1,0:T(8,128)(2,1)}, u32[]{:S(2)}, u32[]{:S(2)}) collective-permute-start(bf16[512,1792]{1,0:T(8,128)(2,1)} %get-tuple-element.262), channel_id=1, source_target_pairs={{0,4},{4,0},{1,5},{5,1},{2,6},{6,2},{3,7},{7,3},{8,12},{12,8},{9,1... | collective-permute-start | bytes 5505032 | tf_op jit(solution)/shard_map/ppermute | solution.py:985
  280.0 446.3 %all-gather.11.cloned.1.call-start = ((), (), s32[]{:S(2)}) async-start(), calls=%async_computation.2 | async-start | bytes 9175040 | tf_op jit(solution)/shard_map/all_gather | solution.py:1408
  316.9 41.6 %collective-permute-start.30 = (bf16[912,896]{1,0:T(8,128)(2,1)}, bf16[912,896]{1,0:T(8,128)(2,1)}, u32[]{:S(2)}, u32[]{:S(2)}) collective-permute-start(bf16[912,896]{1,0:T(8,128)(2,1)} %get-tuple-element.270.refs_7_), channel_id=1, source_target_pairs={{0,8},{8,0},{16,24},{24,16},{1,9},{9,1},{17,25},{25,17},{2,10},{10... | collective-permute-start | bytes 4902920 | tf_op jit(solution)/shard_map/ppermute | solution.py:990
  318.4 40.2 %collective-permute-start.31 = (bf16[912,896]{1,0:T(8,128)(2,1)}, bf16[912,896]{1,0:T(8,128)(2,1)}, u32[]{:S(2)}, u32[]{:S(2)}) collective-permute-start(bf16[912,896]{1,0:T(8,128)(2,1)} %get-tuple-element.270.refs_7_), channel_id=1, source_target_pairs={{0,16},{8,24},{16,0},{24,8},{1,17},{9,25},{17,1},{25,9},{2,18},{10... | collective-permute-start | bytes 4902920 | tf_op jit(solution)/shard_map/ppermute | solution.py:990
  358.6 68.3 %collective-permute-start.34 = (bf16[912,896]{1,0:T(8,128)(2,1)}, bf16[912,896]{1,0:T(8,128)(2,1)}, u32[]{:S(2)}, u32[]{:S(2)}) collective-permute-start(bf16[912,896]{1,0:T(8,128)(2,1)} %get-tuple-element.287.refs_7_), channel_id=1, source_target_pairs={{0,8},{8,0},{16,24},{24,16},{1,9},{9,1},{17,25},{25,17},{2,10},{10... | collective-permute-start | bytes 4902920 | tf_op jit(solution)/shard_map/ppermute | solution.py:990
  359.8 67.2 %collective-permute-start.35 = (bf16[912,896]{1,0:T(8,128)(2,1)}, bf16[912,896]{1,0:T(8,128)(2,1)}, u32[]{:S(2)}, u32[]{:S(2)}) collective-permute-start(bf16[912,896]{1,0:T(8,128)(2,1)} %get-tuple-element.287.refs_7_), channel_id=1, source_target_pairs={{0,16},{8,24},{16,0},{24,8},{1,17},{9,25},{17,1},{25,9},{2,18},{10... | collective-permute-start | bytes 4902920 | tf_op jit(solution)/shard_map/ppermute | solution.py:990
  362.3 64.6 %collective-permute-start.36 = (bf16[464,896]{1,0:T(8,128)(2,1)}, bf16[464,896]{1,0:T(8,128)(2,1)S(1)}, u32[]{:S(2)}, u32[]{:S(2)}) collective-permute-start(bf16[464,896]{1,0:T(8,128)(2,1)} %slice.173), channel_id=1, source_target_pairs={{0,8},{8,0},{16,24},{24,16},{1,9},{9,1},{17,25},{25,17},{2,10},{10... | collective-permute-start | bytes 2494472 | tf_op jit(solution)/shard_map/ppermute | solution.py:990
  365.5 61.4 %collective-permute-start.37 = (bf16[448,896]{1,0:T(8,128)(2,1)}, bf16[448,896]{1,0:T(8,128)(2,1)}, u32[]{:S(2)}, u32[]{:S(2)}) collective-permute-start(bf16[448,896]{1,0:T(8,128)(2,1)} %slice.174), channel_id=1, source_target_pairs={{0,16},{8,24},{16,0},{24,8},{1,17},{9,25},{17,1},{25,9},{2,18},{10... | collective-permute-start | bytes 2408456 | tf_op jit(solution)/shard_map/ppermute | solution.py:990
  577.3 56.6 %collective-permute-start.45 = (bf16[4,320,128]{2,1,0:T(8,128)(2,1)}, bf16[4,320,128]{2,1,0:T(8,128)(2,1)}, u32[]{:S(2)}, u32[]{:S(2)}) collective-permute-start(bf16[4,320,128]{2,1,0:T(8,128)(2,1)} %constant_dynamic-update-slice_fusion.6), channel_id=1, source_target_pairs={{0,8},{8,0},{16,24},{24,16},{1,9},{9,1},{17,25},{25,17},{2,10},{10... | collective-permute-start | bytes 983048 | tf_op jit(solution)/shard_map/ppermute | solution.py:990
  578.1 55.9 %collective-permute-start.46 = (bf16[4,320,128]{2,1,0:T(8,128)(2,1)}, bf16[4,320,128]{2,1,0:T(8,128)(2,1)}, u32[]{:S(2)}, u32[]{:S(2)}) collective-permute-start(bf16[4,320,128]{2,1,0:T(8,128)(2,1)} %constant_dynamic-update-slice_fusion.6), channel_id=1, source_target_pairs={{0,16},{8,24},{16,0},{24,8},{1,17},{9,25},{17,1},{25,9},{2,18},{10... | collective-permute-start | bytes 983048 | tf_op jit(solution)/shard_map/ppermute | solution.py:990
  579.6 54.3 %collective-permute-start.47 = (bf16[4,320,128]{2,1,0:T(8,128)(2,1)}, bf16[4,320,128]{2,1,0:T(8,128)(2,1)}, u32[]{:S(2)}, u32[]{:S(2)}) collective-permute-start(bf16[4,320,128]{2,1,0:T(8,128)(2,1)} %constant_dynamic-update-slice_fusion.6), channel_id=1, source_target_pairs={{0,24},{8,16},{16,8},{24,0},{1,25},{9,17},{17,9},{25,1},{2,26},{10... | collective-permute-start | bytes 983048 | tf_op jit(solution)/shard_map/ppermute | solution.py:990
  777.4 41.6 %collective-permute-start.64 = (bf16[256,1792]{1,0:T(8,128)(2,1)}, bf16[256,1792]{1,0:T(8,128)(2,1)}, u32[]{:S(2)}, u32[]{:S(2)}) collective-permute-start(bf16[256,1792]{1,0:T(8,128)(2,1)} %get-tuple-element.387.refs_8_), channel_id=1, source_target_pairs={{0,1},{1,0},{2,3},{3,2},{4,5},{5,4},{6,7},{7,6},{8,9},{9,8},{10,11... | collective-permute-start | bytes 2752520 | tf_op jit(solution)/shard_map/ppermute | solution.py:994
  821.7 46.6 %collective-permute-start.69 = (bf16[256,1792]{1,0:T(8,128)(2,1)}, bf16[256,1792]{1,0:T(8,128)(2,1)S(1)}, u32[]{:S(2)}, u32[]{:S(2)}) collective-permute-start(bf16[256,1792]{1,0:T(8,128)(2,1)} %get-tuple-element.400), channel_id=1, source_target_pairs={{1,0},{2,3},{5,4},{6,7},{9,8},{10,11},{13,12},{14,15},{17,16},{18,... | collective-permute-start | bytes 2752520 | tf_op jit(solution)/shard_map/ppermute | solution.py:1037
  (244 other events, 2602.2 us)
Sparse Core Ops, SparseCore 0:
  198.9 30.7 all-gather.6
  280.1 32.3 all-gather.8
  532.7 132.9 all-gather.10

commit v3 on v2

--- a/solution.py
+++ b/solution.py
@@ -19,10 +19,11 @@
 HCOLS = 704
 SLOTS = 4
 HEAD_PAD = 7 * PD
-FEATS = 1 + FD + FD * (FD + 1) // 2
 STATE = 160
 CHUNK = 256
 QB = 128
+BACK_QB = 256
+PACK = STATE + 2 * WIN + 32
 
 epsilon = 1e-05
 masked = -1e30
@@ -46,22 +47,18 @@
 def feature_tables():
     leading, trailing = np.triu_indices(FD)
     pick = np.zeros((PD, 1280), np.float32)
-    bias = np.zeros((1, 512), np.float32)
-    coef = np.zeros((1, 256), np.float32)
-    bias[0, 0] = 1.0
-    bias[0, 256 : 256 + 1 + FD] = 1.0
-    coef[0, : 1 + FD] = 1.0
-    coef[0, 1 + FD : FEATS] = np.where(leading == trailing, np.sqrt(0.5), 1.0)
     for base, row in ((0, 0), (512, FD)):
+        pick[PD - 1, base] = 1.0
+        pick[PD - 1, base + 256 : base + 256 + 1 + FD] = 1.0
         for i in range(FD):
             pick[row + i, base + 1 + i] = 0.5
         for n, (i, j) in enumerate(zip(leading, trailing)):
-            pick[row + i, base + 1 + FD + n] = 0.5
+            pick[row + i, base + 1 + FD + n] = 0.25 if i == j and base == 0 else 0.5
             pick[row + j, base + 256 + 1 + FD + n] = 0.5
     for i in range(FD):
         pick[FD + i, 1024 + i] = 0.25
         pick[i, 1152 + FD + i] = 0.25
-    return pick, bias, coef
+    return pick
 
 
 HEAD_SEGMENTS = [(0, 2 * FD, 0)] + [(2 * FD + HD * i, HD, PD * (i + 1)) for i in range(6)]
@@ -190,10 +187,10 @@
         dest[pad * i + half : pad * (i + 1)] = jnp.zeros((pad - half, dest.shape[1]), bf16)
 
 
-def features(picked, bias, coef, at):
-    one = picked[:, at : at + 256] + bias[:, :256]
-    two = picked[:, at + 256 : at + 512] + bias[:, 256:]
-    return one, two, one * two * coef
+def features(picked, at):
+    one = picked[:, at : at + 256]
+    two = picked[:, at + 256 : at + 512]
+    return one, two, (one * two).astype(bf16)
 
 
 class Table:
@@ -210,10 +207,10 @@
     return pltpu.CompilerParams(vmem_limit_bytes=mib * 2**20, **more)
 
 
-def project_kernel(own, first, rank, table, pick, bias, coef, *rest):
+def project_kernel(own, first, rank, table, pick, *rest):
     count = 1 if own else 5
     refs = rest[:count]
-    proj, tails, state, weight, sems = rest[count:]
+    proj, packed, weight, sems = rest[count:]
     copies = mixer_copies(refs, own, weight, 0)
     run_copies(copies, sems, 0)
     mixer_pads(weight, 0)
@@ -226,19 +223,21 @@
             rows = pl.ds(pl.multiple_of(block * CHUNK, CHUNK), CHUNK)
             result = nt(first[rows, :], weight[cols, :]) + nn(rank[rows, :], table[:, cols])
             rounded = result.astype(bf16)
+            lane = lax.broadcasted_iota(jnp.int32, (CHUNK, PD), 1)
+            base = jnp.where(lane == PD - 1, 1.0, result[:, :PD]).astype(bf16)
             proj[rows, cols] = rounded
-            picked = nn(rounded[:, :PD], pick[...][:, 512:1024])
-            _, _, feat = features(picked, bias[...], coef[...], 0)
-            return carry + tn(feat.astype(bf16), rounded[:, PD : 2 * PD])
+            proj[rows, HEAD_PAD * head : HEAD_PAD * head + PD] = base
+            _, _, feat = features(nn(base, pick[:, 512:1024]), 0)
+            return carry + tn(feat, rounded[:, PD : 2 * PD])
 
         total = lax.fori_loop(0, blocks, one, jnp.zeros((256, PD), f32))
-        state[head] = total[:STATE].astype(bf16)
+        packed[head, 0:STATE] = total[:STATE].astype(bf16)
         last = first.shape[0]
         at = HEAD_PAD * head
-        tails[head, 0:WIN, 0:PD] = proj[last - WIN :, at + 3 * PD : at + 4 * PD]
-        tails[head, 0:WIN, PD : 2 * PD] = proj[last - WIN :, at + 4 * PD : at + 5 * PD]
-        tails[head, WIN : WIN + 16, 0:PD] = proj[last - 16 :, at + 5 * PD : at + 6 * PD]
-        tails[head, WIN : WIN + 16, PD : 2 * PD] = jnp.zeros((16, PD), bf16)
+        packed[head, STATE : STATE + WIN] = proj[last - WIN :, at + 3 * PD : at + 4 * PD]
+        packed[head, STATE + WIN : STATE + 2 * WIN] = proj[last - WIN :, at + 4 * PD : at + 5 * PD]
+        packed[head, PACK - 32 : PACK - 16] = proj[last - 16 :, at + 5 * PD : at + 6 * PD]
+        packed[head, PACK - 16 : PACK] = jnp.zeros((16, PD), bf16)
 
 
 def project(own, first, rank, table, tables, refs):
@@ -248,11 +247,10 @@
         functools.partial(project_kernel, own),
         out_shape=(
             jax.ShapeDtypeStruct((rows, 2 * HEAD_PAD), bf16),
-            jax.ShapeDtypeStruct((2, WIN + 16, 2 * PD), bf16),
-            jax.ShapeDtypeStruct((2, STATE, PD), bf16),
-        ),
-        in_specs=[vm] * 6 + [ANY] * len(refs),
-        out_specs=(vm, vm, vm),
+            jax.ShapeDtypeStruct((2, PACK, PD), bf16),
+        ),
+        in_specs=[vm] * 4 + [ANY] * len(refs),
+        out_specs=(vm, vm),
         scratch_shapes=[pltpu.VMEM((2 * HEAD_PAD, width), bf16), pltpu.SemaphoreType.DMA((40,))],
         compiler_params=params(48),
         cost_estimate=pl.CostEstimate(
@@ -262,22 +260,20 @@
     )(first, rank, table, *tables, *refs)
 
 
-def window_mask(number):
-    query = lax.broadcasted_iota(jnp.int32, (QB, QB + WIN), 0)
-    key = lax.broadcasted_iota(jnp.int32, (QB, QB + WIN), 1)
-    allowed = (key > query) & (key <= query + WIN)
-    if number == 0:
-        lead = jnp.where(lax.axis_index("chip") > 0, 0, WIN)
-        allowed = allowed & (key >= lead)
-    return allowed
-
-
-def window_prob(query, keys, number):
+def window_masks(count):
+    query = lax.broadcasted_iota(jnp.int32, (count, count + WIN), 0)
+    key = lax.broadcasted_iota(jnp.int32, (count, count + WIN), 1)
+    others = (key > query) & (key <= query + WIN)
+    lead = jnp.where(lax.axis_index("chip") > 0, 0, WIN)
+    return others & (key >= lead), others
+
+
+def window_prob(query, keys, allowed):
     scores = nt(query, keys) * HD ** (-0.5)
-    scores = jnp.where(window_mask(number), scores, masked)
+    scores = jnp.where(allowed, scores, masked)
     largest = jnp.max(scores, -1, keepdims=True)
     expo = jnp.exp(scores - largest)
-    return expo / jnp.sum(expo, -1, keepdims=True)
+    return expo * (1.0 / jnp.sum(expo, -1, keepdims=True))
 
 
 def causal_mask():
@@ -293,33 +289,37 @@
     return result
 
 
-def attend_kernel(spots, proj, tails, prior, table, pick, bias, coef, mixed, numer, keys, vals, conv):
+def attend_kernel(spots, proj, tails, prior, table, pick, mixed, numer, states, keys, vals, conv):
     rows = proj.shape[0]
-    keys[0:WIN, :] = tails[0, 0:WIN, 0:PD]
-    vals[0:WIN, :] = tails[0, 0:WIN, PD : 2 * PD]
-    conv[0:16, :] = tails[0, WIN : WIN + 16, 0:PD].astype(f32)
+    keys[0:WIN, :] = tails[0, 0:WIN]
+    vals[0:WIN, :] = tails[0, WIN : 2 * WIN]
+    conv[0:16, :] = tails[0, 2 * WIN : 2 * WIN + 16].astype(f32)
     keys[WIN:, :] = proj[:, 3 * PD : 4 * PD]
     vals[WIN:, :] = proj[:, 4 * PD : 5 * PD]
     conv[16:, :] = proj[:, 5 * PD : 6 * PD].astype(f32)
     tap = head_taps(spots, table)
     state = whole_state(prior[0])
     causal = causal_mask()
+    first_mask, mask = window_masks(QB)
     for chunk in range(rows // CHUNK):
+        states[0, chunk] = state.astype(bf16)
         at = chunk * CHUNK
         span = slice(at, at + CHUNK)
         base = proj[span, 0:PD]
         value = proj[span, PD : 2 * PD]
         picked = nn(base, pick[:, :1152])
-        _, _, feat_q = features(picked, bias[...], coef[...], 0)
-        _, _, feat_k = features(picked, bias[...], coef[...], 512)
+        _, _, feat_q = features(picked, 0)
         score = nt(base, picked[:, 1024:1152].astype(bf16))
         weight = jnp.where(causal, 1.0 + score + 0.5 * score * score, 0.0).astype(bf16)
-        total = nn(weight, value) + nn(feat_q.astype(bf16), state.astype(bf16))
-        state = state + tn(feat_k.astype(bf16), value)
+        total = nn(weight, value) + nn(feat_q, state.astype(bf16))
+        if at + CHUNK < rows:
+            _, _, feat_k = features(picked, 512)
+            state = state + tn(feat_k, value)
         parts = []
         for number in range(chunk * CHUNK // QB, (chunk + 1) * CHUNK // QB):
             query = proj[number * QB : (number + 1) * QB, 2 * PD : 3 * PD]
-            prob = window_prob(query, keys[number * QB : number * QB + QB + WIN, :], number)
+            allowed = mask if number else first_mask
+            prob = window_prob(query, keys[number * QB : number * QB + QB + WIN, :], allowed)
             parts.append(nn(prob.astype(bf16), vals[number * QB : number * QB + QB + WIN, :]))
         window = jnp.concatenate(parts, 0)
         scale = lax.rsqrt(jnp.sum(total * total, -1, keepdims=True) * (1.0 / HD) + epsilon)
@@ -347,10 +347,11 @@
         out_shape=(
             jax.ShapeDtypeStruct((rows, 2 * PD), bf16),
             jax.ShapeDtypeStruct((rows, 2 * PD), bf16),
+            jax.ShapeDtypeStruct((2, rows // CHUNK, 256, PD), bf16),
         ),
         in_specs=[
             pl.BlockSpec((rows, HEAD_PAD), lambda h: (0, h)),
-            pl.BlockSpec((1, WIN + 16, 2 * PD), lambda h: (2 * number + h, 0, 0)),
+            pl.BlockSpec((1, PACK - STATE, PD), lambda h: (2 * number + h, 0, 0)),
             pl.BlockSpec((1, STATE, PD), lambda h: (2 * number + h, 0, 0)),
             whole(table),
         ]
@@ -358,6 +359,7 @@
         out_specs=(
             pl.BlockSpec((rows, PD), lambda h: (0, h)),
             pl.BlockSpec((rows, PD), lambda h: (0, h)),
+            pl.BlockSpec((1, rows // CHUNK, 256, PD), lambda h: (h, 0, 0, 0)),
         ),
         scratch_shapes=[
             pltpu.VMEM((rows + WIN, PD), bf16),
@@ -553,8 +555,8 @@
     mixer_up, orgrad, weight = refs[:3]
     tables, numers, mixeds = refs[3:5], refs[5:7], refs[7:9]
     bases, heads, tails = refs[9:13], refs[13:15], refs[15]
-    pick, bias, coef = refs[16:19]
-    up_out, grad_out, state, lent, left_out, total_state, left0, left1 = refs[19:]
+    pick = refs[16]
+    up_out, grad_out, packed, left_out, total_state, left0, left1 = refs[17:]
     step = pl.program_id(0)
 
     @pl.when(step == 0)
@@ -578,13 +580,12 @@
             grad = (scale * up - total * (scale * scale * scale * inner)).astype(bf16)
             up_out[:, wide] = up.astype(bf16)
             grad_out[:, wide] = grad
-            picked = nn(bases[2 * n + head][...], pick[:, 0:512])
-            _, _, feat = features(picked, bias[...], coef[...], 0)
-            total_state[2 * n + head] += tn(feat.astype(bf16), grad)
+            _, _, feat = features(nn(bases[2 * n + head][...], pick[:, 0:512]), 0)
+            total_state[2 * n + head] += tn(feat, grad)
 
     @pl.when(step == pl.num_programs(0) - 1)
     def _():
-        state[...] = total_state[:, :STATE, :].astype(bf16)
+        packed[:, 0:STATE, :] = total_state[:, :STATE, :].astype(bf16)
         left_out[0] = left0[...].astype(bf16)
         left_out[1] = left1[...].astype(bf16)
 
@@ -593,7 +594,7 @@
         for n in range(2):
             for head in range(2):
                 give_back(
-                    spots, tables[n], heads[n], tails.at[2 * n + head], up_out, lent.at[2 * n + head], n, head
+                    spots, tables[n], heads[n], tails.at[2 * n + head], up_out, packed.at[2 * n + head], n, head
                 )
 
 
@@ -601,15 +602,15 @@
     at = HEAD_PAD * head
     wide = slice(PD * (2 * n + head), PD * (2 * n + head + 1))
     query = rows[:, at + 2 * PD : at + 3 * PD]
-    keys = jnp.concatenate([tails[0:WIN, 0:PD], rows[:, at + 3 * PD : at + 4 * PD]], 0)
-    vals = jnp.concatenate([tails[0:WIN, PD : 2 * PD], rows[:, at + 4 * PD : at + 5 * PD]], 0)
-    prob = window_prob(query, keys, 0)
+    keys = jnp.concatenate([tails[0:WIN, :], rows[:, at + 3 * PD : at + 4 * PD]], 0)
+    vals = jnp.concatenate([tails[WIN : 2 * WIN, :], rows[:, at + 4 * PD : at + 5 * PD]], 0)
+    prob = window_prob(query, keys, window_masks(QB)[0])
     up = up_out[0:QB, wide]
     prob_grad = nt(up, vals)
     inner = jnp.sum(prob * prob_grad, -1, keepdims=True)
     score = (prob * (prob_grad - inner)).astype(bf16)
-    lent[0:WIN, 0:PD] = (tn(score, query)[:WIN] * HD ** (-0.5)).astype(bf16)
-    lent[0:WIN, PD : 2 * PD] = tn(prob.astype(bf16), up)[:WIN].astype(bf16)
+    lent[STATE : STATE + WIN, :] = (tn(score, query)[:WIN] * HD ** (-0.5)).astype(bf16)
+    lent[STATE + WIN : STATE + 2 * WIN, :] = tn(prob.astype(bf16), up)[:WIN].astype(bf16)
     start = spots.taps.start + PD * head
     tap = table[:, start : start + PD].astype(f32)
     gate = rows[0:16, at + 6 * PD : at + 7 * PD].astype(f32)
@@ -618,8 +619,8 @@
     row1 = tap[1:2] * flow[0:1] + tap[2:3] * flow[1:2]
     index = lax.broadcasted_iota(jnp.int32, (16, PD), 0)
     edge_rows = jnp.where(index == 14, row0, jnp.where(index == 15, row1, 0.0))
-    lent[WIN : WIN + 16, 0:PD] = edge_rows.astype(bf16)
-    lent[WIN : WIN + 16, PD : 2 * PD] = jnp.zeros((16, PD), bf16)
+    lent[PACK - 32 : PACK - 16, :] = edge_rows.astype(bf16)
+    lent[PACK - 16 : PACK, :] = jnp.zeros((16, PD), bf16)
 
 
 def turn(pair, spots, mixer_up, orgrad, weight, slot_tables, numer, mixed, projs, tails, tables):
@@ -633,8 +634,7 @@
         out_shape=(
             jax.ShapeDtypeStruct((rows, 4 * PD), bf16),
             jax.ShapeDtypeStruct((rows, 4 * PD), bf16),
-            jax.ShapeDtypeStruct((4, STATE, PD), bf16),
-            jax.ShapeDtypeStruct((4, WIN + 16, 2 * PD), bf16),
+            jax.ShapeDtypeStruct((4, PACK, PD), bf16),
             jax.ShapeDtypeStruct((2, R, 2 * PD), bf16),
         ),
         in_specs=[
@@ -651,8 +651,7 @@
         out_specs=(
             tall(4 * PD, 0),
             tall(4 * PD, 0),
-            flat(4, STATE, PD),
-            flat(4, WIN + 16, 2 * PD),
+            flat(4, PACK, PD),
             flat(2, R, 2 * PD),
         ),
         scratch_shapes=[pltpu.VMEM((4, 256, PD), f32)] + [pltpu.VMEM((R, 2 * PD), f32)] * 2,
@@ -667,35 +666,46 @@
     )
 
 
+def window_back(proj, keys, vals, ups, out, number, allowed, held):
+    start = number * BACK_QB
+    span = slice(start, start + BACK_QB)
+    band = slice(start, start + BACK_QB + WIN)
+    query = proj[span, 2 * PD : 3 * PD]
+    key = keys[band, :]
+    prob = window_prob(query, key, allowed)
+    up = ups[span, :]
+    prob_grad = nt(up, vals[band, :])
+    inner = jnp.sum(prob * prob_grad, -1, keepdims=True)
+    score = (prob * (prob_grad - inner)).astype(bf16)
+    out[span, 2 * PD : 3 * PD] = (nn(score, key) * HD ** (-0.5)).astype(bf16)
+    dkey = tn(score, query) * HD ** (-0.5)
+    dval = tn(prob.astype(bf16), up)
+    for piece, new, more in ((3, dkey, held[0]), (4, dval, held[1])):
+        cols = slice(piece * PD, (piece + 1) * PD)
+        out[start : start + BACK_QB - WIN, cols] = new[WIN:BACK_QB].astype(bf16)
+        out[start + BACK_QB - WIN : start + BACK_QB, cols] = (new[BACK_QB:] + more).astype(bf16)
+    return dkey[:WIN], dval[:WIN]
+
+
 def attend_back_kernel(
-    spots, proj, tails, prior, later, lent, ups, grads, table, rank, pick, bias, coef,
-    out, rank_grad, right_grad, keys, vals, conv, flow, dkeys, dvals, states
+    spots, proj, tails, states, later, lent, ups, grads, table, rank, pick,
+    out, rank_grad, right_grad, keys, vals, conv, flow
 ):
     rows = proj.shape[0]
     chunks = rows // CHUNK
-    keys[0:WIN, :] = tails[0, 0:WIN, 0:PD]
-    vals[0:WIN, :] = tails[0, 0:WIN, PD : 2 * PD]
-    conv[0:16, :] = tails[0, WIN : WIN + 16, 0:PD].astype(f32)
+    keys[0:WIN, :] = tails[0, 0:WIN]
+    vals[0:WIN, :] = tails[0, WIN : 2 * WIN]
+    conv[0:16, :] = tails[0, 2 * WIN : 2 * WIN + 16].astype(f32)
     keys[WIN:, :] = proj[:, 3 * PD : 4 * PD]
     vals[WIN:, :] = proj[:, 4 * PD : 5 * PD]
     conv[16:, :] = proj[:, 5 * PD : 6 * PD].astype(f32)
     tap = head_taps(spots, table)
     right = table.at[:, pl.ds(pl.multiple_of(HEAD_PAD * pl.program_id(0), PD), HEAD_PAD)]
-    dkeys[...] = jnp.zeros(dkeys.shape, f32)
-    dvals[...] = jnp.zeros(dvals.shape, f32)
-    dkeys[rows:, :] = lent[0, 0:WIN, 0:PD].astype(f32)
-    dvals[rows:, :] = lent[0, 0:WIN, PD : 2 * PD].astype(f32)
     flow[rows:, :] = jnp.zeros((16, PD), f32)
-    state = whole_state(prior[0])
-    for chunk in range(chunks):
-        span = slice(chunk * CHUNK, (chunk + 1) * CHUNK)
-        states[chunk] = state.astype(bf16)
-        if chunk + 1 < chunks:
-            _, _, feat = features(nn(proj[span, 0:PD], pick[:, 512:1024]), bias[...], coef[...], 0)
-            state = state + tn(feat.astype(bf16), proj[span, PD : 2 * PD])
     follow = whole_state(later[0])
     causal = causal_mask()
-    coefs = coef[...]
+    first_mask, mask = window_masks(BACK_QB)
+    held = (lent[0, 0:WIN].astype(f32), lent[0, WIN : 2 * WIN].astype(f32))
     for chunk in range(chunks - 1, -1, -1):
         at = chunk * CHUNK
         span = slice(at, at + CHUNK)
@@ -703,53 +713,40 @@
         value = proj[span, PD : 2 * PD]
         grad = grads[span, :]
         picked = nn(base, pick[...])
-        q_one, q_two, feat_q = features(picked, bias[...], coefs, 0)
-        k_one, k_two, feat_k = features(picked, bias[...], coefs, 512)
+        q_one, q_two, feat_q = features(picked, 0)
+        k_one, k_two, feat_k = features(picked, 512)
         key_low = picked[:, 1024:1152].astype(bf16)
         query_high = picked[:, 1152:1280].astype(bf16)
         score = nt(base, key_low)
         weight = jnp.where(causal, 1.0 + score + 0.5 * score * score, 0.0).astype(bf16)
         slope = jnp.where(causal, nt(grad, value) * (1.0 + score), 0.0).astype(bf16)
         follow_round = follow.astype(bf16)
-        q_up = nt(grad, states[chunk]) * coefs
-        k_up = nt(value, follow_round) * coefs
-        low = nn(slope, key_low) + tn(slope, query_high)
-        low = low + nt((q_up * q_two).astype(bf16), pick[:, 0:256])
-        low = low + nt((q_up * q_one).astype(bf16), pick[:, 256:512])
-        low = low + nt((k_up * k_two).astype(bf16), pick[:, 512:768])
-        low = low + nt((k_up * k_one).astype(bf16), pick[:, 768:1024])
+        q_up = nt(grad, states[0, chunk])
+        k_up = nt(value, follow_round)
+        inside = [q_up * q_two, q_up * q_one, k_up * k_two, k_up * k_one]
+        inside = jnp.concatenate([part.astype(bf16) for part in inside], 1)
+        low = nn(slope, key_low) + tn(slope, query_high) + nt(inside, pick[:, :1024])
         out[span, 0:PD] = low.astype(bf16)
-        out[span, PD : 2 * PD] = (
-            tn(weight, grad) + nn(feat_k.astype(bf16), follow_round)
-        ).astype(bf16)
-        follow = follow + tn(feat_q.astype(bf16), grad)
+        out[span, PD : 2 * PD] = (tn(weight, grad) + nn(feat_k, follow_round)).astype(bf16)
+        if chunk:
+            follow = follow + tn(feat_q, grad)
         gate = proj[span, 6 * PD : 7 * PD].astype(f32)
         up = ups[span, :].astype(f32)
         sig = jax.nn.sigmoid(gate)
-        flow[span, :] = up * gate * sig
-        slope_gate = sig * (1.0 + gate * (1.0 - sig))
+        act = gate * sig
+        flow[span, :] = up * act
+        for number in range((at + CHUNK) // BACK_QB - 1, at // BACK_QB - 1, -1):
+            held = window_back(
+                proj, keys, vals, ups, out, number, mask if number else first_mask, held
+            )
+        slope_gate = sig + act * (1.0 - sig)
         out[span, 6 * PD : 7 * PD] = (up * conv_of(conv, tap, at, CHUNK) * slope_gate).astype(bf16)
-    for number in range(rows // QB):
-        span = slice(number * QB, (number + 1) * QB)
-        band = slice(number * QB, number * QB + QB + WIN)
-        query = proj[span, 2 * PD : 3 * PD]
-        key = keys[band, :]
-        prob = window_prob(query, key, number)
-        up = ups[span, :]
-        prob_grad = nt(up, vals[band, :])
-        inner = jnp.sum(prob * prob_grad, -1, keepdims=True)
-        score = (prob * (prob_grad - inner)).astype(bf16)
-        out[span, 2 * PD : 3 * PD] = (nn(score, key) * HD ** (-0.5)).astype(bf16)
-        dkeys[band, :] += tn(score, query) * HD ** (-0.5)
-        dvals[band, :] += tn(prob.astype(bf16), up)
-    out[:, 3 * PD : 4 * PD] = dkeys[WIN:, :].astype(bf16)
-    out[:, 4 * PD : 5 * PD] = dvals[WIN:, :].astype(bf16)
     grad_in = tap[0:1] * flow[0:rows, :]
     for offset in range(1, KW):
         grad_in = grad_in + tap[offset : offset + 1] * flow[offset : offset + rows, :]
     out[:, 5 * PD : 6 * PD] = grad_in.astype(bf16)
     last = slice(rows - 16, rows)
-    edge = grad_in[rows - 16 :, :] + lent[0, WIN : WIN + 16, 0:PD].astype(f32)
+    edge = grad_in[rows - 16 :, :] + lent[0, 2 * WIN : 2 * WIN + 16].astype(f32)
     out[last, 5 * PD : 6 * PD] = edge.astype(bf16)
     right_grad[...] = tn(rank[...], out[...]).astype(bf16)
 
@@ -762,11 +759,11 @@
         rank_grad[...] += nt(out[...], right[...])
 
 
-def attend_back(spots, number, proj, tails, prior, later, lent, ups, grads, table, rank, tables):
+def attend_back(spots, number, proj, tails, states, later, lent, ups, grads, table, rank, tables):
     rows = proj.shape[0]
     whole = lambda a: pl.BlockSpec(a.shape, lambda h: (0,) * a.ndim)
     head = pl.BlockSpec((rows, HEAD_PAD), lambda h: (0, h))
-    edge = pl.BlockSpec((1, WIN + 16, 2 * PD), lambda h: (2 * number + h, 0, 0))
+    edge = pl.BlockSpec((1, PACK - STATE, PD), lambda h: (2 * number + h, 0, 0))
     state = pl.BlockSpec((1, STATE, PD), lambda h: (2 * number + h, 0, 0))
     column = pl.BlockSpec((rows, PD), lambda h: (0, 2 * number + h))
     return pl.pallas_call(
@@ -777,7 +774,17 @@
             jax.ShapeDtypeStruct((rows, R), f32),
             jax.ShapeDtypeStruct((R, 2 * HEAD_PAD), bf16),
         ),
-        in_specs=[head, edge, state, state, edge, column, column, whole(table), whole(rank)]
+        in_specs=[
+            head,
+            edge,
+            pl.BlockSpec((1, rows // CHUNK, 256, PD), lambda h: (h, 0, 0, 0)),
+            state,
+            edge,
+            column,
+            column,
+            whole(table),
+            whole(rank),
+        ]
         + [whole(t) for t in tables],
         out_specs=(
             head,
@@ -789,16 +796,13 @@
             pltpu.VMEM((rows + WIN, PD), bf16),
             pltpu.VMEM((rows + 16, PD), f32),
             pltpu.VMEM((rows + 16, PD), f32),
-            pltpu.VMEM((rows + WIN, PD), f32),
-            pltpu.VMEM((rows + WIN, PD), f32),
-            pltpu.VMEM((rows // CHUNK, 256, PD), bf16),
         ],
         compiler_params=params(48),
         cost_estimate=pl.CostEstimate(
             flops=100_000_000, bytes_accessed=300_000, transcendentals=0
         ),
         name="attend_back",
-    )(proj, tails, prior, later, lent, ups, grads, table, rank, *tables)
+    )(proj, tails, states, later, lent, ups, grads, table, rank, *tables)
 
 
 def first_back_kernel(*refs):
@@ -995,7 +999,10 @@
 
 
 def both_cores(own):
-    other = swap_core(own)
+    return order_cores(own, swap_core(own))
+
+
+def order_cores(own, other):
     lead = lax.axis_index("core") == 0
     return jnp.concatenate([jnp.where(lead, own, other), jnp.where(lead, other, own)], 0)
 
@@ -1085,13 +1092,7 @@
         at = jnp.minimum(chip + 1, count - 1) if backward else jnp.maximum(chip - 1, 0)
         near = lax.dynamic_index_in_dim(parts[0], at, 0, False)
     inside = (chip < count - 1) if backward else (chip > 0)
-    rows = jnp.where(inside, near[:, STATE:], 0.0).astype(bf16)
-    rows = rows.reshape(near.shape[0], WIN + 16, 2 * PD)
-    return total, rows
-
-
-def pack_states(states, rows):
-    return jnp.concatenate([states, rows.reshape(rows.shape[0], 2 * (WIN + 16), PD)], 1)
+    return total, jnp.where(inside, near[:, STATE:], 0.0).astype(bf16)
 
 
 def copy_kernel(source, dest):
@@ -1181,8 +1182,7 @@
     pad = (half + PD - 1) // PD * PD
     quarter = half // 2
 
-    pick, bias, coef = feature_tables()
-    tables = (jnp.asarray(pick, bf16), jnp.asarray(bias), jnp.asarray(coef))
+    tables = (jnp.asarray(feature_tables(), bf16),)
 
     w_mix = jnp.transpose(frozen_mixer_weight, (1, 2, 0)).reshape(heads_here * HCOLS, width)
     w_gate = jnp.transpose(frozen_gate_up_weight, (1, 2, 0)).reshape(2 * ff_here, width)
@@ -1254,47 +1254,44 @@
     both_input = both_cores(own_input)
     first = norm_rows(both_input.astype(f32), gain_one)[0].astype(bf16)
     mixer_rank = nn(first, my_mixer_left).astype(bf16)
-    e_m, c_m, mixer_rank, packed, both_input = hold(e_m, c_m, mixer_rank, packed, both_input)
-
-    projs, tails, states = [], [], []
-    borrowed, prior, mixed, numer = [None, None], [None, None], [], []
+    upstream_other = swap_core(upstream_own)
+    upstream_own, upstream_other, e_m, c_m, mixer_rank, packed, both_input = hold(
+        upstream_own, upstream_other, e_m, c_m, mixer_rank, packed, both_input
+    )
+
+    projs, packs = [], []
+    borrowed, prior, mixed, numer, chunk_states = [None, None], [None, None], [], [], []
     slots = [packed[0], None, None, None]
 
     def attend_slot(slot):
         pair, n = slot // 2, slot % 2
         out = attend(spots, n, projs[slot], borrowed[pair], prior[pair], slots[slot], tables)
-        for kept, value in zip((mixed, numer), out):
+        for kept, value in zip((mixed, numer, chunk_states), out):
             kept.append(value)
 
     def project_slot(slot, refs):
         out = project(slot == 0, first, mixer_rank, slots[slot], tables, refs)
-        for kept, value in zip((projs, tails, states), out):
+        for kept, value in zip((projs, packs), out):
             kept.append(value)
-
-    def exchange(slot):
-        rows_here = jnp.concatenate(tails[slot : slot + 2], 0)
-        states_here = jnp.concatenate(states[slot : slot + 2], 0)
-        return lax.all_gather(pack_states(states_here, rows_here), "chip")
-
-    def use_exchange(slot, gathered):
-        prior[slot // 2], borrowed[slot // 2] = use_states((gathered,), False)
 
     x1, y1 = hop_xy(e_m)
     c2_m, f_m = cross(e_m), edge(c_m)
     table1 = swap_tp(packed[1], 1)
     project_slot(0, (w_mix,))
     slot2 = pick_inner(c2_m, f_m)
-    x1, y1, slot2, c2_m, c_m, tails[0], states[0], table1, feed_piece, packed = hold(
-        x1, y1, slot2, c2_m, c_m, tails[0], states[0], table1, feed_piece, packed
+    x1, y1, slot2, c2_m, c_m, packs[0], table1, feed_piece, packed = hold(
+        x1, y1, slot2, c2_m, c_m, packs[0], table1, feed_piece, packed
     )
     slots[1] = table1
     d1 = hop_diag(x1, y1, M_CUT)
     x2, y2 = hop_xy(slot2)
     f2_m = edge(c2_m)
     table2, table3 = swap_tp(packed[2], 2), swap_tp(packed[3], 3)
+    upstream = order_cores(upstream_own, upstream_other)
+    down_rgrad = nt(upstream, my_down_right).astype(bf16)
     slot3 = pick_inner(c_m, f2_m)
-    x2, y2, slot3, feed_piece, table2, table3, *d1 = hold(
-        x2, y2, slot3, feed_piece, table2, table3, *d1
+    x2, y2, slot3, feed_piece, table2, table3, upstream, down_rgrad, *d1 = hold(
+        x2, y2, slot3, feed_piece, table2, table3, upstream, down_rgrad, *d1
     )
     slots[2], slots[3] = table2, table3
     d2 = hop_diag(x2, y2, M_CUT)
@@ -1302,47 +1299,44 @@
     e_f = swap_tp(feed_piece, 1)
     set1 = (e_m, x1, y1, *d1)
     project_slot(1, set1)
-    x3, y3, e_f, tails[0], tails[1], states[0], states[1], upstream_own, *d2 = hold(
-        x3, y3, e_f, tails[0], tails[1], states[0], states[1], upstream_own, *d2
-    )
+    x3, y3, e_f, packs[0], packs[1], *d2 = hold(x3, y3, e_f, packs[0], packs[1], *d2)
     d3 = hop_diag(x3, y3, M_CUT)
     c_f = cross(feed_piece)
-    exchanged = exchange(0)
+    gathered = lax.all_gather(jnp.concatenate(packs[:2], 0), "chip")
     set2 = (slot2, x2, y2, *d2)
     project_slot(2, set2)
-    use_exchange(0, exchanged)
-    d3_a, d3_b, c_f, states[2], upstream_own, prior[0], borrowed[0] = hold(
-        *d3, c_f, states[2], upstream_own, prior[0], borrowed[0]
+    prior[0], borrowed[0] = use_states((gathered,), False)
+    d3_a, d3_b, c_f, packs[2], prior[0], borrowed[0] = hold(
+        *d3, c_f, packs[2], prior[0], borrowed[0]
     )
     fx1, fy1 = hop_xy(e_f)
     c2_f, f_f = cross(e_f), edge(c_f)
     set3 = (slot3, x3, y3, d3_a, d3_b)
     project_slot(3, set3)
     fslot2 = pick_inner(c2_f, f_f)
-    fx1, fy1, fslot2, c2_f, c_f, prior[0], tails[3], states[3] = hold(
-        fx1, fy1, fslot2, c2_f, c_f, prior[0], tails[3], states[3]
-    )
-    fd1 = hop_diag(fx1, fy1, feed_cut(quarter))
-    f2_f = edge(c2_f)
-    exchanged = exchange(2)
+    fx1, fy1, fslot2, c2_f, c_f, packs[2], packs[3] = hold(
+        fx1, fy1, fslot2, c2_f, c_f, packs[2], packs[3]
+    )
+    crossing = swap_states(jnp.concatenate(packs[2:], 0))
     attend_slot(0)
     attend_slot(1)
-    upstream = both_cores(upstream_own)
-    down_rgrad = nt(upstream, my_down_right).astype(bf16)
-    mixed[0], mixed[1], down_rgrad, upstream, fslot2, exchanged, *fd1 = hold(
-        mixed[0], mixed[1], down_rgrad, upstream, fslot2, exchanged, *fd1
-    )
+    fd1 = hop_diag(fx1, fy1, feed_cut(quarter))
+    mixed[0], mixed[1], fslot2, c2_f, fd1_a, fd1_b, *crossing = hold(
+        mixed[0], mixed[1], fslot2, c2_f, *fd1, *crossing
+    )
+    fd1 = (fd1_a, fd1_b)
     fx2, fy2 = hop_xy(fslot2)
-    use_exchange(2, exchanged)
+    f2_f = edge(c2_f)
+    prior[1], borrowed[1] = use_states(crossing, False)
     attend_slot(2)
     attend_slot(3)
     fslot3 = pick_inner(c_f, f2_f)
     sets = list(set1) + list(set2) + list(set3)
     out_part, out_rank, out_weight = mix_out(spots, mixed, slots, my_output_right, [w_out] + sets)
-    fx2, fy2, fslot3, out_part = hold(fx2, fy2, fslot3, out_part)
-
+    fx2, fy2, out_part, fslot3 = hold(fx2, fy2, out_part, fslot3)
     other_part = swap_core(out_part)
     middle, second, gate_rank = norm_two(out_part, other_part, both_input, gain_two, my_gateup_left)
+
     gateup_left_t = my_gateup_left.T
 
     def feed_slots(which, sources, carry):
@@ -1380,11 +1374,12 @@
         back_part, other_back, middle, upstream, gain_two, my_output_right
     )
 
-    output_rgrad, down_part, middle, ranks = hold(output_rgrad, down_part, middle, ranks)
+    output_rgrad, down_part, middle = hold(output_rgrad, down_part, middle)
     other_down = swap_core(own_rows(down_part, 1 - core))
     own_down = own_rows(down_part, core).astype(f32)
     own_output = own_rows(middle, core) + (own_down + other_down.astype(f32))
-    own_output = own_output.astype(bf16)
+    output_rgrad, own_output = hold(output_rgrad, own_output.astype(bf16))
+    block_output = lax.all_gather(own_output, "tp")
 
     def turn_pair(pair):
         both = slice(2 * pair, 2 * pair + 2)
@@ -1402,16 +1397,25 @@
             tables,
         )
 
-    up0, grad0, states0, lent0, left_grads0 = turn_pair(0)
-    states0, lent0, own_output = hold(states0, lent0, own_output)
-    packed0 = pack_states(states0, lent0)
-    block_output = lax.all_gather(own_output, "tp")
+    up0, grad0, packed0, left_grads0 = turn_pair(0)
+    up1, grad1, packed1, left_grads1 = turn_pair(1)
+    packed0, packed1, left_grads1, ranks, out_rank = hold(
+        packed0, packed1, left_grads1, ranks, out_rank
+    )
     crossing = swap_states(packed0)
-    up1, grad1, states1, lent1, left_grads1 = turn_pair(1)
     left_grads = [left_grads0[0], left_grads0[1], left_grads1[0], left_grads1[1]]
-    states1, lent1, ranks, out_rank, *crossing = hold(states1, lent1, ranks, out_rank, *crossing)
-    packed1 = pack_states(states1, lent1)
     down_rank, gateup_rgrad = ranks[:, :R].astype(bf16), ranks[:, R:].astype(bf16)
+    shared = jnp.stack(
+        [
+            tn(out_rank.astype(bf16), mixer_up),
+            tn(gateup_rgrad, second),
+            tn(down_rank, upstream),
+        ]
+    )
+    owned = jnp.stack(
+        [jnp.concatenate([left_grads[i], gate_grads[i], down_grads[i]], 1) for i in range(SLOTS)]
+    )
+    packed1, shared, owned, *crossing = hold(packed1, shared, owned, *crossing)
     backs = []
 
     def back_slots(pair, which, later, returned):
@@ -1423,7 +1427,7 @@
                     n,
                     projs[slot],
                     borrowed[pair],
-                    prior[pair],
+                    chunk_states[slot],
                     later,
                     returned,
                     (up0, up1)[pair],
@@ -1437,33 +1441,29 @@
     def join(array, other):
         return (array.astype(f32) + other.astype(f32)).astype(array.dtype)
 
+    def packs_of(owned, shared):
+        flat = jnp.concatenate(list(shared), 1).astype(bf16)
+        return [jnp.concatenate([owned[k], flat], 1) for k in range(SLOTS)]
+
     next_crossing = swap_states(packed1)
     back_slots(0, (0, 1), *use_states(crossing, True))
     early_rank = backs[0][1] + backs[1][1]
-    shared = jnp.stack(
-        [
-            tn(out_rank.astype(bf16), mixer_up),
-            tn(gateup_rgrad, second),
-            tn(down_rank, upstream),
-        ]
-    )
-    owned = jnp.stack(
-        [jnp.concatenate([left_grads[i], gate_grads[i], down_grads[i]], 1) for i in range(SLOTS)]
-    )
-    early_rank, shared, owned, *crossing = hold(early_rank, shared, owned, *next_crossing)
     shared_x, owned_x = swap_chip(shared, 1), swap_chip(owned, 1)
+    early_rank, shared_x, owned_x, *crossing = hold(
+        early_rank, shared_x, owned_x, *next_crossing
+    )
+    shared, owned = add_rest(join(shared, shared_x)), add_rest(join(owned, owned_x))
     later, returned = use_states(crossing, True)
     back_slots(1, (0,), later, returned)
     early_rank = early_rank + backs[2][1]
-    early_rank, later, shared_x, owned_x = hold(early_rank, later, shared_x, owned_x)
-    shared, owned = add_rest(join(shared, shared_x)), add_rest(join(owned, owned_x))
+    early_rank, later, shared, owned = hold(early_rank, later, shared, owned)
+    early = packs_of(owned, shared)
+    early = [early[0]] + [swap_tp(early[bit], bit) for bit in (1, 2, 3)]
     back_slots(1, (1,), later, returned)
     rank_grad = early_rank + backs[3][1]
-    rank_grad, shared, owned = hold(rank_grad, shared, owned)
-
-    def packs_of(owned, shared):
-        flat = jnp.concatenate(list(shared), 1).astype(bf16)
-        return [jnp.concatenate([owned[k], flat], 1) for k in range(SLOTS)]
+    rank_grad, *early = hold(rank_grad, *early)
+    early = jnp.stack(early)
+    early_other = swap_core(early)
 
     mixer_all = jnp.concatenate(
         [
@@ -1473,16 +1473,13 @@
         0,
     )
     mixer_x = swap_chip(mixer_all, 1)
-    early = packs_of(owned, shared)
-    early = [early[0]] + [swap_tp(early[bit], bit) for bit in (1, 2, 3)]
     proj_grads = [back[0] for back in backs]
     left_t = my_mixer_left.T
     flat_mix = [w_mix] + sets
     part_a = first_back(0, proj_grads, rank_grad, left_t, flat_mix)
-    part_a, rank_grad, mixer_x, *early = hold(
-        part_a, rank_grad, mixer_x, *early, after=(block_output,)
-    )
-    early = jnp.stack(early)
+    part_a, rank_grad, mixer_x, early, early_other = hold(
+        part_a, rank_grad, mixer_x, early, early_other, after=(block_output,)
+    )
     mixer_all = join(mixer_all, mixer_x)
     block = length // 2
 
@@ -1500,9 +1497,8 @@
     done_a = finish(part_a, 0)
     e_a, c_a = swap_tp(done_a, 1), cross(done_a)
     mixer_all = add_rest(mixer_all)
-    early_other = swap_core(early)
     part_b = first_back(1, proj_grads, rank_grad, left_t, flat_mix)
-    e_a, c_a, part_b, mixer_all, early_other = hold(e_a, c_a, part_b, mixer_all, early_other)
+    e_a, c_a, part_b, mixer_all = hold(e_a, c_a, part_b, mixer_all)
     c2_a, f_a = cross(e_a), edge(c_a)
     done_b = finish(part_b, 1)
     done_b, early, early_other, mixer_all = hold(done_b, early, early_other, mixer_all)

time: 910 us -> 894 us (0.982)
  Pallas kernels: 403 us -> 389 us
  waiting for transfers between devices: 167 us -> 157 us
    ppermute x8, waiting for transfers between devices: 79.2 us -> 65.3 us  [edge(): return lax.ppermute(array, 'tp', [(1, 0), (2, 3)])]
    pallas_call x4, Pallas kernels: 80.7 us -> 69.2 us  [attend_back(): pl.pallas_call(functools.partial(attend_back_kernel, spots), grid=(2,), o...]
    ppermute x36 -> x39, waiting for transfers between devices: 32.9 us -> 39 us  [swap_chip(): return lax.ppermute(array, 'chip', [(i, i ^ bit) for i in range(count)])]
    ppermute x36 -> x39, starting transfers between devices: 39.5 us -> 41.8 us  [swap_chip(): return lax.ppermute(array, 'chip', [(i, i ^ bit) for i in range(count)])]
    unnamed x391 -> x402, local copies, waits for them, and re-layouts: 67.7 us -> 68.1 us
  transfers between devices with their start and end apart: 77 -> 79, of which waited for: 21 -> 22; matrix products, arithmetic and copies ran while one was open for 14% -> 14% of each run, Pallas kernels for 41% -> 40%
where the time goes in v3:
time: 894 us; the launch traced here: 883 us
  Pallas kernels  389 us (44%)
  waiting for transfers between devices  157 us (18%)
  local copies, waits for them, and re-layouts  121 us (14%)
  starting transfers between devices  105 us (12%)
  other arithmetic  83 us (9%)
  between operations  17 us (2%)
  matrix products  12.5 us (1%)
    pallas_call x3, Pallas kernels, feed(): pl.pallas_call(functools.partial(feed_kernel, slots, last, half, pad, spo...  104 us
    pallas_call x4, Pallas kernels, project(): pl.pallas_call(functools.partial(project_kernel, own), out_shape=(jax.Sha...  71.3 us
    pallas_call x4, Pallas kernels, attend_back(): pl.pallas_call(functools.partial(attend_back_kernel, spots), grid=(2,), o...  69.2 us
    unnamed x402, local copies, waits for them, and re-layouts  68.1 us
    ppermute x8, waiting for transfers between devices, edge(): return lax.ppermute(array, 'tp', [(1, 0), (2, 3)])  65.3 us
    pallas_call x2, Pallas kernels, first_back(): pl.pallas_call(first_back_kernel, grid=(2,), out_shape=jax.ShapeDtypeStru...  50.3 us
    ppermute x39, starting transfers between devices, swap_chip(): return lax.ppermute(array, 'chip', [(i, i ^ bit) for i in range(count)])  41.8 us
    ppermute x13, starting transfers between devices, swap_tp(): return lax.ppermute(array, 'tp', [(i, i ^ bit) for i in range(4)])  41.2 us
  transfers between devices with their start and end apart: 79, of which 22 were waited for; matrix products, arithmetic and copies ran while one was open for 14% of the time, Pallas kernels for 40%

profile of v3, /device:TPU:0, one launch (start us, length us, event | category | flops | bytes accessed | tf_op | source)
XLA Modules:
  0.0 883.5 jit_solution(7440763134288336124)
XLA Ops:
  61.7 17.1 %project.4 = (bf16[1024,1792]{1,0:T(8,128)(2,1)S(1)}, bf16[2,320,128]{2,1,0:T(8,128)(2,1)S(1)}) custom-call(bf16[1024,1792]{1,0:T(8,128)(2,1)} %copy-done.115, bf16[1024,16]{1,0:T(8,128)(2,1)S(1)} %copy-done.18, bf16[16,4224]{1,0:T(8,128)(2,1)S(1)} %get-tuple-element.425.table.refs_4_.refs_6_.refs_3_, bf16[128,1280]{1,0:T(8,128)(2,1)S(1)} %copy-done.7, ...), custom_call_target="tpu_custom_call" | custom-call | flops 100000000 | bytes 300000 | tf_op jit(solution)/shard_map/project/pallas_call | solution.py:246
  116.7 14.5 %collective-permute-done.11 = bf16[816,896]{1,0:T(8,128)(2,1)} collective-permute-done((bf16[816,896]{1,0:T(8,128)(2,1)}, bf16[816,896]{1,0:T(8,128)(2,1)}, u32[]{:S(2)}, u32[]{:S(2)}) %collective-permute-start.11) | collective-permute-done | bytes 1462304 | tf_op jit(solution)/shard_map/ppermute | solution.py:1044
  152.3 18.1 %project.5 = (bf16[1024,1792]{1,0:T(8,128)(2,1)}, bf16[2,320,128]{2,1,0:T(8,128)(2,1)S(1)}) custom-call(bf16[1024,1792]{1,0:T(8,128)(2,1)} %copy-done.115, bf16[1024,16]{1,0:T(8,128)(2,1)S(1)} %copy-done.19, bf16[16,4224]{1,0:T(8,128)(2,1)S(1)} %copy-done.48, bf16[128,1280]{1,0:T(8,128)(2,1)S(1)} %copy-done.7, ...), custom_call_target="tpu_custom_call" | custom-call | flops 100000000 | bytes 300000 | tf_op jit(solution)/shard_map/project/pallas_call | solution.py:246
  171.1 18.4 %collective-permute-done.19.refs_5_ = bf16[368,896]{1,0:T(8,128)(2,1)S(1)} collective-permute-done((bf16[368,896]{1,0:T(8,128)(2,1)S(1)}, bf16[368,896]{1,0:T(8,128)(2,1)S(1)}, u32[]{:S(2)}, u32[]{:S(2)}) %collective-permute-start.19) | collective-permute-done | bytes 659488 | tf_op jit(solution)/shard_map/ppermute | solution.py:994
  210.9 18.2 %project.6 = (bf16[1024,1792]{1,0:T(8,128)(2,1)}, bf16[2,320,128]{2,1,0:T(8,128)(2,1)S(1)}) custom-call(bf16[1024,1792]{1,0:T(8,128)(2,1)} %copy-done.115, bf16[1024,16]{1,0:T(8,128)(2,1)S(1)} %copy-done.19, bf16[16,4224]{1,0:T(8,128)(2,1)S(1)} %copy-done.44, bf16[128,1280]{1,0:T(8,128)(2,1)S(1)} %copy-done.7, bf16[816,896]{1,0:T(8,128)(2,1)S(1)} %copy-done.10, ...), custom_call_target="tpu_custom_call" | custom-call | flops 100000000 | bytes 300000 | tf_op jit(solution)/shard_map/project/pallas_call | solution.py:246
  244.3 17.9 %project.7 = (bf16[1024,1792]{1,0:T(8,128)(2,1)}, bf16[2,320,128]{2,1,0:T(8,128)(2,1)S(1)}) custom-call(bf16[1024,1792]{1,0:T(8,128)(2,1)} %copy-done.115, bf16[1024,16]{1,0:T(8,128)(2,1)S(1)} %copy-done.19, bf16[16,4224]{1,0:T(8,128)(2,1)S(1)} %copy-done.53, bf16[128,1280]{1,0:T(8,128)(2,1)S(1)} %copy-done.7, bf16[816,896]{1,0:T(8,128)(2,1)S(1)} %copy-done.11, ...), custom_call_target="tpu_custom_call" | custom-call | flops 100000000 | bytes 300000 | tf_op jit(solution)/shard_map/project/pallas_call | solution.py:246
  262.2 15.5 %collective-permute-done.27 = bf16[912,896]{1,0:T(8,128)(2,1)S(1)} collective-permute-done((bf16[912,896]{1,0:T(8,128)(2,1)}, bf16[912,896]{1,0:T(8,128)(2,1)S(1)}, u32[]{:S(2)}, u32[]{:S(2)}) %collective-permute-start.27) | collective-permute-done | bytes 1634336 | tf_op jit(solution)/shard_map/ppermute | solution.py:1044
  342.8 10.2 %mix_out.1 = (bf16[1024,1792]{1,0:T(8,128)(2,1)}, f32[1024,16]{1,0:T(8,128)S(1)}, bf16[1024,1792]{1,0:T(8,128)(2,1)}) custom-call(bf16[1024,256]{1,0:T(8,128)(2,1)S(1)} %copy-done.66, bf16[1024,256]{1,0:T(8,128)(2,1)S(1)} %copy-done.69, bf16[1024,256]{1,0:T(8,128)(2,1)S(1)} %get-tuple-element.268.refs_2_.refs_7_, ...), custom_call_target="tpu_custom_call" | custom-call | flops 100000000 | bytes 300000 | tf_op jit(solution)/shard_map/mix_out/pallas_call | solution.py:414
  368.2 7.7 norm_two.1
  378.4 46.3 %feed.3 = (f32[1024,1792]{1,0:T(8,128)}, f32[1024,1792]{1,0:T(8,128)}, f32[1024,32]{1,0:T(8,128)}, bf16[16,1280]{1,0:T(8,128)(2,1)}, bf16[16,1280]{1,0:T(8,128)(...) custom-call(bf16[1024,1792]{1,0:T(8,128)(2,1)} %copy-done.8, ...), custom_call_target="tpu_custom_call" | custom-call | flops 100000000 | bytes 300000 | tf_op jit(solution)/shard_map/feed/pallas_call | solution.py:522
  430.5 28.3 %feed.4 = (f32[1024,1792]{1,0:T(8,128)}, f32[1024,1792]{1,0:T(8,128)}, f32[1024,32]{1,0:T(8,128)}, bf16[16,1280]{1,0:T(8,128)(2,1)}, bf16[16,640]{1,0:T(8,128)(2,1)}) custom-call(bf16[1024,1792]{1,0:T(8,128)(2,1)} %copy-done.8, bf16[1024,1792]{1,0:T(8,128)(2,1)} %get-tuple-element.277.refs_1_.upstream, bf16[1024,16]{1,0:T(8,128)(2,1)} %copy-done.83, ...), custom_call_target="tpu_custom_call" | custom-call | flops 100000000 | bytes 300000 | tf_op jit(solution)/shard_map/feed/pallas_call | solution.py:522
  460.1 29.6 %feed.5 = (bf16[1024,1792]{1,0:T(8,128)(2,1)}, bf16[1024,1792]{1,0:T(8,128)(2,1)}, f32[1024,32]{1,0:T(8,128)}, bf16[16,1280]{1,0:T(8,128)(2,1)}, bf16[16,640]{1,0:T(8,128)(2,1)}) custom-call(bf16[1024,1792]{1,0:T(8,128)(2,1)} %copy-done.8, bf16[1024,1792]{1,0:T(8,128)(2,1)} %get-tuple-element.277.refs_1_.upstream, bf16[1024,16]{1,0:T(8,128)(2,1)} %copy-done.83, ...), custom_call_target="tpu_custom_call" | custom-call | flops 100000000 | bytes 300000 | tf_op jit(solution)/shard_map/feed/pallas_call | solution.py:522
  523.4 12.5 %turn.2 = (bf16[1024,512]{1,0:T(8,128)(2,1)S(1)}, bf16[1024,512]{1,0:T(8,128)(2,1)S(1)}, bf16[4,320,128]{2,1,0:T(8,128)(2,1)S(1)}, bf16[2,16,256]{2,1,0:T(8,128)(2,1)S(1)}) custom-call(bf16[1024,1792]{1,0:T(8,128)(2,1)} %copy-done.16, bf16[1024,16]{1,0:T(8,128)(2,1)S(1)} %copy-done.72, bf16[1024,1792]{1,0:T(8,128)(2,1)} %get-tuple-element.309.refs_2_, ...), custom_call_target="tpu_custom_call" | custom-call | flops 100000000 | bytes 300000 | tf_op jit(solution)/shard_map/turn/pallas_call | solution.py:631
  537.8 12.7 %turn.3 = (bf16[1024,512]{1,0:T(8,128)(2,1)S(1)}, bf16[1024,512]{1,0:T(8,128)(2,1)S(1)}, bf16[4,320,128]{2,1,0:T(8,128)(2,1)S(1)}, bf16[2,16,256]{2,1,0:T(8,128)(2,1)S(1)}) custom-call(bf16[1024,1792]{1,0:T(8,128)(2,1)} %copy-done.16, bf16[1024,16]{1,0:T(8,128)(2,1)S(1)} %copy-done.72, bf16[1024,1792]{1,0:T(8,128)(2,1)} %get-tuple-element.309.refs_2_, ...), custom_call_target="tpu_custom_call" | custom-call | flops 100000000 | bytes 300000 | tf_op jit(solution)/shard_map/turn/pallas_call | solution.py:631
  580.6 17.1 %attend_back.4 = (bf16[1024,1792]{1,0:T(8,128)(2,1)}, f32[1024,16]{1,0:T(8,128)S(1)}, bf16[16,1792]{1,0:T(8,128)(2,1)S(1)}) custom-call(bf16[1024,1792]{1,0:T(8,128)(2,1)} %copy-done.2, bf16[4,160,128]{2,1,0:T(8,128)(2,1)S(1)} %copy-done.42, bf16[2,4,256,128]{3,2,1,0:T(8,128)(2,1)S(1)} %copy-done.108, f32[4,160,128]{2,1,0:T(8,128)S(1)} %select_add_fusion.1.later, ...), custom_call_target="tpu_custom_call" | custom-call | flops 100000000 | bytes 300000 | tf_op jit(solution)/shard_map/attend_back/pallas_call | solution.py:769
  597.7 17.3 %attend_back.5 = (bf16[1024,1792]{1,0:T(8,128)(2,1)}, f32[1024,16]{1,0:T(8,128)S(1)}, bf16[16,1792]{1,0:T(8,128)(2,1)S(1)}) custom-call(bf16[1024,1792]{1,0:T(8,128)(2,1)} %get-tuple-element.246.proj.refs_11_.refs_12_.refs_14_, bf16[4,160,128]{2,1,0:T(8,128)(2,1)S(1)} %copy-done.42, bf16[2,4,256,128]{3,2,1,0:T(8,128)(2,1)S(1)} %copy-done.106, ...), custom_call_target="tpu_custom_call" | custom-call | flops 100000000 | bytes 300000 | tf_op jit(solution)/shard_map/attend_back/pallas_call | solution.py:769
  625.6 17.5 %attend_back.6 = (bf16[1024,1792]{1,0:T(8,128)(2,1)}, f32[1024,16]{1,0:T(8,128)S(1)}, bf16[16,1792]{1,0:T(8,128)(2,1)S(1)}) custom-call(bf16[1024,1792]{1,0:T(8,128)(2,1)} %get-tuple-element.264.proj.refs_9_.refs_10_.refs_13_, bf16[4,160,128]{2,1,0:T(8,128)(2,1)S(1)} %copy-done.61, bf16[2,4,256,128]{3,2,1,0:T(8,128)(2,1)S(1)} %copy-done.110, ...), custom_call_target="tpu_custom_call" | custom-call | flops 100000000 | bytes 300000 | tf_op jit(solution)/shard_map/attend_back/pallas_call | solution.py:769
  656.1 17.3 %attend_back.7 = (bf16[1024,1792]{1,0:T(8,128)(2,1)}, f32[1024,16]{1,0:T(8,128)S(1)}, bf16[16,1792]{1,0:T(8,128)(2,1)S(1)}) custom-call(bf16[1024,1792]{1,0:T(8,128)(2,1)} %get-tuple-element.269.proj.refs_11_.refs_12_.refs_14_, bf16[4,160,128]{2,1,0:T(8,128)(2,1)S(1)} %copy-done.61, bf16[2,4,256,128]{3,2,1,0:T(8,128)(2,1)S(1)} %copy-done.104, ...), custom_call_target="tpu_custom_call" | custom-call | flops 100000000 | bytes 300000 | tf_op jit(solution)/shard_map/attend_back/pallas_call | solution.py:769
  682.1 25.1 %first_back.2.refs_0_ = bf16[512,1792]{1,0:T(8,128)(2,1)} custom-call(bf16[1024,1792]{1,0:T(8,128)(2,1)} %get-tuple-element.338.refs_0_, bf16[1024,1792]{1,0:T(8,128)(2,1)} %get-tuple-element.340.refs_1_, bf16[1024,1792]{1,0:T(8,128)(2,1)} %get-tuple-element.352.refs_2_, bf16[1024,1792]{1,0:T(8,128)(2,1)} %get-tuple-element.359.refs_3_, ...), custom_call_target="tpu_custom_call" | custom-call | flops 100000000 | bytes 300000 | tf_op jit(solution)/shard_map/first_back/pallas_call | solution.py:844
  721.8 25.2 %first_back.3.refs_2_ = bf16[512,1792]{1,0:T(8,128)(2,1)} custom-call(bf16[1024,1792]{1,0:T(8,128)(2,1)} %get-tuple-element.338.refs_0_, bf16[1024,1792]{1,0:T(8,128)(2,1)} %get-tuple-element.340.refs_1_, bf16[1024,1792]{1,0:T(8,128)(2,1)} %get-tuple-element.352.refs_2_, bf16[1024,1792]{1,0:T(8,128)(2,1)} %get-tuple-element.359.refs_3_, ...), custom_call_target="tpu_custom_call" | custom-call | flops 100000000 | bytes 300000 | tf_op jit(solution)/shard_map/first_back/pallas_call | solution.py:844
  780.0 21.6 %collective-permute-done.69.refs_4_ = bf16[16,3584]{1,0:T(8,128)(2,1)S(1)} collective-permute-done((bf16[16,3584]{1,0:T(8,128)(2,1)S(1)}, bf16[16,3584]{1,0:T(8,128)(2,1)S(1)}, u32[]{:S(2)}, u32[]{:S(2)}) %collective-permute-start.69) | collective-permute-done | bytes 114720 | tf_op jit(solution)/shard_map/ppermute | solution.py:998
  824.1 14.1 %collective-permute-done.73.refs_3_ = bf16[16,3584]{1,0:T(8,128)(2,1)S(1)} collective-permute-done((bf16[16,3584]{1,0:T(8,128)(2,1)}, bf16[16,3584]{1,0:T(8,128)(2,1)S(1)}, u32[]{:S(2)}, u32[]{:S(2)}) %collective-permute-start.73) | collective-permute-done | bytes 114720 | tf_op jit(solution)/shard_map/ppermute | solution.py:998
  838.3 12.7 %collective-permute-done.72.refs_2_ = bf16[256,1792]{1,0:T(8,128)(2,1)S(1)} collective-permute-done((bf16[256,1792]{1,0:T(8,128)(2,1)}, bf16[256,1792]{1,0:T(8,128)(2,1)S(1)}, u32[]{:S(2)}, u32[]{:S(2)}) %collective-permute-start.72) | collective-permute-done | bytes 917536 | tf_op jit(solution)/shard_map/ppermute | solution.py:1044
  862.3 12.7 %collective-permute-done.75 = bf16[256,1792]{1,0:T(8,128)(2,1)S(1)} collective-permute-done((bf16[256,1792]{1,0:T(8,128)(2,1)}, bf16[256,1792]{1,0:T(8,128)(2,1)S(1)}, u32[]{:S(2)}, u32[]{:S(2)}) %collective-permute-start.75) | collective-permute-done | bytes 917536 | tf_op jit(solution)/shard_map/ppermute | solution.py:1044
  (726 shorter events, 418.8 us)
Async XLA Ops:
  7.2 224.6 %all-gather.5.cloned.1.call-start = ((), (), s32[]{:S(2)}) async-start(), calls=%async_computation | async-start | bytes 1638400 | tf_op jit(solution)/shard_map/all_gather | solution.py:1305
  47.4 45.3 %collective-permute-start.4 = (bf16[816,896]{1,0:T(8,128)(2,1)}, bf16[816,896]{1,0:T(8,128)(2,1)S(1)}, u32[]{:S(2)}, u32[]{:S(2)}) collective-permute-start(bf16[816,896]{1,0:T(8,128)(2,1)} %get-tuple-element.214.rest_0_.refs_10_.refs_7_), channel_id=1, source_target_pairs={{0,8},{8,0},{16,24},{24,16},{1,9},{9,1},{17,25},{25,17},{2,10},{10... | collective-permute-start | bytes 4386824 | tf_op jit(solution)/shard_map/ppermute | solution.py:994
  48.9 43.8 %collective-permute-start.5 = (bf16[816,896]{1,0:T(8,128)(2,1)}, bf16[816,896]{1,0:T(8,128)(2,1)}, u32[]{:S(2)}, u32[]{:S(2)}) collective-permute-start(bf16[816,896]{1,0:T(8,128)(2,1)} %get-tuple-element.214.rest_0_.refs_10_.refs_7_), channel_id=1, source_target_pairs={{0,16},{8,24},{16,0},{24,8},{1,17},{9,25},{17,1},{25,9},{2,18},{10... | collective-permute-start | bytes 4386824 | tf_op jit(solution)/shard_map/ppermute | solution.py:994
  51.2 40.1 %collective-permute-start.7 = (bf16[816,896]{1,0:T(8,128)(2,1)}, bf16[816,896]{1,0:T(8,128)(2,1)S(1)}, u32[]{:S(2)}, u32[]{:S(2)}) collective-permute-start(bf16[816,896]{1,0:T(8,128)(2,1)} %get-tuple-element.215.refs_4_), channel_id=1, source_target_pairs={{1,0},{2,3},{5,4},{6,7},{9,8},{10,11},{13,12},{14,15},{17,16},{18,... | collective-permute-start | bytes 4386824 | tf_op jit(solution)/shard_map/ppermute | solution.py:1044
  93.9 49.3 %collective-permute-start.9 = (bf16[816,896]{1,0:T(8,128)(2,1)}, bf16[816,896]{1,0:T(8,128)(2,1)}, u32[]{:S(2)}, u32[]{:S(2)}) collective-permute-start(bf16[816,896]{1,0:T(8,128)(2,1)} %get-tuple-element.217.rest_0_.refs_15_.refs_12_), channel_id=1, source_target_pairs={{0,8},{8,0},{16,24},{24,16},{1,9},{9,1},{17,25},{25,17},{2,10},{10... | collective-permute-start | bytes 4386824 | tf_op jit(solution)/shard_map/ppermute | solution.py:994
  94.4 48.8 %collective-permute-start.10 = (bf16[816,896]{1,0:T(8,128)(2,1)}, bf16[816,896]{1,0:T(8,128)(2,1)S(1)}, u32[]{:S(2)}, u32[]{:S(2)}) collective-permute-start(bf16[816,896]{1,0:T(8,128)(2,1)} %get-tuple-element.217.rest_0_.refs_15_.refs_12_), channel_id=1, source_target_pairs={{0,16},{8,24},{16,0},{24,8},{1,17},{9,25},{17,1},{25,9},{2,18},{10... | collective-permute-start | bytes 4386824 | tf_op jit(solution)/shard_map/ppermute | solution.py:994
  144.6 50.1 %collective-permute-start.18 = (bf16[912,896]{1,0:T(8,128)(2,1)}, bf16[912,896]{1,0:T(8,128)(2,1)S(1)}, u32[]{:S(2)}, u32[]{:S(2)}) collective-permute-start(bf16[912,896]{1,0:T(8,128)(2,1)} %get-tuple-element.227), channel_id=1, source_target_pairs={{0,1},{1,0},{2,3},{3,2},{4,5},{5,4},{6,7},{7,6},{8,9},{9,8},{10,11... | collective-permute-start | bytes 4902920 | tf_op jit(solution)/shard_map/ppermute | solution.py:998
  144.6 49.1 %collective-permute-start.16 = (bf16[816,896]{1,0:T(8,128)(2,1)}, bf16[816,896]{1,0:T(8,128)(2,1)S(1)}, u32[]{:S(2)}, u32[]{:S(2)}) collective-permute-start(bf16[816,896]{1,0:T(8,128)(2,1)} %get-tuple-element.226.rest_0_.refs_20_.refs_17_), channel_id=1, source_target_pairs={{0,8},{8,0},{16,24},{24,16},{1,9},{9,1},{17,25},{25,17},{2,10},{10... | collective-permute-start | bytes 4386824 | tf_op jit(solution)/shard_map/ppermute | solution.py:994
  146.2 48.4 %collective-permute-start.17 = (bf16[816,896]{1,0:T(8,128)(2,1)}, bf16[816,896]{1,0:T(8,128)(2,1)S(1)}, u32[]{:S(2)}, u32[]{:S(2)}) collective-permute-start(bf16[816,896]{1,0:T(8,128)(2,1)} %get-tuple-element.226.rest_0_.refs_20_.refs_17_), channel_id=1, source_target_pairs={{0,16},{8,24},{16,0},{24,8},{1,17},{9,25},{17,1},{25,9},{2,18},{10... | collective-permute-start | bytes 4386824 | tf_op jit(solution)/shard_map/ppermute | solution.py:994
  147.9 45.8 %collective-permute-start.20 = (bf16[448,896]{1,0:T(8,128)(2,1)S(1)}, bf16[448,896]{1,0:T(8,128)(2,1)S(1)}, u32[]{:S(2)}, u32[]{:S(2)}) collective-permute-start(bf16[448,896]{1,0:T(8,128)(2,1)S(1)} %slice.170), channel_id=1, source_target_pairs={{0,16},{8,24},{16,0},{24,8},{1,17},{9,25},{17,1},{25,9},{2,18},{10... | collective-permute-start | bytes 2408456 | tf_op jit(solution)/shard_map/ppermute | solution.py:994
  198.8 508.5 %all-gather.7.cloned.1.call-start = ((), (), s32[]{:S(2)}) async-start(), calls=%async_computation.1 | async-start | bytes 9175040 | tf_op jit(solution)/shard_map/all_gather | solution.py:1382
  205.9 56.4 %collective-permute-start.26 = (bf16[912,896]{1,0:T(8,128)(2,1)}, bf16[912,896]{1,0:T(8,128)(2,1)}, u32[]{:S(2)}, u32[]{:S(2)}) collective-permute-start(bf16[912,896]{1,0:T(8,128)(2,1)} %get-tuple-element.248.refs_10_), channel_id=1, source_target_pairs={{1,2},{2,1},{5,6},{6,5},{9,10},{10,9},{13,14},{14,13},{17,18},{18,... | collective-permute-start | bytes 4902920 | tf_op jit(solution)/shard_map/ppermute | solution.py:1040
  237.4 40.4 %collective-permute-start.27 = (bf16[912,896]{1,0:T(8,128)(2,1)}, bf16[912,896]{1,0:T(8,128)(2,1)S(1)}, u32[]{:S(2)}, u32[]{:S(2)}) collective-permute-start(bf16[912,896]{1,0:T(8,128)(2,1)} %get-tuple-element.249.refs_4_), channel_id=1, source_target_pairs={{1,0},{2,3},{5,4},{6,7},{9,8},{10,11},{13,12},{14,15},{17,16},{18,... | collective-permute-start | bytes 4902920 | tf_op jit(solution)/shard_map/ppermute | solution.py:1044
  356.1 68.6 %collective-permute-start.37 = (bf16[912,896]{1,0:T(8,128)(2,1)}, bf16[912,896]{1,0:T(8,128)(2,1)}, u32[]{:S(2)}, u32[]{:S(2)}) collective-permute-start(bf16[912,896]{1,0:T(8,128)(2,1)} %get-tuple-element.280.refs_7_), channel_id=1, source_target_pairs={{0,8},{8,0},{16,24},{24,16},{1,9},{9,1},{17,25},{25,17},{2,10},{10... | collective-permute-start | bytes 4902920 | tf_op jit(solution)/shard_map/ppermute | solution.py:994
  357.1 67.7 %collective-permute-start.38 = (bf16[912,896]{1,0:T(8,128)(2,1)}, bf16[912,896]{1,0:T(8,128)(2,1)S(1)}, u32[]{:S(2)}, u32[]{:S(2)}) collective-permute-start(bf16[912,896]{1,0:T(8,128)(2,1)} %get-tuple-element.280.refs_7_), channel_id=1, source_target_pairs={{0,16},{8,24},{16,0},{24,8},{1,17},{9,25},{17,1},{25,9},{2,18},{10... | collective-permute-start | bytes 4902920 | tf_op jit(solution)/shard_map/ppermute | solution.py:994
  360.3 64.4 %collective-permute-start.39 = (bf16[464,896]{1,0:T(8,128)(2,1)}, bf16[464,896]{1,0:T(8,128)(2,1)}, u32[]{:S(2)}, u32[]{:S(2)}) collective-permute-start(bf16[464,896]{1,0:T(8,128)(2,1)} %slice.181), channel_id=1, source_target_pairs={{0,8},{8,0},{16,24},{24,16},{1,9},{9,1},{17,25},{25,17},{2,10},{10... | collective-permute-start | bytes 2494472 | tf_op jit(solution)/shard_map/ppermute | solution.py:994
  363.3 61.4 %collective-permute-start.40 = (bf16[448,896]{1,0:T(8,128)(2,1)}, bf16[448,896]{1,0:T(8,128)(2,1)}, u32[]{:S(2)}, u32[]{:S(2)}) collective-permute-start(bf16[448,896]{1,0:T(8,128)(2,1)} %slice.182), channel_id=1, source_target_pairs={{0,16},{8,24},{16,0},{24,8},{1,17},{9,25},{17,1},{25,9},{2,18},{10... | collective-permute-start | bytes 2408456 | tf_op jit(solution)/shard_map/ppermute | solution.py:994
  570.6 45.3 %collective-permute-start.50 = (bf16[4,320,128]{2,1,0:T(8,128)(2,1)}, bf16[4,320,128]{2,1,0:T(8,128)(2,1)S(1)}, u32[]{:S(2)}, u32[]{:S(2)}) collective-permute-start(bf16[4,320,128]{2,1,0:T(8,128)(2,1)} %get-tuple-element.346), channel_id=1, source_target_pairs={{0,8},{8,0},{16,24},{24,16},{1,9},{9,1},{17,25},{25,17},{2,10},{10... | collective-permute-start | bytes 983048 | tf_op jit(solution)/shard_map/ppermute | solution.py:994
  571.7 44.2 %collective-permute-start.51 = (bf16[4,320,128]{2,1,0:T(8,128)(2,1)}, bf16[4,320,128]{2,1,0:T(8,128)(2,1)S(1)}, u32[]{:S(2)}, u32[]{:S(2)}) collective-permute-start(bf16[4,320,128]{2,1,0:T(8,128)(2,1)} %get-tuple-element.346), channel_id=1, source_target_pairs={{0,16},{8,24},{16,0},{24,8},{1,17},{9,25},{17,1},{25,9},{2,18},{10... | collective-permute-start | bytes 983048 | tf_op jit(solution)/shard_map/ppermute | solution.py:994
  572.6 44.0 %collective-permute-start.52 = (bf16[4,320,128]{2,1,0:T(8,128)(2,1)}, bf16[4,320,128]{2,1,0:T(8,128)(2,1)S(1)}, u32[]{:S(2)}, u32[]{:S(2)}) collective-permute-start(bf16[4,320,128]{2,1,0:T(8,128)(2,1)} %get-tuple-element.346), channel_id=1, source_target_pairs={{0,24},{8,16},{16,8},{24,0},{1,25},{9,17},{17,9},{25,1},{2,26},{10... | collective-permute-start | bytes 983048 | tf_op jit(solution)/shard_map/ppermute | solution.py:994
  574.1 44.0 %collective-permute-start.48 = (f32[3,16,1792]{2,1,0:T(8,128)}, f32[3,16,1792]{2,1,0:T(8,128)S(1)}, u32[]{:S(2)}, u32[]{:S(2)}) collective-permute-start(f32[3,16,1792]{2,1,0:T(8,128)} %get-tuple-element.344), channel_id=1, source_target_pairs={{0,8},{8,0},{16,24},{24,16},{1,9},{9,1},{17,25},{25,17},{2,10},{10... | collective-permute-start | bytes 1032200 | tf_op jit(solution)/shard_map/ppermute | solution.py:994
  575.2 40.7 %collective-permute-start.49 = (bf16[4,16,2176]{2,1,0:T(8,128)(2,1)}, bf16[4,16,2176]{2,1,0:T(8,128)(2,1)S(1)}, u32[]{:S(2)}, u32[]{:S(2)}) collective-permute-start(bf16[4,16,2176]{2,1,0:T(8,128)(2,1)} %get-tuple-element.345), channel_id=1, source_target_pairs={{0,8},{8,0},{16,24},{24,16},{1,9},{9,1},{17,25},{25,17},{2,10},{10... | collective-permute-start | bytes 835592 | tf_op jit(solution)/shard_map/ppermute | solution.py:994
  760.4 41.2 %collective-permute-start.67 = (bf16[256,1792]{1,0:T(8,128)(2,1)}, bf16[256,1792]{1,0:T(8,128)(2,1)}, u32[]{:S(2)}, u32[]{:S(2)}) collective-permute-start(bf16[256,1792]{1,0:T(8,128)(2,1)} %get-tuple-element.383.refs_8_), channel_id=1, source_target_pairs={{0,1},{1,0},{2,3},{3,2},{4,5},{5,4},{6,7},{7,6},{8,9},{9,8},{10,11... | collective-permute-start | bytes 2752520 | tf_op jit(solution)/shard_map/ppermute | solution.py:998
  804.3 46.6 %collective-permute-start.72 = (bf16[256,1792]{1,0:T(8,128)(2,1)}, bf16[256,1792]{1,0:T(8,128)(2,1)S(1)}, u32[]{:S(2)}, u32[]{:S(2)}) collective-permute-start(bf16[256,1792]{1,0:T(8,128)(2,1)} %get-tuple-element.396), channel_id=1, source_target_pairs={{1,0},{2,3},{5,4},{6,7},{9,8},{10,11},{13,12},{14,15},{17,16},{18,... | collective-permute-start | bytes 2752520 | tf_op jit(solution)/shard_map/ppermute | solution.py:1044
  (252 other events, 2649.3 us)
Sparse Core Ops, SparseCore 0:
  199.0 32.7 all-gather.4
  520.0 135.9 all-gather.6

commit v4 on v3

--- a/solution.py
+++ b/solution.py
@@ -23,6 +23,7 @@
 CHUNK = 256
 QB = 128
 BACK_QB = 256
+BACK_CHUNK = 512
 PACK = STATE + 2 * WIN + 32
 
 epsilon = 1e-05
@@ -276,9 +277,9 @@
     return expo * (1.0 / jnp.sum(expo, -1, keepdims=True))
 
 
-def causal_mask():
-    row = lax.broadcasted_iota(jnp.int32, (CHUNK, CHUNK), 0)
-    col = lax.broadcasted_iota(jnp.int32, (CHUNK, CHUNK), 1)
+def causal_mask(size):
+    row = lax.broadcasted_iota(jnp.int32, (size, size), 0)
+    col = lax.broadcasted_iota(jnp.int32, (size, size), 1)
     return col <= row
 
 
@@ -299,7 +300,7 @@
     conv[16:, :] = proj[:, 5 * PD : 6 * PD].astype(f32)
     tap = head_taps(spots, table)
     state = whole_state(prior[0])
-    causal = causal_mask()
+    causal = causal_mask(CHUNK)
     first_mask, mask = window_masks(QB)
     for chunk in range(rows // CHUNK):
         states[0, chunk] = state.astype(bf16)
@@ -553,23 +554,25 @@
 
 def turn_kernel(spots, *refs):
     mixer_up, orgrad, weight = refs[:3]
-    tables, numers, mixeds = refs[3:5], refs[5:7], refs[7:9]
-    bases, heads, tails = refs[9:13], refs[13:15], refs[15]
-    pick = refs[16]
-    up_out, grad_out, packed, left_out, total_state, left0, left1 = refs[17:]
+    tables, numers, mixeds, bases, heads, tails = (
+        refs[3:7], refs[7:11], refs[11:15], refs[15:23], refs[23:27], refs[27:29]
+    )
+    pick = refs[29]
+    up_out, grad_out, packs, left_out, total_state, left_sums = (
+        refs[30], refs[31], refs[32:34], refs[34], refs[35], refs[36]
+    )
     step = pl.program_id(0)
 
     @pl.when(step == 0)
     def _():
         total_state[...] = jnp.zeros(total_state.shape, f32)
-        left0[...] = jnp.zeros(left0.shape, f32)
-        left1[...] = jnp.zeros(left1.shape, f32)
+        left_sums[...] = jnp.zeros(left_sums.shape, f32)
 
     both = nt(mixer_up[...], weight[...])
-    for n, left_grad in enumerate((left0, left1)):
+    for n in range(SLOTS):
         table = tables[n]
         flow = both[:, 2 * PD * n : 2 * PD * (n + 1)] + nn(orgrad[...], table[:, spots.left])
-        left_grad[...] += tn(orgrad[...], mixeds[n][...])
+        left_sums[n] += tn(orgrad[...], mixeds[n][...])
         for head in range(2):
             cols = slice(PD * head, PD * (head + 1))
             wide = slice(PD * (2 * n + head), PD * (2 * n + head + 1))
@@ -585,17 +588,17 @@
 
     @pl.when(step == pl.num_programs(0) - 1)
     def _():
-        packed[:, 0:STATE, :] = total_state[:, :STATE, :].astype(bf16)
-        left_out[0] = left0[...].astype(bf16)
-        left_out[1] = left1[...].astype(bf16)
+        for pair in range(2):
+            packs[pair][:, 0:STATE, :] = total_state[4 * pair : 4 * pair + 4, :STATE, :].astype(bf16)
+        left_out[...] = left_sums[...].astype(bf16)
 
     @pl.when(step == 0)
     def _():
-        for n in range(2):
+        for n in range(SLOTS):
             for head in range(2):
-                give_back(
-                    spots, tables[n], heads[n], tails.at[2 * n + head], up_out, packed.at[2 * n + head], n, head
-                )
+                at = n % 2 * 2 + head
+                rows = tails[n // 2].at[at]
+                give_back(spots, tables[n], heads[n], rows, up_out, packs[n // 2].at[at], n, head)
 
 
 def give_back(spots, table, rows, tails, up_out, lent, n, head):
@@ -623,38 +626,37 @@
     lent[PACK - 16 : PACK, :] = jnp.zeros((16, PD), bf16)
 
 
-def turn(pair, spots, mixer_up, orgrad, weight, slot_tables, numer, mixed, projs, tails, tables):
+def turn(spots, mixer_up, orgrad, weight, slot_tables, numer, mixed, projs, tails, tables):
     rows, width = mixer_up.shape
     whole = lambda a: pl.BlockSpec(a.shape, lambda i: (0,) * a.ndim)
     flat = lambda *shape: pl.BlockSpec(shape, lambda i: (0,) * len(shape))
     tall = lambda cols, at: pl.BlockSpec((CHUNK, cols), lambda i: (i, at))
+    heads = 2 * SLOTS
     return pl.pallas_call(
         functools.partial(turn_kernel, spots),
         grid=(rows // CHUNK,),
         out_shape=(
-            jax.ShapeDtypeStruct((rows, 4 * PD), bf16),
-            jax.ShapeDtypeStruct((rows, 4 * PD), bf16),
+            jax.ShapeDtypeStruct((rows, heads * PD), bf16),
+            jax.ShapeDtypeStruct((rows, heads * PD), bf16),
             jax.ShapeDtypeStruct((4, PACK, PD), bf16),
-            jax.ShapeDtypeStruct((2, R, 2 * PD), bf16),
-        ),
-        in_specs=[
-            tall(width, 0),
-            tall(R, 0),
-            pl.BlockSpec((4 * PD, width), lambda i: (pair, 0)),
-        ]
+            jax.ShapeDtypeStruct((4, PACK, PD), bf16),
+            jax.ShapeDtypeStruct((SLOTS, R, 2 * PD), bf16),
+        ),
+        in_specs=[tall(width, 0), tall(R, 0), whole(weight)]
         + [whole(t) for t in slot_tables]
-        + [tall(2 * PD, 0)] * 4
-        + [tall(PD, 0), tall(PD, 7)] * 2
-        + [pl.BlockSpec((QB, 2 * HEAD_PAD), lambda i: (0, 0))] * 2
-        + [whole(tails)]
+        + [tall(2 * PD, 0)] * 8
+        + [tall(PD, 0), tall(PD, 7)] * SLOTS
+        + [flat(QB, 2 * HEAD_PAD)] * SLOTS
+        + [whole(t) for t in tails]
         + [whole(t) for t in tables],
         out_specs=(
-            tall(4 * PD, 0),
-            tall(4 * PD, 0),
+            tall(heads * PD, 0),
+            tall(heads * PD, 0),
             flat(4, PACK, PD),
-            flat(2, R, 2 * PD),
-        ),
-        scratch_shapes=[pltpu.VMEM((4, 256, PD), f32)] + [pltpu.VMEM((R, 2 * PD), f32)] * 2,
+            flat(4, PACK, PD),
+            flat(SLOTS, R, 2 * PD),
+        ),
+        scratch_shapes=[pltpu.VMEM((heads, 256, PD), f32), pltpu.VMEM((SLOTS, R, 2 * PD), f32)],
         compiler_params=params(48),
         cost_estimate=pl.CostEstimate(
             flops=100_000_000, bytes_accessed=300_000, transcendentals=0
@@ -662,7 +664,7 @@
         name="turn",
     )(
         mixer_up, orgrad, weight, *slot_tables, *numer, *mixed,
-        projs[0], projs[0], projs[1], projs[1], *projs, tails, *tables,
+        *[proj for proj in projs for _ in range(2)], *projs, *tails, *tables,
     )
 
 
@@ -692,7 +694,7 @@
     out, rank_grad, right_grad, keys, vals, conv, flow
 ):
     rows = proj.shape[0]
-    chunks = rows // CHUNK
+    chunks = rows // BACK_CHUNK
     keys[0:WIN, :] = tails[0, 0:WIN]
     vals[0:WIN, :] = tails[0, WIN : 2 * WIN]
     conv[0:16, :] = tails[0, 2 * WIN : 2 * WIN + 16].astype(f32)
@@ -703,12 +705,12 @@
     right = table.at[:, pl.ds(pl.multiple_of(HEAD_PAD * pl.program_id(0), PD), HEAD_PAD)]
     flow[rows:, :] = jnp.zeros((16, PD), f32)
     follow = whole_state(later[0])
-    causal = causal_mask()
+    causal = causal_mask(BACK_CHUNK)
     first_mask, mask = window_masks(BACK_QB)
     held = (lent[0, 0:WIN].astype(f32), lent[0, WIN : 2 * WIN].astype(f32))
     for chunk in range(chunks - 1, -1, -1):
-        at = chunk * CHUNK
-        span = slice(at, at + CHUNK)
+        at = chunk * BACK_CHUNK
+        span = slice(at, at + BACK_CHUNK)
         base = proj[span, 0:PD]
         value = proj[span, PD : 2 * PD]
         grad = grads[span, :]
@@ -721,7 +723,7 @@
         weight = jnp.where(causal, 1.0 + score + 0.5 * score * score, 0.0).astype(bf16)
         slope = jnp.where(causal, nt(grad, value) * (1.0 + score), 0.0).astype(bf16)
         follow_round = follow.astype(bf16)
-        q_up = nt(grad, states[0, chunk])
+        q_up = nt(grad, states[0, chunk * (BACK_CHUNK // CHUNK)])
         k_up = nt(value, follow_round)
         inside = [q_up * q_two, q_up * q_one, k_up * k_two, k_up * k_one]
         inside = jnp.concatenate([part.astype(bf16) for part in inside], 1)
@@ -735,12 +737,12 @@
         sig = jax.nn.sigmoid(gate)
         act = gate * sig
         flow[span, :] = up * act
-        for number in range((at + CHUNK) // BACK_QB - 1, at // BACK_QB - 1, -1):
+        for number in range((at + BACK_CHUNK) // BACK_QB - 1, at // BACK_QB - 1, -1):
             held = window_back(
                 proj, keys, vals, ups, out, number, mask if number else first_mask, held
             )
         slope_gate = sig + act * (1.0 - sig)
-        out[span, 6 * PD : 7 * PD] = (up * conv_of(conv, tap, at, CHUNK) * slope_gate).astype(bf16)
+        out[span, 6 * PD : 7 * PD] = (up * conv_of(conv, tap, at, BACK_CHUNK) * slope_gate).astype(bf16)
     grad_in = tap[0:1] * flow[0:rows, :]
     for offset in range(1, KW):
         grad_in = grad_in + tap[offset : offset + 1] * flow[offset : offset + rows, :]
@@ -759,13 +761,14 @@
         rank_grad[...] += nt(out[...], right[...])
 
 
-def attend_back(spots, number, proj, tails, states, later, lent, ups, grads, table, rank, tables):
+def attend_back(spots, slot, proj, tails, states, later, lent, ups, grads, table, rank, tables):
     rows = proj.shape[0]
+    number = slot % 2
     whole = lambda a: pl.BlockSpec(a.shape, lambda h: (0,) * a.ndim)
     head = pl.BlockSpec((rows, HEAD_PAD), lambda h: (0, h))
     edge = pl.BlockSpec((1, PACK - STATE, PD), lambda h: (2 * number + h, 0, 0))
     state = pl.BlockSpec((1, STATE, PD), lambda h: (2 * number + h, 0, 0))
-    column = pl.BlockSpec((rows, PD), lambda h: (0, 2 * number + h))
+    column = pl.BlockSpec((rows, PD), lambda h: (0, 2 * slot + h))
     return pl.pallas_call(
         functools.partial(attend_back_kernel, spots),
         grid=(2,),
@@ -824,31 +827,28 @@
         for slot in range(SLOTS):
             mixer_pads(weight, size * slot)
 
-    total = nn(rank_grad[...].astype(bf16), left[...])
+    total = nn(rank_grad[0].astype(bf16), left[...])
     for slot in range(SLOTS):
 
         @pl.when(begin)
         def _():
             wait_copies(groups[slot], sems, 40 * slot)
 
-        total = total + nn(grads[slot][...], weight[size * slot : size * (slot + 1), :])
-    part[...] = total.astype(bf16)
-
-
-def first_back(number, grads, rank_grad, left, sources):
-    rows = rank_grad.shape[0]
+        total = total + nn(grads[slot][0], weight[size * slot : size * (slot + 1), :])
+    part[0] = total.astype(bf16)
+
+
+def first_back(start, count, grads, rank_grad, left, sources):
+    cores, _, size = grads[0].shape
     width = left.shape[1]
-    block = rows // 4
     whole = lambda a: pl.BlockSpec(a.shape, lambda i: (0,) * a.ndim)
-    size = 2 * HEAD_PAD
+    span = lambda cols: pl.BlockSpec((1, count, cols), lambda i: (i, start // count, 0))
     return pl.pallas_call(
         first_back_kernel,
-        grid=(2,),
-        out_shape=jax.ShapeDtypeStruct((rows // 2, width), bf16),
-        in_specs=[pl.BlockSpec((block, size), lambda i: (2 * i + number, 0))] * 4
-        + [pl.BlockSpec((block, R), lambda i: (2 * i + number, 0)), whole(left)]
-        + [ANY] * len(sources),
-        out_specs=pl.BlockSpec((block, width), lambda i: (i, 0)),
+        grid=(cores,),
+        out_shape=jax.ShapeDtypeStruct((cores, count, width), bf16),
+        in_specs=[span(size)] * 4 + [span(R), whole(left)] + [ANY] * len(sources),
+        out_specs=pl.BlockSpec((1, count, width), lambda i: (i, 0, 0)),
         scratch_shapes=[pltpu.VMEM((SLOTS * size, width), bf16), pltpu.SemaphoreType.DMA((160,))],
         compiler_params=params(56),
         cost_estimate=pl.CostEstimate(
@@ -1062,10 +1062,19 @@
     return array
 
 
-def neighbour_chip(array, by):
-    count = lax.axis_size("chip")
-    pairs = [(i, i + by) for i in range(count) if 0 <= i + by < count]
-    return lax.ppermute(array, "chip", pairs)
+def plane_parts(array):
+    if lax.axis_size("chip") == 4:
+        return [swap_chip(array, bit) for bit in (1, 2, 3)]
+    return [add_rest(add_swapped(array, 1))]
+
+
+def plane_sum(array, parts):
+    if len(parts) == 1:
+        return parts[0]
+    total = array.astype(f32)
+    for part in parts:
+        total = total + part.astype(f32)
+    return total.astype(array.dtype)
 
 
 def swap_states(packed):
@@ -1370,40 +1379,23 @@
     gate_grads, down_grads = gate_grads + more_gates, down_grads + more_downs
     down_part, back_part, ranks = carry
     other_back = swap_core(back_part)
+    other_down = swap_core(own_rows(down_part, 1 - core))
     mixer_up, output_rgrad = back_two(
         back_part, other_back, middle, upstream, gain_two, my_output_right
     )
 
-    output_rgrad, down_part, middle = hold(output_rgrad, down_part, middle)
-    other_down = swap_core(own_rows(down_part, 1 - core))
     own_down = own_rows(down_part, core).astype(f32)
-    own_output = own_rows(middle, core) + (own_down + other_down.astype(f32))
-    output_rgrad, own_output = hold(output_rgrad, own_output.astype(bf16))
+    own_output = (own_rows(middle, core) + (own_down + other_down.astype(f32))).astype(bf16)
+    own_output, output_rgrad = hold(own_output, output_rgrad)
     block_output = lax.all_gather(own_output, "tp")
 
-    def turn_pair(pair):
-        both = slice(2 * pair, 2 * pair + 2)
-        return turn(
-            pair,
-            spots,
-            mixer_up,
-            output_rgrad,
-            out_weight,
-            slots[both],
-            numer[both],
-            mixed[both],
-            projs[both],
-            borrowed[pair],
-            tables,
-        )
-
-    up0, grad0, packed0, left_grads0 = turn_pair(0)
-    up1, grad1, packed1, left_grads1 = turn_pair(1)
-    packed0, packed1, left_grads1, ranks, out_rank = hold(
-        packed0, packed1, left_grads1, ranks, out_rank
+    ups, grads, packed0, packed1, left_grads = turn(
+        spots, mixer_up, output_rgrad, out_weight, slots, numer, mixed, projs, borrowed, tables
+    )
+    packed0, packed1, left_grads, ranks, out_rank = hold(
+        packed0, packed1, left_grads, ranks, out_rank
     )
     crossing = swap_states(packed0)
-    left_grads = [left_grads0[0], left_grads0[1], left_grads1[0], left_grads1[1]]
     down_rank, gateup_rgrad = ranks[:, :R].astype(bf16), ranks[:, R:].astype(bf16)
     shared = jnp.stack(
         [
@@ -1424,14 +1416,14 @@
             backs.append(
                 attend_back(
                     spots,
-                    n,
+                    slot,
                     projs[slot],
                     borrowed[pair],
                     chunk_states[slot],
                     later,
                     returned,
-                    (up0, up1)[pair],
-                    (grad0, grad1)[pair],
+                    ups,
+                    grads,
                     slots[slot],
                     mixer_rank,
                     tables,
@@ -1472,39 +1464,45 @@
         ],
         0,
     )
-    mixer_x = swap_chip(mixer_all, 1)
-    proj_grads = [back[0] for back in backs]
+    mixer_x = plane_parts(mixer_all)
+    proj_grads = [back[0].reshape(2, length, 2 * HEAD_PAD) for back in backs]
     left_t = my_mixer_left.T
     flat_mix = [w_mix] + sets
-    part_a = first_back(0, proj_grads, rank_grad, left_t, flat_mix)
-    part_a, rank_grad, mixer_x, early, early_other = hold(
-        part_a, rank_grad, mixer_x, early, early_other, after=(block_output,)
-    )
-    mixer_all = join(mixer_all, mixer_x)
-    block = length // 2
-
-    def finish(part, number):
-        here = lax.dynamic_slice_in_dim(part, core * block, block, 0)
-        there = lax.dynamic_slice_in_dim(part, (1 - core) * block, block, 0)
+    count_a = length // 2
+    count_b = length - count_a
+    rank_rows = rank_grad.reshape(2, length, R)
+    part_a = first_back(0, count_a, proj_grads, rank_rows, left_t, flat_mix)
+    part_a, rank_rows, early, early_other, *mixer_x = hold(
+        part_a, rank_rows, early, early_other, *mixer_x, after=(block_output,)
+    )
+    mixer_all = plane_sum(mixer_all, mixer_x)
+
+    def finish(part, start, count):
+        here = lax.dynamic_index_in_dim(part, core, 0, False)
+        there = lax.dynamic_index_in_dim(part, 1 - core, 0, False)
         total = here.astype(f32) + swap_core(there).astype(f32)
-        wide = own_input[number * block : (number + 1) * block].astype(f32)
+        wide = own_input[start : start + count].astype(f32)
         scale_one = lax.rsqrt(jnp.mean(wide * wide, -1, keepdims=True) + epsilon)
         straight = lax.dynamic_slice_in_dim(
-            mixer_up, core * length + number * block, block, 0
+            mixer_up, core * length + start, count, 0
         ).astype(f32)
         return (straight + norm_back(wide, scale_one, gain_one, total)).astype(bf16)
 
-    done_a = finish(part_a, 0)
+    done_a = finish(part_a, 0, count_a)
     e_a, c_a = swap_tp(done_a, 1), cross(done_a)
-    mixer_all = add_rest(mixer_all)
-    part_b = first_back(1, proj_grads, rank_grad, left_t, flat_mix)
-    e_a, c_a, part_b, mixer_all = hold(e_a, c_a, part_b, mixer_all)
+    late = packs_of(mixer_all[:SLOTS], mixer_all[SLOTS:])
+    late = [late[0]] + [swap_tp(late[bit], bit) for bit in (1, 2, 3)]
+    part_b = first_back(count_a, count_b, proj_grads, rank_rows, left_t, flat_mix)
+    e_a, c_a, part_b, *late = hold(e_a, c_a, part_b, *late)
+    late = jnp.stack(late)
     c2_a, f_a = cross(e_a), edge(c_a)
-    done_b = finish(part_b, 1)
-    done_b, early, early_other, mixer_all = hold(done_b, early, early_other, mixer_all)
+    done_b = finish(part_b, count_a, count_b)
+    done_b, early, early_other, late, block_output = hold(
+        done_b, early, early_other, late, block_output
+    )
+    block_output = copy_of(block_output)
     e_b, c_b = swap_tp(done_b, 1), cross(done_b)
-    late = packs_of(mixer_all[:SLOTS], mixer_all[SLOTS:])
-    late1 = swap_tp(late[1], 1)
+    late_other = swap_core(late)
     hot = jnp.swapaxes(onehot, 0, 1).astype(f32)
     flag = jnp.reshape(core == 0, (1,)).astype(jnp.int32)
     early_tables = tables_of(
@@ -1517,30 +1515,23 @@
         early_other,
     )
     (
-        c2_a, f_a, e_b, c_b, late1, late[2], late[3], done_a, done_b, e_a, block_output
+        c2_a, f_a, e_b, c_b, late, late_other, done_a, done_b, e_a
     ) = hold(
-        c2_a, f_a, e_b, c_b, late1, late[2], late[3], done_a, done_b, e_a, block_output,
-        after=early_tables,
+        c2_a, f_a, e_b, c_b, late, late_other, done_a, done_b, e_a,
+        after=(*early_tables, block_output),
     )
     f2_a, c2_b, f_b = edge(c2_a), cross(e_b), edge(c_b)
-    late2, late3 = swap_tp(late[2], 2), swap_tp(late[3], 3)
-
-    block_output = copy_of(block_output)
+
     input_grad = jnp.zeros(block_input.shape, bf16)
 
     def put(whole, part, slot, number):
-        return lax.dynamic_update_slice(whole, part[None], (z ^ slot, number * block, 0))
+        return lax.dynamic_update_slice(whole, part[None], (z ^ slot, number * count_a, 0))
 
     input_grad = put(input_grad, done_a, 0, 0)
     input_grad = put(input_grad, done_b, 0, 1)
     input_grad = put(input_grad, e_a, 1, 0)
     input_grad = put(input_grad, e_b, 1, 1)
     input_grad = put(input_grad, pick_inner(c2_a, f_a), 2, 0)
-    f2_a, c2_b, f_b, late2, late3, input_grad = hold(
-        f2_a, c2_b, f_b, late2, late3, input_grad, after=(block_output,)
-    )
-    f2_b = edge(c2_b)
-    late = jnp.stack([late[0], late1, late2, late3])
     grad_mixer_right, grad_mixer_left = tables_of(
         late_kernel,
         [(R, heads_here, HCOLS), (R, width)],
@@ -1548,8 +1539,12 @@
         hot,
         flag,
         late,
-        swap_core(late),
-    )
+        late_other,
+    )
+    f2_a, c2_b, f_b, input_grad = hold(
+        f2_a, c2_b, f_b, input_grad, after=(grad_mixer_right, grad_mixer_left)
+    )
+    f2_b = edge(c2_b)
     input_grad = put(input_grad, pick_inner(c_a, f2_a), 3, 0)
     input_grad = put(input_grad, pick_inner(c2_b, f_b), 2, 1)
     input_grad = put(input_grad, pick_inner(c_b, f2_b), 3, 1)

time: 894 us -> 885 us (0.990)
  Pallas kernels: 389 us -> 334 us
  other arithmetic: 83 us -> 136 us
    pallas_call x4 -> x1, Pallas kernels: 69.2 us -> 16.8 us  [attend_back(): pl.pallas_call(functools.partial(attend_back_kernel, spots), grid=(2,), o...]
    pallas_call x0 -> x3, other arithmetic: none -> 50.2 us  [attend_back(): pl.pallas_call(functools.partial(attend_back_kernel, spots), grid=(2,), o...]
    ppermute x8, waiting for transfers between devices: 65.3 us -> 81.1 us  [edge(): return lax.ppermute(array, 'tp', [(1, 0), (2, 3)])]
    ppermute x13, waiting for transfers between devices: 36.6 us -> 23.7 us  [swap_tp(): return lax.ppermute(array, 'tp', [(i, i ^ bit) for i in range(4)])]
    unnamed x402 -> x365, local copies, waits for them, and re-layouts: 68.1 us -> 58.6 us
    pallas_call x2 -> x1, Pallas kernels: 25.1 us -> 23.5 us  [turn(): pl.pallas_call(functools.partial(turn_kernel, spots), grid=(rows // CHUNK...]
    ppermute x39 -> x40, starting transfers between devices: 41.8 us -> 42.6 us  [swap_chip(): return lax.ppermute(array, 'chip', [(i, i ^ bit) for i in range(count)])]
    ppermute x39 -> x40, waiting for transfers between devices: 39 us -> 39.1 us  [swap_chip(): return lax.ppermute(array, 'chip', [(i, i ^ bit) for i in range(count)])]
  transfers between devices with their start and end apart: 79 -> 80, of which waited for: 22 -> 21; matrix products, arithmetic and copies ran while one was open for 14% -> 22% of each run, Pallas kernels for 40% -> 34%
where the time goes in v4:
time: 885 us; the launch traced here: 874 us
  Pallas kernels  334 us (38%)
  waiting for transfers between devices  153 us (17%)
  other arithmetic  136 us (15%)
  local copies, waits for them, and re-layouts  115 us (13%)
  starting transfers between devices  105 us (12%)
  between operations  16.8 us (2%)
  matrix products  13.2 us (1%)
    pallas_call x3, Pallas kernels, feed(): pl.pallas_call(functools.partial(feed_kernel, slots, last, half, pad, spo...  104 us
    ppermute x8, waiting for transfers between devices, edge(): return lax.ppermute(array, 'tp', [(1, 0), (2, 3)])  81.1 us
    pallas_call x4, Pallas kernels, project(): pl.pallas_call(functools.partial(project_kernel, own), out_shape=(jax.Sha...  71.4 us
    unnamed x365, local copies, waits for them, and re-layouts  58.6 us
    pallas_call x2, Pallas kernels, first_back(): pl.pallas_call(first_back_kernel, grid=(cores,), out_shape=jax.ShapeDtype...  50.4 us
    pallas_call x3, other arithmetic, attend_back(): pl.pallas_call(functools.partial(attend_back_kernel, spots), grid=(2,), o...  50.2 us
    ppermute x40, starting transfers between devices, swap_chip(): return lax.ppermute(array, 'chip', [(i, i ^ bit) for i in range(count)])  42.6 us
    ppermute x13, starting transfers between devices, swap_tp(): return lax.ppermute(array, 'tp', [(i, i ^ bit) for i in range(4)])  40.7 us
  transfers between devices with their start and end apart: 80, of which 21 were waited for; matrix products, arithmetic and copies ran while one was open for 22% of the time, Pallas kernels for 34%

profile of v4, /device:TPU:0, one launch (start us, length us, event | category | flops | bytes accessed | tf_op | source)
XLA Modules:
  0.0 873.9 jit_solution(15359431189041240104)
XLA Ops:
  61.7 17.1 %project.4 = (bf16[1024,1792]{1,0:T(8,128)(2,1)S(1)}, bf16[2,320,128]{2,1,0:T(8,128)(2,1)S(1)}) custom-call(bf16[1024,1792]{1,0:T(8,128)(2,1)} %copy-done.105, bf16[1024,16]{1,0:T(8,128)(2,1)S(1)} %copy-done.19, bf16[16,4224]{1,0:T(8,128)(2,1)S(1)} %get-tuple-element.435.table.refs_4_.refs_6_.refs_3_, bf16[128,1280]{1,0:T(8,128)(2,1)S(1)} %copy-done.11, ...), custom_call_target="tpu_custom_call" | custom-call | flops 100000000 | bytes 300000 | tf_op jit(solution)/shard_map/project/pallas_call | solution.py:247
  116.7 14.6 %collective-permute-done.11 = bf16[816,896]{1,0:T(8,128)(2,1)} collective-permute-done((bf16[816,896]{1,0:T(8,128)(2,1)}, bf16[816,896]{1,0:T(8,128)(2,1)}, u32[]{:S(2)}, u32[]{:S(2)}) %collective-permute-start.11) | collective-permute-done | bytes 1462304 | tf_op jit(solution)/shard_map/ppermute | solution.py:1044
  152.4 18.1 %project.5 = (bf16[1024,1792]{1,0:T(8,128)(2,1)}, bf16[2,320,128]{2,1,0:T(8,128)(2,1)S(1)}) custom-call(bf16[1024,1792]{1,0:T(8,128)(2,1)} %copy-done.105, bf16[1024,16]{1,0:T(8,128)(2,1)S(1)} %copy-done.20, bf16[16,4224]{1,0:T(8,128)(2,1)S(1)} %copy-done.52, bf16[128,1280]{1,0:T(8,128)(2,1)S(1)} %copy-done.11, ...), custom_call_target="tpu_custom_call" | custom-call | flops 100000000 | bytes 300000 | tf_op jit(solution)/shard_map/project/pallas_call | solution.py:247
  171.2 18.4 %collective-permute-done.19.refs_5_ = bf16[368,896]{1,0:T(8,128)(2,1)S(1)} collective-permute-done((bf16[368,896]{1,0:T(8,128)(2,1)S(1)}, bf16[368,896]{1,0:T(8,128)(2,1)S(1)}, u32[]{:S(2)}, u32[]{:S(2)}) %collective-permute-start.19) | collective-permute-done | bytes 659488 | tf_op jit(solution)/shard_map/ppermute | solution.py:994
  210.9 18.3 %project.6 = (bf16[1024,1792]{1,0:T(8,128)(2,1)}, bf16[2,320,128]{2,1,0:T(8,128)(2,1)S(1)}) custom-call(bf16[1024,1792]{1,0:T(8,128)(2,1)} %copy-done.105, bf16[1024,16]{1,0:T(8,128)(2,1)S(1)} %copy-done.20, bf16[16,4224]{1,0:T(8,128)(2,1)S(1)} %copy-done.48, bf16[128,1280]{1,0:T(8,128)(2,1)S(1)} %copy-done.11, bf16[816,896]{1,0:T(8,128)(2,1)S(1)} %copy-done.12, ...), custom_call_target="tpu_custom_call" | custom-call | flops 100000000 | bytes 300000 | tf_op jit(solution)/shard_map/project/pallas_call | solution.py:247
  244.3 17.9 %project.7 = (bf16[1024,1792]{1,0:T(8,128)(2,1)}, bf16[2,320,128]{2,1,0:T(8,128)(2,1)S(1)}) custom-call(bf16[1024,1792]{1,0:T(8,128)(2,1)} %copy-done.105, bf16[1024,16]{1,0:T(8,128)(2,1)S(1)} %copy-done.20, bf16[16,4224]{1,0:T(8,128)(2,1)S(1)} %copy-done.56, bf16[128,1280]{1,0:T(8,128)(2,1)S(1)} %copy-done.11, bf16[816,896]{1,0:T(8,128)(2,1)S(1)} %copy-done.13, ...), custom_call_target="tpu_custom_call" | custom-call | flops 100000000 | bytes 300000 | tf_op jit(solution)/shard_map/project/pallas_call | solution.py:247
  262.2 15.5 %collective-permute-done.27 = bf16[912,896]{1,0:T(8,128)(2,1)S(1)} collective-permute-done((bf16[912,896]{1,0:T(8,128)(2,1)}, bf16[912,896]{1,0:T(8,128)(2,1)S(1)}, u32[]{:S(2)}, u32[]{:S(2)}) %collective-permute-start.27) | collective-permute-done | bytes 1634336 | tf_op jit(solution)/shard_map/ppermute | solution.py:1044
  333.8 7.3 attend.7
  341.2 10.4 %mix_out.1 = (bf16[1024,1792]{1,0:T(8,128)(2,1)}, f32[1024,16]{1,0:T(8,128)S(1)}, bf16[1024,1792]{1,0:T(8,128)(2,1)}) custom-call(bf16[1024,256]{1,0:T(8,128)(2,1)S(1)} %copy-done.66, bf16[1024,256]{1,0:T(8,128)(2,1)S(1)} %copy-done.68, bf16[1024,256]{1,0:T(8,128)(2,1)S(1)} %get-tuple-element.264.refs_2_.refs_13_, ...), custom_call_target="tpu_custom_call" | custom-call | flops 100000000 | bytes 300000 | tf_op jit(solution)/shard_map/mix_out/pallas_call | solution.py:415
  366.9 7.7 norm_two.1
  377.1 46.3 %feed.3 = (f32[1024,1792]{1,0:T(8,128)}, f32[1024,1792]{1,0:T(8,128)}, f32[1024,32]{1,0:T(8,128)}, bf16[16,1280]{1,0:T(8,128)(2,1)}, bf16[16,1280]{1,0:T(8,128)(...) custom-call(bf16[1024,1792]{1,0:T(8,128)(2,1)} %copy-done.9, ...), custom_call_target="tpu_custom_call" | custom-call | flops 100000000 | bytes 300000 | tf_op jit(solution)/shard_map/feed/pallas_call | solution.py:523
  428.1 28.3 %feed.4 = (f32[1024,1792]{1,0:T(8,128)}, f32[1024,1792]{1,0:T(8,128)}, f32[1024,32]{1,0:T(8,128)}, bf16[16,1280]{1,0:T(8,128)(2,1)}, bf16[16,640]{1,0:T(8,128)(2,1)}) custom-call(bf16[1024,1792]{1,0:T(8,128)(2,1)} %copy-done.9, bf16[1024,1792]{1,0:T(8,128)(2,1)} %get-tuple-element.273.refs_1_.upstream, bf16[1024,16]{1,0:T(8,128)(2,1)} %copy-done.70, ...), custom_call_target="tpu_custom_call" | custom-call | flops 100000000 | bytes 300000 | tf_op jit(solution)/shard_map/feed/pallas_call | solution.py:523
  458.2 29.6 %feed.5 = (bf16[1024,1792]{1,0:T(8,128)(2,1)}, bf16[1024,1792]{1,0:T(8,128)(2,1)}, f32[1024,32]{1,0:T(8,128)}, bf16[16,1280]{1,0:T(8,128)(2,1)}, bf16[16,640]{1,0:T(8,128)(2,1)}) custom-call(bf16[1024,1792]{1,0:T(8,128)(2,1)} %copy-done.9, bf16[1024,1792]{1,0:T(8,128)(2,1)} %get-tuple-element.273.refs_1_.upstream, bf16[1024,16]{1,0:T(8,128)(2,1)} %copy-done.70, ...), custom_call_target="tpu_custom_call" | custom-call | flops 100000000 | bytes 300000 | tf_op jit(solution)/shard_map/feed/pallas_call | solution.py:523
  502.4 7.4 back_two.1
  518.0 23.5 %turn.1 = (bf16[1024,1024]{1,0:T(8,128)(2,1)}, bf16[1024,1024]{1,0:T(8,128)(2,1)}, bf16[4,320,128]{2,1,0:T(8,128)(2,1)S(1)}, bf16[4,320,128]{2,1,0:T(8,128)(2,1)S(1)}, bf16[4,16,256]{2,1,0:T(8,128)(2,1)S(1)}) custom-call(bf16[1024,1792]{1,0:T(8,128)(2,1)} %copy-done.21, bf16[1024,16]{1,0:T(8,128)(2,1)S(1)} %copy-done.82, ...), custom_call_target="tpu_custom_call" | custom-call | flops 100000000 | bytes 300000 | tf_op jit(solution)/shard_map/turn/pallas_call | solution.py:635
  569.9 16.8 %attend_back.4 = (bf16[1024,1792]{1,0:T(8,128)(2,1)}, f32[1024,16]{1,0:T(8,128)S(1)}, bf16[16,1792]{1,0:T(8,128)(2,1)S(1)}) custom-call(bf16[1024,1792]{1,0:T(8,128)(2,1)} %copy-done.2, bf16[4,160,128]{2,1,0:T(8,128)(2,1)S(1)} %copy-done.45, bf16[2,4,256,128]{3,2,1,0:T(8,128)(2,1)S(1)} %copy-done.98, f32[4,160,128]{2,1,0:T(8,128)S(1)} %select_add_fusion.1.later, ...), custom_call_target="tpu_custom_call" | custom-call | flops 100000000 | bytes 300000 | tf_op jit(solution)/shard_map/attend_back/pallas_call | solution.py:772
  587.4 16.0 %attend_back.7 = (bf16[5,16,1792]{2,1,0:T(8,128)(2,1)}, bf16[1024,1792]{1,0:T(8,128)(2,1)}, f32[1024,16]{1,0:T(8,128)S(1)}) fusion(bf16[5,16,1792]{2,1,0:T(8,128)(2,1)} %bitcast_dynamic-update-slice_fusion.11, bf16[1024,1792]{1,0:T(8,128)(2,1)S(1)} %copy-done.6, bf16[4,160,128]{2,1,0:T(8,128)(2,1)S(1)} %copy-done.45, ...), kind=kCustom, calls=%fused_computation.139 | custom fusion | flops 100000000 | bytes 13332480 | tf_op jit(solution)/shard_map/attend_back/pallas_call | solution.py:772
  611.2 17.2 %attend_back.6 = (bf16[5,16,1792]{2,1,0:T(8,128)(2,1)}, bf16[1024,1792]{1,0:T(8,128)(2,1)}, f32[1024,16]{1,0:T(8,128)S(1)}) fusion(bf16[5,16,1792]{2,1,0:T(8,128)(2,1)} %get-tuple-element.411, bf16[1024,1792]{1,0:T(8,128)(2,1)} %get-tuple-element.260.proj.refs_19_.refs_20_.refs_25_, bf16[4,160,128]{2,1,0:T(8,128)(2,1)S(1)} %copy-done.63, ...), kind=kCustom, calls=%fused_computation.138 | custom fusion | flops 100000000 | bytes 13332480 | tf_op jit(solution)/shard_map/attend_back/pallas_call | solution.py:772
  641.7 16.9 %attend_back.5 = (bf16[5,16,1792]{2,1,0:T(8,128)(2,1)}, bf16[1024,1792]{1,0:T(8,128)(2,1)}, f32[1024,16]{1,0:T(8,128)S(1)}) fusion(bf16[5,16,1792]{2,1,0:T(8,128)(2,1)} %get-tuple-element.417, bf16[1024,1792]{1,0:T(8,128)(2,1)} %get-tuple-element.265.proj.refs_21_.refs_22_.refs_26_, bf16[4,160,128]{2,1,0:T(8,128)(2,1)S(1)} %copy-done.63, ...), kind=kCustom, calls=%fused_computation.137 | custom fusion | flops 100000000 | bytes 13332480 | tf_op jit(solution)/shard_map/attend_back/pallas_call | solution.py:772
  673.0 25.2 %first_back.2.refs_0_ = bf16[2,256,1792]{2,1,0:T(8,128)(2,1)} custom-call(bf16[2,512,1792]{2,1,0:T(8,128)(2,1)} %bitcast.216, bf16[2,512,1792]{2,1,0:T(8,128)(2,1)} %bitcast.208, bf16[2,512,1792]{2,1,0:T(8,128)(2,1)} %bitcast.210, bf16[2,512,1792]{2,1,0:T(8,128)(2,1)} %bitcast.212, f32[2,512,16]{2,1,0:T(8,128)} %bitcast.214, ...), custom_call_target="tpu_custom_call" | custom-call | flops 100000000 | bytes 300000 | tf_op jit(solution)/shard_map/first_back/pallas_call | solution.py:846
  720.5 25.2 %first_back.3.refs_2_ = bf16[2,256,1792]{2,1,0:T(8,128)(2,1)} custom-call(bf16[2,512,1792]{2,1,0:T(8,128)(2,1)} %bitcast.217, bf16[2,512,1792]{2,1,0:T(8,128)(2,1)} %bitcast.209, bf16[2,512,1792]{2,1,0:T(8,128)(2,1)} %bitcast.211, bf16[2,512,1792]{2,1,0:T(8,128)(2,1)} %bitcast.213, f32[2,512,16]{2,1,0:T(8,128)} %get-tuple-element.365.refs_4_, ...), custom_call_target="tpu_custom_call" | custom-call | flops 100000000 | bytes 300000 | tf_op jit(solution)/shard_map/first_back/pallas_call | solution.py:846
  777.9 18.6 %collective-permute-done.71.refs_2_ = bf16[256,1792]{1,0:T(8,128)(2,1)S(1)} collective-permute-done((bf16[256,1792]{1,0:T(8,128)(2,1)}, bf16[256,1792]{1,0:T(8,128)(2,1)S(1)}, u32[]{:S(2)}, u32[]{:S(2)}) %collective-permute-start.71) | collective-permute-done | bytes 917536 | tf_op jit(solution)/shard_map/ppermute | solution.py:998
  822.8 18.4 %collective-permute-done.76.refs_2_ = bf16[256,1792]{1,0:T(8,128)(2,1)S(1)} collective-permute-done((bf16[256,1792]{1,0:T(8,128)(2,1)}, bf16[256,1792]{1,0:T(8,128)(2,1)S(1)}, u32[]{:S(2)}, u32[]{:S(2)}) %collective-permute-start.76) | collective-permute-done | bytes 917536 | tf_op jit(solution)/shard_map/ppermute | solution.py:1044
  847.0 18.4 %collective-permute-done.77 = bf16[256,1792]{1,0:T(8,128)(2,1)S(1)} collective-permute-done((bf16[256,1792]{1,0:T(8,128)(2,1)}, bf16[256,1792]{1,0:T(8,128)(2,1)S(1)}, u32[]{:S(2)}, u32[]{:S(2)}) %collective-permute-start.77) | collective-permute-done | bytes 917536 | tf_op jit(solution)/shard_map/ppermute | solution.py:1044
  (686 shorter events, 403.9 us)
Async XLA Ops:
  7.2 224.6 %all-gather.5.cloned.1.call-start = ((), (), s32[]{:S(2)}) async-start(), calls=%async_computation | async-start | bytes 1638400 | tf_op jit(solution)/shard_map/all_gather | solution.py:1314
  47.4 45.3 %collective-permute-start.4 = (bf16[816,896]{1,0:T(8,128)(2,1)}, bf16[816,896]{1,0:T(8,128)(2,1)S(1)}, u32[]{:S(2)}, u32[]{:S(2)}) collective-permute-start(bf16[816,896]{1,0:T(8,128)(2,1)} %get-tuple-element.210.rest_0_.refs_10_.refs_7_), channel_id=1, source_target_pairs={{0,8},{8,0},{16,24},{24,16},{1,9},{9,1},{17,25},{25,17},{2,10},{10... | collective-permute-start | bytes 4386824 | tf_op jit(solution)/shard_map/ppermute | solution.py:994
  48.9 43.8 %collective-permute-start.5 = (bf16[816,896]{1,0:T(8,128)(2,1)}, bf16[816,896]{1,0:T(8,128)(2,1)}, u32[]{:S(2)}, u32[]{:S(2)}) collective-permute-start(bf16[816,896]{1,0:T(8,128)(2,1)} %get-tuple-element.210.rest_0_.refs_10_.refs_7_), channel_id=1, source_target_pairs={{0,16},{8,24},{16,0},{24,8},{1,17},{9,25},{17,1},{25,9},{2,18},{10... | collective-permute-start | bytes 4386824 | tf_op jit(solution)/shard_map/ppermute | solution.py:994
  51.2 40.1 %collective-permute-start.7 = (bf16[816,896]{1,0:T(8,128)(2,1)}, bf16[816,896]{1,0:T(8,128)(2,1)S(1)}, u32[]{:S(2)}, u32[]{:S(2)}) collective-permute-start(bf16[816,896]{1,0:T(8,128)(2,1)} %get-tuple-element.211.refs_4_), channel_id=1, source_target_pairs={{1,0},{2,3},{5,4},{6,7},{9,8},{10,11},{13,12},{14,15},{17,16},{18,... | collective-permute-start | bytes 4386824 | tf_op jit(solution)/shard_map/ppermute | solution.py:1044
  93.9 49.3 %collective-permute-start.9 = (bf16[816,896]{1,0:T(8,128)(2,1)}, bf16[816,896]{1,0:T(8,128)(2,1)}, u32[]{:S(2)}, u32[]{:S(2)}) collective-permute-start(bf16[816,896]{1,0:T(8,128)(2,1)} %get-tuple-element.213.rest_0_.refs_15_.refs_12_), channel_id=1, source_target_pairs={{0,8},{8,0},{16,24},{24,16},{1,9},{9,1},{17,25},{25,17},{2,10},{10... | collective-permute-start | bytes 4386824 | tf_op jit(solution)/shard_map/ppermute | solution.py:994
  94.5 48.8 %collective-permute-start.10 = (bf16[816,896]{1,0:T(8,128)(2,1)}, bf16[816,896]{1,0:T(8,128)(2,1)S(1)}, u32[]{:S(2)}, u32[]{:S(2)}) collective-permute-start(bf16[816,896]{1,0:T(8,128)(2,1)} %get-tuple-element.213.rest_0_.refs_15_.refs_12_), channel_id=1, source_target_pairs={{0,16},{8,24},{16,0},{24,8},{1,17},{9,25},{17,1},{25,9},{2,18},{10... | collective-permute-start | bytes 4386824 | tf_op jit(solution)/shard_map/ppermute | solution.py:994
  144.6 50.1 %collective-permute-start.18 = (bf16[912,896]{1,0:T(8,128)(2,1)}, bf16[912,896]{1,0:T(8,128)(2,1)S(1)}, u32[]{:S(2)}, u32[]{:S(2)}) collective-permute-start(bf16[912,896]{1,0:T(8,128)(2,1)} %get-tuple-element.223), channel_id=1, source_target_pairs={{0,1},{1,0},{2,3},{3,2},{4,5},{5,4},{6,7},{7,6},{8,9},{9,8},{10,11... | collective-permute-start | bytes 4902920 | tf_op jit(solution)/shard_map/ppermute | solution.py:998
  144.7 49.1 %collective-permute-start.16 = (bf16[816,896]{1,0:T(8,128)(2,1)}, bf16[816,896]{1,0:T(8,128)(2,1)S(1)}, u32[]{:S(2)}, u32[]{:S(2)}) collective-permute-start(bf16[816,896]{1,0:T(8,128)(2,1)} %get-tuple-element.222.rest_0_.refs_20_.refs_17_), channel_id=1, source_target_pairs={{0,8},{8,0},{16,24},{24,16},{1,9},{9,1},{17,25},{25,17},{2,10},{10... | collective-permute-start | bytes 4386824 | tf_op jit(solution)/shard_map/ppermute | solution.py:994
  146.3 48.5 %collective-permute-start.17 = (bf16[816,896]{1,0:T(8,128)(2,1)}, bf16[816,896]{1,0:T(8,128)(2,1)S(1)}, u32[]{:S(2)}, u32[]{:S(2)}) collective-permute-start(bf16[816,896]{1,0:T(8,128)(2,1)} %get-tuple-element.222.rest_0_.refs_20_.refs_17_), channel_id=1, source_target_pairs={{0,16},{8,24},{16,0},{24,8},{1,17},{9,25},{17,1},{25,9},{2,18},{10... | collective-permute-start | bytes 4386824 | tf_op jit(solution)/shard_map/ppermute | solution.py:994
  148.0 45.9 %collective-permute-start.20 = (bf16[448,896]{1,0:T(8,128)(2,1)S(1)}, bf16[448,896]{1,0:T(8,128)(2,1)S(1)}, u32[]{:S(2)}, u32[]{:S(2)}) collective-permute-start(bf16[448,896]{1,0:T(8,128)(2,1)S(1)} %slice.170), channel_id=1, source_target_pairs={{0,16},{8,24},{16,0},{24,8},{1,17},{9,25},{17,1},{25,9},{2,18},{10... | collective-permute-start | bytes 2408456 | tf_op jit(solution)/shard_map/ppermute | solution.py:994
  150.7 38.9 %collective-permute-start.19 = (bf16[368,896]{1,0:T(8,128)(2,1)S(1)}, bf16[368,896]{1,0:T(8,128)(2,1)S(1)}, u32[]{:S(2)}, u32[]{:S(2)}) collective-permute-start(bf16[368,896]{1,0:T(8,128)(2,1)S(1)} %slice.169), channel_id=1, source_target_pairs={{0,8},{8,0},{16,24},{24,16},{1,9},{9,1},{17,25},{25,17},{2,10},{10... | collective-permute-start | bytes 1978376 | tf_op jit(solution)/shard_map/ppermute | solution.py:994
  198.9 499.4 %all-gather.7.cloned.1.call-start = ((), (), s32[]{:S(2)}) async-start(), calls=%async_computation.1 | async-start | bytes 9175040 | tf_op jit(solution)/shard_map/all_gather | solution.py:1390
  205.9 56.3 %collective-permute-start.26 = (bf16[912,896]{1,0:T(8,128)(2,1)}, bf16[912,896]{1,0:T(8,128)(2,1)}, u32[]{:S(2)}, u32[]{:S(2)}) collective-permute-start(bf16[912,896]{1,0:T(8,128)(2,1)} %get-tuple-element.244.refs_10_), channel_id=1, source_target_pairs={{1,2},{2,1},{5,6},{6,5},{9,10},{10,9},{13,14},{14,13},{17,18},{18,... | collective-permute-start | bytes 4902920 | tf_op jit(solution)/shard_map/ppermute | solution.py:1040
  237.4 40.4 %collective-permute-start.27 = (bf16[912,896]{1,0:T(8,128)(2,1)}, bf16[912,896]{1,0:T(8,128)(2,1)S(1)}, u32[]{:S(2)}, u32[]{:S(2)}) collective-permute-start(bf16[912,896]{1,0:T(8,128)(2,1)} %get-tuple-element.245.refs_4_), channel_id=1, source_target_pairs={{1,0},{2,3},{5,4},{6,7},{9,8},{10,11},{13,12},{14,15},{17,16},{18,... | collective-permute-start | bytes 4902920 | tf_op jit(solution)/shard_map/ppermute | solution.py:1044
  239.1 40.1 %collective-permute-start.24 = (bf16[912,896]{1,0:T(8,128)(2,1)}, bf16[912,896]{1,0:T(8,128)(2,1)S(1)}, u32[]{:S(2)}, u32[]{:S(2)}) collective-permute-start(bf16[912,896]{1,0:T(8,128)(2,1)} %get-tuple-element.244.refs_10_), channel_id=1, source_target_pairs={{0,8},{8,0},{16,24},{24,16},{1,9},{9,1},{17,25},{25,17},{2,10},{10... | collective-permute-start | bytes 4902920 | tf_op jit(solution)/shard_map/ppermute | solution.py:994
  354.8 68.6 %collective-permute-start.37 = (bf16[912,896]{1,0:T(8,128)(2,1)}, bf16[912,896]{1,0:T(8,128)(2,1)}, u32[]{:S(2)}, u32[]{:S(2)}) collective-permute-start(bf16[912,896]{1,0:T(8,128)(2,1)} %get-tuple-element.276.refs_7_), channel_id=1, source_target_pairs={{0,8},{8,0},{16,24},{24,16},{1,9},{9,1},{17,25},{25,17},{2,10},{10... | collective-permute-start | bytes 4902920 | tf_op jit(solution)/shard_map/ppermute | solution.py:994
  355.7 67.7 %collective-permute-start.38 = (bf16[912,896]{1,0:T(8,128)(2,1)}, bf16[912,896]{1,0:T(8,128)(2,1)}, u32[]{:S(2)}, u32[]{:S(2)}) collective-permute-start(bf16[912,896]{1,0:T(8,128)(2,1)} %get-tuple-element.276.refs_7_), channel_id=1, source_target_pairs={{0,16},{8,24},{16,0},{24,8},{1,17},{9,25},{17,1},{25,9},{2,18},{10... | collective-permute-start | bytes 4902920 | tf_op jit(solution)/shard_map/ppermute | solution.py:994
  359.0 64.3 %collective-permute-start.39 = (bf16[464,896]{1,0:T(8,128)(2,1)}, bf16[464,896]{1,0:T(8,128)(2,1)}, u32[]{:S(2)}, u32[]{:S(2)}) collective-permute-start(bf16[464,896]{1,0:T(8,128)(2,1)} %slice.181), channel_id=1, source_target_pairs={{0,8},{8,0},{16,24},{24,16},{1,9},{9,1},{17,25},{25,17},{2,10},{10... | collective-permute-start | bytes 2494472 | tf_op jit(solution)/shard_map/ppermute | solution.py:994
  362.0 61.4 %collective-permute-start.40 = (bf16[448,896]{1,0:T(8,128)(2,1)}, bf16[448,896]{1,0:T(8,128)(2,1)}, u32[]{:S(2)}, u32[]{:S(2)}) collective-permute-start(bf16[448,896]{1,0:T(8,128)(2,1)} %slice.182), channel_id=1, source_target_pairs={{0,16},{8,24},{16,0},{24,8},{1,17},{9,25},{17,1},{25,9},{2,18},{10... | collective-permute-start | bytes 2408456 | tf_op jit(solution)/shard_map/ppermute | solution.py:994
  561.1 43.2 %collective-permute-start.50 = (bf16[4,320,128]{2,1,0:T(8,128)(2,1)}, bf16[4,320,128]{2,1,0:T(8,128)(2,1)}, u32[]{:S(2)}, u32[]{:S(2)}) collective-permute-start(bf16[4,320,128]{2,1,0:T(8,128)(2,1)} %get-tuple-element.338), channel_id=1, source_target_pairs={{0,8},{8,0},{16,24},{24,16},{1,9},{9,1},{17,25},{25,17},{2,10},{10... | collective-permute-start | bytes 983048 | tf_op jit(solution)/shard_map/ppermute | solution.py:994
  562.3 42.0 %collective-permute-start.51 = (bf16[4,320,128]{2,1,0:T(8,128)(2,1)}, bf16[4,320,128]{2,1,0:T(8,128)(2,1)}, u32[]{:S(2)}, u32[]{:S(2)}) collective-permute-start(bf16[4,320,128]{2,1,0:T(8,128)(2,1)} %get-tuple-element.338), channel_id=1, source_target_pairs={{0,16},{8,24},{16,0},{24,8},{1,17},{9,25},{17,1},{25,9},{2,18},{10... | collective-permute-start | bytes 983048 | tf_op jit(solution)/shard_map/ppermute | solution.py:994
  563.1 41.2 %collective-permute-start.52 = (bf16[4,320,128]{2,1,0:T(8,128)(2,1)}, bf16[4,320,128]{2,1,0:T(8,128)(2,1)}, u32[]{:S(2)}, u32[]{:S(2)}) collective-permute-start(bf16[4,320,128]{2,1,0:T(8,128)(2,1)} %get-tuple-element.338), channel_id=1, source_target_pairs={{0,24},{8,16},{16,8},{24,0},{1,25},{9,17},{17,9},{25,1},{2,26},{10... | collective-permute-start | bytes 983048 | tf_op jit(solution)/shard_map/ppermute | solution.py:994
  564.6 39.7 %collective-permute-start.48 = (f32[3,16,1792]{2,1,0:T(8,128)}, f32[3,16,1792]{2,1,0:T(8,128)}, u32[]{:S(2)}, u32[]{:S(2)}) collective-permute-start(f32[3,16,1792]{2,1,0:T(8,128)} %get-tuple-element.336), channel_id=1, source_target_pairs={{0,8},{8,0},{16,24},{24,16},{1,9},{9,1},{17,25},{25,17},{2,10},{10... | collective-permute-start | bytes 1032200 | tf_op jit(solution)/shard_map/ppermute | solution.py:994
  799.5 41.7 %collective-permute-start.76 = (bf16[256,1792]{1,0:T(8,128)(2,1)}, bf16[256,1792]{1,0:T(8,128)(2,1)S(1)}, u32[]{:S(2)}, u32[]{:S(2)}) collective-permute-start(bf16[256,1792]{1,0:T(8,128)(2,1)} %get-tuple-element.391), channel_id=1, source_target_pairs={{1,0},{2,3},{5,4},{6,7},{9,8},{10,11},{13,12},{14,15},{17,16},{18,... | collective-permute-start | bytes 2752520 | tf_op jit(solution)/shard_map/ppermute | solution.py:1044
  (236 other events, 2701.7 us)
Sparse Core Ops, SparseCore 0:
  199.1 32.7 all-gather.4
  512.6 140.1 all-gather.6

commit v5 on v4

--- a/solution.py
+++ b/solution.py
@@ -21,6 +21,7 @@
 HEAD_PAD = 7 * PD
 STATE = 160
 CHUNK = 256
+TURN = 1024
 QB = 128
 BACK_QB = 256
 BACK_CHUNK = 512
@@ -249,10 +250,11 @@
         out_shape=(
             jax.ShapeDtypeStruct((rows, 2 * HEAD_PAD), bf16),
             jax.ShapeDtypeStruct((2, PACK, PD), bf16),
+            jax.ShapeDtypeStruct((2 * HEAD_PAD, width), bf16),
         ),
         in_specs=[vm] * 4 + [ANY] * len(refs),
-        out_specs=(vm, vm),
-        scratch_shapes=[pltpu.VMEM((2 * HEAD_PAD, width), bf16), pltpu.SemaphoreType.DMA((40,))],
+        out_specs=(vm, vm, vm),
+        scratch_shapes=[pltpu.SemaphoreType.DMA((40,))],
         compiler_params=params(48),
         cost_estimate=pl.CostEstimate(
             flops=100_000_000, bytes_accessed=300_000, transcendentals=0
@@ -630,11 +632,11 @@
     rows, width = mixer_up.shape
     whole = lambda a: pl.BlockSpec(a.shape, lambda i: (0,) * a.ndim)
     flat = lambda *shape: pl.BlockSpec(shape, lambda i: (0,) * len(shape))
-    tall = lambda cols, at: pl.BlockSpec((CHUNK, cols), lambda i: (i, at))
+    tall = lambda cols, at: pl.BlockSpec((TURN, cols), lambda i: (i, at))
     heads = 2 * SLOTS
     return pl.pallas_call(
         functools.partial(turn_kernel, spots),
-        grid=(rows // CHUNK,),
+        grid=(rows // TURN,),
         out_shape=(
             jax.ShapeDtypeStruct((rows, heads * PD), bf16),
             jax.ShapeDtypeStruct((rows, heads * PD), bf16),
@@ -657,7 +659,7 @@
             flat(SLOTS, R, 2 * PD),
         ),
         scratch_shapes=[pltpu.VMEM((heads, 256, PD), f32), pltpu.VMEM((SLOTS, R, 2 * PD), f32)],
-        compiler_params=params(48),
+        compiler_params=params(58),
         cost_estimate=pl.CostEstimate(
             flops=100_000_000, bytes_accessed=300_000, transcendentals=0
         ),
@@ -811,28 +813,22 @@
 def first_back_kernel(*refs):
     grads = refs[0:4]
     rank_grad, left = refs[4:6]
-    sources = refs[6 : 6 + 16]
-    part, weight, sems = refs[22:]
-    groups = []
+    sources = refs[6:10]
+    part, weight, sems = refs[10:]
     size = 2 * HEAD_PAD
-    for slot in range(SLOTS):
-        pieces = sources[0:1] if slot == 0 else sources[1 + 5 * (slot - 1) : 1 + 5 * slot]
-        groups.append(mixer_copies(pieces, slot == 0, weight, size * slot))
+    copies = [(sources[n], weight.at[size * n : size * (n + 1)]) for n in range(SLOTS)]
     begin = pl.program_id(0) == 0
 
     @pl.when(begin)
     def _():
-        for slot in range(SLOTS):
-            run_copies(groups[slot], sems, 40 * slot)
-        for slot in range(SLOTS):
-            mixer_pads(weight, size * slot)
+        run_copies(copies, sems, 0)
 
     total = nn(rank_grad[0].astype(bf16), left[...])
     for slot in range(SLOTS):
 
         @pl.when(begin)
         def _():
-            wait_copies(groups[slot], sems, 40 * slot)
+            wait_copies(copies[slot : slot + 1], sems, slot)
 
         total = total + nn(grads[slot][0], weight[size * slot : size * (slot + 1), :])
     part[0] = total.astype(bf16)
@@ -849,7 +845,7 @@
         out_shape=jax.ShapeDtypeStruct((cores, count, width), bf16),
         in_specs=[span(size)] * 4 + [span(R), whole(left)] + [ANY] * len(sources),
         out_specs=pl.BlockSpec((1, count, width), lambda i: (i, 0, 0)),
-        scratch_shapes=[pltpu.VMEM((SLOTS * size, width), bf16), pltpu.SemaphoreType.DMA((160,))],
+        scratch_shapes=[pltpu.VMEM((SLOTS * size, width), bf16), pltpu.SemaphoreType.DMA((SLOTS,))],
         compiler_params=params(56),
         cost_estimate=pl.CostEstimate(
             flops=100_000_000, bytes_accessed=300_000, transcendentals=0
@@ -1268,7 +1264,7 @@
         upstream_own, upstream_other, e_m, c_m, mixer_rank, packed, both_input
     )
 
-    projs, packs = [], []
+    projs, packs, wides = [], [], []
     borrowed, prior, mixed, numer, chunk_states = [None, None], [None, None], [], [], []
     slots = [packed[0], None, None, None]
 
@@ -1280,7 +1276,7 @@
 
     def project_slot(slot, refs):
         out = project(slot == 0, first, mixer_rank, slots[slot], tables, refs)
-        for kept, value in zip((projs, packs), out):
+        for kept, value in zip((projs, packs, wides), out):
             kept.append(value)
 
     x1, y1 = hop_xy(e_m)
@@ -1380,14 +1376,14 @@
     down_part, back_part, ranks = carry
     other_back = swap_core(back_part)
     other_down = swap_core(own_rows(down_part, 1 - core))
+    own_down = own_rows(down_part, core).astype(f32)
+    own_output = (own_rows(middle, core) + (own_down + other_down.astype(f32))).astype(bf16)
+    own_output, other_back = hold(own_output, other_back)
+    block_output = lax.all_gather(own_output, "tp")
     mixer_up, output_rgrad = back_two(
         back_part, other_back, middle, upstream, gain_two, my_output_right
     )
 
-    own_down = own_rows(down_part, core).astype(f32)
-    own_output = (own_rows(middle, core) + (own_down + other_down.astype(f32))).astype(bf16)
-    own_output, output_rgrad = hold(own_output, output_rgrad)
-    block_output = lax.all_gather(own_output, "tp")
 
     ups, grads, packed0, packed1, left_grads = turn(
         spots, mixer_up, output_rgrad, out_weight, slots, numer, mixed, projs, borrowed, tables
@@ -1467,11 +1463,10 @@
     mixer_x = plane_parts(mixer_all)
     proj_grads = [back[0].reshape(2, length, 2 * HEAD_PAD) for back in backs]
     left_t = my_mixer_left.T
-    flat_mix = [w_mix] + sets
     count_a = length // 2
     count_b = length - count_a
     rank_rows = rank_grad.reshape(2, length, R)
-    part_a = first_back(0, count_a, proj_grads, rank_rows, left_t, flat_mix)
+    part_a = first_back(0, count_a, proj_grads, rank_rows, left_t, wides)
     part_a, rank_rows, early, early_other, *mixer_x = hold(
         part_a, rank_rows, early, early_other, *mixer_x, after=(block_output,)
     )
@@ -1492,7 +1487,7 @@
     e_a, c_a = swap_tp(done_a, 1), cross(done_a)
     late = packs_of(mixer_all[:SLOTS], mixer_all[SLOTS:])
     late = [late[0]] + [swap_tp(late[bit], bit) for bit in (1, 2, 3)]
-    part_b = first_back(count_a, count_b, proj_grads, rank_rows, left_t, flat_mix)
+    part_b = first_back(count_a, count_b, proj_grads, rank_rows, left_t, wides)
     e_a, c_a, part_b, *late = hold(e_a, c_a, part_b, *late)
     late = jnp.stack(late)
     c2_a, f_a = cross(e_a), edge(c_a)

time: 885 us -> 874 us (0.988)
    unnamed x365 -> x339, local copies, waits for them, and re-layouts: 58.6 us -> 52 us
  transfers between devices with their start and end apart: 80 -> 80, of which waited for: 21 -> 21; matrix products, arithmetic and copies ran while one was open for 22% -> 22% of each run, Pallas kernels for 34% -> 35%
where the time goes in v5:
time: 874 us; the launch traced here: 864 us
  Pallas kernels  332 us (38%)
  waiting for transfers between devices  155 us (18%)
  other arithmetic  136 us (16%)
  local copies, waits for them, and re-layouts  108 us (12%)
  starting transfers between devices  102 us (12%)
  between operations  16.9 us (2%)
  matrix products  13.2 us (2%)
    pallas_call x3, Pallas kernels, feed(): pl.pallas_call(functools.partial(feed_kernel, slots, last, half, pad, spo...  104 us
    ppermute x8, waiting for transfers between devices, edge(): return lax.ppermute(array, 'tp', [(1, 0), (2, 3)])  80.9 us
    pallas_call x4, Pallas kernels, project(): pl.pallas_call(functools.partial(project_kernel, own), out_shape=(jax.Sha...  74.4 us
    unnamed x339, local copies, waits for them, and re-layouts  52 us
    pallas_call x3, other arithmetic, attend_back(): pl.pallas_call(functools.partial(attend_back_kernel, spots), grid=(2,), o...  50.2 us
    pallas_call x2, Pallas kernels, first_back(): pl.pallas_call(first_back_kernel, grid=(cores,), out_shape=jax.ShapeDtype...  47.9 us
    ppermute x40, starting transfers between devices, swap_chip(): return lax.ppermute(array, 'chip', [(i, i ^ bit) for i in range(count)])  44.4 us
    ppermute x40, waiting for transfers between devices, swap_chip(): return lax.ppermute(array, 'chip', [(i, i ^ bit) for i in range(count)])  40.3 us
  transfers between devices with their start and end apart: 80, of which 21 were waited for; matrix products, arithmetic and copies ran while one was open for 22% of the time, Pallas kernels for 35%

profile of v5, /device:TPU:0, one launch (start us, length us, event | category | flops | bytes accessed | tf_op | source)
XLA Modules:
  0.0 863.5 jit_solution(3729247204523862508)
XLA Ops:
  62.3 18.3 %project.4 = (bf16[1024,1792]{1,0:T(8,128)(2,1)S(1)}, bf16[2,320,128]{2,1,0:T(8,128)(2,1)S(1)}, bf16[1792,1792]{1,0:T(8,128)(2,1)}) custom-call(bf16[1024,1792]{1,0:T(8,128)(2,1)} %copy-done.93, bf16[1024,16]{1,0:T(8,128)(2,1)S(1)} %copy-done.14, bf16[16,4224]{1,0:T(8,128)(2,1)S(1)} %get-tuple-element.443.table.refs_4_.refs_6_.refs_3_, ...), custom_call_target="tpu_custom_call" | custom-call | flops 100000000 | bytes 300000 | tf_op jit(solution)/shard_map/project/pallas_call | solution.py:248
  118.2 16.2 %collective-permute-done.11 = bf16[816,896]{1,0:T(8,128)(2,1)} collective-permute-done((bf16[816,896]{1,0:T(8,128)(2,1)}, bf16[816,896]{1,0:T(8,128)(2,1)}, u32[]{:S(2)}, u32[]{:S(2)}) %collective-permute-start.11) | collective-permute-done | bytes 1462304 | tf_op jit(solution)/shard_map/ppermute | solution.py:1040
  156.9 18.6 %project.5 = (bf16[1024,1792]{1,0:T(8,128)(2,1)}, bf16[2,320,128]{2,1,0:T(8,128)(2,1)S(1)}, bf16[1792,1792]{1,0:T(8,128)(2,1)}) custom-call(bf16[1024,1792]{1,0:T(8,128)(2,1)} %copy-done.93, bf16[1024,16]{1,0:T(8,128)(2,1)S(1)} %copy-done.15, bf16[16,4224]{1,0:T(8,128)(2,1)S(1)} %copy-done.47, bf16[128,1280]{1,0:T(8,128)(2,1)S(1)} %copy-done.11, ...), custom_call_target="tpu_custom_call" | custom-call | flops 100000000 | bytes 300000 | tf_op jit(solution)/shard_map/project/pallas_call | solution.py:248
  176.2 17.6 %collective-permute-done.19.refs_5_ = bf16[368,896]{1,0:T(8,128)(2,1)S(1)} collective-permute-done((bf16[368,896]{1,0:T(8,128)(2,1)S(1)}, bf16[368,896]{1,0:T(8,128)(2,1)S(1)}, u32[]{:S(2)}, u32[]{:S(2)}) %collective-permute-start.19) | collective-permute-done | bytes 659488 | tf_op jit(solution)/shard_map/ppermute | solution.py:990
  214.9 18.6 %project.6 = (bf16[1024,1792]{1,0:T(8,128)(2,1)}, bf16[2,320,128]{2,1,0:T(8,128)(2,1)S(1)}, bf16[1792,1792]{1,0:T(8,128)(2,1)}) custom-call(bf16[1024,1792]{1,0:T(8,128)(2,1)} %copy-done.93, bf16[1024,16]{1,0:T(8,128)(2,1)S(1)} %copy-done.15, bf16[16,4224]{1,0:T(8,128)(2,1)S(1)} %copy-done.44, bf16[128,1280]{1,0:T(8,128)(2,1)S(1)} %copy-done.11, ...), custom_call_target="tpu_custom_call" | custom-call | flops 100000000 | bytes 300000 | tf_op jit(solution)/shard_map/project/pallas_call | solution.py:248
  245.7 18.9 %project.7 = (bf16[1024,1792]{1,0:T(8,128)(2,1)}, bf16[2,320,128]{2,1,0:T(8,128)(2,1)S(1)}, bf16[1792,1792]{1,0:T(8,128)(2,1)}) custom-call(bf16[1024,1792]{1,0:T(8,128)(2,1)} %copy-done.93, bf16[1024,16]{1,0:T(8,128)(2,1)S(1)} %copy-done.15, bf16[16,4224]{1,0:T(8,128)(2,1)S(1)} %copy-done.50, bf16[128,1280]{1,0:T(8,128)(2,1)S(1)} %copy-done.11, ...), custom_call_target="tpu_custom_call" | custom-call | flops 100000000 | bytes 300000 | tf_op jit(solution)/shard_map/project/pallas_call | solution.py:248
  264.6 13.7 %collective-permute-done.27 = bf16[912,896]{1,0:T(8,128)(2,1)S(1)} collective-permute-done((bf16[912,896]{1,0:T(8,128)(2,1)}, bf16[912,896]{1,0:T(8,128)(2,1)S(1)}, u32[]{:S(2)}, u32[]{:S(2)}) %collective-permute-start.27) | collective-permute-done | bytes 1634336 | tf_op jit(solution)/shard_map/ppermute | solution.py:1040
  290.6 7.3 attend.4
  342.0 10.4 %mix_out.1 = (bf16[1024,1792]{1,0:T(8,128)(2,1)}, f32[1024,16]{1,0:T(8,128)S(1)}, bf16[1024,1792]{1,0:T(8,128)(2,1)}) custom-call(bf16[1024,256]{1,0:T(8,128)(2,1)S(1)} %copy-done.65, bf16[1024,256]{1,0:T(8,128)(2,1)S(1)} %copy-done.67, bf16[1024,256]{1,0:T(8,128)(2,1)S(1)} %get-tuple-element.268.refs_2_.refs_13_, ...), custom_call_target="tpu_custom_call" | custom-call | flops 100000000 | bytes 300000 | tf_op jit(solution)/shard_map/mix_out/pallas_call | solution.py:417
  368.0 7.7 norm_two.1
  378.3 46.3 %feed.3 = (f32[1024,1792]{1,0:T(8,128)}, f32[1024,1792]{1,0:T(8,128)}, f32[1024,32]{1,0:T(8,128)}, bf16[16,1280]{1,0:T(8,128)(2,1)}, bf16[16,1280]{1,0:T(8,128)(...) custom-call(bf16[1024,1792]{1,0:T(8,128)(2,1)} %copy-done.9, ...), custom_call_target="tpu_custom_call" | custom-call | flops 100000000 | bytes 300000 | tf_op jit(solution)/shard_map/feed/pallas_call | solution.py:525
  431.7 28.3 %feed.4 = (f32[1024,1792]{1,0:T(8,128)}, f32[1024,1792]{1,0:T(8,128)}, f32[1024,32]{1,0:T(8,128)}, bf16[16,1280]{1,0:T(8,128)(2,1)}, bf16[16,640]{1,0:T(8,128)(2,1)}) custom-call(bf16[1024,1792]{1,0:T(8,128)(2,1)} %copy-done.9, bf16[1024,1792]{1,0:T(8,128)(2,1)} %get-tuple-element.277.refs_1_.upstream, bf16[1024,16]{1,0:T(8,128)(2,1)} %copy-done.69, ...), custom_call_target="tpu_custom_call" | custom-call | flops 100000000 | bytes 300000 | tf_op jit(solution)/shard_map/feed/pallas_call | solution.py:525
  461.2 29.7 %feed.5 = (bf16[1024,1792]{1,0:T(8,128)(2,1)}, bf16[1024,1792]{1,0:T(8,128)(2,1)}, f32[1024,32]{1,0:T(8,128)}, bf16[16,1280]{1,0:T(8,128)(2,1)}, bf16[16,640]{1,0:T(8,128)(2,1)}) custom-call(bf16[1024,1792]{1,0:T(8,128)(2,1)} %copy-done.9, bf16[1024,1792]{1,0:T(8,128)(2,1)} %get-tuple-element.277.refs_1_.upstream, bf16[1024,16]{1,0:T(8,128)(2,1)} %copy-done.69, ...), custom_call_target="tpu_custom_call" | custom-call | flops 100000000 | bytes 300000 | tf_op jit(solution)/shard_map/feed/pallas_call | solution.py:525
  506.7 7.8 back_two.1
  517.1 20.4 %turn.1 = (bf16[1024,1024]{1,0:T(8,128)(2,1)}, bf16[1024,1024]{1,0:T(8,128)(2,1)}, bf16[4,320,128]{2,1,0:T(8,128)(2,1)}, bf16[4,320,128]{2,1,0:T(8,128)(2,1)}, bf16[4,16,256]{2,1,0:T(8,128)(2,1)}) custom-call(bf16[1024,1792]{1,0:T(8,128)(2,1)} %copy-done.18, bf16[1024,16]{1,0:T(8,128)(2,1)} %copy-done.92, bf16[1024,1792]{1,0:T(8,128)(2,1)} %get-tuple-element.306.refs_2_, ...), custom_call_target="tpu_custom_call" | custom-call | flops 100000000 | bytes 300000 | tf_op jit(solution)/shard_map/turn/pallas_call | solution.py:637
  563.2 16.8 %attend_back.4 = (bf16[1024,1792]{1,0:T(8,128)(2,1)}, f32[1024,16]{1,0:T(8,128)S(1)}, bf16[16,1792]{1,0:T(8,128)(2,1)S(1)}) custom-call(bf16[1024,1792]{1,0:T(8,128)(2,1)} %copy-done.2, bf16[4,160,128]{2,1,0:T(8,128)(2,1)S(1)} %copy-done.34, bf16[2,4,256,128]{3,2,1,0:T(8,128)(2,1)S(1)} %copy-done.89, f32[4,160,128]{2,1,0:T(8,128)S(1)} %select_add_fusion.1.later, ...), custom_call_target="tpu_custom_call" | custom-call | flops 100000000 | bytes 300000 | tf_op jit(solution)/shard_map/attend_back/pallas_call | solution.py:774
  580.6 16.3 %attend_back.7 = (bf16[5,16,1792]{2,1,0:T(8,128)(2,1)}, bf16[1024,1792]{1,0:T(8,128)(2,1)}, f32[1024,16]{1,0:T(8,128)S(1)}) fusion(bf16[5,16,1792]{2,1,0:T(8,128)(2,1)} %bitcast_dynamic-update-slice_fusion.11, bf16[1024,1792]{1,0:T(8,128)(2,1)S(1)} %copy-done.6, bf16[4,160,128]{2,1,0:T(8,128)(2,1)S(1)} %copy-done.34, ...), kind=kCustom, calls=%fused_computation.139 | custom fusion | flops 100000000 | bytes 13332480 | tf_op jit(solution)/shard_map/attend_back/pallas_call | solution.py:774
  604.7 17.0 %attend_back.6 = (bf16[5,16,1792]{2,1,0:T(8,128)(2,1)}, bf16[1024,1792]{1,0:T(8,128)(2,1)}, f32[1024,16]{1,0:T(8,128)S(1)}) fusion(bf16[5,16,1792]{2,1,0:T(8,128)(2,1)} %get-tuple-element.419, bf16[1024,1792]{1,0:T(8,128)(2,1)} %get-tuple-element.264.proj.refs_19_.refs_20_.refs_25_, bf16[4,160,128]{2,1,0:T(8,128)(2,1)S(1)} %copy-done.62, ...), kind=kCustom, calls=%fused_computation.138 | custom fusion | flops 100000000 | bytes 13332480 | tf_op jit(solution)/shard_map/attend_back/pallas_call | solution.py:774
  632.7 17.0 %attend_back.5 = (bf16[5,16,1792]{2,1,0:T(8,128)(2,1)}, bf16[1024,1792]{1,0:T(8,128)(2,1)}, f32[1024,16]{1,0:T(8,128)S(1)}) fusion(bf16[5,16,1792]{2,1,0:T(8,128)(2,1)} %get-tuple-element.413, bf16[1024,1792]{1,0:T(8,128)(2,1)} %get-tuple-element.269.proj.refs_21_.refs_22_.refs_26_, bf16[4,160,128]{2,1,0:T(8,128)(2,1)S(1)} %copy-done.62, ...), kind=kCustom, calls=%fused_computation.137 | custom fusion | flops 100000000 | bytes 13332480 | tf_op jit(solution)/shard_map/attend_back/pallas_call | solution.py:774
  664.0 24.0 %first_back.2.refs_0_ = bf16[2,256,1792]{2,1,0:T(8,128)(2,1)} custom-call(bf16[2,512,1792]{2,1,0:T(8,128)(2,1)} %bitcast.212, bf16[2,512,1792]{2,1,0:T(8,128)(2,1)} %bitcast.204, bf16[2,512,1792]{2,1,0:T(8,128)(2,1)} %bitcast.206, bf16[2,512,1792]{2,1,0:T(8,128)(2,1)} %bitcast.208, f32[2,512,16]{2,1,0:T(8,128)} %bitcast.210, ...), custom_call_target="tpu_custom_call" | custom-call | flops 100000000 | bytes 300000 | tf_op jit(solution)/shard_map/first_back/pallas_call | solution.py:842
  710.1 23.9 %first_back.3.refs_2_ = bf16[2,256,1792]{2,1,0:T(8,128)(2,1)} custom-call(bf16[2,512,1792]{2,1,0:T(8,128)(2,1)} %bitcast.213, bf16[2,512,1792]{2,1,0:T(8,128)(2,1)} %bitcast.205, bf16[2,512,1792]{2,1,0:T(8,128)(2,1)} %bitcast.207, bf16[2,512,1792]{2,1,0:T(8,128)(2,1)} %bitcast.209, f32[2,512,16]{2,1,0:T(8,128)} %get-tuple-element.373.refs_4_, ...), custom_call_target="tpu_custom_call" | custom-call | flops 100000000 | bytes 300000 | tf_op jit(solution)/shard_map/first_back/pallas_call | solution.py:842
  767.5 18.6 %collective-permute-done.71.refs_2_ = bf16[256,1792]{1,0:T(8,128)(2,1)S(1)} collective-permute-done((bf16[256,1792]{1,0:T(8,128)(2,1)}, bf16[256,1792]{1,0:T(8,128)(2,1)S(1)}, u32[]{:S(2)}, u32[]{:S(2)}) %collective-permute-start.71) | collective-permute-done | bytes 917536 | tf_op jit(solution)/shard_map/ppermute | solution.py:994
  812.4 18.4 %collective-permute-done.76.refs_2_ = bf16[256,1792]{1,0:T(8,128)(2,1)S(1)} collective-permute-done((bf16[256,1792]{1,0:T(8,128)(2,1)}, bf16[256,1792]{1,0:T(8,128)(2,1)S(1)}, u32[]{:S(2)}, u32[]{:S(2)}) %collective-permute-start.76) | collective-permute-done | bytes 917536 | tf_op jit(solution)/shard_map/ppermute | solution.py:1040
  836.6 18.4 %collective-permute-done.77 = bf16[256,1792]{1,0:T(8,128)(2,1)S(1)} collective-permute-done((bf16[256,1792]{1,0:T(8,128)(2,1)}, bf16[256,1792]{1,0:T(8,128)(2,1)S(1)}, u32[]{:S(2)}, u32[]{:S(2)}) %collective-permute-start.77) | collective-permute-done | bytes 917536 | tf_op jit(solution)/shard_map/ppermute | solution.py:1040
  (660 shorter events, 396.3 us)
Async XLA Ops:
  7.2 226.6 %all-gather.5.cloned.1.call-start = ((), (), s32[]{:S(2)}) async-start(), calls=%async_computation | async-start | bytes 1638400 | tf_op jit(solution)/shard_map/all_gather | solution.py:1310
  10.0 39.3 %collective-permute-start.2 = (bf16[816,896]{1,0:T(8,128)(2,1)}, bf16[816,896]{1,0:T(8,128)(2,1)S(1)}, u32[]{:S(2)}, u32[]{:S(2)}) collective-permute-start(bf16[816,896]{1,0:T(8,128)(2,1)} %pad_maximum_fusion.3), channel_id=1, source_target_pairs={{0,1},{1,0},{2,3},{3,2},{4,5},{5,4},{6,7},{7,6},{8,9},{9,8},{10,11... | collective-permute-start | bytes 4386824 | tf_op jit(solution)/shard_map/ppermute | solution.py:994
  50.5 44.3 %collective-permute-start.4 = (bf16[816,896]{1,0:T(8,128)(2,1)}, bf16[816,896]{1,0:T(8,128)(2,1)S(1)}, u32[]{:S(2)}, u32[]{:S(2)}) collective-permute-start(bf16[816,896]{1,0:T(8,128)(2,1)} %get-tuple-element.214.rest_0_.refs_10_), channel_id=1, source_target_pairs={{0,8},{8,0},{16,24},{24,16},{1,9},{9,1},{17,25},{25,17},{2,10},{10... | collective-permute-start | bytes 4386824 | tf_op jit(solution)/shard_map/ppermute | solution.py:990
  52.0 42.8 %collective-permute-start.5 = (bf16[816,896]{1,0:T(8,128)(2,1)}, bf16[816,896]{1,0:T(8,128)(2,1)}, u32[]{:S(2)}, u32[]{:S(2)}) collective-permute-start(bf16[816,896]{1,0:T(8,128)(2,1)} %get-tuple-element.214.rest_0_.refs_10_), channel_id=1, source_target_pairs={{0,16},{8,24},{16,0},{24,8},{1,17},{9,25},{17,1},{25,9},{2,18},{10... | collective-permute-start | bytes 4386824 | tf_op jit(solution)/shard_map/ppermute | solution.py:990
  95.9 50.5 %collective-permute-start.9 = (bf16[816,896]{1,0:T(8,128)(2,1)}, bf16[816,896]{1,0:T(8,128)(2,1)S(1)}, u32[]{:S(2)}, u32[]{:S(2)}) collective-permute-start(bf16[816,896]{1,0:T(8,128)(2,1)} %get-tuple-element.217.rest_0_.refs_15_), channel_id=1, source_target_pairs={{0,8},{8,0},{16,24},{24,16},{1,9},{9,1},{17,25},{25,17},{2,10},{10... | collective-permute-start | bytes 4386824 | tf_op jit(solution)/shard_map/ppermute | solution.py:990
  96.4 50.0 %collective-permute-start.10 = (bf16[816,896]{1,0:T(8,128)(2,1)}, bf16[816,896]{1,0:T(8,128)(2,1)}, u32[]{:S(2)}, u32[]{:S(2)}) collective-permute-start(bf16[816,896]{1,0:T(8,128)(2,1)} %get-tuple-element.217.rest_0_.refs_15_), channel_id=1, source_target_pairs={{0,16},{8,24},{16,0},{24,8},{1,17},{9,25},{17,1},{25,9},{2,18},{10... | collective-permute-start | bytes 4386824 | tf_op jit(solution)/shard_map/ppermute | solution.py:990
  106.3 40.1 %collective-permute-start.15 = (bf16[448,896]{1,0:T(8,128)(2,1)}, bf16[448,896]{1,0:T(8,128)(2,1)S(1)}, u32[]{:S(2)}, u32[]{:S(2)}) collective-permute-start(bf16[448,896]{1,0:T(8,128)(2,1)} %slice.168), channel_id=1, source_target_pairs={{0,16},{8,24},{16,0},{24,8},{1,17},{9,25},{17,1},{25,9},{2,18},{10... | collective-permute-start | bytes 2408456 | tf_op jit(solution)/shard_map/ppermute | solution.py:990
  147.7 51.6 %collective-permute-start.18 = (bf16[912,896]{1,0:T(8,128)(2,1)}, bf16[912,896]{1,0:T(8,128)(2,1)S(1)}, u32[]{:S(2)}, u32[]{:S(2)}) collective-permute-start(bf16[912,896]{1,0:T(8,128)(2,1)} %get-tuple-element.227), channel_id=1, source_target_pairs={{0,1},{1,0},{2,3},{3,2},{4,5},{5,4},{6,7},{7,6},{8,9},{9,8},{10,11... | collective-permute-start | bytes 4902920 | tf_op jit(solution)/shard_map/ppermute | solution.py:994
  147.8 50.3 %collective-permute-start.16 = (bf16[816,896]{1,0:T(8,128)(2,1)}, bf16[816,896]{1,0:T(8,128)(2,1)S(1)}, u32[]{:S(2)}, u32[]{:S(2)}) collective-permute-start(bf16[816,896]{1,0:T(8,128)(2,1)} %get-tuple-element.226.rest_0_.refs_20_), channel_id=1, source_target_pairs={{0,8},{8,0},{16,24},{24,16},{1,9},{9,1},{17,25},{25,17},{2,10},{10... | collective-permute-start | bytes 4386824 | tf_op jit(solution)/shard_map/ppermute | solution.py:990
  149.4 48.8 %collective-permute-start.17 = (bf16[816,896]{1,0:T(8,128)(2,1)}, bf16[816,896]{1,0:T(8,128)(2,1)S(1)}, u32[]{:S(2)}, u32[]{:S(2)}) collective-permute-start(bf16[816,896]{1,0:T(8,128)(2,1)} %get-tuple-element.226.rest_0_.refs_20_), channel_id=1, source_target_pairs={{0,16},{8,24},{16,0},{24,8},{1,17},{9,25},{17,1},{25,9},{2,18},{10... | collective-permute-start | bytes 4386824 | tf_op jit(solution)/shard_map/ppermute | solution.py:990
  151.1 47.0 %collective-permute-start.20 = (bf16[448,896]{1,0:T(8,128)(2,1)S(1)}, bf16[448,896]{1,0:T(8,128)(2,1)S(1)}, u32[]{:S(2)}, u32[]{:S(2)}) collective-permute-start(bf16[448,896]{1,0:T(8,128)(2,1)S(1)} %slice.170), channel_id=1, source_target_pairs={{0,16},{8,24},{16,0},{24,8},{1,17},{9,25},{17,1},{25,9},{2,18},{10... | collective-permute-start | bytes 2408456 | tf_op jit(solution)/shard_map/ppermute | solution.py:990
  153.8 40.0 %collective-permute-start.19 = (bf16[368,896]{1,0:T(8,128)(2,1)S(1)}, bf16[368,896]{1,0:T(8,128)(2,1)S(1)}, u32[]{:S(2)}, u32[]{:S(2)}) collective-permute-start(bf16[368,896]{1,0:T(8,128)(2,1)S(1)} %slice.169), channel_id=1, source_target_pairs={{0,8},{8,0},{16,24},{24,16},{1,9},{9,1},{17,25},{25,17},{2,10},{10... | collective-permute-start | bytes 1978376 | tf_op jit(solution)/shard_map/ppermute | solution.py:990
  202.4 485.8 %all-gather.7.cloned.1.call-start = ((), (), s32[]{:S(2)}) async-start(), calls=%async_computation.1 | async-start | bytes 9175040 | tf_op jit(solution)/shard_map/all_gather | solution.py:1382
  209.4 55.2 %collective-permute-start.26 = (bf16[912,896]{1,0:T(8,128)(2,1)}, bf16[912,896]{1,0:T(8,128)(2,1)}, u32[]{:S(2)}, u32[]{:S(2)}) collective-permute-start(bf16[912,896]{1,0:T(8,128)(2,1)} %get-tuple-element.248.refs_10_), channel_id=1, source_target_pairs={{1,2},{2,1},{5,6},{6,5},{9,10},{10,9},{13,14},{14,13},{17,18},{18,... | collective-permute-start | bytes 4902920 | tf_op jit(solution)/shard_map/ppermute | solution.py:1036
  238.4 39.9 %collective-permute-start.27 = (bf16[912,896]{1,0:T(8,128)(2,1)}, bf16[912,896]{1,0:T(8,128)(2,1)S(1)}, u32[]{:S(2)}, u32[]{:S(2)}) collective-permute-start(bf16[912,896]{1,0:T(8,128)(2,1)} %get-tuple-element.249.refs_4_), channel_id=1, source_target_pairs={{1,0},{2,3},{5,4},{6,7},{9,8},{10,11},{13,12},{14,15},{17,16},{18,... | collective-permute-start | bytes 4902920 | tf_op jit(solution)/shard_map/ppermute | solution.py:1040
  240.2 39.4 %collective-permute-start.24 = (bf16[912,896]{1,0:T(8,128)(2,1)}, bf16[912,896]{1,0:T(8,128)(2,1)S(1)}, u32[]{:S(2)}, u32[]{:S(2)}) collective-permute-start(bf16[912,896]{1,0:T(8,128)(2,1)} %get-tuple-element.248.refs_10_), channel_id=1, source_target_pairs={{0,8},{8,0},{16,24},{24,16},{1,9},{9,1},{17,25},{25,17},{2,10},{10... | collective-permute-start | bytes 4902920 | tf_op jit(solution)/shard_map/ppermute | solution.py:990
  355.5 69.1 %collective-permute-start.37 = (bf16[912,896]{1,0:T(8,128)(2,1)}, bf16[912,896]{1,0:T(8,128)(2,1)}, u32[]{:S(2)}, u32[]{:S(2)}) collective-permute-start(bf16[912,896]{1,0:T(8,128)(2,1)} %get-tuple-element.280.refs_7_), channel_id=1, source_target_pairs={{0,8},{8,0},{16,24},{24,16},{1,9},{9,1},{17,25},{25,17},{2,10},{10... | collective-permute-start | bytes 4902920 | tf_op jit(solution)/shard_map/ppermute | solution.py:990
  356.4 68.2 %collective-permute-start.38 = (bf16[912,896]{1,0:T(8,128)(2,1)}, bf16[912,896]{1,0:T(8,128)(2,1)S(1)}, u32[]{:S(2)}, u32[]{:S(2)}) collective-permute-start(bf16[912,896]{1,0:T(8,128)(2,1)} %get-tuple-element.280.refs_7_), channel_id=1, source_target_pairs={{0,16},{8,24},{16,0},{24,8},{1,17},{9,25},{17,1},{25,9},{2,18},{10... | collective-permute-start | bytes 4902920 | tf_op jit(solution)/shard_map/ppermute | solution.py:990
  361.4 63.2 %collective-permute-start.39 = (bf16[464,896]{1,0:T(8,128)(2,1)}, bf16[464,896]{1,0:T(8,128)(2,1)}, u32[]{:S(2)}, u32[]{:S(2)}) collective-permute-start(bf16[464,896]{1,0:T(8,128)(2,1)} %slice.181), channel_id=1, source_target_pairs={{0,8},{8,0},{16,24},{24,16},{1,9},{9,1},{17,25},{25,17},{2,10},{10... | collective-permute-start | bytes 2494472 | tf_op jit(solution)/shard_map/ppermute | solution.py:990
  364.2 60.4 %collective-permute-start.40 = (bf16[448,896]{1,0:T(8,128)(2,1)}, bf16[448,896]{1,0:T(8,128)(2,1)}, u32[]{:S(2)}, u32[]{:S(2)}) collective-permute-start(bf16[448,896]{1,0:T(8,128)(2,1)} %slice.182), channel_id=1, source_target_pairs={{0,16},{8,24},{16,0},{24,8},{1,17},{9,25},{17,1},{25,9},{2,18},{10... | collective-permute-start | bytes 2408456 | tf_op jit(solution)/shard_map/ppermute | solution.py:990
  555.1 42.7 %collective-permute-start.50 = (bf16[4,320,128]{2,1,0:T(8,128)(2,1)}, bf16[4,320,128]{2,1,0:T(8,128)(2,1)}, u32[]{:S(2)}, u32[]{:S(2)}) collective-permute-start(bf16[4,320,128]{2,1,0:T(8,128)(2,1)} %get-tuple-element.342), channel_id=1, source_target_pairs={{0,8},{8,0},{16,24},{24,16},{1,9},{9,1},{17,25},{25,17},{2,10},{10... | collective-permute-start | bytes 983048 | tf_op jit(solution)/shard_map/ppermute | solution.py:990
  556.4 41.4 %collective-permute-start.51 = (bf16[4,320,128]{2,1,0:T(8,128)(2,1)}, bf16[4,320,128]{2,1,0:T(8,128)(2,1)}, u32[]{:S(2)}, u32[]{:S(2)}) collective-permute-start(bf16[4,320,128]{2,1,0:T(8,128)(2,1)} %get-tuple-element.342), channel_id=1, source_target_pairs={{0,16},{8,24},{16,0},{24,8},{1,17},{9,25},{17,1},{25,9},{2,18},{10... | collective-permute-start | bytes 983048 | tf_op jit(solution)/shard_map/ppermute | solution.py:990
  557.0 40.8 %collective-permute-start.52 = (bf16[4,320,128]{2,1,0:T(8,128)(2,1)}, bf16[4,320,128]{2,1,0:T(8,128)(2,1)}, u32[]{:S(2)}, u32[]{:S(2)}) collective-permute-start(bf16[4,320,128]{2,1,0:T(8,128)(2,1)} %get-tuple-element.342), channel_id=1, source_target_pairs={{0,24},{8,16},{16,8},{24,0},{1,25},{9,17},{17,9},{25,1},{2,26},{10... | collective-permute-start | bytes 983048 | tf_op jit(solution)/shard_map/ppermute | solution.py:990
  789.0 41.7 %collective-permute-start.76 = (bf16[256,1792]{1,0:T(8,128)(2,1)}, bf16[256,1792]{1,0:T(8,128)(2,1)S(1)}, u32[]{:S(2)}, u32[]{:S(2)}) collective-permute-start(bf16[256,1792]{1,0:T(8,128)(2,1)} %get-tuple-element.399), channel_id=1, source_target_pairs={{1,0},{2,3},{5,4},{6,7},{9,8},{10,11},{13,12},{14,15},{17,16},{18,... | collective-permute-start | bytes 2752520 | tf_op jit(solution)/shard_map/ppermute | solution.py:1040
  (223 other events, 2492.0 us)
Sparse Core Ops, SparseCore 0:
  202.5 31.1 all-gather.4
  504.8 138.1 all-gather.6

commit v6 on v5

--- a/solution.py
+++ b/solution.py
@@ -25,6 +25,7 @@
 QB = 128
 BACK_QB = 256
 BACK_CHUNK = 512
+ATT = 512
 PACK = STATE + 2 * WIN + 32
 
 epsilon = 1e-05
@@ -302,12 +303,12 @@
     conv[16:, :] = proj[:, 5 * PD : 6 * PD].astype(f32)
     tap = head_taps(spots, table)
     state = whole_state(prior[0])
-    causal = causal_mask(CHUNK)
+    causal = causal_mask(ATT)
     first_mask, mask = window_masks(QB)
-    for chunk in range(rows // CHUNK):
+    for chunk in range(rows // ATT):
         states[0, chunk] = state.astype(bf16)
-        at = chunk * CHUNK
-        span = slice(at, at + CHUNK)
+        at = chunk * ATT
+        span = slice(at, at + ATT)
         base = proj[span, 0:PD]
         value = proj[span, PD : 2 * PD]
         picked = nn(base, pick[:, :1152])
@@ -315,11 +316,11 @@
         score = nt(base, picked[:, 1024:1152].astype(bf16))
         weight = jnp.where(causal, 1.0 + score + 0.5 * score * score, 0.0).astype(bf16)
         total = nn(weight, value) + nn(feat_q, state.astype(bf16))
-        if at + CHUNK < rows:
+        if at + ATT < rows:
             _, _, feat_k = features(picked, 512)
             state = state + tn(feat_k, value)
         parts = []
-        for number in range(chunk * CHUNK // QB, (chunk + 1) * CHUNK // QB):
+        for number in range(chunk * ATT // QB, (chunk + 1) * ATT // QB):
             query = proj[number * QB : (number + 1) * QB, 2 * PD : 3 * PD]
             allowed = mask if number else first_mask
             prob = window_prob(query, keys[number * QB : number * QB + QB + WIN, :], allowed)
@@ -327,7 +328,7 @@
         window = jnp.concatenate(parts, 0)
         scale = lax.rsqrt(jnp.sum(total * total, -1, keepdims=True) * (1.0 / HD) + epsilon)
         gate = proj[span, 6 * PD : 7 * PD].astype(f32)
-        branch = conv_of(conv, tap, at, CHUNK) * (gate * jax.nn.sigmoid(gate))
+        branch = conv_of(conv, tap, at, ATT) * (gate * jax.nn.sigmoid(gate))
         mixed[span, :] = (total * scale + window + branch).astype(bf16)
         numer[span, :] = total.astype(bf16)
 
@@ -350,7 +351,7 @@
         out_shape=(
             jax.ShapeDtypeStruct((rows, 2 * PD), bf16),
             jax.ShapeDtypeStruct((rows, 2 * PD), bf16),
-            jax.ShapeDtypeStruct((2, rows // CHUNK, 256, PD), bf16),
+            jax.ShapeDtypeStruct((2, rows // ATT, 256, PD), bf16),
         ),
         in_specs=[
             pl.BlockSpec((rows, HEAD_PAD), lambda h: (0, h)),
@@ -362,7 +363,7 @@
         out_specs=(
             pl.BlockSpec((rows, PD), lambda h: (0, h)),
             pl.BlockSpec((rows, PD), lambda h: (0, h)),
-            pl.BlockSpec((1, rows // CHUNK, 256, PD), lambda h: (h, 0, 0, 0)),
+            pl.BlockSpec((1, rows // ATT, 256, PD), lambda h: (h, 0, 0, 0)),
         ),
         scratch_shapes=[
             pltpu.VMEM((rows + WIN, PD), bf16),
@@ -725,7 +726,7 @@
         weight = jnp.where(causal, 1.0 + score + 0.5 * score * score, 0.0).astype(bf16)
         slope = jnp.where(causal, nt(grad, value) * (1.0 + score), 0.0).astype(bf16)
         follow_round = follow.astype(bf16)
-        q_up = nt(grad, states[0, chunk * (BACK_CHUNK // CHUNK)])
+        q_up = nt(grad, states[0, chunk * (BACK_CHUNK // ATT)])
         k_up = nt(value, follow_round)
         inside = [q_up * q_two, q_up * q_one, k_up * k_two, k_up * k_one]
         inside = jnp.concatenate([part.astype(bf16) for part in inside], 1)
@@ -782,7 +783,7 @@
         in_specs=[
             head,
             edge,
-            pl.BlockSpec((1, rows // CHUNK, 256, PD), lambda h: (h, 0, 0, 0)),
+            pl.BlockSpec((1, rows // ATT, 256, PD), lambda h: (h, 0, 0, 0)),
             state,
             edge,
             column,
@@ -810,11 +811,11 @@
     )(proj, tails, states, later, lent, ups, grads, table, rank, *tables)
 
 
-def first_back_kernel(*refs):
+def first_back_kernel(core, *refs):
     grads = refs[0:4]
     rank_grad, left = refs[4:6]
     sources = refs[6:10]
-    part, weight, sems = refs[10:]
+    own, sibling, weight, sems = refs[10:]
     size = 2 * HEAD_PAD
     copies = [(sources[n], weight.at[size * n : size * (n + 1)]) for n in range(SLOTS)]
     begin = pl.program_id(0) == 0
@@ -831,27 +832,43 @@
             wait_copies(copies[slot : slot + 1], sems, slot)
 
         total = total + nn(grads[slot][0], weight[size * slot : size * (slot + 1), :])
-    part[0] = total.astype(bf16)
-
-
-def first_back(start, count, grads, rank_grad, left, sources):
-    cores, _, size = grads[0].shape
+
+    @pl.when(begin)
+    def _():
+        own[...] = total.astype(bf16)
+
+    @pl.when(jnp.logical_not(begin))
+    def _():
+        sibling[...] = total.astype(bf16)
+
+
+def first_back(core, start, count, grads, rank_grad, left, sources):
+    _, _, size = grads[0].shape
     width = left.shape[1]
-    whole = lambda a: pl.BlockSpec(a.shape, lambda i: (0,) * a.ndim)
-    span = lambda cols: pl.BlockSpec((1, count, cols), lambda i: (i, start // count, 0))
+    whole = lambda a: pl.BlockSpec(a.shape, lambda i, c: (0,) * a.ndim)
+    span = lambda cols: pl.BlockSpec(
+        (1, count, cols), lambda i, c: (lax.rem(c[0] + i, 2), start // count, 0)
+    )
+    flat = pl.BlockSpec((count, width), lambda i, c: (0, 0))
     return pl.pallas_call(
         first_back_kernel,
-        grid=(cores,),
-        out_shape=jax.ShapeDtypeStruct((cores, count, width), bf16),
-        in_specs=[span(size)] * 4 + [span(R), whole(left)] + [ANY] * len(sources),
-        out_specs=pl.BlockSpec((1, count, width), lambda i: (i, 0, 0)),
-        scratch_shapes=[pltpu.VMEM((SLOTS * size, width), bf16), pltpu.SemaphoreType.DMA((SLOTS,))],
+        out_shape=(jax.ShapeDtypeStruct((count, width), bf16),) * 2,
+        grid_spec=pltpu.PrefetchScalarGridSpec(
+            num_scalar_prefetch=1,
+            grid=(2,),
+            in_specs=[span(size)] * 4 + [span(R), whole(left)] + [ANY] * len(sources),
+            out_specs=(flat, flat),
+            scratch_shapes=[
+                pltpu.VMEM((SLOTS * size, width), bf16),
+                pltpu.SemaphoreType.DMA((SLOTS,)),
+            ],
+        ),
         compiler_params=params(56),
         cost_estimate=pl.CostEstimate(
             flops=100_000_000, bytes_accessed=300_000, transcendentals=0
         ),
         name="first_back",
-    )(*grads, rank_grad, left, *sources)
+    )(core, *grads, rank_grad, left, *sources)
 
 
 def norm_two_kernel(own, other, wide, gain, left, middle, second, rank):
@@ -1466,15 +1483,14 @@
     count_a = length // 2
     count_b = length - count_a
     rank_rows = rank_grad.reshape(2, length, R)
-    part_a = first_back(0, count_a, proj_grads, rank_rows, left_t, wides)
-    part_a, rank_rows, early, early_other, *mixer_x = hold(
-        part_a, rank_rows, early, early_other, *mixer_x, after=(block_output,)
+    core_array = jnp.reshape(core, (1,)).astype(jnp.int32)
+    here_a, there_a = first_back(core_array, 0, count_a, proj_grads, rank_rows, left_t, wides)
+    here_a, there_a, rank_rows, early, early_other, *mixer_x = hold(
+        here_a, there_a, rank_rows, early, early_other, *mixer_x, after=(block_output,)
     )
     mixer_all = plane_sum(mixer_all, mixer_x)
 
-    def finish(part, start, count):
-        here = lax.dynamic_index_in_dim(part, core, 0, False)
-        there = lax.dynamic_index_in_dim(part, 1 - core, 0, False)
+    def finish(here, there, start, count):
         total = here.astype(f32) + swap_core(there).astype(f32)
         wide = own_input[start : start + count].astype(f32)
         scale_one = lax.rsqrt(jnp.mean(wide * wide, -1, keepdims=True) + epsilon)
@@ -1483,15 +1499,15 @@
         ).astype(f32)
         return (straight + norm_back(wide, scale_one, gain_one, total)).astype(bf16)
 
-    done_a = finish(part_a, 0, count_a)
+    done_a = finish(here_a, there_a, 0, count_a)
     e_a, c_a = swap_tp(done_a, 1), cross(done_a)
     late = packs_of(mixer_all[:SLOTS], mixer_all[SLOTS:])
     late = [late[0]] + [swap_tp(late[bit], bit) for bit in (1, 2, 3)]
-    part_b = first_back(count_a, count_b, proj_grads, rank_rows, left_t, wides)
-    e_a, c_a, part_b, *late = hold(e_a, c_a, part_b, *late)
+    here_b, there_b = first_back(core_array, count_a, count_b, proj_grads, rank_rows, left_t, wides)
+    e_a, c_a, here_b, there_b, *late = hold(e_a, c_a, here_b, there_b, *late)
     late = jnp.stack(late)
     c2_a, f_a = cross(e_a), edge(c_a)
-    done_b = finish(part_b, count_a, count_b)
+    done_b = finish(here_b, there_b, count_a, count_b)
     done_b, early, early_other, late, block_output = hold(
         done_b, early, early_other, late, block_output
     )

time: 874 us -> 866 us (level)
    unnamed x339 -> x341, local copies, waits for them, and re-layouts: 52 us -> 50.4 us
  transfers between devices with their start and end apart: 80 -> 80, of which waited for: 21 -> 23; matrix products, arithmetic and copies ran while one was open for 22% -> 22% of each run, Pallas kernels for 35% -> 35%
where the time goes in v6:
time: 866 us; the launch traced here: 856 us
  Pallas kernels  332 us (38%)
  waiting for transfers between devices  158 us (18%)
  other arithmetic  134 us (15%)
  local copies, waits for them, and re-layouts  103 us (12%)
  starting transfers between devices  101 us (12%)
  between operations  16.9 us (2%)
  matrix products  12.5 us (1%)
    pallas_call x3, Pallas kernels, feed(): pl.pallas_call(functools.partial(feed_kernel, slots, last, half, pad, spo...  104 us
    ppermute x8, waiting for transfers between devices, edge(): return lax.ppermute(array, 'tp', [(1, 0), (2, 3)])  82.3 us
    pallas_call x4, Pallas kernels, project(): pl.pallas_call(functools.partial(project_kernel, own), out_shape=(jax.Sha...  74.4 us
    unnamed x341, local copies, waits for them, and re-layouts  50.4 us
    pallas_call x3, other arithmetic, attend_back(): pl.pallas_call(functools.partial(attend_back_kernel, spots), grid=(2,), o...  50.1 us
    pallas_call x2, Pallas kernels, first_back(): pl.pallas_call(first_back_kernel, out_shape=(jax.ShapeDtypeStruct((count,...  48.7 us
    ppermute x40, starting transfers between devices, swap_chip(): return lax.ppermute(array, 'chip', [(i, i ^ bit) for i in range(count)])  44.7 us
    ppermute x40, waiting for transfers between devices, swap_chip(): return lax.ppermute(array, 'chip', [(i, i ^ bit) for i in range(count)])  40.9 us
  transfers between devices with their start and end apart: 80, of which 23 were waited for; matrix products, arithmetic and copies ran while one was open for 22% of the time, Pallas kernels for 35%

profile of v6, /device:TPU:0, one launch (start us, length us, event | category | flops | bytes accessed | tf_op | source)
XLA Modules:
  0.0 856.1 jit_solution(111124458632304357)
XLA Ops:
  62.3 18.2 %project.4 = (bf16[1024,1792]{1,0:T(8,128)(2,1)S(1)}, bf16[2,320,128]{2,1,0:T(8,128)(2,1)S(1)}, bf16[1792,1792]{1,0:T(8,128)(2,1)}) custom-call(bf16[1024,1792]{1,0:T(8,128)(2,1)} %copy-done.93, bf16[1024,16]{1,0:T(8,128)(2,1)S(1)} %copy-done.14, bf16[16,4224]{1,0:T(8,128)(2,1)S(1)} %get-tuple-element.455.table.refs_4_.refs_6_.refs_3_, ...), custom_call_target="tpu_custom_call" | custom-call | flops 100000000 | bytes 300000 | tf_op jit(solution)/shard_map/project/pallas_call | solution.py:249
  118.0 16.3 %collective-permute-done.11 = bf16[816,896]{1,0:T(8,128)(2,1)} collective-permute-done((bf16[816,896]{1,0:T(8,128)(2,1)}, bf16[816,896]{1,0:T(8,128)(2,1)}, u32[]{:S(2)}, u32[]{:S(2)}) %collective-permute-start.11) | collective-permute-done | bytes 1462304 | tf_op jit(solution)/shard_map/ppermute | solution.py:1057
  156.8 18.7 %project.5 = (bf16[1024,1792]{1,0:T(8,128)(2,1)}, bf16[2,320,128]{2,1,0:T(8,128)(2,1)S(1)}, bf16[1792,1792]{1,0:T(8,128)(2,1)}) custom-call(bf16[1024,1792]{1,0:T(8,128)(2,1)} %copy-done.93, bf16[1024,16]{1,0:T(8,128)(2,1)S(1)} %copy-done.15, bf16[16,4224]{1,0:T(8,128)(2,1)S(1)} %copy-done.47, bf16[128,1280]{1,0:T(8,128)(2,1)S(1)} %copy-done.11, ...), custom_call_target="tpu_custom_call" | custom-call | flops 100000000 | bytes 300000 | tf_op jit(solution)/shard_map/project/pallas_call | solution.py:249
  176.2 17.6 %collective-permute-done.19.refs_5_ = bf16[368,896]{1,0:T(8,128)(2,1)S(1)} collective-permute-done((bf16[368,896]{1,0:T(8,128)(2,1)S(1)}, bf16[368,896]{1,0:T(8,128)(2,1)S(1)}, u32[]{:S(2)}, u32[]{:S(2)}) %collective-permute-start.19) | collective-permute-done | bytes 659488 | tf_op jit(solution)/shard_map/ppermute | solution.py:1007
  214.8 18.6 %project.6 = (bf16[1024,1792]{1,0:T(8,128)(2,1)}, bf16[2,320,128]{2,1,0:T(8,128)(2,1)S(1)}, bf16[1792,1792]{1,0:T(8,128)(2,1)}) custom-call(bf16[1024,1792]{1,0:T(8,128)(2,1)} %copy-done.93, bf16[1024,16]{1,0:T(8,128)(2,1)S(1)} %copy-done.15, bf16[16,4224]{1,0:T(8,128)(2,1)S(1)} %copy-done.44, bf16[128,1280]{1,0:T(8,128)(2,1)S(1)} %copy-done.11, ...), custom_call_target="tpu_custom_call" | custom-call | flops 100000000 | bytes 300000 | tf_op jit(solution)/shard_map/project/pallas_call | solution.py:249
  245.6 18.9 %project.7 = (bf16[1024,1792]{1,0:T(8,128)(2,1)}, bf16[2,320,128]{2,1,0:T(8,128)(2,1)S(1)}, bf16[1792,1792]{1,0:T(8,128)(2,1)}) custom-call(bf16[1024,1792]{1,0:T(8,128)(2,1)} %copy-done.93, bf16[1024,16]{1,0:T(8,128)(2,1)S(1)} %copy-done.15, bf16[16,4224]{1,0:T(8,128)(2,1)S(1)} %copy-done.50, bf16[128,1280]{1,0:T(8,128)(2,1)S(1)} %copy-done.11, ...), custom_call_target="tpu_custom_call" | custom-call | flops 100000000 | bytes 300000 | tf_op jit(solution)/shard_map/project/pallas_call | solution.py:249
  264.5 13.7 %collective-permute-done.27 = bf16[912,896]{1,0:T(8,128)(2,1)S(1)} collective-permute-done((bf16[912,896]{1,0:T(8,128)(2,1)}, bf16[912,896]{1,0:T(8,128)(2,1)S(1)}, u32[]{:S(2)}, u32[]{:S(2)}) %collective-permute-start.27) | collective-permute-done | bytes 1634336 | tf_op jit(solution)/shard_map/ppermute | solution.py:1057
  341.1 10.3 %mix_out.1 = (bf16[1024,1792]{1,0:T(8,128)(2,1)}, f32[1024,16]{1,0:T(8,128)S(1)}, bf16[1024,1792]{1,0:T(8,128)(2,1)}) custom-call(bf16[1024,256]{1,0:T(8,128)(2,1)S(1)} %copy-done.65, bf16[1024,256]{1,0:T(8,128)(2,1)S(1)} %copy-done.67, bf16[1024,256]{1,0:T(8,128)(2,1)S(1)} %get-tuple-element.274.refs_2_.refs_13_, ...), custom_call_target="tpu_custom_call" | custom-call | flops 100000000 | bytes 300000 | tf_op jit(solution)/shard_map/mix_out/pallas_call | solution.py:418
  367.9 7.7 norm_two.1
  378.2 46.3 %feed.3 = (f32[1024,1792]{1,0:T(8,128)}, f32[1024,1792]{1,0:T(8,128)}, f32[1024,32]{1,0:T(8,128)}, bf16[16,1280]{1,0:T(8,128)(2,1)}, bf16[16,1280]{1,0:T(8,128)(...) custom-call(bf16[1024,1792]{1,0:T(8,128)(2,1)} %copy-done.9, ...), custom_call_target="tpu_custom_call" | custom-call | flops 100000000 | bytes 300000 | tf_op jit(solution)/shard_map/feed/pallas_call | solution.py:526
  431.6 28.3 %feed.4 = (f32[1024,1792]{1,0:T(8,128)}, f32[1024,1792]{1,0:T(8,128)}, f32[1024,32]{1,0:T(8,128)}, bf16[16,1280]{1,0:T(8,128)(2,1)}, bf16[16,640]{1,0:T(8,128)(2,1)}) custom-call(bf16[1024,1792]{1,0:T(8,128)(2,1)} %copy-done.9, bf16[1024,1792]{1,0:T(8,128)(2,1)} %get-tuple-element.283.refs_1_.upstream, bf16[1024,16]{1,0:T(8,128)(2,1)} %copy-done.69, ...), custom_call_target="tpu_custom_call" | custom-call | flops 100000000 | bytes 300000 | tf_op jit(solution)/shard_map/feed/pallas_call | solution.py:526
  461.1 29.6 %feed.5 = (bf16[1024,1792]{1,0:T(8,128)(2,1)}, bf16[1024,1792]{1,0:T(8,128)(2,1)}, f32[1024,32]{1,0:T(8,128)}, bf16[16,1280]{1,0:T(8,128)(2,1)}, bf16[16,640]{1,0:T(8,128)(2,1)}) custom-call(bf16[1024,1792]{1,0:T(8,128)(2,1)} %copy-done.9, bf16[1024,1792]{1,0:T(8,128)(2,1)} %get-tuple-element.283.refs_1_.upstream, bf16[1024,16]{1,0:T(8,128)(2,1)} %copy-done.69, ...), custom_call_target="tpu_custom_call" | custom-call | flops 100000000 | bytes 300000 | tf_op jit(solution)/shard_map/feed/pallas_call | solution.py:526
  506.5 8.2 back_two.1
  517.3 20.2 %turn.1 = (bf16[1024,1024]{1,0:T(8,128)(2,1)}, bf16[1024,1024]{1,0:T(8,128)(2,1)}, bf16[4,320,128]{2,1,0:T(8,128)(2,1)}, bf16[4,320,128]{2,1,0:T(8,128)(2,1)}, bf16[4,16,256]{2,1,0:T(8,128)(2,1)}) custom-call(bf16[1024,1792]{1,0:T(8,128)(2,1)} %copy-done.18, bf16[1024,16]{1,0:T(8,128)(2,1)} %copy-done.84, bf16[1024,1792]{1,0:T(8,128)(2,1)} %get-tuple-element.312.refs_2_, ...), custom_call_target="tpu_custom_call" | custom-call | flops 100000000 | bytes 300000 | tf_op jit(solution)/shard_map/turn/pallas_call | solution.py:638
  562.9 16.8 %attend_back.4 = (bf16[1024,1792]{1,0:T(8,128)(2,1)}, f32[1024,16]{1,0:T(8,128)S(1)}, bf16[16,1792]{1,0:T(8,128)(2,1)S(1)}) custom-call(bf16[1024,1792]{1,0:T(8,128)(2,1)} %copy-done.2, bf16[4,160,128]{2,1,0:T(8,128)(2,1)S(1)} %copy-done.34, bf16[2,2,256,128]{3,2,1,0:T(8,128)(2,1)S(1)} %copy-done.90, f32[4,160,128]{2,1,0:T(8,128)S(1)} %select_add_fusion.1.later, ...), custom_call_target="tpu_custom_call" | custom-call | flops 100000000 | bytes 300000 | tf_op jit(solution)/shard_map/attend_back/pallas_call | solution.py:775
  579.8 16.2 %attend_back.7 = (bf16[5,16,1792]{2,1,0:T(8,128)(2,1)S(1)}, bf16[1024,1792]{1,0:T(8,128)(2,1)}, f32[1024,16]{1,0:T(8,128)S(1)}) fusion(bf16[5,16,1792]{2,1,0:T(8,128)(2,1)S(1)} %bitcast_dynamic-update-slice_fusion.11, bf16[1024,1792]{1,0:T(8,128)(2,1)S(1)} %copy-done.6, bf16[4,160,128]{2,1,0:T(8,128)(2,1)S(1)} %copy-done.34, ...), kind=kCustom, calls=%fused_computation.137 | custom fusion | flops 100000000 | bytes 13758464 | tf_op jit(solution)/shard_map/attend_back/pallas_call | solution.py:775
  603.9 16.9 %attend_back.6 = (bf16[5,16,1792]{2,1,0:T(8,128)(2,1)}, bf16[1024,1792]{1,0:T(8,128)(2,1)}, f32[1024,16]{1,0:T(8,128)S(1)}) fusion(bf16[5,16,1792]{2,1,0:T(8,128)(2,1)} %copy-done.144, bf16[1024,1792]{1,0:T(8,128)(2,1)} %get-tuple-element.270.proj.refs_19_.refs_20_.refs_25_, bf16[4,160,128]{2,1,0:T(8,128)(2,1)S(1)} %copy-done.62, ...), kind=kCustom, calls=%fused_computation.136 | custom fusion | flops 100000000 | bytes 13070336 | tf_op jit(solution)/shard_map/attend_back/pallas_call | solution.py:775
  631.1 17.0 %attend_back.5 = (bf16[5,16,1792]{2,1,0:T(8,128)(2,1)}, bf16[1024,1792]{1,0:T(8,128)(2,1)}, f32[1024,16]{1,0:T(8,128)S(1)}) fusion(bf16[5,16,1792]{2,1,0:T(8,128)(2,1)} %get-tuple-element.437, bf16[1024,1792]{1,0:T(8,128)(2,1)} %get-tuple-element.275.proj.refs_21_.refs_22_.refs_26_, bf16[4,160,128]{2,1,0:T(8,128)(2,1)S(1)} %copy-done.62, ...), kind=kCustom, calls=%fused_computation.135 | custom fusion | flops 100000000 | bytes 13070336 | tf_op jit(solution)/shard_map/attend_back/pallas_call | solution.py:775
  662.1 24.3 %first_back.2 = (bf16[256,1792]{1,0:T(8,128)(2,1)}, bf16[256,1792]{1,0:T(8,128)(2,1)}) custom-call(s32[1]{0:T(128)} %bitcast.29.core, bf16[2,512,1792]{2,1,0:T(8,128)(2,1)} %bitcast.201, bf16[2,512,1792]{2,1,0:T(8,128)(2,1)} %bitcast.193, bf16[2,512,1792]{2,1,0:T(8,128)(2,1)} %bitcast.195, bf16[2,512,1792]{2,1,0:T(8,128)(2,1)} %bitcast.197, ...), custom_call_target="tpu_custom_call" | custom-call | flops 100000000 | bytes 300000 | tf_op jit(solution)/shard_map/first_back/pallas_call | solution.py:853
  705.8 24.4 %first_back.3 = (bf16[256,1792]{1,0:T(8,128)(2,1)}, bf16[256,1792]{1,0:T(8,128)(2,1)}) custom-call(s32[1]{0:T(128)} %bitcast.29.core, bf16[2,512,1792]{2,1,0:T(8,128)(2,1)} %bitcast.202, bf16[2,512,1792]{2,1,0:T(8,128)(2,1)} %bitcast.194, bf16[2,512,1792]{2,1,0:T(8,128)(2,1)} %bitcast.196, bf16[2,512,1792]{2,1,0:T(8,128)(2,1)} %bitcast.198, ...), custom_call_target="tpu_custom_call" | custom-call | flops 100000000 | bytes 300000 | tf_op jit(solution)/shard_map/first_back/pallas_call | solution.py:853
  760.2 19.4 %collective-permute-done.71.refs_2_ = bf16[256,1792]{1,0:T(8,128)(2,1)} collective-permute-done((bf16[256,1792]{1,0:T(8,128)(2,1)}, bf16[256,1792]{1,0:T(8,128)(2,1)}, u32[]{:S(2)}, u32[]{:S(2)}) %collective-permute-start.71) | collective-permute-done | bytes 917536 | tf_op jit(solution)/shard_map/ppermute | solution.py:1011
  797.6 7.3 collective-permute-done.74.refs_0_
  804.9 18.4 %collective-permute-done.76.refs_2_ = bf16[256,1792]{1,0:T(8,128)(2,1)S(1)} collective-permute-done((bf16[256,1792]{1,0:T(8,128)(2,1)}, bf16[256,1792]{1,0:T(8,128)(2,1)S(1)}, u32[]{:S(2)}, u32[]{:S(2)}) %collective-permute-start.76) | collective-permute-done | bytes 917536 | tf_op jit(solution)/shard_map/ppermute | solution.py:1057
  829.2 18.4 %collective-permute-done.77 = bf16[256,1792]{1,0:T(8,128)(2,1)S(1)} collective-permute-done((bf16[256,1792]{1,0:T(8,128)(2,1)}, bf16[256,1792]{1,0:T(8,128)(2,1)S(1)}, u32[]{:S(2)}, u32[]{:S(2)}) %collective-permute-start.77) | collective-permute-done | bytes 917536 | tf_op jit(solution)/shard_map/ppermute | solution.py:1057
  (660 shorter events, 387.3 us)
Async XLA Ops:
  7.2 226.5 %all-gather.5.cloned.1.call-start = ((), (), s32[]{:S(2)}) async-start(), calls=%async_computation | async-start | bytes 1638400 | tf_op jit(solution)/shard_map/all_gather | solution.py:1327
  10.0 39.3 %collective-permute-start.2 = (bf16[816,896]{1,0:T(8,128)(2,1)}, bf16[816,896]{1,0:T(8,128)(2,1)S(1)}, u32[]{:S(2)}, u32[]{:S(2)}) collective-permute-start(bf16[816,896]{1,0:T(8,128)(2,1)} %pad_maximum_fusion.3), channel_id=1, source_target_pairs={{0,1},{1,0},{2,3},{3,2},{4,5},{5,4},{6,7},{7,6},{8,9},{9,8},{10,11... | collective-permute-start | bytes 4386824 | tf_op jit(solution)/shard_map/ppermute | solution.py:1011
  50.5 44.2 %collective-permute-start.4 = (bf16[816,896]{1,0:T(8,128)(2,1)}, bf16[816,896]{1,0:T(8,128)(2,1)S(1)}, u32[]{:S(2)}, u32[]{:S(2)}) collective-permute-start(bf16[816,896]{1,0:T(8,128)(2,1)} %get-tuple-element.220.rest_0_.refs_10_), channel_id=1, source_target_pairs={{0,8},{8,0},{16,24},{24,16},{1,9},{9,1},{17,25},{25,17},{2,10},{10... | collective-permute-start | bytes 4386824 | tf_op jit(solution)/shard_map/ppermute | solution.py:1007
  51.9 42.7 %collective-permute-start.5 = (bf16[816,896]{1,0:T(8,128)(2,1)}, bf16[816,896]{1,0:T(8,128)(2,1)}, u32[]{:S(2)}, u32[]{:S(2)}) collective-permute-start(bf16[816,896]{1,0:T(8,128)(2,1)} %get-tuple-element.220.rest_0_.refs_10_), channel_id=1, source_target_pairs={{0,16},{8,24},{16,0},{24,8},{1,17},{9,25},{17,1},{25,9},{2,18},{10... | collective-permute-start | bytes 4386824 | tf_op jit(solution)/shard_map/ppermute | solution.py:1007
  95.8 50.5 %collective-permute-start.9 = (bf16[816,896]{1,0:T(8,128)(2,1)}, bf16[816,896]{1,0:T(8,128)(2,1)S(1)}, u32[]{:S(2)}, u32[]{:S(2)}) collective-permute-start(bf16[816,896]{1,0:T(8,128)(2,1)} %get-tuple-element.223.rest_0_.refs_15_), channel_id=1, source_target_pairs={{0,8},{8,0},{16,24},{24,16},{1,9},{9,1},{17,25},{25,17},{2,10},{10... | collective-permute-start | bytes 4386824 | tf_op jit(solution)/shard_map/ppermute | solution.py:1007
  96.4 50.0 %collective-permute-start.10 = (bf16[816,896]{1,0:T(8,128)(2,1)}, bf16[816,896]{1,0:T(8,128)(2,1)}, u32[]{:S(2)}, u32[]{:S(2)}) collective-permute-start(bf16[816,896]{1,0:T(8,128)(2,1)} %get-tuple-element.223.rest_0_.refs_15_), channel_id=1, source_target_pairs={{0,16},{8,24},{16,0},{24,8},{1,17},{9,25},{17,1},{25,9},{2,18},{10... | collective-permute-start | bytes 4386824 | tf_op jit(solution)/shard_map/ppermute | solution.py:1007
  106.2 40.1 %collective-permute-start.15 = (bf16[448,896]{1,0:T(8,128)(2,1)}, bf16[448,896]{1,0:T(8,128)(2,1)S(1)}, u32[]{:S(2)}, u32[]{:S(2)}) collective-permute-start(bf16[448,896]{1,0:T(8,128)(2,1)} %slice.168), channel_id=1, source_target_pairs={{0,16},{8,24},{16,0},{24,8},{1,17},{9,25},{17,1},{25,9},{2,18},{10... | collective-permute-start | bytes 2408456 | tf_op jit(solution)/shard_map/ppermute | solution.py:1007
  147.7 51.6 %collective-permute-start.18 = (bf16[912,896]{1,0:T(8,128)(2,1)}, bf16[912,896]{1,0:T(8,128)(2,1)S(1)}, u32[]{:S(2)}, u32[]{:S(2)}) collective-permute-start(bf16[912,896]{1,0:T(8,128)(2,1)} %get-tuple-element.233), channel_id=1, source_target_pairs={{0,1},{1,0},{2,3},{3,2},{4,5},{5,4},{6,7},{7,6},{8,9},{9,8},{10,11... | collective-permute-start | bytes 4902920 | tf_op jit(solution)/shard_map/ppermute | solution.py:1011
  147.8 50.3 %collective-permute-start.16 = (bf16[816,896]{1,0:T(8,128)(2,1)}, bf16[816,896]{1,0:T(8,128)(2,1)S(1)}, u32[]{:S(2)}, u32[]{:S(2)}) collective-permute-start(bf16[816,896]{1,0:T(8,128)(2,1)} %get-tuple-element.232.rest_0_.refs_20_), channel_id=1, source_target_pairs={{0,8},{8,0},{16,24},{24,16},{1,9},{9,1},{17,25},{25,17},{2,10},{10... | collective-permute-start | bytes 4386824 | tf_op jit(solution)/shard_map/ppermute | solution.py:1007
  149.3 48.8 %collective-permute-start.17 = (bf16[816,896]{1,0:T(8,128)(2,1)}, bf16[816,896]{1,0:T(8,128)(2,1)S(1)}, u32[]{:S(2)}, u32[]{:S(2)}) collective-permute-start(bf16[816,896]{1,0:T(8,128)(2,1)} %get-tuple-element.232.rest_0_.refs_20_), channel_id=1, source_target_pairs={{0,16},{8,24},{16,0},{24,8},{1,17},{9,25},{17,1},{25,9},{2,18},{10... | collective-permute-start | bytes 4386824 | tf_op jit(solution)/shard_map/ppermute | solution.py:1007
  151.0 47.0 %collective-permute-start.20 = (bf16[448,896]{1,0:T(8,128)(2,1)S(1)}, bf16[448,896]{1,0:T(8,128)(2,1)S(1)}, u32[]{:S(2)}, u32[]{:S(2)}) collective-permute-start(bf16[448,896]{1,0:T(8,128)(2,1)S(1)} %slice.170), channel_id=1, source_target_pairs={{0,16},{8,24},{16,0},{24,8},{1,17},{9,25},{17,1},{25,9},{2,18},{10... | collective-permute-start | bytes 2408456 | tf_op jit(solution)/shard_map/ppermute | solution.py:1007
  153.8 40.0 %collective-permute-start.19 = (bf16[368,896]{1,0:T(8,128)(2,1)S(1)}, bf16[368,896]{1,0:T(8,128)(2,1)S(1)}, u32[]{:S(2)}, u32[]{:S(2)}) collective-permute-start(bf16[368,896]{1,0:T(8,128)(2,1)S(1)} %slice.169), channel_id=1, source_target_pairs={{0,8},{8,0},{16,24},{24,16},{1,9},{9,1},{17,25},{25,17},{2,10},{10... | collective-permute-start | bytes 1978376 | tf_op jit(solution)/shard_map/ppermute | solution.py:1007
  202.4 484.2 %all-gather.7.cloned.1.call-start = ((), (), s32[]{:S(2)}) async-start(), calls=%async_computation.1 | async-start | bytes 9175040 | tf_op jit(solution)/shard_map/all_gather | solution.py:1399
  209.4 55.1 %collective-permute-start.26 = (bf16[912,896]{1,0:T(8,128)(2,1)}, bf16[912,896]{1,0:T(8,128)(2,1)}, u32[]{:S(2)}, u32[]{:S(2)}) collective-permute-start(bf16[912,896]{1,0:T(8,128)(2,1)} %get-tuple-element.254.refs_10_), channel_id=1, source_target_pairs={{1,2},{2,1},{5,6},{6,5},{9,10},{10,9},{13,14},{14,13},{17,18},{18,... | collective-permute-start | bytes 4902920 | tf_op jit(solution)/shard_map/ppermute | solution.py:1053
  238.3 39.9 %collective-permute-start.27 = (bf16[912,896]{1,0:T(8,128)(2,1)}, bf16[912,896]{1,0:T(8,128)(2,1)S(1)}, u32[]{:S(2)}, u32[]{:S(2)}) collective-permute-start(bf16[912,896]{1,0:T(8,128)(2,1)} %get-tuple-element.255.refs_4_), channel_id=1, source_target_pairs={{1,0},{2,3},{5,4},{6,7},{9,8},{10,11},{13,12},{14,15},{17,16},{18,... | collective-permute-start | bytes 4902920 | tf_op jit(solution)/shard_map/ppermute | solution.py:1057
  240.2 39.4 %collective-permute-start.24 = (bf16[912,896]{1,0:T(8,128)(2,1)}, bf16[912,896]{1,0:T(8,128)(2,1)S(1)}, u32[]{:S(2)}, u32[]{:S(2)}) collective-permute-start(bf16[912,896]{1,0:T(8,128)(2,1)} %get-tuple-element.254.refs_10_), channel_id=1, source_target_pairs={{0,8},{8,0},{16,24},{24,16},{1,9},{9,1},{17,25},{25,17},{2,10},{10... | collective-permute-start | bytes 4902920 | tf_op jit(solution)/shard_map/ppermute | solution.py:1007
  355.2 69.3 %collective-permute-start.37 = (bf16[912,896]{1,0:T(8,128)(2,1)}, bf16[912,896]{1,0:T(8,128)(2,1)}, u32[]{:S(2)}, u32[]{:S(2)}) collective-permute-start(bf16[912,896]{1,0:T(8,128)(2,1)} %get-tuple-element.286.refs_7_), channel_id=1, source_target_pairs={{0,8},{8,0},{16,24},{24,16},{1,9},{9,1},{17,25},{25,17},{2,10},{10... | collective-permute-start | bytes 4902920 | tf_op jit(solution)/shard_map/ppermute | solution.py:1007
  356.0 68.5 %collective-permute-start.38 = (bf16[912,896]{1,0:T(8,128)(2,1)}, bf16[912,896]{1,0:T(8,128)(2,1)S(1)}, u32[]{:S(2)}, u32[]{:S(2)}) collective-permute-start(bf16[912,896]{1,0:T(8,128)(2,1)} %get-tuple-element.286.refs_7_), channel_id=1, source_target_pairs={{0,16},{8,24},{16,0},{24,8},{1,17},{9,25},{17,1},{25,9},{2,18},{10... | collective-permute-start | bytes 4902920 | tf_op jit(solution)/shard_map/ppermute | solution.py:1007
  361.3 63.1 %collective-permute-start.39 = (bf16[464,896]{1,0:T(8,128)(2,1)}, bf16[464,896]{1,0:T(8,128)(2,1)}, u32[]{:S(2)}, u32[]{:S(2)}) collective-permute-start(bf16[464,896]{1,0:T(8,128)(2,1)} %slice.181), channel_id=1, source_target_pairs={{0,8},{8,0},{16,24},{24,16},{1,9},{9,1},{17,25},{25,17},{2,10},{10... | collective-permute-start | bytes 2494472 | tf_op jit(solution)/shard_map/ppermute | solution.py:1007
  364.1 60.3 %collective-permute-start.40 = (bf16[448,896]{1,0:T(8,128)(2,1)}, bf16[448,896]{1,0:T(8,128)(2,1)}, u32[]{:S(2)}, u32[]{:S(2)}) collective-permute-start(bf16[448,896]{1,0:T(8,128)(2,1)} %slice.182), channel_id=1, source_target_pairs={{0,16},{8,24},{16,0},{24,8},{1,17},{9,25},{17,1},{25,9},{2,18},{10... | collective-permute-start | bytes 2408456 | tf_op jit(solution)/shard_map/ppermute | solution.py:1007
  554.9 42.0 %collective-permute-start.50 = (bf16[4,320,128]{2,1,0:T(8,128)(2,1)}, bf16[4,320,128]{2,1,0:T(8,128)(2,1)}, u32[]{:S(2)}, u32[]{:S(2)}) collective-permute-start(bf16[4,320,128]{2,1,0:T(8,128)(2,1)} %get-tuple-element.348), channel_id=1, source_target_pairs={{0,8},{8,0},{16,24},{24,16},{1,9},{9,1},{17,25},{25,17},{2,10},{10... | collective-permute-start | bytes 983048 | tf_op jit(solution)/shard_map/ppermute | solution.py:1007
  556.3 40.6 %collective-permute-start.51 = (bf16[4,320,128]{2,1,0:T(8,128)(2,1)}, bf16[4,320,128]{2,1,0:T(8,128)(2,1)}, u32[]{:S(2)}, u32[]{:S(2)}) collective-permute-start(bf16[4,320,128]{2,1,0:T(8,128)(2,1)} %get-tuple-element.348), channel_id=1, source_target_pairs={{0,16},{8,24},{16,0},{24,8},{1,17},{9,25},{17,1},{25,9},{2,18},{10... | collective-permute-start | bytes 983048 | tf_op jit(solution)/shard_map/ppermute | solution.py:1007
  556.9 40.1 %collective-permute-start.52 = (bf16[4,320,128]{2,1,0:T(8,128)(2,1)}, bf16[4,320,128]{2,1,0:T(8,128)(2,1)}, u32[]{:S(2)}, u32[]{:S(2)}) collective-permute-start(bf16[4,320,128]{2,1,0:T(8,128)(2,1)} %get-tuple-element.348), channel_id=1, source_target_pairs={{0,24},{8,16},{16,8},{24,0},{1,25},{9,17},{17,9},{25,1},{2,26},{10... | collective-permute-start | bytes 983048 | tf_op jit(solution)/shard_map/ppermute | solution.py:1007
  781.6 41.7 %collective-permute-start.76 = (bf16[256,1792]{1,0:T(8,128)(2,1)}, bf16[256,1792]{1,0:T(8,128)(2,1)S(1)}, u32[]{:S(2)}, u32[]{:S(2)}) collective-permute-start(bf16[256,1792]{1,0:T(8,128)(2,1)} %get-tuple-element.411), channel_id=1, source_target_pairs={{1,0},{2,3},{5,4},{6,7},{9,8},{10,11},{13,12},{14,15},{17,16},{18,... | collective-permute-start | bytes 2752520 | tf_op jit(solution)/shard_map/ppermute | solution.py:1057
  (224 other events, 2502.7 us)
Sparse Core Ops, SparseCore 0:
  202.5 31.1 all-gather.4
  504.6 137.5 all-gather.6

commit v7 on v6

--- a/solution.py
+++ b/solution.py
@@ -22,6 +22,7 @@
 STATE = 160
 CHUNK = 256
 TURN = 1024
+WIDE = 512
 QB = 128
 BACK_QB = 256
 BACK_CHUNK = 512
@@ -882,18 +883,18 @@
 
 def norm_two(own, other, wide, gain, left):
     rows, width = own.shape
-    block = pl.BlockSpec((CHUNK, width), lambda i: (i, 0))
+    block = pl.BlockSpec((WIDE, width), lambda i: (i, 0))
     whole = lambda a: pl.BlockSpec(a.shape, lambda i: (0,) * a.ndim)
     return pl.pallas_call(
         norm_two_kernel,
-        grid=(rows // CHUNK,),
+        grid=(rows // WIDE,),
         out_shape=(
             jax.ShapeDtypeStruct((rows, width), f32),
             jax.ShapeDtypeStruct((rows, width), bf16),
             jax.ShapeDtypeStruct((rows, R), bf16),
         ),
         in_specs=[block, block, block, whole(gain), whole(left)],
-        out_specs=(block, block, pl.BlockSpec((CHUNK, R), lambda i: (i, 0))),
+        out_specs=(block, block, pl.BlockSpec((WIDE, R), lambda i: (i, 0))),
         compiler_params=params(40),
         cost_estimate=pl.CostEstimate(
             flops=100_000_000, bytes_accessed=300_000, transcendentals=0

time: 866 us -> 865 us (level)
  no operation moved by 1% of the time
where the time goes in v7:
time: 865 us; the launch traced here: 855 us
  Pallas kernels  331 us (38%)
  waiting for transfers between devices  158 us (18%)
  other arithmetic  134 us (15%)
  local copies, waits for them, and re-layouts  103 us (12%)
  starting transfers between devices  101 us (12%)
  between operations  16.9 us (2%)
  matrix products  12.5 us (1%)
    pallas_call x3, Pallas kernels, feed(): pl.pallas_call(functools.partial(feed_kernel, slots, last, half, pad, spo...  104 us
    ppermute x8, waiting for transfers between devices, edge(): return lax.ppermute(array, 'tp', [(1, 0), (2, 3)])  82.3 us
    pallas_call x4, Pallas kernels, project(): pl.pallas_call(functools.partial(project_kernel, own), out_shape=(jax.Sha...  74.4 us
    unnamed x341, local copies, waits for them, and re-layouts  50.4 us
    pallas_call x3, other arithmetic, attend_back(): pl.pallas_call(functools.partial(attend_back_kernel, spots), grid=(2,), o...  50.1 us
    pallas_call x2, Pallas kernels, first_back(): pl.pallas_call(first_back_kernel, out_shape=(jax.ShapeDtypeStruct((count,...  48.7 us
    ppermute x40, starting transfers between devices, swap_chip(): return lax.ppermute(array, 'chip', [(i, i ^ bit) for i in range(count)])  44.7 us
    ppermute x40, waiting for transfers between devices, swap_chip(): return lax.ppermute(array, 'chip', [(i, i ^ bit) for i in range(count)])  40.9 us
  transfers between devices with their start and end apart: 80, of which 23 were waited for; matrix products, arithmetic and copies ran while one was open for 22% of the time, Pallas kernels for 35%

profile of v7, /device:TPU:0, one launch (start us, length us, event | category | flops | bytes accessed | tf_op | source)
XLA Modules:
  0.0 855.1 jit_solution(3783116012131647583)
XLA Ops:
  62.3 18.2 %project.4 = (bf16[1024,1792]{1,0:T(8,128)(2,1)S(1)}, bf16[2,320,128]{2,1,0:T(8,128)(2,1)S(1)}, bf16[1792,1792]{1,0:T(8,128)(2,1)}) custom-call(bf16[1024,1792]{1,0:T(8,128)(2,1)} %copy-done.93, bf16[1024,16]{1,0:T(8,128)(2,1)S(1)} %copy-done.14, bf16[16,4224]{1,0:T(8,128)(2,1)S(1)} %get-tuple-element.455.table.refs_4_.refs_6_.refs_3_, ...), custom_call_target="tpu_custom_call" | custom-call | flops 100000000 | bytes 300000 | tf_op jit(solution)/shard_map/project/pallas_call | solution.py:250
  86.1 7.0 collective-permute-done.7
  118.0 16.3 %collective-permute-done.11 = bf16[816,896]{1,0:T(8,128)(2,1)} collective-permute-done((bf16[816,896]{1,0:T(8,128)(2,1)}, bf16[816,896]{1,0:T(8,128)(2,1)}, u32[]{:S(2)}, u32[]{:S(2)}) %collective-permute-start.11) | collective-permute-done | bytes 1462304 | tf_op jit(solution)/shard_map/ppermute | solution.py:1058
  156.8 18.7 %project.5 = (bf16[1024,1792]{1,0:T(8,128)(2,1)}, bf16[2,320,128]{2,1,0:T(8,128)(2,1)S(1)}, bf16[1792,1792]{1,0:T(8,128)(2,1)}) custom-call(bf16[1024,1792]{1,0:T(8,128)(2,1)} %copy-done.93, bf16[1024,16]{1,0:T(8,128)(2,1)S(1)} %copy-done.15, bf16[16,4224]{1,0:T(8,128)(2,1)S(1)} %copy-done.47, bf16[128,1280]{1,0:T(8,128)(2,1)S(1)} %copy-done.11, ...), custom_call_target="tpu_custom_call" | custom-call | flops 100000000 | bytes 300000 | tf_op jit(solution)/shard_map/project/pallas_call | solution.py:250
  176.2 17.6 %collective-permute-done.19.refs_5_ = bf16[368,896]{1,0:T(8,128)(2,1)S(1)} collective-permute-done((bf16[368,896]{1,0:T(8,128)(2,1)S(1)}, bf16[368,896]{1,0:T(8,128)(2,1)S(1)}, u32[]{:S(2)}, u32[]{:S(2)}) %collective-permute-start.19) | collective-permute-done | bytes 659488 | tf_op jit(solution)/shard_map/ppermute | solution.py:1008
  214.8 18.6 %project.6 = (bf16[1024,1792]{1,0:T(8,128)(2,1)}, bf16[2,320,128]{2,1,0:T(8,128)(2,1)S(1)}, bf16[1792,1792]{1,0:T(8,128)(2,1)}) custom-call(bf16[1024,1792]{1,0:T(8,128)(2,1)} %copy-done.93, bf16[1024,16]{1,0:T(8,128)(2,1)S(1)} %copy-done.15, bf16[16,4224]{1,0:T(8,128)(2,1)S(1)} %copy-done.44, bf16[128,1280]{1,0:T(8,128)(2,1)S(1)} %copy-done.11, ...), custom_call_target="tpu_custom_call" | custom-call | flops 100000000 | bytes 300000 | tf_op jit(solution)/shard_map/project/pallas_call | solution.py:250
  245.6 18.9 %project.7 = (bf16[1024,1792]{1,0:T(8,128)(2,1)}, bf16[2,320,128]{2,1,0:T(8,128)(2,1)S(1)}, bf16[1792,1792]{1,0:T(8,128)(2,1)}) custom-call(bf16[1024,1792]{1,0:T(8,128)(2,1)} %copy-done.93, bf16[1024,16]{1,0:T(8,128)(2,1)S(1)} %copy-done.15, bf16[16,4224]{1,0:T(8,128)(2,1)S(1)} %copy-done.50, bf16[128,1280]{1,0:T(8,128)(2,1)S(1)} %copy-done.11, ...), custom_call_target="tpu_custom_call" | custom-call | flops 100000000 | bytes 300000 | tf_op jit(solution)/shard_map/project/pallas_call | solution.py:250
  264.5 13.7 %collective-permute-done.27 = bf16[912,896]{1,0:T(8,128)(2,1)S(1)} collective-permute-done((bf16[912,896]{1,0:T(8,128)(2,1)}, bf16[912,896]{1,0:T(8,128)(2,1)S(1)}, u32[]{:S(2)}, u32[]{:S(2)}) %collective-permute-start.27) | collective-permute-done | bytes 1634336 | tf_op jit(solution)/shard_map/ppermute | solution.py:1058
  341.1 10.3 %mix_out.1 = (bf16[1024,1792]{1,0:T(8,128)(2,1)}, f32[1024,16]{1,0:T(8,128)S(1)}, bf16[1024,1792]{1,0:T(8,128)(2,1)}) custom-call(bf16[1024,256]{1,0:T(8,128)(2,1)S(1)} %copy-done.65, bf16[1024,256]{1,0:T(8,128)(2,1)S(1)} %copy-done.67, bf16[1024,256]{1,0:T(8,128)(2,1)S(1)} %get-tuple-element.274.refs_2_.refs_13_, ...), custom_call_target="tpu_custom_call" | custom-call | flops 100000000 | bytes 300000 | tf_op jit(solution)/shard_map/mix_out/pallas_call | solution.py:419
  377.2 46.3 %feed.3 = (f32[1024,1792]{1,0:T(8,128)}, f32[1024,1792]{1,0:T(8,128)}, f32[1024,32]{1,0:T(8,128)}, bf16[16,1280]{1,0:T(8,128)(2,1)}, bf16[16,1280]{1,0:T(8,128)(...) custom-call(bf16[1024,1792]{1,0:T(8,128)(2,1)} %copy-done.9, ...), custom_call_target="tpu_custom_call" | custom-call | flops 100000000 | bytes 300000 | tf_op jit(solution)/shard_map/feed/pallas_call | solution.py:527
  430.6 28.3 %feed.4 = (f32[1024,1792]{1,0:T(8,128)}, f32[1024,1792]{1,0:T(8,128)}, f32[1024,32]{1,0:T(8,128)}, bf16[16,1280]{1,0:T(8,128)(2,1)}, bf16[16,640]{1,0:T(8,128)(2,1)}) custom-call(bf16[1024,1792]{1,0:T(8,128)(2,1)} %copy-done.9, bf16[1024,1792]{1,0:T(8,128)(2,1)} %get-tuple-element.283.refs_1_.upstream, bf16[1024,16]{1,0:T(8,128)(2,1)} %copy-done.69, ...), custom_call_target="tpu_custom_call" | custom-call | flops 100000000 | bytes 300000 | tf_op jit(solution)/shard_map/feed/pallas_call | solution.py:527
  460.1 29.6 %feed.5 = (bf16[1024,1792]{1,0:T(8,128)(2,1)}, bf16[1024,1792]{1,0:T(8,128)(2,1)}, f32[1024,32]{1,0:T(8,128)}, bf16[16,1280]{1,0:T(8,128)(2,1)}, bf16[16,640]{1,0:T(8,128)(2,1)}) custom-call(bf16[1024,1792]{1,0:T(8,128)(2,1)} %copy-done.9, bf16[1024,1792]{1,0:T(8,128)(2,1)} %get-tuple-element.283.refs_1_.upstream, bf16[1024,16]{1,0:T(8,128)(2,1)} %copy-done.69, ...), custom_call_target="tpu_custom_call" | custom-call | flops 100000000 | bytes 300000 | tf_op jit(solution)/shard_map/feed/pallas_call | solution.py:527
  505.5 8.2 back_two.1
  516.3 20.2 %turn.1 = (bf16[1024,1024]{1,0:T(8,128)(2,1)}, bf16[1024,1024]{1,0:T(8,128)(2,1)}, bf16[4,320,128]{2,1,0:T(8,128)(2,1)}, bf16[4,320,128]{2,1,0:T(8,128)(2,1)}, bf16[4,16,256]{2,1,0:T(8,128)(2,1)}) custom-call(bf16[1024,1792]{1,0:T(8,128)(2,1)} %copy-done.18, bf16[1024,16]{1,0:T(8,128)(2,1)} %copy-done.84, bf16[1024,1792]{1,0:T(8,128)(2,1)} %get-tuple-element.312.refs_2_, ...), custom_call_target="tpu_custom_call" | custom-call | flops 100000000 | bytes 300000 | tf_op jit(solution)/shard_map/turn/pallas_call | solution.py:639
  562.0 16.8 %attend_back.4 = (bf16[1024,1792]{1,0:T(8,128)(2,1)}, f32[1024,16]{1,0:T(8,128)S(1)}, bf16[16,1792]{1,0:T(8,128)(2,1)S(1)}) custom-call(bf16[1024,1792]{1,0:T(8,128)(2,1)} %copy-done.2, bf16[4,160,128]{2,1,0:T(8,128)(2,1)S(1)} %copy-done.34, bf16[2,2,256,128]{3,2,1,0:T(8,128)(2,1)S(1)} %copy-done.90, f32[4,160,128]{2,1,0:T(8,128)S(1)} %select_add_fusion.1.later, ...), custom_call_target="tpu_custom_call" | custom-call | flops 100000000 | bytes 300000 | tf_op jit(solution)/shard_map/attend_back/pallas_call | solution.py:776
  578.8 16.2 %attend_back.7 = (bf16[5,16,1792]{2,1,0:T(8,128)(2,1)S(1)}, bf16[1024,1792]{1,0:T(8,128)(2,1)}, f32[1024,16]{1,0:T(8,128)S(1)}) fusion(bf16[5,16,1792]{2,1,0:T(8,128)(2,1)S(1)} %bitcast_dynamic-update-slice_fusion.11, bf16[1024,1792]{1,0:T(8,128)(2,1)S(1)} %copy-done.6, bf16[4,160,128]{2,1,0:T(8,128)(2,1)S(1)} %copy-done.34, ...), kind=kCustom, calls=%fused_computation.137 | custom fusion | flops 100000000 | bytes 13758464 | tf_op jit(solution)/shard_map/attend_back/pallas_call | solution.py:776
  603.0 16.9 %attend_back.6 = (bf16[5,16,1792]{2,1,0:T(8,128)(2,1)}, bf16[1024,1792]{1,0:T(8,128)(2,1)}, f32[1024,16]{1,0:T(8,128)S(1)}) fusion(bf16[5,16,1792]{2,1,0:T(8,128)(2,1)} %copy-done.144, bf16[1024,1792]{1,0:T(8,128)(2,1)} %get-tuple-element.270.proj.refs_19_.refs_20_.refs_25_, bf16[4,160,128]{2,1,0:T(8,128)(2,1)S(1)} %copy-done.62, ...), kind=kCustom, calls=%fused_computation.136 | custom fusion | flops 100000000 | bytes 13070336 | tf_op jit(solution)/shard_map/attend_back/pallas_call | solution.py:776
  630.1 17.0 %attend_back.5 = (bf16[5,16,1792]{2,1,0:T(8,128)(2,1)}, bf16[1024,1792]{1,0:T(8,128)(2,1)}, f32[1024,16]{1,0:T(8,128)S(1)}) fusion(bf16[5,16,1792]{2,1,0:T(8,128)(2,1)} %get-tuple-element.437, bf16[1024,1792]{1,0:T(8,128)(2,1)} %get-tuple-element.275.proj.refs_21_.refs_22_.refs_26_, bf16[4,160,128]{2,1,0:T(8,128)(2,1)S(1)} %copy-done.62, ...), kind=kCustom, calls=%fused_computation.135 | custom fusion | flops 100000000 | bytes 13070336 | tf_op jit(solution)/shard_map/attend_back/pallas_call | solution.py:776
  661.1 24.3 %first_back.2 = (bf16[256,1792]{1,0:T(8,128)(2,1)}, bf16[256,1792]{1,0:T(8,128)(2,1)}) custom-call(s32[1]{0:T(128)} %bitcast.29.core, bf16[2,512,1792]{2,1,0:T(8,128)(2,1)} %bitcast.201, bf16[2,512,1792]{2,1,0:T(8,128)(2,1)} %bitcast.193, bf16[2,512,1792]{2,1,0:T(8,128)(2,1)} %bitcast.195, bf16[2,512,1792]{2,1,0:T(8,128)(2,1)} %bitcast.197, ...), custom_call_target="tpu_custom_call" | custom-call | flops 100000000 | bytes 300000 | tf_op jit(solution)/shard_map/first_back/pallas_call | solution.py:854
  704.8 24.4 %first_back.3 = (bf16[256,1792]{1,0:T(8,128)(2,1)}, bf16[256,1792]{1,0:T(8,128)(2,1)}) custom-call(s32[1]{0:T(128)} %bitcast.29.core, bf16[2,512,1792]{2,1,0:T(8,128)(2,1)} %bitcast.202, bf16[2,512,1792]{2,1,0:T(8,128)(2,1)} %bitcast.194, bf16[2,512,1792]{2,1,0:T(8,128)(2,1)} %bitcast.196, bf16[2,512,1792]{2,1,0:T(8,128)(2,1)} %bitcast.198, ...), custom_call_target="tpu_custom_call" | custom-call | flops 100000000 | bytes 300000 | tf_op jit(solution)/shard_map/first_back/pallas_call | solution.py:854
  759.2 19.4 %collective-permute-done.71.refs_2_ = bf16[256,1792]{1,0:T(8,128)(2,1)} collective-permute-done((bf16[256,1792]{1,0:T(8,128)(2,1)}, bf16[256,1792]{1,0:T(8,128)(2,1)}, u32[]{:S(2)}, u32[]{:S(2)}) %collective-permute-start.71) | collective-permute-done | bytes 917536 | tf_op jit(solution)/shard_map/ppermute | solution.py:1012
  796.7 7.3 collective-permute-done.74.refs_0_
  803.9 18.4 %collective-permute-done.76.refs_2_ = bf16[256,1792]{1,0:T(8,128)(2,1)S(1)} collective-permute-done((bf16[256,1792]{1,0:T(8,128)(2,1)}, bf16[256,1792]{1,0:T(8,128)(2,1)S(1)}, u32[]{:S(2)}, u32[]{:S(2)}) %collective-permute-start.76) | collective-permute-done | bytes 917536 | tf_op jit(solution)/shard_map/ppermute | solution.py:1058
  828.2 18.4 %collective-permute-done.77 = bf16[256,1792]{1,0:T(8,128)(2,1)S(1)} collective-permute-done((bf16[256,1792]{1,0:T(8,128)(2,1)}, bf16[256,1792]{1,0:T(8,128)(2,1)S(1)}, u32[]{:S(2)}, u32[]{:S(2)}) %collective-permute-start.77) | collective-permute-done | bytes 917536 | tf_op jit(solution)/shard_map/ppermute | solution.py:1058
  (660 shorter events, 387.0 us)
Async XLA Ops:
  7.2 226.5 %all-gather.5.cloned.1.call-start = ((), (), s32[]{:S(2)}) async-start(), calls=%async_computation | async-start | bytes 1638400 | tf_op jit(solution)/shard_map/all_gather | solution.py:1328
  10.0 39.3 %collective-permute-start.2 = (bf16[816,896]{1,0:T(8,128)(2,1)}, bf16[816,896]{1,0:T(8,128)(2,1)S(1)}, u32[]{:S(2)}, u32[]{:S(2)}) collective-permute-start(bf16[816,896]{1,0:T(8,128)(2,1)} %pad_maximum_fusion.3), channel_id=1, source_target_pairs={{0,1},{1,0},{2,3},{3,2},{4,5},{5,4},{6,7},{7,6},{8,9},{9,8},{10,11... | collective-permute-start | bytes 4386824 | tf_op jit(solution)/shard_map/ppermute | solution.py:1012
  50.5 44.2 %collective-permute-start.4 = (bf16[816,896]{1,0:T(8,128)(2,1)}, bf16[816,896]{1,0:T(8,128)(2,1)S(1)}, u32[]{:S(2)}, u32[]{:S(2)}) collective-permute-start(bf16[816,896]{1,0:T(8,128)(2,1)} %get-tuple-element.220.rest_0_.refs_10_), channel_id=1, source_target_pairs={{0,8},{8,0},{16,24},{24,16},{1,9},{9,1},{17,25},{25,17},{2,10},{10... | collective-permute-start | bytes 4386824 | tf_op jit(solution)/shard_map/ppermute | solution.py:1008
  51.9 42.7 %collective-permute-start.5 = (bf16[816,896]{1,0:T(8,128)(2,1)}, bf16[816,896]{1,0:T(8,128)(2,1)}, u32[]{:S(2)}, u32[]{:S(2)}) collective-permute-start(bf16[816,896]{1,0:T(8,128)(2,1)} %get-tuple-element.220.rest_0_.refs_10_), channel_id=1, source_target_pairs={{0,16},{8,24},{16,0},{24,8},{1,17},{9,25},{17,1},{25,9},{2,18},{10... | collective-permute-start | bytes 4386824 | tf_op jit(solution)/shard_map/ppermute | solution.py:1008
  95.8 50.5 %collective-permute-start.9 = (bf16[816,896]{1,0:T(8,128)(2,1)}, bf16[816,896]{1,0:T(8,128)(2,1)S(1)}, u32[]{:S(2)}, u32[]{:S(2)}) collective-permute-start(bf16[816,896]{1,0:T(8,128)(2,1)} %get-tuple-element.223.rest_0_.refs_15_), channel_id=1, source_target_pairs={{0,8},{8,0},{16,24},{24,16},{1,9},{9,1},{17,25},{25,17},{2,10},{10... | collective-permute-start | bytes 4386824 | tf_op jit(solution)/shard_map/ppermute | solution.py:1008
  96.4 50.0 %collective-permute-start.10 = (bf16[816,896]{1,0:T(8,128)(2,1)}, bf16[816,896]{1,0:T(8,128)(2,1)}, u32[]{:S(2)}, u32[]{:S(2)}) collective-permute-start(bf16[816,896]{1,0:T(8,128)(2,1)} %get-tuple-element.223.rest_0_.refs_15_), channel_id=1, source_target_pairs={{0,16},{8,24},{16,0},{24,8},{1,17},{9,25},{17,1},{25,9},{2,18},{10... | collective-permute-start | bytes 4386824 | tf_op jit(solution)/shard_map/ppermute | solution.py:1008
  106.2 40.1 %collective-permute-start.15 = (bf16[448,896]{1,0:T(8,128)(2,1)}, bf16[448,896]{1,0:T(8,128)(2,1)S(1)}, u32[]{:S(2)}, u32[]{:S(2)}) collective-permute-start(bf16[448,896]{1,0:T(8,128)(2,1)} %slice.168), channel_id=1, source_target_pairs={{0,16},{8,24},{16,0},{24,8},{1,17},{9,25},{17,1},{25,9},{2,18},{10... | collective-permute-start | bytes 2408456 | tf_op jit(solution)/shard_map/ppermute | solution.py:1008
  147.7 51.6 %collective-permute-start.18 = (bf16[912,896]{1,0:T(8,128)(2,1)}, bf16[912,896]{1,0:T(8,128)(2,1)S(1)}, u32[]{:S(2)}, u32[]{:S(2)}) collective-permute-start(bf16[912,896]{1,0:T(8,128)(2,1)} %get-tuple-element.233), channel_id=1, source_target_pairs={{0,1},{1,0},{2,3},{3,2},{4,5},{5,4},{6,7},{7,6},{8,9},{9,8},{10,11... | collective-permute-start | bytes 4902920 | tf_op jit(solution)/shard_map/ppermute | solution.py:1012
  147.8 50.3 %collective-permute-start.16 = (bf16[816,896]{1,0:T(8,128)(2,1)}, bf16[816,896]{1,0:T(8,128)(2,1)S(1)}, u32[]{:S(2)}, u32[]{:S(2)}) collective-permute-start(bf16[816,896]{1,0:T(8,128)(2,1)} %get-tuple-element.232.rest_0_.refs_20_), channel_id=1, source_target_pairs={{0,8},{8,0},{16,24},{24,16},{1,9},{9,1},{17,25},{25,17},{2,10},{10... | collective-permute-start | bytes 4386824 | tf_op jit(solution)/shard_map/ppermute | solution.py:1008
  149.3 48.8 %collective-permute-start.17 = (bf16[816,896]{1,0:T(8,128)(2,1)}, bf16[816,896]{1,0:T(8,128)(2,1)S(1)}, u32[]{:S(2)}, u32[]{:S(2)}) collective-permute-start(bf16[816,896]{1,0:T(8,128)(2,1)} %get-tuple-element.232.rest_0_.refs_20_), channel_id=1, source_target_pairs={{0,16},{8,24},{16,0},{24,8},{1,17},{9,25},{17,1},{25,9},{2,18},{10... | collective-permute-start | bytes 4386824 | tf_op jit(solution)/shard_map/ppermute | solution.py:1008
  151.0 47.0 %collective-permute-start.20 = (bf16[448,896]{1,0:T(8,128)(2,1)S(1)}, bf16[448,896]{1,0:T(8,128)(2,1)S(1)}, u32[]{:S(2)}, u32[]{:S(2)}) collective-permute-start(bf16[448,896]{1,0:T(8,128)(2,1)S(1)} %slice.170), channel_id=1, source_target_pairs={{0,16},{8,24},{16,0},{24,8},{1,17},{9,25},{17,1},{25,9},{2,18},{10... | collective-permute-start | bytes 2408456 | tf_op jit(solution)/shard_map/ppermute | solution.py:1008
  153.8 40.0 %collective-permute-start.19 = (bf16[368,896]{1,0:T(8,128)(2,1)S(1)}, bf16[368,896]{1,0:T(8,128)(2,1)S(1)}, u32[]{:S(2)}, u32[]{:S(2)}) collective-permute-start(bf16[368,896]{1,0:T(8,128)(2,1)S(1)} %slice.169), channel_id=1, source_target_pairs={{0,8},{8,0},{16,24},{24,16},{1,9},{9,1},{17,25},{25,17},{2,10},{10... | collective-permute-start | bytes 1978376 | tf_op jit(solution)/shard_map/ppermute | solution.py:1008
  202.4 483.2 %all-gather.7.cloned.1.call-start = ((), (), s32[]{:S(2)}) async-start(), calls=%async_computation.1 | async-start | bytes 9175040 | tf_op jit(solution)/shard_map/all_gather | solution.py:1400
  209.4 55.1 %collective-permute-start.26 = (bf16[912,896]{1,0:T(8,128)(2,1)}, bf16[912,896]{1,0:T(8,128)(2,1)}, u32[]{:S(2)}, u32[]{:S(2)}) collective-permute-start(bf16[912,896]{1,0:T(8,128)(2,1)} %get-tuple-element.254.refs_10_), channel_id=1, source_target_pairs={{1,2},{2,1},{5,6},{6,5},{9,10},{10,9},{13,14},{14,13},{17,18},{18,... | collective-permute-start | bytes 4902920 | tf_op jit(solution)/shard_map/ppermute | solution.py:1054
  238.3 39.9 %collective-permute-start.27 = (bf16[912,896]{1,0:T(8,128)(2,1)}, bf16[912,896]{1,0:T(8,128)(2,1)S(1)}, u32[]{:S(2)}, u32[]{:S(2)}) collective-permute-start(bf16[912,896]{1,0:T(8,128)(2,1)} %get-tuple-element.255.refs_4_), channel_id=1, source_target_pairs={{1,0},{2,3},{5,4},{6,7},{9,8},{10,11},{13,12},{14,15},{17,16},{18,... | collective-permute-start | bytes 4902920 | tf_op jit(solution)/shard_map/ppermute | solution.py:1058
  240.2 39.4 %collective-permute-start.24 = (bf16[912,896]{1,0:T(8,128)(2,1)}, bf16[912,896]{1,0:T(8,128)(2,1)S(1)}, u32[]{:S(2)}, u32[]{:S(2)}) collective-permute-start(bf16[912,896]{1,0:T(8,128)(2,1)} %get-tuple-element.254.refs_10_), channel_id=1, source_target_pairs={{0,8},{8,0},{16,24},{24,16},{1,9},{9,1},{17,25},{25,17},{2,10},{10... | collective-permute-start | bytes 4902920 | tf_op jit(solution)/shard_map/ppermute | solution.py:1008
  355.2 68.3 %collective-permute-start.37 = (bf16[912,896]{1,0:T(8,128)(2,1)}, bf16[912,896]{1,0:T(8,128)(2,1)}, u32[]{:S(2)}, u32[]{:S(2)}) collective-permute-start(bf16[912,896]{1,0:T(8,128)(2,1)} %get-tuple-element.286.refs_7_), channel_id=1, source_target_pairs={{0,8},{8,0},{16,24},{24,16},{1,9},{9,1},{17,25},{25,17},{2,10},{10... | collective-permute-start | bytes 4902920 | tf_op jit(solution)/shard_map/ppermute | solution.py:1008
  356.0 67.5 %collective-permute-start.38 = (bf16[912,896]{1,0:T(8,128)(2,1)}, bf16[912,896]{1,0:T(8,128)(2,1)S(1)}, u32[]{:S(2)}, u32[]{:S(2)}) collective-permute-start(bf16[912,896]{1,0:T(8,128)(2,1)} %get-tuple-element.286.refs_7_), channel_id=1, source_target_pairs={{0,16},{8,24},{16,0},{24,8},{1,17},{9,25},{17,1},{25,9},{2,18},{10... | collective-permute-start | bytes 4902920 | tf_op jit(solution)/shard_map/ppermute | solution.py:1008
  361.3 62.1 %collective-permute-start.39 = (bf16[464,896]{1,0:T(8,128)(2,1)}, bf16[464,896]{1,0:T(8,128)(2,1)}, u32[]{:S(2)}, u32[]{:S(2)}) collective-permute-start(bf16[464,896]{1,0:T(8,128)(2,1)} %slice.181), channel_id=1, source_target_pairs={{0,8},{8,0},{16,24},{24,16},{1,9},{9,1},{17,25},{25,17},{2,10},{10... | collective-permute-start | bytes 2494472 | tf_op jit(solution)/shard_map/ppermute | solution.py:1008
  364.1 59.3 %collective-permute-start.40 = (bf16[448,896]{1,0:T(8,128)(2,1)}, bf16[448,896]{1,0:T(8,128)(2,1)}, u32[]{:S(2)}, u32[]{:S(2)}) collective-permute-start(bf16[448,896]{1,0:T(8,128)(2,1)} %slice.182), channel_id=1, source_target_pairs={{0,16},{8,24},{16,0},{24,8},{1,17},{9,25},{17,1},{25,9},{2,18},{10... | collective-permute-start | bytes 2408456 | tf_op jit(solution)/shard_map/ppermute | solution.py:1008
  553.9 42.0 %collective-permute-start.50 = (bf16[4,320,128]{2,1,0:T(8,128)(2,1)}, bf16[4,320,128]{2,1,0:T(8,128)(2,1)}, u32[]{:S(2)}, u32[]{:S(2)}) collective-permute-start(bf16[4,320,128]{2,1,0:T(8,128)(2,1)} %get-tuple-element.348), channel_id=1, source_target_pairs={{0,8},{8,0},{16,24},{24,16},{1,9},{9,1},{17,25},{25,17},{2,10},{10... | collective-permute-start | bytes 983048 | tf_op jit(solution)/shard_map/ppermute | solution.py:1008
  555.4 40.6 %collective-permute-start.51 = (bf16[4,320,128]{2,1,0:T(8,128)(2,1)}, bf16[4,320,128]{2,1,0:T(8,128)(2,1)}, u32[]{:S(2)}, u32[]{:S(2)}) collective-permute-start(bf16[4,320,128]{2,1,0:T(8,128)(2,1)} %get-tuple-element.348), channel_id=1, source_target_pairs={{0,16},{8,24},{16,0},{24,8},{1,17},{9,25},{17,1},{25,9},{2,18},{10... | collective-permute-start | bytes 983048 | tf_op jit(solution)/shard_map/ppermute | solution.py:1008
  555.9 40.1 %collective-permute-start.52 = (bf16[4,320,128]{2,1,0:T(8,128)(2,1)}, bf16[4,320,128]{2,1,0:T(8,128)(2,1)}, u32[]{:S(2)}, u32[]{:S(2)}) collective-permute-start(bf16[4,320,128]{2,1,0:T(8,128)(2,1)} %get-tuple-element.348), channel_id=1, source_target_pairs={{0,24},{8,16},{16,8},{24,0},{1,25},{9,17},{17,9},{25,1},{2,26},{10... | collective-permute-start | bytes 983048 | tf_op jit(solution)/shard_map/ppermute | solution.py:1008
  780.6 41.7 %collective-permute-start.76 = (bf16[256,1792]{1,0:T(8,128)(2,1)}, bf16[256,1792]{1,0:T(8,128)(2,1)S(1)}, u32[]{:S(2)}, u32[]{:S(2)}) collective-permute-start(bf16[256,1792]{1,0:T(8,128)(2,1)} %get-tuple-element.411), channel_id=1, source_target_pairs={{1,0},{2,3},{5,4},{6,7},{9,8},{10,11},{13,12},{14,15},{17,16},{18,... | collective-permute-start | bytes 2752520 | tf_op jit(solution)/shard_map/ppermute | solution.py:1058
  (224 other events, 2502.8 us)
Sparse Core Ops, SparseCore 0:
  202.5 31.1 all-gather.4
  503.6 137.5 all-gather.6
